TPU v7x, 512 devices: a whole 4x4x16 slice. The times are simulated.
512 devices in a mesh: tok: 16 (over z), exp: 32 (over y, x, core).
Axes of the slice: x: 4, y: 4, z: 16, core: 2. Of those that a mesh axis runs over, the one named last changes fastest.
Arguments:
- tokens: bfloat16 [4096, 4096], P('exp', 'tok'), may hold values from -6 to 6
- picked_blocks: int32 [8, 8], replicated, may hold values from 0 to 31, as said below
- gate_scale: float32 [8, 1024], replicated, may hold values from 0.1 to 1
- w_gate: bfloat16 [32, 4096, 2048], P('exp', None, 'tok'), may hold values from -0.09375 to 0.09375
- w_up: bfloat16 [32, 4096, 2048], P('exp', None, 'tok'), may hold values from -0.09375 to 0.09375
- w_down: bfloat16 [32, 2048, 4096], P('exp', None, 'tok'), may hold values from -0.0625 to 0.0625
Outputs:
- combined: bfloat16 [4096, 4096], P('exp', 'tok')
Inputs may be any that keep to these rules, and one draw needn't show every extreme that they name: `picked_blocks`: each row names 8 different blocks, and every block is named by exactly two experts.
All inputs are finite; a program needn't handle non-finite values.
Results may differ from a plain program's by a relative error of at most 0.0049.
Values may be sent and summed in bfloat16 or wider, within the bound.
No kernel may reach another device: no remote copies, remote signals or barrier semaphores. Data moves between devices by JAX's collectives and lax.ppermute only.
A program may use at most 64 MiB of HBM per device.

v0:
```python
import jax
import jax.numpy as jnp
from jax import lax
from jax.sharding import PartitionSpec as P

BLOCK = 128
SPAN = 4


def shards(tokens, picked_blocks, gate_scale, w_gate, w_up, w_down):
    owners = lax.axis_size("exp")
    position = lax.axis_index("exp")
    expert = position // SPAN
    own_rows, feature_count = tokens.shape
    blocks_all = own_rows * owners // BLOCK
    chosen = lax.dynamic_index_in_dim(picked_blocks, expert, 0, keepdims=False)
    scale_row = lax.dynamic_index_in_dim(gate_scale, expert, 0, keepdims=False)
    block_count = chosen.shape[0]
    row_total = block_count * BLOCK
    gathered = lax.all_gather(tokens, "exp", axis=0, tiled=True)
    selected = gathered.reshape(blocks_all, BLOCK, feature_count)[chosen].reshape(
        row_total, feature_count
    )
    gate_local = w_gate[0]
    up_local = w_up[0]
    down_local = w_down[0]
    full_rows = lax.all_gather(selected, "tok", axis=1, tiled=True)
    gate_sum = jnp.dot(full_rows, gate_local, preferred_element_type=jnp.float32)
    up_sum = jnp.dot(full_rows, up_local, preferred_element_type=jnp.float32)
    hidden = (jax.nn.silu(gate_sum) * up_sum).astype(jnp.bfloat16)
    output_rows = jnp.dot(
        lax.all_gather(hidden, "tok", axis=1, tiled=True),
        down_local,
        preferred_element_type=jnp.float32,
    )
    scaled = output_rows * scale_row[:, None]
    buffer = jnp.zeros((blocks_all, BLOCK, feature_count), jnp.float32)
    buffer = (
        buffer.at[chosen]
        .set(scaled.reshape(block_count, BLOCK, feature_count))
        .reshape(blocks_all * BLOCK, feature_count)
    )
    return lax.psum_scatter(buffer, "exp", scatter_dimension=0, tiled=True).astype(jnp.bfloat16)


def solution(mesh):
    return jax.shard_map(
        shards,
        mesh=mesh,
        in_specs=(
            P("exp", "tok"),
            P(),
            P(),
            P("exp", None, "tok"),
            P("exp", None, "tok"),
            P("exp", None, "tok"),
        ),
        out_specs=P("exp", "tok"),
        check_vma=False,
    )
```

profile of v0, /device:TPU:1, one launch (start us, length us, event | category | flops | bytes accessed | tf_op | source)
XLA Modules:
  0.0 423.7 jit_solution(6507193222056906932)
XLA Ops:
  6.5 0.0 copy-start
  6.5 0.0 all-gather.4.cloned.1.call-start
  6.5 0.7 all-gather.4.cloned.1.call-update
  7.3 0.0 all-gather.6.cloned.1.call-start
  7.3 0.7 fusion.5
  8.0 67.4 %all-gather.4.cloned.1.call-done = bf16[4096,256]{1,0:T(8,128)(2,1)} async-done(((bf16[128,256]{1,0:T(8,128)(2,1)}), bf16[4096,256]{1,0:T(8,128)(2,1)}) %all-gather.4.cloned.1.call-update) | async-done | bytes 2097168 | tf_op jit(solution)/shard_map/all_gather | solution.py:20
  75.4 3.0 gather_fusion
  78.4 0.0 all-gather.6.cloned.1.call-update
  78.4 0.0 copy-start.2
  78.4 0.0 all-gather.8.cloned.1.call-start
  78.5 120.3 %all-gather.6.cloned.1.call-done = bf16[1024,4096]{1,0:T(8,128)(2,1)} async-done(((bf16[1024,256]{1,0:T(8,128)(2,1)}), bf16[1024,4096]{1,0:T(8,128)(2,1)}) %all-gather.6.cloned.1.call-update) | async-done | bytes 8388624 | tf_op jit(solution)/shard_map/all_gather | solution.py:27
  198.8 0.0 copy-start.1
  198.8 6.1 %fusion.3 = f32[1024,128]{1,0:T(8,128)S(1)} fusion(bf16[1024,4096]{1,0:T(8,128)(2,1)} %all-gather.6.cloned.1.call-done, bf16[1,4096,128]{2,1,0:T(8,128)(2,1)} %param.9), kind=kOutput, calls=%fused_computation.7 | convolution fusion | flops 1073741824 | bytes 9961472 | tf_op jit(solution)/shard_map/dot_general | solution.py:28
  204.9 0.0 copy-done.2
  204.9 0.0 copy-done.1
  204.9 3.0 fusion
  207.9 0.0 all-gather.8.cloned.1.call-update
  208.0 0.0 reduce-scatter.2.cloned.1.call-start
  208.0 0.8 constant_dynamic-slice_fusion
  208.8 88.8 %all-gather.8.cloned.1.call-done = bf16[1024,2048]{1,0:T(8,128)(2,1)} async-done(((bf16[1024,128]{1,0:T(8,128)(2,1)}), bf16[1024,2048]{1,0:T(8,128)(2,1)}) %all-gather.8.cloned.1.call-update) | async-done | bytes 4194320 | tf_op jit(solution)/shard_map/all_gather | solution.py:32
  297.6 0.0 copy-done
  297.6 3.4 convolution_multiply_fusion
  301.1 2.4 broadcast_in_dim.2
  303.5 2.9 scatter_fusion
  306.4 0.0 reduce-scatter.2.cloned.1.call-update
  306.4 109.1 %reduce-scatter.2.cloned.1.call-done = f32[128,256]{1,0:T(8,128)} async-done(((f32[4096,256]{1,0:T(8,128)}), f32[128,256]{1,0:T(8,128)}) %reduce-scatter.2.cloned.1.call-update) | async-done | bytes 131088 | tf_op jit(solution)/shard_map/reduce_scatter | solution.py:43
  415.6 1.5 convert_element_type.7
  (1 shorter events, 0.0 us)
Async XLA Ops:
  6.5 291.1 %copy-start = (bf16[1,2048,256]{2,1,0:T(8,128)(2,1)S(1)}, bf16[1,2048,256]{2,1,0:T(8,128)(2,1)}, u32[]{:S(2)}) copy-start(bf16[1,2048,256]{2,1,0:T(8,128)(2,1)} %param.11) | copy-start | bytes 3145732
  6.5 68.9 %all-gather.4.cloned.1.call-start = ((), (), s32[]{:S(2)}) async-start(), calls=%async_computation.1 | async-start | bytes 2162688 | tf_op jit(solution)/shard_map/all_gather | solution.py:20
  7.3 191.6 %all-gather.6.cloned.1.call-start = ((), (), s32[]{:S(2)}) async-start(), calls=%async_computation.2 | async-start | bytes 8912896 | tf_op jit(solution)/shard_map/all_gather | solution.py:27
  78.4 126.5 %copy-start.2 = (bf16[1,4096,128]{2,1,0:T(8,128)(2,1)S(1)}, bf16[1,4096,128]{2,1,0:T(8,128)(2,1)}, u32[]{:S(2)}) copy-start(bf16[1,4096,128]{2,1,0:T(8,128)(2,1)} %param.10) | copy-start | bytes 3145732
  78.4 219.2 %all-gather.8.cloned.1.call-start = ((), (), s32[]{:S(2)}) async-start(), calls=%async_computation.3 | async-start | bytes 4456448 | tf_op jit(solution)/shard_map/all_gather | solution.py:32
  198.8 6.1 %copy-start.1 = (bf16[1024,4096]{1,0:T(8,128)(2,1)S(1)}, bf16[1024,4096]{1,0:T(8,128)(2,1)}, u32[]{:S(2)}) copy-start(bf16[1024,4096]{1,0:T(8,128)(2,1)} %all-gather.6.cloned.1.call-done) | copy-start | bytes 25165828
  208.0 207.6 %reduce-scatter.2.cloned.1.call-start = ((), (), s32[]{:S(2)}) async-start(), calls=%async_computation.4 | async-start | bytes 4325376 | tf_op jit(solution)/shard_map/reduce_scatter | solution.py:43
Sparse Core Ops, SparseCore 0:
  10.5 64.8 all-gather.3
  78.6 120.2 all-gather.5
  208.1 89.4 all-gather.7
  306.6 108.9 reduce-scatter.1
where the time goes:
time: 424 us
  waiting for transfers between devices  386 us (91%)
  between operations  13.2 us (3%)
  matrix products  12.5 us (3%)
  local copies, waits for them, and re-layouts  9.12 us (2%)
    all_gather x1, waiting for transfers between devices, shards(): full_rows = lax.all_gather(selected, 'tok', axis=1, tiled=True)  120 us
    reduce_scatter x1, waiting for transfers between devices, shards(): lax.psum_scatter(buffer, 'exp', scatter_dimension=0, tiled=True)  109 us
    all_gather x1, waiting for transfers between devices, shards(): lax.all_gather(hidden, 'tok', axis=1, tiled=True)  88.8 us
    all_gather x1, waiting for transfers between devices, shards(): gathered = lax.all_gather(tokens, 'exp', axis=0, tiled=True)  67.4 us
  transfers between devices with their start and end apart: 4, of which 4 were waited for; matrix products, arithmetic and copies ran while one was open for 0% of the time, Pallas kernels for 0%

commit v1 on v0

v1 whole, which is shorter than its diff:
```python
import jax
import jax.numpy as jnp
from jax import lax
from jax.experimental import pallas as pl
from jax.experimental.pallas import tpu as pltpu
from jax.sharding import PartitionSpec as P

BLOCK = 128
SPAN = 4
ACROSS = 4
CHIPS = 16
DEPTH = 16
OWNERS = 32
SAME_CORE = [[2 * chip + core for chip in range(CHIPS)] for core in range(2)]


def swap_core(value):
    return lax.ppermute(value, "exp", [(p, p ^ 1) for p in range(OWNERS)])


def partner_along(z, turn):
    if (z + turn) % 2 == 0:
        return (z + 1) % DEPTH
    return (z - 1) % DEPTH


def swap_depth(value, step):
    pairs = []
    for z in range(DEPTH):
        for p in range(OWNERS):
            pairs.append((z * OWNERS + p, partner_along(z, (step + p) % 2) * OWNERS + p))
    return lax.ppermute(value, ("tok", "exp"), pairs)


def gather_depth(chunk, odd):
    other = swap_depth(chunk, 0)
    pair = jnp.stack([jnp.where(odd, other, chunk), jnp.where(odd, chunk, other)])
    items = [pair]
    for step in range(1, DEPTH // 2):
        items.append(swap_depth(items[-1], step))
    return items


def pair_order(z, core):
    turned = lax.rem(z - core + DEPTH, DEPTH)
    pair, odd = turned // 2, lax.rem(turned, 2)
    away = jnp.where(odd == 1, 1, -1)
    pairs = [pair]
    for step in range(1, DEPTH // 2):
        reach = (step + 1) // 2
        pairs.append(pair + (away * reach if step % 2 else -away * reach))
    chunks = [2 * p + half + core for p in pairs for half in range(2)]
    return odd == 1, jnp.stack([lax.rem(chunk + 2 * DEPTH, DEPTH) for chunk in chunks]).astype(jnp.int32)


def hidden_kernel(order, *refs):
    items, weights, out = refs[: DEPTH // 2], refs[DEPTH // 2 : -1], refs[-1]
    sets = len(weights) // 2
    units = weights[0].shape[1]
    features = items[0].shape[2]
    total = None
    for number in range(DEPTH):
        rows = pl.ds(pl.multiple_of(order[number] * features, features), features)
        right = jnp.concatenate([w[rows, :] for w in weights], axis=1)
        term = jnp.dot(items[number // 2][number % 2], right, preferred_element_type=jnp.float32)
        total = term if total is None else total + term
    gate, up = total[:, : sets * units], total[:, sets * units :]
    out[...] = (gate / (1.0 + jnp.exp(-gate)) * up).astype(out.dtype)


def hidden_of(order, items, gates, ups):
    rows = items[0].shape[1]
    sets, units = len(gates), gates[0].shape[1]
    whole = pl.BlockSpec(memory_space=pltpu.VMEM)
    return pl.pallas_call(
        hidden_kernel,
        out_shape=jax.ShapeDtypeStruct((rows, sets * units), jnp.bfloat16),
        in_specs=[pl.BlockSpec(memory_space=pltpu.SMEM)] + [whole] * (len(items) + 2 * sets),
        out_specs=whole,
        compiler_params=pltpu.CompilerParams(vmem_limit_bytes=32 << 20),
        cost_estimate=pl.CostEstimate(
            flops=2 * rows * gates[0].shape[0] * 2 * sets * units,
            bytes_accessed=2 * sets * gates[0].size * 2,
            transcendentals=rows * sets * units,
        ),
        name="hidden",
    )(order, *items, *gates, *ups)


def down_kernel(order, *refs):
    items, scale, weights, out = refs[: DEPTH // 2], refs[DEPTH // 2], refs[DEPTH // 2 + 1 : -1], refs[-1]
    sets = len(weights)
    units = items[0].shape[2] // sets
    total = None
    for number in range(DEPTH):
        rows = pl.ds(pl.multiple_of(order[number] * units, units), units)
        right = jnp.concatenate([w[rows, :] for w in weights], axis=0)
        term = jnp.dot(items[number // 2][number % 2], right, preferred_element_type=jnp.float32)
        total = term if total is None else total + term
    out[...] = (total * scale[...]).astype(out.dtype)


def down_of(order, items, scale, downs):
    rows = items[0].shape[1]
    features = downs[0].shape[1]
    whole = pl.BlockSpec(memory_space=pltpu.VMEM)
    return pl.pallas_call(
        down_kernel,
        out_shape=jax.ShapeDtypeStruct((rows, features), jnp.bfloat16),
        in_specs=[pl.BlockSpec(memory_space=pltpu.SMEM)] + [whole] * (len(items) + 1 + len(downs)),
        out_specs=whole,
        compiler_params=pltpu.CompilerParams(vmem_limit_bytes=32 << 20),
        cost_estimate=pl.CostEstimate(
            flops=2 * rows * features * sum(w.shape[0] for w in downs),
            bytes_accessed=2 * sum(w.size for w in downs),
            transcendentals=0,
        ),
        name="down",
    )(order, *items, scale, *downs)


def shards(tokens, picked_blocks, gate_scale, w_gate, w_up, w_down):
    position = lax.axis_index("exp")
    z = lax.axis_index("tok")
    core = lax.rem(position, 2)
    expert = position // SPAN
    features = tokens.shape[1]
    chosen = lax.dynamic_index_in_dim(picked_blocks, expert, 0, keepdims=False)
    half = chosen.shape[0] // 2

    gates = [w_gate[0], swap_core(w_gate[0])]
    ups = [w_up[0], swap_core(w_up[0])]
    downs = [w_down[0], swap_core(w_down[0])]

    spread = jnp.broadcast_to(tokens[None], (CHIPS,) + tokens.shape)
    held = lax.all_to_all(spread, "exp", 0, 0, axis_index_groups=SAME_CORE, tiled=True)
    mine = lax.dynamic_slice_in_dim(chosen, core * half, half)
    theirs = lax.dynamic_slice_in_dim(chosen, (1 - core) * half, half)
    lent = swap_core(held[theirs // 2])
    here = (lax.rem(mine, 2) == core)[:, None, None]
    selected = jnp.where(here, held[mine // 2], lent)

    odd, order = pair_order(z, core)
    scale = lax.dynamic_index_in_dim(gate_scale, expert, 0, keepdims=False).reshape(2, 2, -1, 1)
    scale = lax.dynamic_index_in_dim(scale, core, 0, keepdims=False)
    parts = []
    for part in range(2):
        rows = selected[part * half // 2 : (part + 1) * half // 2].reshape(-1, features)
        hidden = hidden_of(order, gather_depth(rows, odd), gates, ups)
        parts.append(down_of(order, gather_depth(hidden, odd), scale[part], downs))
    done = jnp.concatenate(parts).reshape(half, BLOCK, features)

    others = swap_core(done)
    all_done = jnp.concatenate([done, others])
    names = jnp.concatenate([mine, theirs])
    match = names[None, :] == (2 * jnp.arange(CHIPS, dtype=jnp.int32) + core)[:, None]
    outgoing = jnp.where(match.any(1)[:, None, None], all_done[jnp.argmax(match, 1)], 0)
    arrived = lax.all_to_all(outgoing, "exp", 0, 0, axis_index_groups=SAME_CORE, tiled=True)
    return jnp.sum(arrived, axis=0, dtype=jnp.float32).astype(jnp.bfloat16)


def solution(mesh):
    return jax.shard_map(
        shards,
        mesh=mesh,
        in_specs=(
            P("exp", "tok"),
            P(),
            P(),
            P("exp", None, "tok"),
            P("exp", None, "tok"),
            P("exp", None, "tok"),
        ),
        out_specs=P("exp", "tok"),
        check_vma=False,
    )
```

time: 424 us -> 240 us (0.57)
  waiting for transfers between devices: 386 us -> 46 us
  starting transfers between devices: 0.12 us -> 135 us
  blocking collectives: 0 us -> 19.3 us
  local copies, waits for them, and re-layouts: 9.12 us -> 24.4 us
  matrix products: 12.5 us -> 0 us
  between operations: 13.2 us -> 1.12 us
  Pallas kernels: 0 us -> 9.09 us
    all_gather x3 -> x0, waiting for transfers between devices: 277 us -> none  [the longest x1 120 us: shards(): full_rows = lax.all_gather(selected, 'tok', axis=1, tiled=True)]
    ppermute x0 -> x37, starting transfers between devices: none -> 128 us  [the longest x32 95.1 us: swap_depth(): return lax.ppermute(value, ('tok', 'exp'), pairs)]
    reduce_scatter x1 -> x0, waiting for transfers between devices: 109 us -> none  [shards(): lax.psum_scatter(buffer, 'exp', scatter_dimension=0, tiled=True)]
    ppermute x0 -> x37, waiting for transfers between devices: none -> 33.1 us  [the longest x32 31.5 us: swap_depth(): return lax.ppermute(value, ('tok', 'exp'), pairs)]
    unnamed x6 -> x76, local copies, waits for them, and re-layouts: 0.01 us -> 19.5 us
    all_to_all x0 -> x1, blocking collectives: none -> 19.3 us  [shards(): lax.all_to_all(outgoing, 'exp', 0, 0, axis_index_groups=SAME_CORE, tiled=...]
    all_to_all x0 -> x1, waiting for transfers between devices: none -> 12.9 us  [shards(): lax.all_to_all(spread, 'exp', 0, 0, axis_index_groups=SAME_CORE, tiled=True)]
    dot_general x3 -> x0, matrix products: 12.5 us -> none  [the longest x1 6.08 us: shards(): jnp.dot(full_rows, gate_local, preferred_element_type=jnp.float32)]
  transfers between devices with their start and end apart: 4 -> 38, of which waited for: 4 -> 22; matrix products, arithmetic and copies ran while one was open for 0% -> 2% of each run, Pallas kernels for 0% -> 3%
where the time goes in v1:
time: 240 us; the launch traced here: 239 us
  starting transfers between devices  135 us (56%)
  waiting for transfers between devices  46 us (19%)
  local copies, waits for them, and re-layouts  24.4 us (10%)
  blocking collectives  19.3 us (8%)
  Pallas kernels  9.09 us (4%)
  other arithmetic  3.63 us (2%)
    ppermute x32, starting transfers between devices, swap_depth(): return lax.ppermute(value, ('tok', 'exp'), pairs)  95.1 us
    ppermute x5, starting transfers between devices, swap_core(): return lax.ppermute(value, 'exp', [(p, p ^ 1) for p in range(OWNERS)])  32.5 us
    ppermute x32, waiting for transfers between devices, swap_depth(): return lax.ppermute(value, ('tok', 'exp'), pairs)  31.5 us
    unnamed x76, local copies, waits for them, and re-layouts  19.5 us
    all_to_all x1, blocking collectives, shards(): lax.all_to_all(outgoing, 'exp', 0, 0, axis_index_groups=SAME_CORE, tiled=...  19.3 us
    all_to_all x1, waiting for transfers between devices, shards(): lax.all_to_all(spread, 'exp', 0, 0, axis_index_groups=SAME_CORE, tiled=True)  12.9 us
    all_to_all x1, starting transfers between devices, shards(): lax.all_to_all(spread, 'exp', 0, 0, axis_index_groups=SAME_CORE, tiled=True)  7.58 us
    pallas_call x2, Pallas kernels, hidden_of(): pl.pallas_call(hidden_kernel, out_shape=jax.ShapeDtypeStruct((rows, sets...  5.45 us
  transfers between devices with their start and end apart: 38, of which 22 were waited for; matrix products, arithmetic and copies ran while one was open for 2% of the time, Pallas kernels for 3%

profile of v1, /device:TPU:1, one launch (start us, length us, event | category | flops | bytes accessed | tf_op | source)
XLA Modules:
  0.0 238.7 jit_solution(13020750012568661776)
XLA Ops:
  2.0 7.6 %all-to-all-start = ((bf16[16,128,256]{2,1,0:T(8,128)(2,1)}), bf16[16,128,256]{2,1,0:T(8,128)(2,1)S(1)}, u32[]{:S(2)}, u32[]{:S(2)}) async-start(bf16[16,128,256]{2,1,0:T(8,128)(2,1)} %broadcast_in_dim.37), calls=%async_computation | async-start | bytes 2097152 | tf_op jit(solution)/shard_map/all_to_all | solution.py:136
  11.1 12.9 %all-to-all-done = bf16[16,128,256]{2,1,0:T(8,128)(2,1)S(1)} async-done(((bf16[16,128,256]{2,1,0:T(8,128)(2,1)}), bf16[16,128,256]{2,1,0:T(8,128)(2,1)S(1)}, u32[]{:S(2)}, u32[]{:S(2)}) %all-to-all-start) | async-done | bytes 1048608 | tf_op jit(solution)/shard_map/all_to_all | solution.py:136
  24.6 6.0 %collective-permute-start = (bf16[4,128,256]{2,1,0:T(8,128)(2,1)S(1)}, bf16[4,128,256]{2,1,0:T(8,128)(2,1)S(1)}, u32[]{:S(2)}, u32[]{:S(2)}) collective-permute-start(bf16[4,128,256]{2,1,0:T(8,128)(2,1)S(1)} %gather_fusion.1), channel_id=1, source_target_pairs={{0,1},{1,0},{2,3},{3,2},{4,5},{5,4},{6,7},{7,6},{8,9},{9,8},{10,11... | collective-permute-start | bytes 786440 | tf_op jit(solution)/shard_map/ppermute | solution.py:18
  31.8 11.2 %collective-permute-start.1 = (bf16[256,256]{1,0:T(8,128)(2,1)S(1)}, bf16[256,256]{1,0:T(8,128)(2,1)S(1)}, u32[]{:S(2)}, u32[]{:S(2)}) collective-permute-start(bf16[256,256]{1,0:T(8,128)(2,1)S(1)} %bitcast.87), channel_id=1, source_target_pairs={{0,32},{1,481},{2,34},{3,483},{4,36},{5,485},{6,38},{7,487},{8,40}... | collective-permute-start | bytes 393224 | tf_op jit(solution)/shard_map/ppermute | solution.py:32
  47.4 2.8 %collective-permute-done.20 = bf16[256,256]{1,0:T(8,128)(2,1)S(1)} collective-permute-done((bf16[256,256]{1,0:T(8,128)(2,1)S(1)}, bf16[256,256]{1,0:T(8,128)(2,1)S(1)}, u32[]{:S(2)}, u32[]{:S(2)}) %collective-permute-start.20) | collective-permute-done | bytes 131104 | tf_op jit(solution)/shard_map/ppermute | solution.py:32
  52.9 4.6 %collective-permute-start.3 = (bf16[2,256,256]{2,1,0:T(8,128)(2,1)S(1)}, bf16[2,256,256]{2,1,0:T(8,128)(2,1)S(1)}, u32[]{:S(2)}, u32[]{:S(2)}) collective-permute-start(bf16[2,256,256]{2,1,0:T(8,128)(2,1)S(1)} %collective-permute-done.2.refs_1_), channel_id=1, source_target_pairs={{0,32},{1,481},{2,34},{3,483},{4,36},{5,485},{6,38},{7,487},{8,40}... | collective-permute-start | bytes 786440 | tf_op jit(solution)/shard_map/ppermute | solution.py:32
  69.1 7.2 %collective-permute-start.10 = (bf16[4096,128]{1,0:T(8,128)(2,1)S(1)}, bf16[4096,128]{1,0:T(8,128)(2,1)S(1)}, u32[]{:S(2)}, u32[]{:S(2)}) collective-permute-start(bf16[4096,128]{1,0:T(8,128)(2,1)S(1)} %bitcast.78), channel_id=1, source_target_pairs={{0,1},{1,0},{2,3},{3,2},{4,5},{5,4},{6,7},{7,6},{8,9},{9,8},{10,11... | collective-permute-start | bytes 3145736 | tf_op jit(solution)/shard_map/ppermute | solution.py:18
  76.3 4.9 %collective-permute-start.5 = (bf16[2,256,256]{2,1,0:T(8,128)(2,1)S(1)}, bf16[2,256,256]{2,1,0:T(8,128)(2,1)S(1)}, u32[]{:S(2)}, u32[]{:S(2)}) collective-permute-start(bf16[2,256,256]{2,1,0:T(8,128)(2,1)S(1)} %collective-permute-done.4.refs_3_), channel_id=1, source_target_pairs={{0,32},{1,481},{2,34},{3,483},{4,36},{5,485},{6,38},{7,487},{8,40}... | collective-permute-start | bytes 786440 | tf_op jit(solution)/shard_map/ppermute | solution.py:32
  89.1 3.0 %collective-permute-done.24.refs_4_ = bf16[2,256,256]{2,1,0:T(8,128)(2,1)S(1)} collective-permute-done((bf16[2,256,256]{2,1,0:T(8,128)(2,1)S(1)}, bf16[2,256,256]{2,1,0:T(8,128)(2,1)S(1)}, u32[]{:S(2)}, u32[]{:S(2)}) %collective-permute-start.24) | collective-permute-done | bytes 262176 | tf_op jit(solution)/shard_map/ppermute | solution.py:32
  95.0 3.4 %collective-permute-start.7 = (bf16[2,256,256]{2,1,0:T(8,128)(2,1)S(1)}, bf16[2,256,256]{2,1,0:T(8,128)(2,1)}, u32[]{:S(2)}, u32[]{:S(2)}) collective-permute-start(bf16[2,256,256]{2,1,0:T(8,128)(2,1)S(1)} %collective-permute-done.6.refs_5_), channel_id=1, source_target_pairs={{0,32},{1,481},{2,34},{3,483},{4,36},{5,485},{6,38},{7,487},{8,40}... | collective-permute-start | bytes 786440 | tf_op jit(solution)/shard_map/ppermute | solution.py:32
  99.2 2.9 %collective-permute-start.26 = (bf16[2,256,256]{2,1,0:T(8,128)(2,1)S(1)}, bf16[2,256,256]{2,1,0:T(8,128)(2,1)}, u32[]{:S(2)}, u32[]{:S(2)}) collective-permute-start(bf16[2,256,256]{2,1,0:T(8,128)(2,1)S(1)} %collective-permute-done.25.refs_5_), channel_id=1, source_target_pairs={{0,32},{1,481},{2,34},{3,483},{4,36},{5,485},{6,38},{7,487},{8,40}... | collective-permute-start | bytes 786440 | tf_op jit(solution)/shard_map/ppermute | solution.py:32
  102.9 2.4 %collective-permute-done.7.refs_6_ = bf16[2,256,256]{2,1,0:T(8,128)(2,1)} collective-permute-done((bf16[2,256,256]{2,1,0:T(8,128)(2,1)S(1)}, bf16[2,256,256]{2,1,0:T(8,128)(2,1)}, u32[]{:S(2)}, u32[]{:S(2)}) %collective-permute-start.7) | collective-permute-done | bytes 262176 | tf_op jit(solution)/shard_map/ppermute | solution.py:32
  108.1 2.5 %collective-permute-start.27 = (bf16[2,256,256]{2,1,0:T(8,128)(2,1)}, bf16[2,256,256]{2,1,0:T(8,128)(2,1)}, u32[]{:S(2)}, u32[]{:S(2)}) collective-permute-start(bf16[2,256,256]{2,1,0:T(8,128)(2,1)} %collective-permute-done.26.refs_6_), channel_id=1, source_target_pairs={{0,480},{1,33},{2,482},{3,35},{4,484},{5,37},{6,486},{7,39},{8,488... | collective-permute-start | bytes 786440 | tf_op jit(solution)/shard_map/ppermute | solution.py:32
  110.9 4.8 %collective-permute-done.8.refs_7_ = bf16[2,256,256]{2,1,0:T(8,128)(2,1)} collective-permute-done((bf16[2,256,256]{2,1,0:T(8,128)(2,1)}, bf16[2,256,256]{2,1,0:T(8,128)(2,1)}, u32[]{:S(2)}, u32[]{:S(2)}) %collective-permute-start.8) | collective-permute-done | bytes 262176 | tf_op jit(solution)/shard_map/ppermute | solution.py:32
  120.6 2.8 %hidden.2 = bf16[256,256]{1,0:T(8,128)(2,1)S(1)} custom-call(s32[16]{0:T(128)S(1)} %stack.103.order, bf16[2,256,256]{2,1,0:T(8,128)(2,1)S(1)} %pad_maximum_fusion.1.refs_0_, bf16[2,256,256]{2,1,0:T(8,128)(2,1)S(1)} %copy-done.7, bf16[2,256,256]{2,1,0:T(8,128)(2,1)S(1)} %copy-done.13, bf16[2,256,256]{2,1,0:T(8,128)(2,1)S(1)} %copy-done.17, ...), custom_call_target="tpu_custom_call" | custom-call | flops 1073741824 | bytes 4194304 | tf_op jit(solution)/shard_map/hidden/pallas_call | solution.py:75
  125.3 2.7 %hidden.3 = bf16[256,256]{1,0:T(8,128)(2,1)S(1)} custom-call(s32[16]{0:T(128)S(1)} %stack.103.order, bf16[2,256,256]{2,1,0:T(8,128)(2,1)S(1)} %copy-done.5, bf16[2,256,256]{2,1,0:T(8,128)(2,1)S(1)} %copy-done.9, bf16[2,256,256]{2,1,0:T(8,128)(2,1)S(1)} %copy-done.11, bf16[2,256,256]{2,1,0:T(8,128)(2,1)S(1)} %copy-done.15, ...), custom_call_target="tpu_custom_call" | custom-call | flops 1073741824 | bytes 4194304 | tf_op jit(solution)/shard_map/hidden/pallas_call | solution.py:75
  128.0 4.7 %collective-permute-start.28 = (bf16[256,256]{1,0:T(8,128)(2,1)S(1)}, bf16[256,256]{1,0:T(8,128)(2,1)S(1)}, u32[]{:S(2)}, u32[]{:S(2)}) collective-permute-start(bf16[256,256]{1,0:T(8,128)(2,1)S(1)} %hidden.3), channel_id=1, source_target_pairs={{0,32},{1,481},{2,34},{3,483},{4,36},{5,485},{6,38},{7,487},{8,40}... | collective-permute-start | bytes 393224 | tf_op jit(solution)/shard_map/ppermute | solution.py:32
  135.1 3.0 %collective-permute-start.29 = (bf16[2,256,256]{2,1,0:T(8,128)(2,1)S(1)}, bf16[2,256,256]{2,1,0:T(8,128)(2,1)S(1)}, u32[]{:S(2)}, u32[]{:S(2)}) collective-permute-start(bf16[2,256,256]{2,1,0:T(8,128)(2,1)S(1)} %pad_maximum_fusion.4.refs_0_), channel_id=1, source_target_pairs={{0,480},{1,33},{2,482},{3,35},{4,484},{5,37},{6,486},{7,39},{8,488... | collective-permute-start | bytes 786440 | tf_op jit(solution)/shard_map/ppermute | solution.py:32
  139.9 3.6 %collective-permute-start.13 = (bf16[2,256,256]{2,1,0:T(8,128)(2,1)S(1)}, bf16[2,256,256]{2,1,0:T(8,128)(2,1)S(1)}, u32[]{:S(2)}, u32[]{:S(2)}) collective-permute-start(bf16[2,256,256]{2,1,0:T(8,128)(2,1)S(1)} %collective-permute-done.12.refs_1_), channel_id=1, source_target_pairs={{0,32},{1,481},{2,34},{3,483},{4,36},{5,485},{6,38},{7,487},{8,40}... | collective-permute-start | bytes 786440 | tf_op jit(solution)/shard_map/ppermute | solution.py:32
  143.5 3.6 %collective-permute-start.30 = (bf16[2,256,256]{2,1,0:T(8,128)(2,1)S(1)}, bf16[2,256,256]{2,1,0:T(8,128)(2,1)S(1)}, u32[]{:S(2)}, u32[]{:S(2)}) collective-permute-start(bf16[2,256,256]{2,1,0:T(8,128)(2,1)S(1)} %collective-permute-done.29.refs_1_), channel_id=1, source_target_pairs={{0,32},{1,481},{2,34},{3,483},{4,36},{5,485},{6,38},{7,487},{8,40}... | collective-permute-start | bytes 786440 | tf_op jit(solution)/shard_map/ppermute | solution.py:32
  147.1 3.8 %collective-permute-done.13.refs_2_ = bf16[2,256,256]{2,1,0:T(8,128)(2,1)S(1)} collective-permute-done((bf16[2,256,256]{2,1,0:T(8,128)(2,1)S(1)}, bf16[2,256,256]{2,1,0:T(8,128)(2,1)S(1)}, u32[]{:S(2)}, u32[]{:S(2)}) %collective-permute-start.13) | collective-permute-done | bytes 262176 | tf_op jit(solution)/shard_map/ppermute | solution.py:32
  150.9 2.6 %collective-permute-start.14 = (bf16[2,256,256]{2,1,0:T(8,128)(2,1)S(1)}, bf16[2,256,256]{2,1,0:T(8,128)(2,1)S(1)}, u32[]{:S(2)}, u32[]{:S(2)}) collective-permute-start(bf16[2,256,256]{2,1,0:T(8,128)(2,1)S(1)} %collective-permute-done.13.refs_2_), channel_id=1, source_target_pairs={{0,480},{1,33},{2,482},{3,35},{4,484},{5,37},{6,486},{7,39},{8,488... | collective-permute-start | bytes 786440 | tf_op jit(solution)/shard_map/ppermute | solution.py:32
  154.2 2.7 %collective-permute-start.31 = (bf16[2,256,256]{2,1,0:T(8,128)(2,1)S(1)}, bf16[2,256,256]{2,1,0:T(8,128)(2,1)S(1)}, u32[]{:S(2)}, u32[]{:S(2)}) collective-permute-start(bf16[2,256,256]{2,1,0:T(8,128)(2,1)S(1)} %collective-permute-done.30.refs_2_), channel_id=1, source_target_pairs={{0,480},{1,33},{2,482},{3,35},{4,484},{5,37},{6,486},{7,39},{8,488... | collective-permute-start | bytes 786440 | tf_op jit(solution)/shard_map/ppermute | solution.py:32
  159.2 2.2 collective-permute-start.15
  163.6 3.4 %collective-permute-start.32 = (bf16[2,256,256]{2,1,0:T(8,128)(2,1)S(1)}, bf16[2,256,256]{2,1,0:T(8,128)(2,1)S(1)}, u32[]{:S(2)}, u32[]{:S(2)}) collective-permute-start(bf16[2,256,256]{2,1,0:T(8,128)(2,1)S(1)} %collective-permute-done.31.refs_3_), channel_id=1, source_target_pairs={{0,32},{1,481},{2,34},{3,483},{4,36},{5,485},{6,38},{7,487},{8,40}... | collective-permute-start | bytes 786440 | tf_op jit(solution)/shard_map/ppermute | solution.py:32
  167.8 12.2 %collective-permute-start.19 = (bf16[2048,256]{1,0:T(8,128)(2,1)S(1)}, bf16[2048,256]{1,0:T(8,128)(2,1)S(1)}, u32[]{:S(2)}, u32[]{:S(2)}) collective-permute-start(bf16[2048,256]{1,0:T(8,128)(2,1)S(1)} %bitcast.81), channel_id=1, source_target_pairs={{0,1},{1,0},{2,3},{3,2},{4,5},{5,4},{6,7},{7,6},{8,9},{9,8},{10,11... | collective-permute-start | bytes 3145736 | tf_op jit(solution)/shard_map/ppermute | solution.py:18
  180.0 3.6 %collective-permute-start.16 = (bf16[2,256,256]{2,1,0:T(8,128)(2,1)S(1)}, bf16[2,256,256]{2,1,0:T(8,128)(2,1)}, u32[]{:S(2)}, u32[]{:S(2)}) collective-permute-start(bf16[2,256,256]{2,1,0:T(8,128)(2,1)S(1)} %collective-permute-done.15.refs_4_), channel_id=1, source_target_pairs={{0,480},{1,33},{2,482},{3,35},{4,484},{5,37},{6,486},{7,39},{8,488... | collective-permute-start | bytes 786440 | tf_op jit(solution)/shard_map/ppermute | solution.py:32
  187.8 3.4 %collective-permute-start.17 = (bf16[2,256,256]{2,1,0:T(8,128)(2,1)}, bf16[2,256,256]{2,1,0:T(8,128)(2,1)}, u32[]{:S(2)}, u32[]{:S(2)}) collective-permute-start(bf16[2,256,256]{2,1,0:T(8,128)(2,1)} %collective-permute-done.16.refs_5_), channel_id=1, source_target_pairs={{0,32},{1,481},{2,34},{3,483},{4,36},{5,485},{6,38},{7,487},{8,40}... | collective-permute-start | bytes 786440 | tf_op jit(solution)/shard_map/ppermute | solution.py:32
  192.0 3.3 %collective-permute-start.34 = (bf16[2,256,256]{2,1,0:T(8,128)(2,1)}, bf16[2,256,256]{2,1,0:T(8,128)(2,1)}, u32[]{:S(2)}, u32[]{:S(2)}) collective-permute-start(bf16[2,256,256]{2,1,0:T(8,128)(2,1)} %collective-permute-done.33.refs_5_), channel_id=1, source_target_pairs={{0,32},{1,481},{2,34},{3,483},{4,36},{5,485},{6,38},{7,487},{8,40}... | collective-permute-start | bytes 786440 | tf_op jit(solution)/shard_map/ppermute | solution.py:32
  196.4 2.4 %collective-permute-start.18 = (bf16[2,256,256]{2,1,0:T(8,128)(2,1)}, bf16[2,256,256]{2,1,0:T(8,128)(2,1)}, u32[]{:S(2)}, u32[]{:S(2)}) collective-permute-start(bf16[2,256,256]{2,1,0:T(8,128)(2,1)} %collective-permute-done.17.refs_6_), channel_id=1, source_target_pairs={{0,480},{1,33},{2,482},{3,35},{4,484},{5,37},{6,486},{7,39},{8,488... | collective-permute-start | bytes 786440 | tf_op jit(solution)/shard_map/ppermute | solution.py:32
  211.6 5.2 %collective-permute-start.36 = (bf16[4,128,256]{2,1,0:T(8,128)(2,1)S(1)}, bf16[4,128,256]{2,1,0:T(8,128)(2,1)S(1)}, u32[]{:S(2)}, u32[]{:S(2)}) collective-permute-start(bf16[4,128,256]{2,1,0:T(8,128)(2,1)S(1)} %bitcast.84), channel_id=1, source_target_pairs={{0,1},{1,0},{2,3},{3,2},{4,5},{5,4},{6,7},{7,6},{8,9},{9,8},{10,11... | collective-permute-start | bytes 786440 | tf_op jit(solution)/shard_map/ppermute | solution.py:18
  218.7 19.3 %all_to_all.10 = bf16[16,128,256]{2,1,0:T(8,128)(2,1)S(1)} all-to-all(bf16[16,128,256]{2,1,0:T(8,128)(2,1)S(1)} %broadcast_select_fusion), channel_id=1, replica_groups={{0,2,4,6,8,10,12,14,16,18,20,22,24,26,28,30},{1,3,5,7,9,11,13,15,17,19,..., dimensions={0} | all-to-all | bytes 2097152 | tf_op jit(solution)/shard_map/all_to_all | solution.py:158
  (159 shorter events, 77.0 us)
Async XLA Ops:
  2.0 22.1 %all-to-all-start = ((bf16[16,128,256]{2,1,0:T(8,128)(2,1)}), bf16[16,128,256]{2,1,0:T(8,128)(2,1)S(1)}, u32[]{:S(2)}, u32[]{:S(2)}) async-start(bf16[16,128,256]{2,1,0:T(8,128)(2,1)} %broadcast_in_dim.37), calls=%async_computation | async-start | bytes 2097152 | tf_op jit(solution)/shard_map/all_to_all | solution.py:136
  31.8 13.5 %collective-permute-start.1 = (bf16[256,256]{1,0:T(8,128)(2,1)S(1)}, bf16[256,256]{1,0:T(8,128)(2,1)S(1)}, u32[]{:S(2)}, u32[]{:S(2)}) collective-permute-start(bf16[256,256]{1,0:T(8,128)(2,1)S(1)} %bitcast.87), channel_id=1, source_target_pairs={{0,32},{1,481},{2,34},{3,483},{4,36},{5,485},{6,38},{7,487},{8,40}... | collective-permute-start | bytes 393224 | tf_op jit(solution)/shard_map/ppermute | solution.py:32
  45.4 7.4 %collective-permute-start.2 = (bf16[2,256,256]{2,1,0:T(8,128)(2,1)S(1)}, bf16[2,256,256]{2,1,0:T(8,128)(2,1)S(1)}, u32[]{:S(2)}, u32[]{:S(2)}) collective-permute-start(bf16[2,256,256]{2,1,0:T(8,128)(2,1)S(1)} %pad_maximum_fusion.1.refs_0_), channel_id=1, source_target_pairs={{0,480},{1,33},{2,482},{3,35},{4,484},{5,37},{6,486},{7,39},{8,488... | collective-permute-start | bytes 786440 | tf_op jit(solution)/shard_map/ppermute | solution.py:32
  50.2 7.9 %collective-permute-start.21 = (bf16[2,256,256]{2,1,0:T(8,128)(2,1)S(1)}, bf16[2,256,256]{2,1,0:T(8,128)(2,1)S(1)}, u32[]{:S(2)}, u32[]{:S(2)}) collective-permute-start(bf16[2,256,256]{2,1,0:T(8,128)(2,1)S(1)} %pad_maximum_fusion.3.refs_0_), channel_id=1, source_target_pairs={{0,480},{1,33},{2,482},{3,35},{4,484},{5,37},{6,486},{7,39},{8,488... | collective-permute-start | bytes 786440 | tf_op jit(solution)/shard_map/ppermute | solution.py:32
  52.9 9.4 %collective-permute-start.3 = (bf16[2,256,256]{2,1,0:T(8,128)(2,1)S(1)}, bf16[2,256,256]{2,1,0:T(8,128)(2,1)S(1)}, u32[]{:S(2)}, u32[]{:S(2)}) collective-permute-start(bf16[2,256,256]{2,1,0:T(8,128)(2,1)S(1)} %collective-permute-done.2.refs_1_), channel_id=1, source_target_pairs={{0,32},{1,481},{2,34},{3,483},{4,36},{5,485},{6,38},{7,487},{8,40}... | collective-permute-start | bytes 786440 | tf_op jit(solution)/shard_map/ppermute | solution.py:32
  58.1 8.3 %collective-permute-start.22 = (bf16[2,256,256]{2,1,0:T(8,128)(2,1)S(1)}, bf16[2,256,256]{2,1,0:T(8,128)(2,1)S(1)}, u32[]{:S(2)}, u32[]{:S(2)}) collective-permute-start(bf16[2,256,256]{2,1,0:T(8,128)(2,1)S(1)} %collective-permute-done.21.refs_1_), channel_id=1, source_target_pairs={{0,32},{1,481},{2,34},{3,483},{4,36},{5,485},{6,38},{7,487},{8,40}... | collective-permute-start | bytes 786440 | tf_op jit(solution)/shard_map/ppermute | solution.py:32
  62.3 14.0 %collective-permute-start.4 = (bf16[2,256,256]{2,1,0:T(8,128)(2,1)S(1)}, bf16[2,256,256]{2,1,0:T(8,128)(2,1)S(1)}, u32[]{:S(2)}, u32[]{:S(2)}) collective-permute-start(bf16[2,256,256]{2,1,0:T(8,128)(2,1)S(1)} %collective-permute-done.3.refs_2_), channel_id=1, source_target_pairs={{0,480},{1,33},{2,482},{3,35},{4,484},{5,37},{6,486},{7,39},{8,488... | collective-permute-start | bytes 786440 | tf_op jit(solution)/shard_map/ppermute | solution.py:32
  66.4 17.3 %collective-permute-start.23 = (bf16[2,256,256]{2,1,0:T(8,128)(2,1)S(1)}, bf16[2,256,256]{2,1,0:T(8,128)(2,1)S(1)}, u32[]{:S(2)}, u32[]{:S(2)}) collective-permute-start(bf16[2,256,256]{2,1,0:T(8,128)(2,1)S(1)} %collective-permute-done.22.refs_2_), channel_id=1, source_target_pairs={{0,480},{1,33},{2,482},{3,35},{4,484},{5,37},{6,486},{7,39},{8,488... | collective-permute-start | bytes 786440 | tf_op jit(solution)/shard_map/ppermute | solution.py:32
  69.1 41.9 %collective-permute-start.10 = (bf16[4096,128]{1,0:T(8,128)(2,1)S(1)}, bf16[4096,128]{1,0:T(8,128)(2,1)S(1)}, u32[]{:S(2)}, u32[]{:S(2)}) collective-permute-start(bf16[4096,128]{1,0:T(8,128)(2,1)S(1)} %bitcast.78), channel_id=1, source_target_pairs={{0,1},{1,0},{2,3},{3,2},{4,5},{5,4},{6,7},{7,6},{8,9},{9,8},{10,11... | collective-permute-start | bytes 3145736 | tf_op jit(solution)/shard_map/ppermute | solution.py:18
  76.3 10.2 %collective-permute-start.5 = (bf16[2,256,256]{2,1,0:T(8,128)(2,1)S(1)}, bf16[2,256,256]{2,1,0:T(8,128)(2,1)S(1)}, u32[]{:S(2)}, u32[]{:S(2)}) collective-permute-start(bf16[2,256,256]{2,1,0:T(8,128)(2,1)S(1)} %collective-permute-done.4.refs_3_), channel_id=1, source_target_pairs={{0,32},{1,481},{2,34},{3,483},{4,36},{5,485},{6,38},{7,487},{8,40}... | collective-permute-start | bytes 786440 | tf_op jit(solution)/shard_map/ppermute | solution.py:32
  81.9 29.1 %collective-permute-start.9 = (bf16[4096,128]{1,0:T(8,128)(2,1)S(1)}, bf16[4096,128]{1,0:T(8,128)(2,1)}, u32[]{:S(2)}, u32[]{:S(2)}) collective-permute-start(bf16[4096,128]{1,0:T(8,128)(2,1)S(1)} %bitcast.75), channel_id=1, source_target_pairs={{0,1},{1,0},{2,3},{3,2},{4,5},{5,4},{6,7},{7,6},{8,9},{9,8},{10,11... | collective-permute-start | bytes 3145736 | tf_op jit(solution)/shard_map/ppermute | solution.py:18
  83.8 8.3 %collective-permute-start.24 = (bf16[2,256,256]{2,1,0:T(8,128)(2,1)S(1)}, bf16[2,256,256]{2,1,0:T(8,128)(2,1)S(1)}, u32[]{:S(2)}, u32[]{:S(2)}) collective-permute-start(bf16[2,256,256]{2,1,0:T(8,128)(2,1)S(1)} %collective-permute-done.23.refs_3_), channel_id=1, source_target_pairs={{0,32},{1,481},{2,34},{3,483},{4,36},{5,485},{6,38},{7,487},{8,40}... | collective-permute-start | bytes 786440 | tf_op jit(solution)/shard_map/ppermute | solution.py:32
  86.5 8.5 %collective-permute-start.6 = (bf16[2,256,256]{2,1,0:T(8,128)(2,1)S(1)}, bf16[2,256,256]{2,1,0:T(8,128)(2,1)S(1)}, u32[]{:S(2)}, u32[]{:S(2)}) collective-permute-start(bf16[2,256,256]{2,1,0:T(8,128)(2,1)S(1)} %collective-permute-done.5.refs_4_), channel_id=1, source_target_pairs={{0,480},{1,33},{2,482},{3,35},{4,484},{5,37},{6,486},{7,39},{8,488... | collective-permute-start | bytes 786440 | tf_op jit(solution)/shard_map/ppermute | solution.py:32
  95.0 10.3 %collective-permute-start.7 = (bf16[2,256,256]{2,1,0:T(8,128)(2,1)S(1)}, bf16[2,256,256]{2,1,0:T(8,128)(2,1)}, u32[]{:S(2)}, u32[]{:S(2)}) collective-permute-start(bf16[2,256,256]{2,1,0:T(8,128)(2,1)S(1)} %collective-permute-done.6.refs_5_), channel_id=1, source_target_pairs={{0,32},{1,481},{2,34},{3,483},{4,36},{5,485},{6,38},{7,487},{8,40}... | collective-permute-start | bytes 786440 | tf_op jit(solution)/shard_map/ppermute | solution.py:32
  99.2 8.9 %collective-permute-start.26 = (bf16[2,256,256]{2,1,0:T(8,128)(2,1)S(1)}, bf16[2,256,256]{2,1,0:T(8,128)(2,1)}, u32[]{:S(2)}, u32[]{:S(2)}) collective-permute-start(bf16[2,256,256]{2,1,0:T(8,128)(2,1)S(1)} %collective-permute-done.25.refs_5_), channel_id=1, source_target_pairs={{0,32},{1,481},{2,34},{3,483},{4,36},{5,485},{6,38},{7,487},{8,40}... | collective-permute-start | bytes 786440 | tf_op jit(solution)/shard_map/ppermute | solution.py:32
  105.3 10.5 %collective-permute-start.8 = (bf16[2,256,256]{2,1,0:T(8,128)(2,1)}, bf16[2,256,256]{2,1,0:T(8,128)(2,1)}, u32[]{:S(2)}, u32[]{:S(2)}) collective-permute-start(bf16[2,256,256]{2,1,0:T(8,128)(2,1)} %collective-permute-done.7.refs_6_), channel_id=1, source_target_pairs={{0,480},{1,33},{2,482},{3,35},{4,484},{5,37},{6,486},{7,39},{8,488... | collective-permute-start | bytes 786440 | tf_op jit(solution)/shard_map/ppermute | solution.py:32
  108.1 17.1 %collective-permute-start.27 = (bf16[2,256,256]{2,1,0:T(8,128)(2,1)}, bf16[2,256,256]{2,1,0:T(8,128)(2,1)}, u32[]{:S(2)}, u32[]{:S(2)}) collective-permute-start(bf16[2,256,256]{2,1,0:T(8,128)(2,1)} %collective-permute-done.26.refs_6_), channel_id=1, source_target_pairs={{0,480},{1,33},{2,482},{3,35},{4,484},{5,37},{6,486},{7,39},{8,488... | collective-permute-start | bytes 786440 | tf_op jit(solution)/shard_map/ppermute | solution.py:32
  123.3 9.4 %collective-permute-start.11 = (bf16[256,256]{1,0:T(8,128)(2,1)S(1)}, bf16[256,256]{1,0:T(8,128)(2,1)S(1)}, u32[]{:S(2)}, u32[]{:S(2)}) collective-permute-start(bf16[256,256]{1,0:T(8,128)(2,1)S(1)} %hidden.2), channel_id=1, source_target_pairs={{0,32},{1,481},{2,34},{3,483},{4,36},{5,485},{6,38},{7,487},{8,40}... | collective-permute-start | bytes 393224 | tf_op jit(solution)/shard_map/ppermute | solution.py:32
  135.1 8.4 %collective-permute-start.29 = (bf16[2,256,256]{2,1,0:T(8,128)(2,1)S(1)}, bf16[2,256,256]{2,1,0:T(8,128)(2,1)S(1)}, u32[]{:S(2)}, u32[]{:S(2)}) collective-permute-start(bf16[2,256,256]{2,1,0:T(8,128)(2,1)S(1)} %pad_maximum_fusion.4.refs_0_), channel_id=1, source_target_pairs={{0,480},{1,33},{2,482},{3,35},{4,484},{5,37},{6,486},{7,39},{8,488... | collective-permute-start | bytes 786440 | tf_op jit(solution)/shard_map/ppermute | solution.py:32
  139.9 11.0 %collective-permute-start.13 = (bf16[2,256,256]{2,1,0:T(8,128)(2,1)S(1)}, bf16[2,256,256]{2,1,0:T(8,128)(2,1)S(1)}, u32[]{:S(2)}, u32[]{:S(2)}) collective-permute-start(bf16[2,256,256]{2,1,0:T(8,128)(2,1)S(1)} %collective-permute-done.12.refs_1_), channel_id=1, source_target_pairs={{0,32},{1,481},{2,34},{3,483},{4,36},{5,485},{6,38},{7,487},{8,40}... | collective-permute-start | bytes 786440 | tf_op jit(solution)/shard_map/ppermute | solution.py:32
  143.5 10.6 %collective-permute-start.30 = (bf16[2,256,256]{2,1,0:T(8,128)(2,1)S(1)}, bf16[2,256,256]{2,1,0:T(8,128)(2,1)S(1)}, u32[]{:S(2)}, u32[]{:S(2)}) collective-permute-start(bf16[2,256,256]{2,1,0:T(8,128)(2,1)S(1)} %collective-permute-done.29.refs_1_), channel_id=1, source_target_pairs={{0,32},{1,481},{2,34},{3,483},{4,36},{5,485},{6,38},{7,487},{8,40}... | collective-permute-start | bytes 786440 | tf_op jit(solution)/shard_map/ppermute | solution.py:32
  150.9 8.3 %collective-permute-start.14 = (bf16[2,256,256]{2,1,0:T(8,128)(2,1)S(1)}, bf16[2,256,256]{2,1,0:T(8,128)(2,1)S(1)}, u32[]{:S(2)}, u32[]{:S(2)}) collective-permute-start(bf16[2,256,256]{2,1,0:T(8,128)(2,1)S(1)} %collective-permute-done.13.refs_2_), channel_id=1, source_target_pairs={{0,480},{1,33},{2,482},{3,35},{4,484},{5,37},{6,486},{7,39},{8,488... | collective-permute-start | bytes 786440 | tf_op jit(solution)/shard_map/ppermute | solution.py:32
  154.2 9.5 %collective-permute-start.31 = (bf16[2,256,256]{2,1,0:T(8,128)(2,1)S(1)}, bf16[2,256,256]{2,1,0:T(8,128)(2,1)S(1)}, u32[]{:S(2)}, u32[]{:S(2)}) collective-permute-start(bf16[2,256,256]{2,1,0:T(8,128)(2,1)S(1)} %collective-permute-done.30.refs_2_), channel_id=1, source_target_pairs={{0,480},{1,33},{2,482},{3,35},{4,484},{5,37},{6,486},{7,39},{8,488... | collective-permute-start | bytes 786440 | tf_op jit(solution)/shard_map/ppermute | solution.py:32
  159.2 20.7 %collective-permute-start.15 = (bf16[2,256,256]{2,1,0:T(8,128)(2,1)S(1)}, bf16[2,256,256]{2,1,0:T(8,128)(2,1)S(1)}, u32[]{:S(2)}, u32[]{:S(2)}) collective-permute-start(bf16[2,256,256]{2,1,0:T(8,128)(2,1)S(1)} %collective-permute-done.14.refs_3_), channel_id=1, source_target_pairs={{0,32},{1,481},{2,34},{3,483},{4,36},{5,485},{6,38},{7,487},{8,40}... | collective-permute-start | bytes 786440 | tf_op jit(solution)/shard_map/ppermute | solution.py:32
  163.6 20.7 %collective-permute-start.32 = (bf16[2,256,256]{2,1,0:T(8,128)(2,1)S(1)}, bf16[2,256,256]{2,1,0:T(8,128)(2,1)S(1)}, u32[]{:S(2)}, u32[]{:S(2)}) collective-permute-start(bf16[2,256,256]{2,1,0:T(8,128)(2,1)S(1)} %collective-permute-done.31.refs_3_), channel_id=1, source_target_pairs={{0,32},{1,481},{2,34},{3,483},{4,36},{5,485},{6,38},{7,487},{8,40}... | collective-permute-start | bytes 786440 | tf_op jit(solution)/shard_map/ppermute | solution.py:32
  167.8 35.4 %collective-permute-start.19 = (bf16[2048,256]{1,0:T(8,128)(2,1)S(1)}, bf16[2048,256]{1,0:T(8,128)(2,1)S(1)}, u32[]{:S(2)}, u32[]{:S(2)}) collective-permute-start(bf16[2048,256]{1,0:T(8,128)(2,1)S(1)} %bitcast.81), channel_id=1, source_target_pairs={{0,1},{1,0},{2,3},{3,2},{4,5},{5,4},{6,7},{7,6},{8,9},{9,8},{10,11... | collective-permute-start | bytes 3145736 | tf_op jit(solution)/shard_map/ppermute | solution.py:18
  180.0 7.8 %collective-permute-start.16 = (bf16[2,256,256]{2,1,0:T(8,128)(2,1)S(1)}, bf16[2,256,256]{2,1,0:T(8,128)(2,1)}, u32[]{:S(2)}, u32[]{:S(2)}) collective-permute-start(bf16[2,256,256]{2,1,0:T(8,128)(2,1)S(1)} %collective-permute-done.15.refs_4_), channel_id=1, source_target_pairs={{0,480},{1,33},{2,482},{3,35},{4,484},{5,37},{6,486},{7,39},{8,488... | collective-permute-start | bytes 786440 | tf_op jit(solution)/shard_map/ppermute | solution.py:32
  184.3 7.6 %collective-permute-start.33 = (bf16[2,256,256]{2,1,0:T(8,128)(2,1)S(1)}, bf16[2,256,256]{2,1,0:T(8,128)(2,1)}, u32[]{:S(2)}, u32[]{:S(2)}) collective-permute-start(bf16[2,256,256]{2,1,0:T(8,128)(2,1)S(1)} %collective-permute-done.32.refs_4_), channel_id=1, source_target_pairs={{0,480},{1,33},{2,482},{3,35},{4,484},{5,37},{6,486},{7,39},{8,488... | collective-permute-start | bytes 786440 | tf_op jit(solution)/shard_map/ppermute | solution.py:32
  187.8 8.6 %collective-permute-start.17 = (bf16[2,256,256]{2,1,0:T(8,128)(2,1)}, bf16[2,256,256]{2,1,0:T(8,128)(2,1)}, u32[]{:S(2)}, u32[]{:S(2)}) collective-permute-start(bf16[2,256,256]{2,1,0:T(8,128)(2,1)} %collective-permute-done.16.refs_5_), channel_id=1, source_target_pairs={{0,32},{1,481},{2,34},{3,483},{4,36},{5,485},{6,38},{7,487},{8,40}... | collective-permute-start | bytes 786440 | tf_op jit(solution)/shard_map/ppermute | solution.py:32
  192.0 8.6 %collective-permute-start.34 = (bf16[2,256,256]{2,1,0:T(8,128)(2,1)}, bf16[2,256,256]{2,1,0:T(8,128)(2,1)}, u32[]{:S(2)}, u32[]{:S(2)}) collective-permute-start(bf16[2,256,256]{2,1,0:T(8,128)(2,1)} %collective-permute-done.33.refs_5_), channel_id=1, source_target_pairs={{0,32},{1,481},{2,34},{3,483},{4,36},{5,485},{6,38},{7,487},{8,40}... | collective-permute-start | bytes 786440 | tf_op jit(solution)/shard_map/ppermute | solution.py:32
  196.4 8.6 %collective-permute-start.18 = (bf16[2,256,256]{2,1,0:T(8,128)(2,1)}, bf16[2,256,256]{2,1,0:T(8,128)(2,1)}, u32[]{:S(2)}, u32[]{:S(2)}) collective-permute-start(bf16[2,256,256]{2,1,0:T(8,128)(2,1)} %collective-permute-done.17.refs_6_), channel_id=1, source_target_pairs={{0,480},{1,33},{2,482},{3,35},{4,484},{5,37},{6,486},{7,39},{8,488... | collective-permute-start | bytes 786440 | tf_op jit(solution)/shard_map/ppermute | solution.py:32
  200.6 9.1 %collective-permute-start.35 = (bf16[2,256,256]{2,1,0:T(8,128)(2,1)}, bf16[2,256,256]{2,1,0:T(8,128)(2,1)S(1)}, u32[]{:S(2)}, u32[]{:S(2)}) collective-permute-start(bf16[2,256,256]{2,1,0:T(8,128)(2,1)} %collective-permute-done.34.refs_6_), channel_id=1, source_target_pairs={{0,480},{1,33},{2,482},{3,35},{4,484},{5,37},{6,486},{7,39},{8,488... | collective-permute-start | bytes 786440 | tf_op jit(solution)/shard_map/ppermute | solution.py:32
  (44 other events, 401.5 us)

commit v2 on v0

v2 whole, which is shorter than its diff:
```python
import functools

import jax
import jax.numpy as jnp
from jax import lax
from jax.experimental import pallas as pl
from jax.experimental.pallas import tpu as pltpu
from jax.sharding import PartitionSpec as P

BLOCK = 128
SPAN = 4
CHIPS = 16
DEPTH = 16
OWNERS = 32
PARTS = 2
SAME_CORE = [[2 * chip + core for chip in range(CHIPS)] for core in range(2)]


def swap_core(value):
    return lax.ppermute(value, "exp", [(p, p ^ 1) for p in range(OWNERS)])


def partner_along(z, turn):
    if (z + turn) % 2 == 0:
        return (z + 1) % DEPTH
    return (z - 1) % DEPTH


def swap_depth(value, step):
    pairs = []
    for z in range(DEPTH):
        for p in range(OWNERS):
            pairs.append((z * OWNERS + p, partner_along(z, (step + p) % 2) * OWNERS + p))
    return lax.ppermute(value, ("tok", "exp"), pairs)


def pair_order(z, core):
    turned = lax.rem(z - core + DEPTH, DEPTH)
    pair, odd = turned // 2, lax.rem(turned, 2)
    away = jnp.where(odd == 1, 1, -1)
    pairs = [pair]
    for step in range(1, DEPTH // 2):
        reach = (step + 1) // 2
        pairs.append(pair + (away * reach if step % 2 else -away * reach))
    chunks = [
        jnp.stack([lax.rem(2 * p + half + core + 2 * DEPTH, DEPTH) for half in range(2)]).astype(jnp.int32)
        for p in pairs
    ]
    return odd == 1, chunks


def step_kernel(join, first, finish, weight_count, order, pair, *refs):
    weights, rest = refs[:weight_count], list(refs[weight_count:])
    begun = None if first else rest.pop(0)
    scale = rest.pop(0) if finish == "scale" else None
    out, held, arrived = rest
    taken = held.shape[2]
    copies = []
    for half in range(2):
        rows = pl.ds(pl.multiple_of(order[half] * taken, taken), taken)
        for number, weight in enumerate(weights):
            copy = pltpu.make_async_copy(weight.at[rows, :], held.at[half, number], arrived.at[half, number])
            copy.start()
            copies.append(copy)
    total = None if first else begun[...]
    for half in range(2):
        for copy in copies[half * weight_count : (half + 1) * weight_count]:
            copy.wait()
        right = jnp.concatenate([held[half, number] for number in range(weight_count)], axis=join)
        term = jnp.dot(pair[half], right, preferred_element_type=jnp.float32)
        total = term if total is None else total + term
    if finish == "silu":
        units = total.shape[1] // 2
        gate, up = total[:, :units], total[:, units:]
        total = gate / (1.0 + jnp.exp(-gate)) * up
    elif finish == "scale":
        total = total * scale[...]
    out[...] = total.astype(out.dtype)


def add_product(order, pair, weights, join, begun, finish="", scale=None):
    _, rows, depth = pair.shape
    count = len(weights)
    taken = depth if join == 1 else depth // count
    columns = weights[0].shape[1] * (count if join == 1 else 1)
    width = columns // 2 if finish == "silu" else columns
    extra = ([] if begun is None else [begun]) + ([] if scale is None else [scale])
    return pl.pallas_call(
        functools.partial(step_kernel, join, begun is None, finish, count),
        out_shape=jax.ShapeDtypeStruct((rows, width), jnp.bfloat16 if finish else jnp.float32),
        in_specs=[pl.BlockSpec(memory_space=pltpu.SMEM), pl.BlockSpec(memory_space=pltpu.VMEM)]
        + [pl.BlockSpec(memory_space=pltpu.HBM)] * count
        + [pl.BlockSpec(memory_space=pltpu.VMEM)] * len(extra),
        out_specs=pl.BlockSpec(memory_space=pltpu.VMEM),
        scratch_shapes=[
            pltpu.VMEM((2, count, taken, weights[0].shape[1]), jnp.bfloat16),
            pltpu.SemaphoreType.DMA((2, count)),
        ],
        compiler_params=pltpu.CompilerParams(vmem_limit_bytes=16 << 20),
        cost_estimate=pl.CostEstimate(
            flops=2 * 2 * rows * depth * columns,
            bytes_accessed=2 * 2 * (rows * depth + depth * columns) + 8 * rows * columns,
            transcendentals=0,
        ),
        name="add_product",
    )(order, pair, *[pltpu.with_memory_space_constraint(w, pltpu.HBM) for w in weights], *extra)


def gathered_product(chunk, odd, orders, weights, join, finish, scale=None):
    other = swap_depth(chunk, 0)
    pair = jnp.stack([jnp.where(odd, other, chunk), jnp.where(odd, chunk, other)])
    total = None
    for step, order in enumerate(orders):
        last = step + 1 == len(orders)
        following = None if last else swap_depth(pair, step + 1)
        total = add_product(order, pair, weights, join, total, finish if last else "", scale if last else None)
        if not last:
            following, total = lax.optimization_barrier((following, total))
        pair = following
    return total


def shards(tokens, picked_blocks, gate_scale, w_gate, w_up, w_down):
    position = lax.axis_index("exp")
    z = lax.axis_index("tok")
    core = lax.rem(position, 2)
    expert = position // SPAN
    features = tokens.shape[1]
    chosen = lax.dynamic_index_in_dim(picked_blocks, expert, 0, keepdims=False)
    half = chosen.shape[0] // 2
    part_rows = BLOCK // PARTS

    ins = [w_gate[0], swap_core(w_gate[0]), w_up[0], swap_core(w_up[0])]
    downs = [w_down[0], swap_core(w_down[0])]

    odd, orders = pair_order(z, core)
    mine = lax.dynamic_slice_in_dim(chosen, core * half, half)
    theirs = lax.dynamic_slice_in_dim(chosen, (1 - core) * half, half)
    here = (lax.rem(mine, 2) == core)[:, None, None]
    scale = lax.dynamic_index_in_dim(gate_scale, expert, 0, keepdims=False).reshape(2, half, PARTS, part_rows)
    scale = lax.dynamic_index_in_dim(scale, core, 0, keepdims=False)
    names = jnp.concatenate([mine, theirs])
    match = names[None, :] == (2 * jnp.arange(CHIPS, dtype=jnp.int32) + core)[:, None]
    wanted, source = match.any(1)[:, None, None], jnp.argmax(match, 1)

    results = []
    for part in range(PARTS):
        own = tokens[part * part_rows : (part + 1) * part_rows]
        spread = jnp.broadcast_to(own[None], (CHIPS,) + own.shape)
        held = lax.all_to_all(spread, "exp", 0, 0, axis_index_groups=SAME_CORE, tiled=True)
        lent = swap_core(held[theirs // 2])
        rows = jnp.where(here, held[mine // 2], lent).reshape(-1, features)
        rows, ins, downs = lax.optimization_barrier((rows, ins, downs))
        hidden = gathered_product(rows, odd, orders, ins, 1, "silu")
        done = gathered_product(hidden, odd, orders, downs, 0, "scale", scale[:, part].reshape(-1, 1))
        done = done.reshape(half, part_rows, features)
        all_done = jnp.concatenate([done, swap_core(done)])
        outgoing = jnp.where(wanted, all_done[source], 0)
        arrived = lax.all_to_all(outgoing, "exp", 0, 0, axis_index_groups=SAME_CORE, tiled=True)
        results.append(jnp.sum(arrived, axis=0, dtype=jnp.float32).astype(jnp.bfloat16))
    return jnp.concatenate(results)


def solution(mesh):
    return jax.shard_map(
        shards,
        mesh=mesh,
        in_specs=(
            P("exp", "tok"),
            P(),
            P(),
            P("exp", None, "tok"),
            P("exp", None, "tok"),
            P("exp", None, "tok"),
        ),
        out_specs=P("exp", "tok"),
        check_vma=False,
    )
```

time: 424 us -> 271 us (0.64)
  waiting for transfers between devices: 386 us -> 27.7 us
  starting transfers between devices: 0.12 us -> 145 us
  Pallas kernels: 0 us -> 61 us
  blocking collectives: 0 us -> 13.6 us
  matrix products: 12.5 us -> 0 us
  between operations: 13.2 us -> 1.29 us
    all_gather x3 -> x0, waiting for transfers between devices: 277 us -> none  [the longest x1 120 us: shards(): full_rows = lax.all_gather(selected, 'tok', axis=1, tiled=True)]
    ppermute x0 -> x39, starting transfers between devices: none -> 127 us  [the longest x32 94.2 us: swap_depth(): return lax.ppermute(value, ('tok', 'exp'), pairs)]
    reduce_scatter x1 -> x0, waiting for transfers between devices: 109 us -> none  [shards(): lax.psum_scatter(buffer, 'exp', scatter_dimension=0, tiled=True)]
    pallas_call x0 -> x32, Pallas kernels: none -> 61 us  [add_product(): pl.pallas_call(functools.partial(step_kernel, join, begun is None, finish...]
    all_to_all x0 -> x3, starting transfers between devices: none -> 18.1 us  [the longest x2 14.5 us: shards(): lax.all_to_all(spread, 'exp', 0, 0, axis_index_groups=SAME_CORE, tiled=True)]
    all_to_all x0 -> x3, waiting for transfers between devices: none -> 14.1 us  [the longest x1 10 us: shards(): lax.all_to_all(outgoing, 'exp', 0, 0, axis_index_groups=SAME_CORE, tiled=...]
    all_to_all x0 -> x1, blocking collectives: none -> 13.6 us  [shards(): lax.all_to_all(outgoing, 'exp', 0, 0, axis_index_groups=SAME_CORE, tiled=...]
    ppermute x0 -> x39, waiting for transfers between devices: none -> 13.6 us  [the longest x32 12.9 us: swap_depth(): return lax.ppermute(value, ('tok', 'exp'), pairs)]
  transfers between devices with their start and end apart: 4 -> 42, of which waited for: 4 -> 12; matrix products, arithmetic and copies ran while one was open for 0% -> 6% of each run, Pallas kernels for 0% -> 23%
where the time goes in v2:
time: 271 us; the launch traced here: 268 us
  starting transfers between devices  145 us (54%)
  Pallas kernels  61 us (23%)
  waiting for transfers between devices  27.7 us (10%)
  blocking collectives  13.6 us (5%)
  local copies, waits for them, and re-layouts  12.6 us (5%)
  other arithmetic  6.14 us (2%)
    ppermute x32, starting transfers between devices, swap_depth(): return lax.ppermute(value, ('tok', 'exp'), pairs)  94.2 us
    pallas_call x32, Pallas kernels, add_product(): pl.pallas_call(functools.partial(step_kernel, join, begun is None, finish...  61 us
    ppermute x7, starting transfers between devices, swap_core(): return lax.ppermute(value, 'exp', [(p, p ^ 1) for p in range(OWNERS)])  33.2 us
    all_to_all x2, starting transfers between devices, shards(): lax.all_to_all(spread, 'exp', 0, 0, axis_index_groups=SAME_CORE, tiled=True)  14.5 us
    all_to_all x1, blocking collectives, shards(): lax.all_to_all(outgoing, 'exp', 0, 0, axis_index_groups=SAME_CORE, tiled=...  13.6 us
    ppermute x32, waiting for transfers between devices, swap_depth(): return lax.ppermute(value, ('tok', 'exp'), pairs)  12.9 us
    all_to_all x1, waiting for transfers between devices, shards(): lax.all_to_all(outgoing, 'exp', 0, 0, axis_index_groups=SAME_CORE, tiled=...  10 us
  transfers between devices with their start and end apart: 42, of which 12 were waited for; matrix products, arithmetic and copies ran while one was open for 6% of the time, Pallas kernels for 23%

profile of v2, /device:TPU:1, one launch (start us, length us, event | category | flops | bytes accessed | tf_op | source)
XLA Modules:
  0.0 267.9 jit_solution(17689409215266301006)
XLA Ops:
  1.7 7.6 %all-to-all-start.2 = ((bf16[16,64,256]{2,1,0:T(8,128)(2,1)}), bf16[16,64,256]{2,1,0:T(8,128)(2,1)}, u32[]{:S(2)}, u32[]{:S(2)}) async-start(bf16[16,64,256]{2,1,0:T(8,128)(2,1)} %broadcast_in_dim.56), calls=%async_computation.2 | async-start | bytes 1048576 | tf_op jit(solution)/shard_map/all_to_all | solution.py:150
  9.4 5.4 %collective-permute-start.1 = (bf16[4096,128]{1,0:T(8,128)(2,1)}, bf16[4096,128]{1,0:T(8,128)(2,1)S(1)}, u32[]{:S(2)}, u32[]{:S(2)}) collective-permute-start(bf16[4096,128]{1,0:T(8,128)(2,1)} %bitcast.90), channel_id=1, source_target_pairs={{0,1},{1,0},{2,3},{3,2},{4,5},{5,4},{6,7},{7,6},{8,9},{9,8},{10,11... | collective-permute-start | bytes 3145736 | tf_op jit(solution)/shard_map/ppermute | solution.py:20
  20.0 6.9 %all-to-all-start = ((bf16[16,64,256]{2,1,0:T(8,128)(2,1)}), bf16[16,64,256]{2,1,0:T(8,128)(2,1)}, u32[]{:S(2)}, u32[]{:S(2)}) async-start(bf16[16,64,256]{2,1,0:T(8,128)(2,1)} %broadcast_in_dim.53), calls=%async_computation | async-start | bytes 1048576 | tf_op jit(solution)/shard_map/all_to_all | solution.py:150
  30.0 3.2 %collective-permute-start.21 = (bf16[4,64,256]{2,1,0:T(8,128)(2,1)S(1)}, bf16[4,64,256]{2,1,0:T(8,128)(2,1)}, u32[]{:S(2)}, u32[]{:S(2)}) collective-permute-start(bf16[4,64,256]{2,1,0:T(8,128)(2,1)S(1)} %gather_fusion.4), channel_id=1, source_target_pairs={{0,1},{1,0},{2,3},{3,2},{4,5},{5,4},{6,7},{7,6},{8,9},{9,8},{10,11... | collective-permute-start | bytes 393224 | tf_op jit(solution)/shard_map/ppermute | solution.py:20
  33.2 4.1 %all-to-all-done = bf16[16,64,256]{2,1,0:T(8,128)(2,1)} async-done(((bf16[16,64,256]{2,1,0:T(8,128)(2,1)}), bf16[16,64,256]{2,1,0:T(8,128)(2,1)}, u32[]{:S(2)}, u32[]{:S(2)}) %all-to-all-start) | async-done | bytes 524320 | tf_op jit(solution)/shard_map/all_to_all | solution.py:150
  38.9 4.0 %collective-permute-start = (bf16[4,64,256]{2,1,0:T(8,128)(2,1)S(1)}, bf16[4,64,256]{2,1,0:T(8,128)(2,1)}, u32[]{:S(2)}, u32[]{:S(2)}) collective-permute-start(bf16[4,64,256]{2,1,0:T(8,128)(2,1)S(1)} %gather_fusion.1), channel_id=1, source_target_pairs={{0,1},{1,0},{2,3},{3,2},{4,5},{5,4},{6,7},{7,6},{8,9},{9,8},{10,11... | collective-permute-start | bytes 393224 | tf_op jit(solution)/shard_map/ppermute | solution.py:20
  48.7 9.3 %collective-permute-start.22 = (bf16[256,256]{1,0:T(8,128)(2,1)S(1)}, bf16[256,256]{1,0:T(8,128)(2,1)S(1)}, u32[]{:S(2)}, u32[]{:S(2)}) collective-permute-start(bf16[256,256]{1,0:T(8,128)(2,1)S(1)} %bitcast.126), channel_id=1, source_target_pairs={{0,32},{1,481},{2,34},{3,483},{4,36},{5,485},{6,38},{7,487},{8,40}... | collective-permute-start | bytes 393224 | tf_op jit(solution)/shard_map/ppermute | solution.py:34
  62.3 2.6 collective-permute-done.4
  69.1 3.4 %collective-permute-start.24 = (bf16[2,256,256]{2,1,0:T(8,128)(2,1)S(1)}, bf16[2,256,256]{2,1,0:T(8,128)(2,1)S(1)}, u32[]{:S(2)}, u32[]{:S(2)}) collective-permute-start(bf16[2,256,256]{2,1,0:T(8,128)(2,1)S(1)} %collective-permute-done.23.pair), channel_id=1, source_target_pairs={{0,32},{1,481},{2,34},{3,483},{4,36},{5,485},{6,38},{7,487},{8,40}... | collective-permute-start | bytes 786440 | tf_op jit(solution)/shard_map/ppermute | solution.py:34
  74.5 3.1 %collective-permute-start.6 = (bf16[2,256,256]{2,1,0:T(8,128)(2,1)S(1)}, bf16[2,256,256]{2,1,0:T(8,128)(2,1)S(1)}, u32[]{:S(2)}, u32[]{:S(2)}) collective-permute-start(bf16[2,256,256]{2,1,0:T(8,128)(2,1)S(1)} %collective-permute-done.5.pair), channel_id=1, source_target_pairs={{0,32},{1,481},{2,34},{3,483},{4,36},{5,485},{6,38},{7,487},{8,40}... | collective-permute-start | bytes 786440 | tf_op jit(solution)/shard_map/ppermute | solution.py:34
  83.7 3.1 %collective-permute-start.7 = (bf16[2,256,256]{2,1,0:T(8,128)(2,1)S(1)}, bf16[2,256,256]{2,1,0:T(8,128)(2,1)}, u32[]{:S(2)}, u32[]{:S(2)}) collective-permute-start(bf16[2,256,256]{2,1,0:T(8,128)(2,1)S(1)} %collective-permute-done.6.pair), channel_id=1, source_target_pairs={{0,480},{1,33},{2,482},{3,35},{4,484},{5,37},{6,486},{7,39},{8,488... | collective-permute-start | bytes 786440 | tf_op jit(solution)/shard_map/ppermute | solution.py:34
  88.8 3.4 %collective-permute-start.26 = (bf16[2,256,256]{2,1,0:T(8,128)(2,1)S(1)}, bf16[2,256,256]{2,1,0:T(8,128)(2,1)S(1)}, u32[]{:S(2)}, u32[]{:S(2)}) collective-permute-start(bf16[2,256,256]{2,1,0:T(8,128)(2,1)S(1)} %collective-permute-done.25.pair), channel_id=1, source_target_pairs={{0,32},{1,481},{2,34},{3,483},{4,36},{5,485},{6,38},{7,487},{8,40}... | collective-permute-start | bytes 786440 | tf_op jit(solution)/shard_map/ppermute | solution.py:34
  94.2 3.1 %collective-permute-start.8 = (bf16[2,256,256]{2,1,0:T(8,128)(2,1)}, bf16[2,256,256]{2,1,0:T(8,128)(2,1)S(1)}, u32[]{:S(2)}, u32[]{:S(2)}) collective-permute-start(bf16[2,256,256]{2,1,0:T(8,128)(2,1)} %collective-permute-done.7.pair), channel_id=1, source_target_pairs={{0,32},{1,481},{2,34},{3,483},{4,36},{5,485},{6,38},{7,487},{8,40}... | collective-permute-start | bytes 786440 | tf_op jit(solution)/shard_map/ppermute | solution.py:34
  103.6 3.4 %collective-permute-start.9 = (bf16[2,256,256]{2,1,0:T(8,128)(2,1)S(1)}, bf16[2,256,256]{2,1,0:T(8,128)(2,1)S(1)}, u32[]{:S(2)}, u32[]{:S(2)}) collective-permute-start(bf16[2,256,256]{2,1,0:T(8,128)(2,1)S(1)} %collective-permute-done.8.pair), channel_id=1, source_target_pairs={{0,480},{1,33},{2,482},{3,35},{4,484},{5,37},{6,486},{7,39},{8,488... | collective-permute-start | bytes 786440 | tf_op jit(solution)/shard_map/ppermute | solution.py:34
  109.0 3.4 %collective-permute-start.28 = (bf16[2,256,256]{2,1,0:T(8,128)(2,1)S(1)}, bf16[2,256,256]{2,1,0:T(8,128)(2,1)S(1)}, u32[]{:S(2)}, u32[]{:S(2)}) collective-permute-start(bf16[2,256,256]{2,1,0:T(8,128)(2,1)S(1)} %collective-permute-done.27.pair), channel_id=1, source_target_pairs={{0,32},{1,481},{2,34},{3,483},{4,36},{5,485},{6,38},{7,487},{8,40}... | collective-permute-start | bytes 786440 | tf_op jit(solution)/shard_map/ppermute | solution.py:34
  114.3 3.1 %collective-permute-start.10 = (bf16[2,256,256]{2,1,0:T(8,128)(2,1)S(1)}, bf16[2,256,256]{2,1,0:T(8,128)(2,1)S(1)}, u32[]{:S(2)}, u32[]{:S(2)}) collective-permute-start(bf16[2,256,256]{2,1,0:T(8,128)(2,1)S(1)} %collective-permute-done.9.pair), channel_id=1, source_target_pairs={{0,32},{1,481},{2,34},{3,483},{4,36},{5,485},{6,38},{7,487},{8,40}... | collective-permute-start | bytes 786440 | tf_op jit(solution)/shard_map/ppermute | solution.py:34
  123.3 3.4 %collective-permute-start.11 = (bf16[2,256,256]{2,1,0:T(8,128)(2,1)S(1)}, bf16[2,256,256]{2,1,0:T(8,128)(2,1)S(1)}, u32[]{:S(2)}, u32[]{:S(2)}) collective-permute-start(bf16[2,256,256]{2,1,0:T(8,128)(2,1)S(1)} %collective-permute-done.10.pair), channel_id=1, source_target_pairs={{0,480},{1,33},{2,482},{3,35},{4,484},{5,37},{6,486},{7,39},{8,488... | collective-permute-start | bytes 786440 | tf_op jit(solution)/shard_map/ppermute | solution.py:34
  131.3 2.9 %collective-permute-start.30 = (bf16[256,256]{1,0:T(8,128)(2,1)S(1)}, bf16[256,256]{1,0:T(8,128)(2,1)S(1)}, u32[]{:S(2)}, u32[]{:S(2)}) collective-permute-start(bf16[256,256]{1,0:T(8,128)(2,1)S(1)} %add_product.55), channel_id=1, source_target_pairs={{0,32},{1,481},{2,34},{3,483},{4,36},{5,485},{6,38},{7,487},{8,40}... | collective-permute-start | bytes 393224 | tf_op jit(solution)/shard_map/ppermute | solution.py:34
  138.0 3.6 %collective-permute-start.12 = (bf16[256,256]{1,0:T(8,128)(2,1)S(1)}, bf16[256,256]{1,0:T(8,128)(2,1)S(1)}, u32[]{:S(2)}, u32[]{:S(2)}) collective-permute-start(bf16[256,256]{1,0:T(8,128)(2,1)S(1)} %add_product.39), channel_id=1, source_target_pairs={{0,32},{1,481},{2,34},{3,483},{4,36},{5,485},{6,38},{7,487},{8,40}... | collective-permute-start | bytes 393224 | tf_op jit(solution)/shard_map/ppermute | solution.py:34
  150.6 3.5 %collective-permute-start.32 = (bf16[2,256,256]{2,1,0:T(8,128)(2,1)S(1)}, bf16[2,256,256]{2,1,0:T(8,128)(2,1)S(1)}, u32[]{:S(2)}, u32[]{:S(2)}) collective-permute-start(bf16[2,256,256]{2,1,0:T(8,128)(2,1)S(1)} %collective-permute-done.31.pair), channel_id=1, source_target_pairs={{0,32},{1,481},{2,34},{3,483},{4,36},{5,485},{6,38},{7,487},{8,40}... | collective-permute-start | bytes 786440 | tf_op jit(solution)/shard_map/ppermute | solution.py:34
  154.1 3.0 %collective-permute-start.14 = (bf16[2,256,256]{2,1,0:T(8,128)(2,1)S(1)}, bf16[2,256,256]{2,1,0:T(8,128)(2,1)S(1)}, u32[]{:S(2)}, u32[]{:S(2)}) collective-permute-start(bf16[2,256,256]{2,1,0:T(8,128)(2,1)S(1)} %collective-permute-done.13.pair), channel_id=1, source_target_pairs={{0,32},{1,481},{2,34},{3,483},{4,36},{5,485},{6,38},{7,487},{8,40}... | collective-permute-start | bytes 786440 | tf_op jit(solution)/shard_map/ppermute | solution.py:34
  160.9 2.8 %collective-permute-start.33 = (bf16[2,256,256]{2,1,0:T(8,128)(2,1)S(1)}, bf16[2,256,256]{2,1,0:T(8,128)(2,1)S(1)}, u32[]{:S(2)}, u32[]{:S(2)}) collective-permute-start(bf16[2,256,256]{2,1,0:T(8,128)(2,1)S(1)} %collective-permute-done.32.pair), channel_id=1, source_target_pairs={{0,480},{1,33},{2,482},{3,35},{4,484},{5,37},{6,486},{7,39},{8,488... | collective-permute-start | bytes 786440 | tf_op jit(solution)/shard_map/ppermute | solution.py:34
  170.6 3.6 %collective-permute-start.34 = (bf16[2,256,256]{2,1,0:T(8,128)(2,1)S(1)}, bf16[2,256,256]{2,1,0:T(8,128)(2,1)S(1)}, u32[]{:S(2)}, u32[]{:S(2)}) collective-permute-start(bf16[2,256,256]{2,1,0:T(8,128)(2,1)S(1)} %collective-permute-done.33.pair), channel_id=1, source_target_pairs={{0,32},{1,481},{2,34},{3,483},{4,36},{5,485},{6,38},{7,487},{8,40}... | collective-permute-start | bytes 786440 | tf_op jit(solution)/shard_map/ppermute | solution.py:34
  174.6 3.2 %collective-permute-start.16 = (bf16[2,256,256]{2,1,0:T(8,128)(2,1)S(1)}, bf16[2,256,256]{2,1,0:T(8,128)(2,1)S(1)}, u32[]{:S(2)}, u32[]{:S(2)}) collective-permute-start(bf16[2,256,256]{2,1,0:T(8,128)(2,1)S(1)} %collective-permute-done.15.pair), channel_id=1, source_target_pairs={{0,32},{1,481},{2,34},{3,483},{4,36},{5,485},{6,38},{7,487},{8,40}... | collective-permute-start | bytes 786440 | tf_op jit(solution)/shard_map/ppermute | solution.py:34
  183.8 3.2 %collective-permute-done.16.pair = bf16[2,256,256]{2,1,0:T(8,128)(2,1)S(1)} collective-permute-done((bf16[2,256,256]{2,1,0:T(8,128)(2,1)S(1)}, bf16[2,256,256]{2,1,0:T(8,128)(2,1)S(1)}, u32[]{:S(2)}, u32[]{:S(2)}) %collective-permute-start.16) | collective-permute-done | bytes 262176 | tf_op jit(solution)/shard_map/ppermute | solution.py:34
  186.9 2.4 collective-permute-start.17
  194.0 3.6 %collective-permute-start.36 = (bf16[2,256,256]{2,1,0:T(8,128)(2,1)S(1)}, bf16[2,256,256]{2,1,0:T(8,128)(2,1)S(1)}, u32[]{:S(2)}, u32[]{:S(2)}) collective-permute-start(bf16[2,256,256]{2,1,0:T(8,128)(2,1)S(1)} %collective-permute-done.35.pair), channel_id=1, source_target_pairs={{0,32},{1,481},{2,34},{3,483},{4,36},{5,485},{6,38},{7,487},{8,40}... | collective-permute-start | bytes 786440 | tf_op jit(solution)/shard_map/ppermute | solution.py:34
  197.6 2.9 %collective-permute-start.18 = (bf16[2,256,256]{2,1,0:T(8,128)(2,1)S(1)}, bf16[2,256,256]{2,1,0:T(8,128)(2,1)S(1)}, u32[]{:S(2)}, u32[]{:S(2)}) collective-permute-start(bf16[2,256,256]{2,1,0:T(8,128)(2,1)S(1)} %collective-permute-done.17.pair), channel_id=1, source_target_pairs={{0,32},{1,481},{2,34},{3,483},{4,36},{5,485},{6,38},{7,487},{8,40}... | collective-permute-start | bytes 786440 | tf_op jit(solution)/shard_map/ppermute | solution.py:34
  216.6 14.4 %collective-permute-start.38 = (bf16[4,64,256]{2,1,0:T(8,128)(2,1)S(1)}, bf16[4,64,256]{2,1,0:T(8,128)(2,1)S(1)}, u32[]{:S(2)}, u32[]{:S(2)}) collective-permute-start(bf16[4,64,256]{2,1,0:T(8,128)(2,1)S(1)} %bitcast.69), channel_id=1, source_target_pairs={{0,1},{1,0},{2,3},{3,2},{4,5},{5,4},{6,7},{7,6},{8,9},{9,8},{10,11... | collective-permute-start | bytes 393224 | tf_op jit(solution)/shard_map/ppermute | solution.py:20
  239.9 13.6 %all_to_all.20 = bf16[16,64,256]{2,1,0:T(8,128)(2,1)S(1)} all-to-all(bf16[16,64,256]{2,1,0:T(8,128)(2,1)S(1)} %get-tuple-element.161), channel_id=1, replica_groups={{0,2,4,6,8,10,12,14,16,18,20,22,24,26,28,30},{1,3,5,7,9,11,13,15,17,19,..., dimensions={0} | all-to-all | bytes 1048576 | tf_op jit(solution)/shard_map/all_to_all | solution.py:159
  253.5 3.6 %all-to-all-start.3 = ((bf16[16,64,256]{2,1,0:T(8,128)(2,1)}), bf16[16,64,256]{2,1,0:T(8,128)(2,1)S(1)}, u32[]{:S(2)}, u32[]{:S(2)}) async-start(bf16[16,64,256]{2,1,0:T(8,128)(2,1)} %get-tuple-element.162), calls=%async_computation.3 | async-start | bytes 1048576 | tf_op jit(solution)/shard_map/all_to_all | solution.py:159
  257.2 10.0 %all-to-all-done.3 = bf16[16,64,256]{2,1,0:T(8,128)(2,1)S(1)} async-done(((bf16[16,64,256]{2,1,0:T(8,128)(2,1)}), bf16[16,64,256]{2,1,0:T(8,128)(2,1)S(1)}, u32[]{:S(2)}, u32[]{:S(2)}) %all-to-all-start.3) | async-done | bytes 524320 | tf_op jit(solution)/shard_map/all_to_all | solution.py:159
  (142 shorter events, 117.8 us)
Async XLA Ops:
  1.7 17.4 %all-to-all-start.2 = ((bf16[16,64,256]{2,1,0:T(8,128)(2,1)}), bf16[16,64,256]{2,1,0:T(8,128)(2,1)}, u32[]{:S(2)}, u32[]{:S(2)}) async-start(bf16[16,64,256]{2,1,0:T(8,128)(2,1)} %broadcast_in_dim.56), calls=%async_computation.2 | async-start | bytes 1048576 | tf_op jit(solution)/shard_map/all_to_all | solution.py:150
  9.4 39.3 %collective-permute-start.1 = (bf16[4096,128]{1,0:T(8,128)(2,1)}, bf16[4096,128]{1,0:T(8,128)(2,1)S(1)}, u32[]{:S(2)}, u32[]{:S(2)}) collective-permute-start(bf16[4096,128]{1,0:T(8,128)(2,1)} %bitcast.90), channel_id=1, source_target_pairs={{0,1},{1,0},{2,3},{3,2},{4,5},{5,4},{6,7},{7,6},{8,9},{9,8},{10,11... | collective-permute-start | bytes 3145736 | tf_op jit(solution)/shard_map/ppermute | solution.py:20
  14.8 33.9 %collective-permute-start.2 = (bf16[4096,128]{1,0:T(8,128)(2,1)}, bf16[4096,128]{1,0:T(8,128)(2,1)}, u32[]{:S(2)}, u32[]{:S(2)}) collective-permute-start(bf16[4096,128]{1,0:T(8,128)(2,1)} %bitcast.107), channel_id=1, source_target_pairs={{0,1},{1,0},{2,3},{3,2},{4,5},{5,4},{6,7},{7,6},{8,9},{9,8},{10,11... | collective-permute-start | bytes 3145736 | tf_op jit(solution)/shard_map/ppermute | solution.py:20
  16.7 32.0 %collective-permute-start.3 = (bf16[2048,256]{1,0:T(8,128)(2,1)S(1)}, bf16[2048,256]{1,0:T(8,128)(2,1)S(1)}, u32[]{:S(2)}, u32[]{:S(2)}) collective-permute-start(bf16[2048,256]{1,0:T(8,128)(2,1)S(1)} %bitcast.89), channel_id=1, source_target_pairs={{0,1},{1,0},{2,3},{3,2},{4,5},{5,4},{6,7},{7,6},{8,9},{9,8},{10,11... | collective-permute-start | bytes 3145736 | tf_op jit(solution)/shard_map/ppermute | solution.py:20
  20.0 17.3 %all-to-all-start = ((bf16[16,64,256]{2,1,0:T(8,128)(2,1)}), bf16[16,64,256]{2,1,0:T(8,128)(2,1)}, u32[]{:S(2)}, u32[]{:S(2)}) async-start(bf16[16,64,256]{2,1,0:T(8,128)(2,1)} %broadcast_in_dim.53), calls=%async_computation | async-start | bytes 1048576 | tf_op jit(solution)/shard_map/all_to_all | solution.py:150
  30.0 17.4 %collective-permute-start.21 = (bf16[4,64,256]{2,1,0:T(8,128)(2,1)S(1)}, bf16[4,64,256]{2,1,0:T(8,128)(2,1)}, u32[]{:S(2)}, u32[]{:S(2)}) collective-permute-start(bf16[4,64,256]{2,1,0:T(8,128)(2,1)S(1)} %gather_fusion.4), channel_id=1, source_target_pairs={{0,1},{1,0},{2,3},{3,2},{4,5},{5,4},{6,7},{7,6},{8,9},{9,8},{10,11... | collective-permute-start | bytes 393224 | tf_op jit(solution)/shard_map/ppermute | solution.py:20
  48.7 11.7 %collective-permute-start.22 = (bf16[256,256]{1,0:T(8,128)(2,1)S(1)}, bf16[256,256]{1,0:T(8,128)(2,1)S(1)}, u32[]{:S(2)}, u32[]{:S(2)}) collective-permute-start(bf16[256,256]{1,0:T(8,128)(2,1)S(1)} %bitcast.126), channel_id=1, source_target_pairs={{0,32},{1,481},{2,34},{3,483},{4,36},{5,485},{6,38},{7,487},{8,40}... | collective-permute-start | bytes 393224 | tf_op jit(solution)/shard_map/ppermute | solution.py:34
  65.0 9.5 %collective-permute-start.5 = (bf16[2,256,256]{2,1,0:T(8,128)(2,1)S(1)}, bf16[2,256,256]{2,1,0:T(8,128)(2,1)S(1)}, u32[]{:S(2)}, u32[]{:S(2)}) collective-permute-start(bf16[2,256,256]{2,1,0:T(8,128)(2,1)S(1)} %pad_maximum_fusion.pair), channel_id=1, source_target_pairs={{0,480},{1,33},{2,482},{3,35},{4,484},{5,37},{6,486},{7,39},{8,488... | collective-permute-start | bytes 786440 | tf_op jit(solution)/shard_map/ppermute | solution.py:34
  69.1 10.5 %collective-permute-start.24 = (bf16[2,256,256]{2,1,0:T(8,128)(2,1)S(1)}, bf16[2,256,256]{2,1,0:T(8,128)(2,1)S(1)}, u32[]{:S(2)}, u32[]{:S(2)}) collective-permute-start(bf16[2,256,256]{2,1,0:T(8,128)(2,1)S(1)} %collective-permute-done.23.pair), channel_id=1, source_target_pairs={{0,32},{1,481},{2,34},{3,483},{4,36},{5,485},{6,38},{7,487},{8,40}... | collective-permute-start | bytes 786440 | tf_op jit(solution)/shard_map/ppermute | solution.py:34
  83.7 10.5 %collective-permute-start.7 = (bf16[2,256,256]{2,1,0:T(8,128)(2,1)S(1)}, bf16[2,256,256]{2,1,0:T(8,128)(2,1)}, u32[]{:S(2)}, u32[]{:S(2)}) collective-permute-start(bf16[2,256,256]{2,1,0:T(8,128)(2,1)S(1)} %collective-permute-done.6.pair), channel_id=1, source_target_pairs={{0,480},{1,33},{2,482},{3,35},{4,484},{5,37},{6,486},{7,39},{8,488... | collective-permute-start | bytes 786440 | tf_op jit(solution)/shard_map/ppermute | solution.py:34
  88.8 10.5 %collective-permute-start.26 = (bf16[2,256,256]{2,1,0:T(8,128)(2,1)S(1)}, bf16[2,256,256]{2,1,0:T(8,128)(2,1)S(1)}, u32[]{:S(2)}, u32[]{:S(2)}) collective-permute-start(bf16[2,256,256]{2,1,0:T(8,128)(2,1)S(1)} %collective-permute-done.25.pair), channel_id=1, source_target_pairs={{0,32},{1,481},{2,34},{3,483},{4,36},{5,485},{6,38},{7,487},{8,40}... | collective-permute-start | bytes 786440 | tf_op jit(solution)/shard_map/ppermute | solution.py:34
  94.2 9.4 %collective-permute-start.8 = (bf16[2,256,256]{2,1,0:T(8,128)(2,1)}, bf16[2,256,256]{2,1,0:T(8,128)(2,1)S(1)}, u32[]{:S(2)}, u32[]{:S(2)}) collective-permute-start(bf16[2,256,256]{2,1,0:T(8,128)(2,1)} %collective-permute-done.7.pair), channel_id=1, source_target_pairs={{0,32},{1,481},{2,34},{3,483},{4,36},{5,485},{6,38},{7,487},{8,40}... | collective-permute-start | bytes 786440 | tf_op jit(solution)/shard_map/ppermute | solution.py:34
  99.3 9.7 %collective-permute-start.27 = (bf16[2,256,256]{2,1,0:T(8,128)(2,1)S(1)}, bf16[2,256,256]{2,1,0:T(8,128)(2,1)S(1)}, u32[]{:S(2)}, u32[]{:S(2)}) collective-permute-start(bf16[2,256,256]{2,1,0:T(8,128)(2,1)S(1)} %collective-permute-done.26.pair), channel_id=1, source_target_pairs={{0,480},{1,33},{2,482},{3,35},{4,484},{5,37},{6,486},{7,39},{8,488... | collective-permute-start | bytes 786440 | tf_op jit(solution)/shard_map/ppermute | solution.py:34
  103.6 10.7 %collective-permute-start.9 = (bf16[2,256,256]{2,1,0:T(8,128)(2,1)S(1)}, bf16[2,256,256]{2,1,0:T(8,128)(2,1)S(1)}, u32[]{:S(2)}, u32[]{:S(2)}) collective-permute-start(bf16[2,256,256]{2,1,0:T(8,128)(2,1)S(1)} %collective-permute-done.8.pair), channel_id=1, source_target_pairs={{0,480},{1,33},{2,482},{3,35},{4,484},{5,37},{6,486},{7,39},{8,488... | collective-permute-start | bytes 786440 | tf_op jit(solution)/shard_map/ppermute | solution.py:34
  109.0 10.4 %collective-permute-start.28 = (bf16[2,256,256]{2,1,0:T(8,128)(2,1)S(1)}, bf16[2,256,256]{2,1,0:T(8,128)(2,1)S(1)}, u32[]{:S(2)}, u32[]{:S(2)}) collective-permute-start(bf16[2,256,256]{2,1,0:T(8,128)(2,1)S(1)} %collective-permute-done.27.pair), channel_id=1, source_target_pairs={{0,32},{1,481},{2,34},{3,483},{4,36},{5,485},{6,38},{7,487},{8,40}... | collective-permute-start | bytes 786440 | tf_op jit(solution)/shard_map/ppermute | solution.py:34
  119.4 9.9 %collective-permute-start.29 = (bf16[2,256,256]{2,1,0:T(8,128)(2,1)S(1)}, bf16[2,256,256]{2,1,0:T(8,128)(2,1)S(1)}, u32[]{:S(2)}, u32[]{:S(2)}) collective-permute-start(bf16[2,256,256]{2,1,0:T(8,128)(2,1)S(1)} %collective-permute-done.28.pair), channel_id=1, source_target_pairs={{0,480},{1,33},{2,482},{3,35},{4,484},{5,37},{6,486},{7,39},{8,488... | collective-permute-start | bytes 786440 | tf_op jit(solution)/shard_map/ppermute | solution.py:34
  123.3 12.7 %collective-permute-start.11 = (bf16[2,256,256]{2,1,0:T(8,128)(2,1)S(1)}, bf16[2,256,256]{2,1,0:T(8,128)(2,1)S(1)}, u32[]{:S(2)}, u32[]{:S(2)}) collective-permute-start(bf16[2,256,256]{2,1,0:T(8,128)(2,1)S(1)} %collective-permute-done.10.pair), channel_id=1, source_target_pairs={{0,480},{1,33},{2,482},{3,35},{4,484},{5,37},{6,486},{7,39},{8,488... | collective-permute-start | bytes 786440 | tf_op jit(solution)/shard_map/ppermute | solution.py:34
  131.3 10.4 %collective-permute-start.30 = (bf16[256,256]{1,0:T(8,128)(2,1)S(1)}, bf16[256,256]{1,0:T(8,128)(2,1)S(1)}, u32[]{:S(2)}, u32[]{:S(2)}) collective-permute-start(bf16[256,256]{1,0:T(8,128)(2,1)S(1)} %add_product.55), channel_id=1, source_target_pairs={{0,32},{1,481},{2,34},{3,483},{4,36},{5,485},{6,38},{7,487},{8,40}... | collective-permute-start | bytes 393224 | tf_op jit(solution)/shard_map/ppermute | solution.py:34
  150.6 10.3 %collective-permute-start.32 = (bf16[2,256,256]{2,1,0:T(8,128)(2,1)S(1)}, bf16[2,256,256]{2,1,0:T(8,128)(2,1)S(1)}, u32[]{:S(2)}, u32[]{:S(2)}) collective-permute-start(bf16[2,256,256]{2,1,0:T(8,128)(2,1)S(1)} %collective-permute-done.31.pair), channel_id=1, source_target_pairs={{0,32},{1,481},{2,34},{3,483},{4,36},{5,485},{6,38},{7,487},{8,40}... | collective-permute-start | bytes 786440 | tf_op jit(solution)/shard_map/ppermute | solution.py:34
  154.1 10.5 %collective-permute-start.14 = (bf16[2,256,256]{2,1,0:T(8,128)(2,1)S(1)}, bf16[2,256,256]{2,1,0:T(8,128)(2,1)S(1)}, u32[]{:S(2)}, u32[]{:S(2)}) collective-permute-start(bf16[2,256,256]{2,1,0:T(8,128)(2,1)S(1)} %collective-permute-done.13.pair), channel_id=1, source_target_pairs={{0,32},{1,481},{2,34},{3,483},{4,36},{5,485},{6,38},{7,487},{8,40}... | collective-permute-start | bytes 786440 | tf_op jit(solution)/shard_map/ppermute | solution.py:34
  160.9 9.7 %collective-permute-start.33 = (bf16[2,256,256]{2,1,0:T(8,128)(2,1)S(1)}, bf16[2,256,256]{2,1,0:T(8,128)(2,1)S(1)}, u32[]{:S(2)}, u32[]{:S(2)}) collective-permute-start(bf16[2,256,256]{2,1,0:T(8,128)(2,1)S(1)} %collective-permute-done.32.pair), channel_id=1, source_target_pairs={{0,480},{1,33},{2,482},{3,35},{4,484},{5,37},{6,486},{7,39},{8,488... | collective-permute-start | bytes 786440 | tf_op jit(solution)/shard_map/ppermute | solution.py:34
  164.6 10.1 %collective-permute-start.15 = (bf16[2,256,256]{2,1,0:T(8,128)(2,1)S(1)}, bf16[2,256,256]{2,1,0:T(8,128)(2,1)S(1)}, u32[]{:S(2)}, u32[]{:S(2)}) collective-permute-start(bf16[2,256,256]{2,1,0:T(8,128)(2,1)S(1)} %collective-permute-done.14.pair), channel_id=1, source_target_pairs={{0,480},{1,33},{2,482},{3,35},{4,484},{5,37},{6,486},{7,39},{8,488... | collective-permute-start | bytes 786440 | tf_op jit(solution)/shard_map/ppermute | solution.py:34
  170.6 11.0 %collective-permute-start.34 = (bf16[2,256,256]{2,1,0:T(8,128)(2,1)S(1)}, bf16[2,256,256]{2,1,0:T(8,128)(2,1)S(1)}, u32[]{:S(2)}, u32[]{:S(2)}) collective-permute-start(bf16[2,256,256]{2,1,0:T(8,128)(2,1)S(1)} %collective-permute-done.33.pair), channel_id=1, source_target_pairs={{0,32},{1,481},{2,34},{3,483},{4,36},{5,485},{6,38},{7,487},{8,40}... | collective-permute-start | bytes 786440 | tf_op jit(solution)/shard_map/ppermute | solution.py:34
  174.6 12.3 %collective-permute-start.16 = (bf16[2,256,256]{2,1,0:T(8,128)(2,1)S(1)}, bf16[2,256,256]{2,1,0:T(8,128)(2,1)S(1)}, u32[]{:S(2)}, u32[]{:S(2)}) collective-permute-start(bf16[2,256,256]{2,1,0:T(8,128)(2,1)S(1)} %collective-permute-done.15.pair), channel_id=1, source_target_pairs={{0,32},{1,481},{2,34},{3,483},{4,36},{5,485},{6,38},{7,487},{8,40}... | collective-permute-start | bytes 786440 | tf_op jit(solution)/shard_map/ppermute | solution.py:34
  181.6 12.4 %collective-permute-start.35 = (bf16[2,256,256]{2,1,0:T(8,128)(2,1)S(1)}, bf16[2,256,256]{2,1,0:T(8,128)(2,1)S(1)}, u32[]{:S(2)}, u32[]{:S(2)}) collective-permute-start(bf16[2,256,256]{2,1,0:T(8,128)(2,1)S(1)} %collective-permute-done.34.pair), channel_id=1, source_target_pairs={{0,480},{1,33},{2,482},{3,35},{4,484},{5,37},{6,486},{7,39},{8,488... | collective-permute-start | bytes 786440 | tf_op jit(solution)/shard_map/ppermute | solution.py:34
  186.9 10.7 %collective-permute-start.17 = (bf16[2,256,256]{2,1,0:T(8,128)(2,1)S(1)}, bf16[2,256,256]{2,1,0:T(8,128)(2,1)S(1)}, u32[]{:S(2)}, u32[]{:S(2)}) collective-permute-start(bf16[2,256,256]{2,1,0:T(8,128)(2,1)S(1)} %collective-permute-done.16.pair), channel_id=1, source_target_pairs={{0,480},{1,33},{2,482},{3,35},{4,484},{5,37},{6,486},{7,39},{8,488... | collective-permute-start | bytes 786440 | tf_op jit(solution)/shard_map/ppermute | solution.py:34
  194.0 11.2 %collective-permute-start.36 = (bf16[2,256,256]{2,1,0:T(8,128)(2,1)S(1)}, bf16[2,256,256]{2,1,0:T(8,128)(2,1)S(1)}, u32[]{:S(2)}, u32[]{:S(2)}) collective-permute-start(bf16[2,256,256]{2,1,0:T(8,128)(2,1)S(1)} %collective-permute-done.35.pair), channel_id=1, source_target_pairs={{0,32},{1,481},{2,34},{3,483},{4,36},{5,485},{6,38},{7,487},{8,40}... | collective-permute-start | bytes 786440 | tf_op jit(solution)/shard_map/ppermute | solution.py:34
  197.6 13.2 %collective-permute-start.18 = (bf16[2,256,256]{2,1,0:T(8,128)(2,1)S(1)}, bf16[2,256,256]{2,1,0:T(8,128)(2,1)S(1)}, u32[]{:S(2)}, u32[]{:S(2)}) collective-permute-start(bf16[2,256,256]{2,1,0:T(8,128)(2,1)S(1)} %collective-permute-done.17.pair), channel_id=1, source_target_pairs={{0,32},{1,481},{2,34},{3,483},{4,36},{5,485},{6,38},{7,487},{8,40}... | collective-permute-start | bytes 786440 | tf_op jit(solution)/shard_map/ppermute | solution.py:34
  205.2 9.4 %collective-permute-start.37 = (bf16[2,256,256]{2,1,0:T(8,128)(2,1)S(1)}, bf16[2,256,256]{2,1,0:T(8,128)(2,1)S(1)}, u32[]{:S(2)}, u32[]{:S(2)}) collective-permute-start(bf16[2,256,256]{2,1,0:T(8,128)(2,1)S(1)} %collective-permute-done.36.pair), channel_id=1, source_target_pairs={{0,480},{1,33},{2,482},{3,35},{4,484},{5,37},{6,486},{7,39},{8,488... | collective-permute-start | bytes 786440 | tf_op jit(solution)/shard_map/ppermute | solution.py:34
  210.8 22.3 %collective-permute-start.19 = (bf16[2,256,256]{2,1,0:T(8,128)(2,1)S(1)}, bf16[2,256,256]{2,1,0:T(8,128)(2,1)S(1)}, u32[]{:S(2)}, u32[]{:S(2)}) collective-permute-start(bf16[2,256,256]{2,1,0:T(8,128)(2,1)S(1)} %collective-permute-done.18.pair), channel_id=1, source_target_pairs={{0,480},{1,33},{2,482},{3,35},{4,484},{5,37},{6,486},{7,39},{8,488... | collective-permute-start | bytes 786440 | tf_op jit(solution)/shard_map/ppermute | solution.py:34
  216.6 20.4 %collective-permute-start.38 = (bf16[4,64,256]{2,1,0:T(8,128)(2,1)S(1)}, bf16[4,64,256]{2,1,0:T(8,128)(2,1)S(1)}, u32[]{:S(2)}, u32[]{:S(2)}) collective-permute-start(bf16[4,64,256]{2,1,0:T(8,128)(2,1)S(1)} %bitcast.69), channel_id=1, source_target_pairs={{0,1},{1,0},{2,3},{3,2},{4,5},{5,4},{6,7},{7,6},{8,9},{9,8},{10,11... | collective-permute-start | bytes 393224 | tf_op jit(solution)/shard_map/ppermute | solution.py:20
  253.5 13.7 %all-to-all-start.3 = ((bf16[16,64,256]{2,1,0:T(8,128)(2,1)}), bf16[16,64,256]{2,1,0:T(8,128)(2,1)S(1)}, u32[]{:S(2)}, u32[]{:S(2)}) async-start(bf16[16,64,256]{2,1,0:T(8,128)(2,1)} %get-tuple-element.162), calls=%async_computation.3 | async-start | bytes 1048576 | tf_op jit(solution)/shard_map/all_to_all | solution.py:159
  (14 other events, 327.6 us)

commit v3 on v0

v3 whole, which is shorter than its diff:
```python
import jax
import jax.numpy as jnp
from jax import lax
from jax.experimental import pallas as pl
from jax.experimental.pallas import tpu as pltpu
from jax.sharding import PartitionSpec as P

BLOCK = 128
SPAN = 4
CHIPS = 16
DEPTH = 16
OWNERS = 32
SAME_CORE = [[2 * chip + core for chip in range(CHIPS)] for core in range(2)]
TURNS = (15, 4, 2, 1)
MASKS = [0]
for turn in TURNS:
    MASKS += [mask ^ turn for mask in MASKS]


def swap_core(value):
    return lax.ppermute(value, "exp", [(p, p ^ 1) for p in range(OWNERS)])


def swap_across(value):
    return lax.ppermute(value, "exp", [(p, p ^ 2) for p in range(OWNERS)])


def swap_tok(value, partner):
    pairs = [(z * OWNERS + p, partner(z, p % 2) * OWNERS + p) for z in range(DEPTH) for p in range(OWNERS)]
    return lax.ppermute(value, ("tok", "exp"), pairs)


def swap_near(value, step):
    def partner(z, core):
        return (z + 1) % DEPTH if (z + step + core) % 2 == 0 else (z - 1) % DEPTH

    return swap_tok(value, partner)


def swap_turn(value, turn):
    return swap_tok(value, lambda z, core: (((z + 4 * core) % DEPTH ^ turn) - 4 * core) % DEPTH)


def near_order(z, core):
    turned = lax.rem(z - core + DEPTH, DEPTH)
    pair, odd = turned // 2, lax.rem(turned, 2)
    away = jnp.where(odd == 1, 1, -1)
    pairs = [pair]
    for step in range(1, DEPTH // 2):
        reach = (step + 1) // 2
        pairs.append(pair + (away * reach if step % 2 else -away * reach))
    chunks = [2 * p + half + core for p in pairs for half in range(2)]
    return odd == 1, lax.rem(jnp.stack(chunks) + 2 * DEPTH, DEPTH).astype(jnp.int32)


def turn_order(z, core):
    place = lax.rem(z + 4 * core, DEPTH)
    places = jnp.bitwise_xor(place, jnp.array(MASKS, jnp.int32))
    return lax.rem(places - 4 * core + DEPTH, DEPTH).astype(jnp.int32)


def start_rows(order, weights, held, arrived):
    taken = held.shape[2]
    copies = []
    for number in range(DEPTH):
        rows = pl.ds(pl.multiple_of(order[number] * taken, taken), taken)
        for which, weight in enumerate(weights):
            copy = pltpu.make_async_copy(weight.at[rows, :], held.at[number, which], arrived.at[number, which])
            copy.start()
            copies.append(copy)
    return copies


def hidden_kernel(order, first_low, first_high, second_low, second_high, *refs):
    ins, (out, held, arrived) = refs[:-3], refs[-3:]
    count = 2 * len(ins)
    weights = [w.at[kind] for kind in range(2) for w in ins]
    copies = start_rows(order, weights, held, arrived)
    total = None
    for number in range(DEPTH):
        first, second = (first_low, second_low) if number < DEPTH // 2 else (first_high, second_high)
        place = number % (DEPTH // 2)
        left = jnp.concatenate([first[place], second[place]], axis=0)
        for copy in copies[number * count : (number + 1) * count]:
            copy.wait()
        right = jnp.concatenate([held[number, which] for which in range(count)], axis=1)
        term = jnp.dot(left, right, preferred_element_type=jnp.float32)
        total = term if total is None else total + term
    units = total.shape[1] // 2
    gate, up = total[:, :units], total[:, units:]
    out[...] = (gate / (1.0 + jnp.exp(-gate)) * up).astype(out.dtype)


def down_kernel(order, scale, *refs):
    items, downs, (out, held, arrived) = refs[:DEPTH], refs[DEPTH:-3], refs[-3:]
    count = len(downs)
    copies = start_rows(order, downs, held, arrived)
    total = None
    for number in range(DEPTH):
        pair, half = number // 2, number % 2
        left = jnp.concatenate([items[pair][half], items[DEPTH // 2 + pair][half]], axis=0)
        for copy in copies[number * count : (number + 1) * count]:
            copy.wait()
        right = jnp.concatenate([held[number, which] for which in range(count)], axis=0)
        term = jnp.dot(left, right, preferred_element_type=jnp.float32)
        total = term if total is None else total + term
    out[...] = (total * scale[...]).astype(out.dtype)


def kernel_call(kernel, name, order, inner, weights, rows, columns, width, taken, count, wide):
    in_vmem = pl.BlockSpec(memory_space=pltpu.VMEM)
    return pl.pallas_call(
        kernel,
        out_shape=jax.ShapeDtypeStruct((rows, width), jnp.bfloat16),
        in_specs=[pl.BlockSpec(memory_space=pltpu.SMEM)]
        + [in_vmem] * len(inner)
        + [pl.BlockSpec(memory_space=pltpu.HBM)] * len(weights),
        out_specs=in_vmem,
        scratch_shapes=[
            pltpu.VMEM((DEPTH, count, taken, wide), jnp.bfloat16),
            pltpu.SemaphoreType.DMA((DEPTH, count)),
        ],
        compiler_params=pltpu.CompilerParams(vmem_limit_bytes=24 << 20),
        cost_estimate=pl.CostEstimate(
            flops=2 * rows * DEPTH * taken * count * wide,
            bytes_accessed=2 * DEPTH * taken * count * wide,
            transcendentals=0,
        ),
        name=name,
    )(order, *inner, *[pltpu.with_memory_space_constraint(w, pltpu.HBM) for w in weights])


def gather_half(chunk):
    held = chunk[None]
    for turn in TURNS[:-1]:
        held = jnp.concatenate([held, swap_turn(held, turn)])
    return held


def gather_near(chunk, odd):
    other = swap_near(chunk, 0)
    items = [jnp.stack([jnp.where(odd, other, chunk), jnp.where(odd, chunk, other)])]
    for step in range(1, DEPTH // 2):
        items.append(swap_near(items[-1], step))
    return items


def shards(tokens, picked_blocks, gate_scale, w_gate, w_up, w_down):
    position = lax.axis_index("exp")
    z = lax.axis_index("tok")
    core = lax.rem(position, 2)
    share = lax.rem(position, SPAN)
    expert = position // SPAN
    features = tokens.shape[1]
    chosen = lax.dynamic_index_in_dim(picked_blocks, expert, 0, keepdims=False)
    blocks = chosen.shape[0] // SPAN
    rows = blocks * BLOCK
    mine = lax.dynamic_slice_in_dim(chosen, blocks * share, blocks)
    theirs = lax.dynamic_slice_in_dim(chosen, blocks * jnp.bitwise_xor(share, 1), blocks)
    here = (lax.rem(mine, 2) == core)[:, None, None]
    odd, near = near_order(z, core)
    turns = turn_order(z, core)
    scale = lax.dynamic_index_in_dim(gate_scale, expert, 0, keepdims=False).reshape(SPAN, rows, 1)
    scale = lax.dynamic_index_in_dim(scale, share, 0, keepdims=False)
    names = jnp.concatenate([mine, theirs])
    match = names[None, :] == (2 * jnp.arange(CHIPS, dtype=jnp.int32) + core)[:, None]
    wanted, source = match.any(1)[:, None, None], jnp.argmax(match, 1)

    in_own = jnp.stack([w_gate[0], w_up[0]])
    down_own = w_down[0]
    spread = jnp.broadcast_to(tokens[None], (CHIPS,) + tokens.shape)
    held = lax.all_to_all(spread, "exp", 0, 0, axis_index_groups=SAME_CORE, tiled=True)
    in_near, down_near = swap_core(in_own), swap_core(down_own)
    held, in_own, down_own = lax.optimization_barrier((held, in_own, down_own))
    lent = swap_core(held[theirs // 2])
    selected = jnp.where(here, held[mine // 2], lent)
    selected, in_near, down_near, near, turns, wanted, source, odd, scale = lax.optimization_barrier(
        (selected, in_near, down_near, near, turns, wanted, source, odd, scale)
    )

    in_far = swap_across(in_own)
    lows = [gather_half(selected[block]) for block in range(blocks)]
    parts = [(low, swap_turn(low, TURNS[-1])) for low in lows]
    in_far, down_own, _ = lax.optimization_barrier((in_far, down_own, lows))
    down_far = swap_across(down_own)
    ins = [in_own, in_near, in_far, swap_core(in_far)]
    units = w_gate.shape[2]
    hidden = kernel_call(
        hidden_kernel, "hidden", turns, [p for part in parts for p in part], ins,
        rows, 2 * SPAN * units, SPAN * units, features, 2 * SPAN, units,
    )

    items = [item for block in range(blocks) for item in gather_near(hidden[block * BLOCK : (block + 1) * BLOCK], odd)]
    downs = [down_own, down_near, down_far, swap_core(down_far)]
    done = kernel_call(
        down_kernel, "down", near, [scale] + items, downs,
        rows, features, features, units, SPAN, features,
    )
    done = done.reshape(blocks, BLOCK, features)

    all_done = jnp.concatenate([done, swap_core(done)])
    outgoing = jnp.where(wanted, all_done[source], 0)
    arrived = lax.all_to_all(outgoing, "exp", 0, 0, axis_index_groups=SAME_CORE, tiled=True)
    return jnp.sum(arrived, axis=0, dtype=jnp.float32).astype(jnp.bfloat16)


def solution(mesh):
    return jax.shard_map(
        shards,
        mesh=mesh,
        in_specs=(
            P("exp", "tok"),
            P(),
            P(),
            P("exp", None, "tok"),
            P("exp", None, "tok"),
            P("exp", None, "tok"),
        ),
        out_specs=P("exp", "tok"),
        check_vma=False,
    )
```

time: 424 us -> 255 us (0.60)
  waiting for transfers between devices: 386 us -> 88.3 us
  starting transfers between devices: 0.12 us -> 122 us
  blocking collectives: 0 us -> 19.3 us
  between operations: 13.2 us -> 0.67 us
  matrix products: 12.5 us -> 0 us
  Pallas kernels: 0 us -> 12.3 us
    all_gather x3 -> x0, waiting for transfers between devices: 277 us -> none  [the longest x1 120 us: shards(): full_rows = lax.all_gather(selected, 'tok', axis=1, tiled=True)]
    ppermute x0 -> x32, starting transfers between devices: none -> 118 us  [the longest x24 79.9 us: swap_tok(): return lax.ppermute(value, ('tok', 'exp'), pairs)]
    reduce_scatter x1 -> x0, waiting for transfers between devices: 109 us -> none  [shards(): lax.psum_scatter(buffer, 'exp', scatter_dimension=0, tiled=True)]
    ppermute x0 -> x32, waiting for transfers between devices: none -> 73.5 us  [the longest x24 72.1 us: swap_tok(): return lax.ppermute(value, ('tok', 'exp'), pairs)]
    all_to_all x0 -> x1, blocking collectives: none -> 19.3 us  [shards(): lax.all_to_all(outgoing, 'exp', 0, 0, axis_index_groups=SAME_CORE, tiled=...]
    all_to_all x0 -> x1, waiting for transfers between devices: none -> 14.8 us  [shards(): lax.all_to_all(spread, 'exp', 0, 0, axis_index_groups=SAME_CORE, tiled=True)]
    dot_general x3 -> x0, matrix products: 12.5 us -> none  [the longest x1 6.08 us: shards(): jnp.dot(full_rows, gate_local, preferred_element_type=jnp.float32)]
    pallas_call x0 -> x2, Pallas kernels: none -> 12.3 us  [kernel_call(): pl.pallas_call(kernel, out_shape=jax.ShapeDtypeStruct((rows, width), jnp....]
  transfers between devices with their start and end apart: 4 -> 33, of which waited for: 4 -> 22; matrix products, arithmetic and copies ran while one was open for 0% -> 3% of each run, Pallas kernels for 0% -> 0%
where the time goes in v3:
time: 255 us; the launch traced here: 254 us
  starting transfers between devices  122 us (48%)
  waiting for transfers between devices  88.3 us (35%)
  blocking collectives  19.3 us (8%)
  Pallas kernels  12.3 us (5%)
  local copies, waits for them, and re-layouts  7.62 us (3%)
  other arithmetic  3.66 us (1%)
    ppermute x24, starting transfers between devices, swap_tok(): return lax.ppermute(value, ('tok', 'exp'), pairs)  79.9 us
    ppermute x24, waiting for transfers between devices, swap_tok(): return lax.ppermute(value, ('tok', 'exp'), pairs)  72.1 us
    ppermute x6, starting transfers between devices, swap_core(): return lax.ppermute(value, 'exp', [(p, p ^ 1) for p in range(OWNERS)])  33 us
    all_to_all x1, blocking collectives, shards(): lax.all_to_all(outgoing, 'exp', 0, 0, axis_index_groups=SAME_CORE, tiled=...  19.3 us
    all_to_all x1, waiting for transfers between devices, shards(): lax.all_to_all(spread, 'exp', 0, 0, axis_index_groups=SAME_CORE, tiled=True)  14.8 us
    pallas_call x2, Pallas kernels, kernel_call(): pl.pallas_call(kernel, out_shape=jax.ShapeDtypeStruct((rows, width), jnp....  12.3 us
    ppermute x2, starting transfers between devices, swap_across(): return lax.ppermute(value, 'exp', [(p, p ^ 2) for p in range(OWNERS)])  5.55 us
  transfers between devices with their start and end apart: 33, of which 22 were waited for; matrix products, arithmetic and copies ran while one was open for 3% of the time, Pallas kernels for 0%

profile of v3, /device:TPU:1, one launch (start us, length us, event | category | flops | bytes accessed | tf_op | source)
XLA Modules:
  0.0 253.9 jit_solution(14319168358218589760)
XLA Ops:
  1.7 8.9 %collective-permute-start.1 = (bf16[2,4096,128]{2,1,0:T(8,128)(2,1)S(1)}, bf16[2,4096,128]{2,1,0:T(8,128)(2,1)}, u32[]{:S(2)}, u32[]{:S(2)}) collective-permute-start(bf16[2,4096,128]{2,1,0:T(8,128)(2,1)S(1)} %constant_dynamic-update-slice_fusion.refs_0_), channel_id=1, source_target_pairs={{0,1},{1,0},{2,3},{3,2},{4,5},{5,4},{6,7},{7,6},{8,9},{9,8},{10,11... | collective-permute-start | bytes 6291464 | tf_op jit(solution)/shard_map/ppermute | solution.py:21
  11.8 3.7 %all-to-all-start = ((bf16[16,128,256]{2,1,0:T(8,128)(2,1)}), bf16[16,128,256]{2,1,0:T(8,128)(2,1)S(1)}, u32[]{:S(2)}, u32[]{:S(2)}) async-start(bf16[16,128,256]{2,1,0:T(8,128)(2,1)} %broadcast_in_dim.40), calls=%async_computation | async-start | bytes 2097152 | tf_op jit(solution)/shard_map/all_to_all | solution.py:172
  19.8 14.8 %all-to-all-done = bf16[16,128,256]{2,1,0:T(8,128)(2,1)S(1)} async-done(((bf16[16,128,256]{2,1,0:T(8,128)(2,1)}), bf16[16,128,256]{2,1,0:T(8,128)(2,1)S(1)}, u32[]{:S(2)}, u32[]{:S(2)}) %all-to-all-start) | async-done | bytes 1048608 | tf_op jit(solution)/shard_map/all_to_all | solution.py:172
  38.5 2.7 %collective-permute-start = (bf16[2,128,256]{2,1,0:T(8,128)(2,1)}, bf16[2,128,256]{2,1,0:T(8,128)(2,1)S(1)}, u32[]{:S(2)}, u32[]{:S(2)}) collective-permute-start(bf16[2,128,256]{2,1,0:T(8,128)(2,1)} %gather_fusion.1), channel_id=1, source_target_pairs={{0,1},{1,0},{2,3},{3,2},{4,5},{5,4},{6,7},{7,6},{8,9},{9,8},{10,11... | collective-permute-start | bytes 393224 | tf_op jit(solution)/shard_map/ppermute | solution.py:21
  42.5 9.6 %collective-permute-start.7 = (bf16[1,128,256]{2,1,0:T(8,128)(2,1)S(1)}, bf16[1,128,256]{2,1,0:T(8,128)(2,1)S(1)}, u32[]{:S(2)}, u32[]{:S(2)}) collective-permute-start(bf16[1,128,256]{2,1,0:T(8,128)(2,1)S(1)} %get-tuple-element.42), channel_id=1, source_target_pairs={{0,480},{1,225},{2,482},{3,227},{4,484},{5,229},{6,486},{7,231},{8... | collective-permute-start | bytes 196616 | tf_op jit(solution)/shard_map/ppermute | solution.py:30
  54.5 3.7 %collective-permute-start.8 = (bf16[2,128,256]{2,1,0:T(8,128)(2,1)S(1)}, bf16[2,128,256]{2,1,0:T(8,128)(2,1)S(1)}, u32[]{:S(2)}, u32[]{:S(2)}) collective-permute-start(bf16[2,128,256]{2,1,0:T(8,128)(2,1)S(1)} %pad_maximum_fusion.8), channel_id=1, source_target_pairs={{0,128},{1,385},{2,130},{3,387},{4,132},{5,389},{6,134},{7,391},{8... | collective-permute-start | bytes 393224 | tf_op jit(solution)/shard_map/ppermute | solution.py:30
  58.3 5.6 %collective-permute-done.3 = bf16[1,128,256]{2,1,0:T(8,128)(2,1)S(1)} collective-permute-done((bf16[1,128,256]{2,1,0:T(8,128)(2,1)S(1)}, bf16[1,128,256]{2,1,0:T(8,128)(2,1)S(1)}, u32[]{:S(2)}, u32[]{:S(2)}) %collective-permute-start.3) | collective-permute-done | bytes 65568 | tf_op jit(solution)/shard_map/ppermute | solution.py:30
  65.8 5.3 %collective-permute-start.9 = (bf16[4,128,256]{2,1,0:T(8,128)(2,1)S(1)}, bf16[4,128,256]{2,1,0:T(8,128)(2,1)S(1)}, u32[]{:S(2)}, u32[]{:S(2)}) collective-permute-start(bf16[4,128,256]{2,1,0:T(8,128)(2,1)S(1)} %pad_maximum_fusion.3), channel_id=1, source_target_pairs={{0,64},{1,65},{2,66},{3,67},{4,68},{5,69},{6,70},{7,71},{8,72},{9,... | collective-permute-start | bytes 786440 | tf_op jit(solution)/shard_map/ppermute | solution.py:30
  71.2 4.2 %collective-permute-done.4 = bf16[2,128,256]{2,1,0:T(8,128)(2,1)S(1)} collective-permute-done((bf16[2,128,256]{2,1,0:T(8,128)(2,1)S(1)}, bf16[2,128,256]{2,1,0:T(8,128)(2,1)S(1)}, u32[]{:S(2)}, u32[]{:S(2)}) %collective-permute-start.4) | collective-permute-done | bytes 131104 | tf_op jit(solution)/shard_map/ppermute | solution.py:30
  75.4 2.6 %collective-permute-start.5 = (bf16[4,128,256]{2,1,0:T(8,128)(2,1)S(1)}, bf16[4,128,256]{2,1,0:T(8,128)(2,1)S(1)}, u32[]{:S(2)}, u32[]{:S(2)}) collective-permute-start(bf16[4,128,256]{2,1,0:T(8,128)(2,1)S(1)} %pad_maximum_fusion.2), channel_id=1, source_target_pairs={{0,64},{1,65},{2,66},{3,67},{4,68},{5,69},{6,70},{7,71},{8,72},{9,... | collective-permute-start | bytes 786440 | tf_op jit(solution)/shard_map/ppermute | solution.py:30
  78.0 12.9 %collective-permute-done.9 = bf16[4,128,256]{2,1,0:T(8,128)(2,1)S(1)} collective-permute-done((bf16[4,128,256]{2,1,0:T(8,128)(2,1)S(1)}, bf16[4,128,256]{2,1,0:T(8,128)(2,1)S(1)}, u32[]{:S(2)}, u32[]{:S(2)}) %collective-permute-start.9) | collective-permute-done | bytes 262176 | tf_op jit(solution)/shard_map/ppermute | solution.py:30
  91.0 5.6 %collective-permute-done.5 = bf16[4,128,256]{2,1,0:T(8,128)(2,1)S(1)} collective-permute-done((bf16[4,128,256]{2,1,0:T(8,128)(2,1)S(1)}, bf16[4,128,256]{2,1,0:T(8,128)(2,1)S(1)}, u32[]{:S(2)}, u32[]{:S(2)}) %collective-permute-start.5) | collective-permute-done | bytes 262176 | tf_op jit(solution)/shard_map/ppermute | solution.py:30
  96.6 4.9 %collective-permute-start.12 = (bf16[2,4096,128]{2,1,0:T(8,128)(2,1)}, bf16[2,4096,128]{2,1,0:T(8,128)(2,1)S(1)}, u32[]{:S(2)}, u32[]{:S(2)}) collective-permute-start(bf16[2,4096,128]{2,1,0:T(8,128)(2,1)} %collective-permute-done.11.refs_2_), channel_id=1, source_target_pairs={{0,1},{1,0},{2,3},{3,2},{4,5},{5,4},{6,7},{7,6},{8,9},{9,8},{10,11... | collective-permute-start | bytes 6291464 | tf_op jit(solution)/shard_map/ppermute | solution.py:21
  103.4 3.4 %collective-permute-start.6 = (bf16[8,128,256]{2,1,0:T(8,128)(2,1)S(1)}, bf16[8,128,256]{2,1,0:T(8,128)(2,1)S(1)}, u32[]{:S(2)}, u32[]{:S(2)}) collective-permute-start(bf16[8,128,256]{2,1,0:T(8,128)(2,1)S(1)} %pad_maximum_fusion.first_low), channel_id=1, source_target_pairs={{0,32},{1,33},{2,34},{3,35},{4,36},{5,37},{6,38},{7,39},{8,40},{9,... | collective-permute-start | bytes 1572872 | tf_op jit(solution)/shard_map/ppermute | solution.py:30
  106.8 10.1 %collective-permute-done.10.second_high = bf16[8,128,256]{2,1,0:T(8,128)(2,1)S(1)} collective-permute-done((bf16[8,128,256]{2,1,0:T(8,128)(2,1)S(1)}, bf16[8,128,256]{2,1,0:T(8,128)(2,1)S(1)}, u32[]{:S(2)}, u32[]{:S(2)}) %collective-permute-start.10) | collective-permute-done | bytes 524320 | tf_op jit(solution)/shard_map/ppermute | solution.py:30
  117.0 11.2 %collective-permute-done.6.first_high = bf16[8,128,256]{2,1,0:T(8,128)(2,1)S(1)} collective-permute-done((bf16[8,128,256]{2,1,0:T(8,128)(2,1)S(1)}, bf16[8,128,256]{2,1,0:T(8,128)(2,1)S(1)}, u32[]{:S(2)}, u32[]{:S(2)}) %collective-permute-start.6) | collective-permute-done | bytes 524320 | tf_op jit(solution)/shard_map/ppermute | solution.py:30
  129.6 6.3 %hidden.1 = bf16[256,512]{1,0:T(8,128)(2,1)S(1)} custom-call(s32[16]{0:T(128)S(1)} %get-tuple-element.26.order, bf16[8,128,256]{2,1,0:T(8,128)(2,1)S(1)} %pad_maximum_fusion.first_low, bf16[8,128,256]{2,1,0:T(8,128)(2,1)S(1)} %collective-permute-done.6.first_high, bf16[8,128,256]{2,1,0:T(8,128)(2,1)S(1)} %pad_maximum_fusion.1.second_low, ...), custom_call_target="tpu_custom_call" | custom-call | flops 2147483648 | bytes 8388608 | tf_op jit(solution)/shard_map/hidden/pallas_call | solution.py:112
  135.9 4.6 %collective-permute-start.21 = (bf16[128,512]{1,0:T(8,128)(2,1)S(1)}, bf16[128,512]{1,0:T(8,128)(2,1)S(1)}, u32[]{:S(2)}, u32[]{:S(2)}) collective-permute-start(bf16[128,512]{1,0:T(8,128)(2,1)S(1)} %slice.23), channel_id=1, source_target_pairs={{0,32},{1,481},{2,34},{3,483},{4,36},{5,485},{6,38},{7,487},{8,40}... | collective-permute-start | bytes 393224 | tf_op jit(solution)/shard_map/ppermute | solution.py:30
  142.9 4.6 %collective-permute-start.13 = (bf16[128,512]{1,0:T(8,128)(2,1)S(1)}, bf16[128,512]{1,0:T(8,128)(2,1)S(1)}, u32[]{:S(2)}, u32[]{:S(2)}) collective-permute-start(bf16[128,512]{1,0:T(8,128)(2,1)S(1)} %get-tuple-element.41), channel_id=1, source_target_pairs={{0,32},{1,481},{2,34},{3,483},{4,36},{5,485},{6,38},{7,487},{8,40}... | collective-permute-start | bytes 393224 | tf_op jit(solution)/shard_map/ppermute | solution.py:30
  147.5 3.6 %collective-permute-start.29 = (bf16[2048,256]{1,0:T(8,128)(2,1)S(1)}, bf16[2048,256]{1,0:T(8,128)(2,1)}, u32[]{:S(2)}, u32[]{:S(2)}) collective-permute-start(bf16[2048,256]{1,0:T(8,128)(2,1)S(1)} %bitcast.63), channel_id=1, source_target_pairs={{0,2},{1,3},{2,0},{3,1},{4,6},{5,7},{6,4},{7,5},{8,10},{9,11},{10,... | collective-permute-start | bytes 3145736 | tf_op jit(solution)/shard_map/ppermute | solution.py:25
  153.2 3.4 %collective-permute-start.14 = (bf16[2,128,512]{2,1,0:T(8,128)(2,1)S(1)}, bf16[2,128,512]{2,1,0:T(8,128)(2,1)S(1)}, u32[]{:S(2)}, u32[]{:S(2)}) collective-permute-start(bf16[2,128,512]{2,1,0:T(8,128)(2,1)S(1)} %pad_maximum_fusion.4.refs_0_), channel_id=1, source_target_pairs={{0,480},{1,33},{2,482},{3,35},{4,484},{5,37},{6,486},{7,39},{8,488... | collective-permute-start | bytes 786440 | tf_op jit(solution)/shard_map/ppermute | solution.py:30
  161.5 3.7 %collective-permute-start.15 = (bf16[2,128,512]{2,1,0:T(8,128)(2,1)S(1)}, bf16[2,128,512]{2,1,0:T(8,128)(2,1)S(1)}, u32[]{:S(2)}, u32[]{:S(2)}) collective-permute-start(bf16[2,128,512]{2,1,0:T(8,128)(2,1)S(1)} %collective-permute-done.14.refs_1_), channel_id=1, source_target_pairs={{0,32},{1,481},{2,34},{3,483},{4,36},{5,485},{6,38},{7,487},{8,40}... | collective-permute-start | bytes 786440 | tf_op jit(solution)/shard_map/ppermute | solution.py:30
  169.8 2.7 %collective-permute-start.16 = (bf16[2,128,512]{2,1,0:T(8,128)(2,1)S(1)}, bf16[2,128,512]{2,1,0:T(8,128)(2,1)S(1)}, u32[]{:S(2)}, u32[]{:S(2)}) collective-permute-start(bf16[2,128,512]{2,1,0:T(8,128)(2,1)S(1)} %collective-permute-done.15.refs_2_), channel_id=1, source_target_pairs={{0,480},{1,33},{2,482},{3,35},{4,484},{5,37},{6,486},{7,39},{8,488... | collective-permute-start | bytes 786440 | tf_op jit(solution)/shard_map/ppermute | solution.py:30
  177.6 4.0 %collective-permute-start.17 = (bf16[2,128,512]{2,1,0:T(8,128)(2,1)S(1)}, bf16[2,128,512]{2,1,0:T(8,128)(2,1)S(1)}, u32[]{:S(2)}, u32[]{:S(2)}) collective-permute-start(bf16[2,128,512]{2,1,0:T(8,128)(2,1)S(1)} %collective-permute-done.16.refs_3_), channel_id=1, source_target_pairs={{0,32},{1,481},{2,34},{3,483},{4,36},{5,485},{6,38},{7,487},{8,40}... | collective-permute-start | bytes 786440 | tf_op jit(solution)/shard_map/ppermute | solution.py:30
  181.6 6.3 %collective-permute-start.30 = (bf16[2048,256]{1,0:T(8,128)(2,1)}, bf16[2048,256]{1,0:T(8,128)(2,1)}, u32[]{:S(2)}, u32[]{:S(2)}) collective-permute-start(bf16[2048,256]{1,0:T(8,128)(2,1)} %collective-permute-done.29.refs_18_), channel_id=1, source_target_pairs={{0,1},{1,0},{2,3},{3,2},{4,5},{5,4},{6,7},{7,6},{8,9},{9,8},{10,11... | collective-permute-start | bytes 3145736 | tf_op jit(solution)/shard_map/ppermute | solution.py:21
  187.9 3.6 %collective-permute-start.26 = (bf16[2,128,512]{2,1,0:T(8,128)(2,1)S(1)}, bf16[2,128,512]{2,1,0:T(8,128)(2,1)S(1)}, u32[]{:S(2)}, u32[]{:S(2)}) collective-permute-start(bf16[2,128,512]{2,1,0:T(8,128)(2,1)S(1)} %collective-permute-done.25.refs_12_), channel_id=1, source_target_pairs={{0,480},{1,33},{2,482},{3,35},{4,484},{5,37},{6,486},{7,39},{8,488... | collective-permute-start | bytes 786440 | tf_op jit(solution)/shard_map/ppermute | solution.py:30
  195.6 5.9 %collective-permute-start.27 = (bf16[2,128,512]{2,1,0:T(8,128)(2,1)S(1)}, bf16[2,128,512]{2,1,0:T(8,128)(2,1)}, u32[]{:S(2)}, u32[]{:S(2)}) collective-permute-start(bf16[2,128,512]{2,1,0:T(8,128)(2,1)S(1)} %collective-permute-done.26.refs_13_), channel_id=1, source_target_pairs={{0,32},{1,481},{2,34},{3,483},{4,36},{5,485},{6,38},{7,487},{8,40}... | collective-permute-start | bytes 786440 | tf_op jit(solution)/shard_map/ppermute | solution.py:30
  201.5 2.8 %collective-permute-start.19 = (bf16[2,128,512]{2,1,0:T(8,128)(2,1)S(1)}, bf16[2,128,512]{2,1,0:T(8,128)(2,1)}, u32[]{:S(2)}, u32[]{:S(2)}) collective-permute-start(bf16[2,128,512]{2,1,0:T(8,128)(2,1)S(1)} %collective-permute-done.18.refs_5_), channel_id=1, source_target_pairs={{0,32},{1,481},{2,34},{3,483},{4,36},{5,485},{6,38},{7,487},{8,40}... | collective-permute-start | bytes 786440 | tf_op jit(solution)/shard_map/ppermute | solution.py:30
  212.0 3.3 %collective-permute-done.28.refs_15_ = bf16[2,128,512]{2,1,0:T(8,128)(2,1)} collective-permute-done((bf16[2,128,512]{2,1,0:T(8,128)(2,1)}, bf16[2,128,512]{2,1,0:T(8,128)(2,1)}, u32[]{:S(2)}, u32[]{:S(2)}) %collective-permute-start.28) | collective-permute-done | bytes 262176 | tf_op jit(solution)/shard_map/ppermute | solution.py:30
  217.8 6.0 %down.1 = bf16[256,256]{1,0:T(8,128)(2,1)S(1)} custom-call(s32[16]{0:T(128)S(1)} %get-tuple-element.23.order, f32[256,1]{1,0:T(8,128)S(1)} %copy.9.scale, bf16[2,128,512]{2,1,0:T(8,128)(2,1)S(1)} %pad_maximum_fusion.4.refs_0_, bf16[2,128,512]{2,1,0:T(8,128)(2,1)S(1)} %collective-permute-done.14.refs_1_, ...), custom_call_target="tpu_custom_call" | custom-call | flops 1073741824 | bytes 4194304 | tf_op jit(solution)/shard_map/down/pallas_call | solution.py:112
  223.9 8.2 %collective-permute-start.31 = (bf16[2,128,256]{2,1,0:T(8,128)(2,1)S(1)}, bf16[2,128,256]{2,1,0:T(8,128)(2,1)S(1)}, u32[]{:S(2)}, u32[]{:S(2)}) collective-permute-start(bf16[2,128,256]{2,1,0:T(8,128)(2,1)S(1)} %bitcast.59), channel_id=1, source_target_pairs={{0,1},{1,0},{2,3},{3,2},{4,5},{5,4},{6,7},{7,6},{8,9},{9,8},{10,11... | collective-permute-start | bytes 393224 | tf_op jit(solution)/shard_map/ppermute | solution.py:21
  233.9 19.3 %all_to_all.10 = bf16[16,128,256]{2,1,0:T(8,128)(2,1)S(1)} all-to-all(bf16[16,128,256]{2,1,0:T(8,128)(2,1)S(1)} %broadcast_select_fusion), channel_id=1, replica_groups={{0,2,4,6,8,10,12,14,16,18,20,22,24,26,28,30},{1,3,5,7,9,11,13,15,17,19,..., dimensions={0} | all-to-all | bytes 2097152 | tf_op jit(solution)/shard_map/all_to_all | solution.py:203
  (89 shorter events, 55.7 us)
Async XLA Ops:
  1.7 40.8 %collective-permute-start.1 = (bf16[2,4096,128]{2,1,0:T(8,128)(2,1)S(1)}, bf16[2,4096,128]{2,1,0:T(8,128)(2,1)}, u32[]{:S(2)}, u32[]{:S(2)}) collective-permute-start(bf16[2,4096,128]{2,1,0:T(8,128)(2,1)S(1)} %constant_dynamic-update-slice_fusion.refs_0_), channel_id=1, source_target_pairs={{0,1},{1,0},{2,3},{3,2},{4,5},{5,4},{6,7},{7,6},{8,9},{9,8},{10,11... | collective-permute-start | bytes 6291464 | tf_op jit(solution)/shard_map/ppermute | solution.py:21
  11.8 22.8 %all-to-all-start = ((bf16[16,128,256]{2,1,0:T(8,128)(2,1)}), bf16[16,128,256]{2,1,0:T(8,128)(2,1)S(1)}, u32[]{:S(2)}, u32[]{:S(2)}) async-start(bf16[16,128,256]{2,1,0:T(8,128)(2,1)} %broadcast_in_dim.40), calls=%async_computation | async-start | bytes 2097152 | tf_op jit(solution)/shard_map/all_to_all | solution.py:172
  15.4 27.1 %collective-permute-start.2 = (bf16[2048,256]{1,0:T(8,128)(2,1)}, bf16[2048,256]{1,0:T(8,128)(2,1)}, u32[]{:S(2)}, u32[]{:S(2)}) collective-permute-start(bf16[2048,256]{1,0:T(8,128)(2,1)} %bitcast.61), channel_id=1, source_target_pairs={{0,1},{1,0},{2,3},{3,2},{4,5},{5,4},{6,7},{7,6},{8,9},{9,8},{10,11... | collective-permute-start | bytes 3145736 | tf_op jit(solution)/shard_map/ppermute | solution.py:21
  34.5 62.0 %collective-permute-start.11 = (bf16[2,4096,128]{2,1,0:T(8,128)(2,1)S(1)}, bf16[2,4096,128]{2,1,0:T(8,128)(2,1)}, u32[]{:S(2)}, u32[]{:S(2)}) collective-permute-start(bf16[2,4096,128]{2,1,0:T(8,128)(2,1)S(1)} %constant_dynamic-update-slice_fusion.refs_0_), channel_id=1, source_target_pairs={{0,2},{1,3},{2,0},{3,1},{4,6},{5,7},{6,4},{7,5},{8,10},{9,11},{10,... | collective-permute-start | bytes 6291464 | tf_op jit(solution)/shard_map/ppermute | solution.py:25
  42.5 12.0 %collective-permute-start.7 = (bf16[1,128,256]{2,1,0:T(8,128)(2,1)S(1)}, bf16[1,128,256]{2,1,0:T(8,128)(2,1)S(1)}, u32[]{:S(2)}, u32[]{:S(2)}) collective-permute-start(bf16[1,128,256]{2,1,0:T(8,128)(2,1)S(1)} %get-tuple-element.42), channel_id=1, source_target_pairs={{0,480},{1,225},{2,482},{3,227},{4,484},{5,229},{6,486},{7,231},{8... | collective-permute-start | bytes 196616 | tf_op jit(solution)/shard_map/ppermute | solution.py:30
  52.2 11.7 %collective-permute-start.3 = (bf16[1,128,256]{2,1,0:T(8,128)(2,1)S(1)}, bf16[1,128,256]{2,1,0:T(8,128)(2,1)S(1)}, u32[]{:S(2)}, u32[]{:S(2)}) collective-permute-start(bf16[1,128,256]{2,1,0:T(8,128)(2,1)S(1)} %get-tuple-element.43), channel_id=1, source_target_pairs={{0,480},{1,225},{2,482},{3,227},{4,484},{5,229},{6,486},{7,231},{8... | collective-permute-start | bytes 196616 | tf_op jit(solution)/shard_map/ppermute | solution.py:30
  54.5 11.3 %collective-permute-start.8 = (bf16[2,128,256]{2,1,0:T(8,128)(2,1)S(1)}, bf16[2,128,256]{2,1,0:T(8,128)(2,1)S(1)}, u32[]{:S(2)}, u32[]{:S(2)}) collective-permute-start(bf16[2,128,256]{2,1,0:T(8,128)(2,1)S(1)} %pad_maximum_fusion.8), channel_id=1, source_target_pairs={{0,128},{1,385},{2,130},{3,387},{4,132},{5,389},{6,134},{7,391},{8... | collective-permute-start | bytes 393224 | tf_op jit(solution)/shard_map/ppermute | solution.py:30
  63.9 11.5 %collective-permute-start.4 = (bf16[2,128,256]{2,1,0:T(8,128)(2,1)S(1)}, bf16[2,128,256]{2,1,0:T(8,128)(2,1)S(1)}, u32[]{:S(2)}, u32[]{:S(2)}) collective-permute-start(bf16[2,128,256]{2,1,0:T(8,128)(2,1)S(1)} %pad_maximum_fusion.7), channel_id=1, source_target_pairs={{0,128},{1,385},{2,130},{3,387},{4,132},{5,389},{6,134},{7,391},{8... | collective-permute-start | bytes 393224 | tf_op jit(solution)/shard_map/ppermute | solution.py:30
  65.8 25.1 %collective-permute-start.9 = (bf16[4,128,256]{2,1,0:T(8,128)(2,1)S(1)}, bf16[4,128,256]{2,1,0:T(8,128)(2,1)S(1)}, u32[]{:S(2)}, u32[]{:S(2)}) collective-permute-start(bf16[4,128,256]{2,1,0:T(8,128)(2,1)S(1)} %pad_maximum_fusion.3), channel_id=1, source_target_pairs={{0,64},{1,65},{2,66},{3,67},{4,68},{5,69},{6,70},{7,71},{8,72},{9,... | collective-permute-start | bytes 786440 | tf_op jit(solution)/shard_map/ppermute | solution.py:30
  75.4 21.1 %collective-permute-start.5 = (bf16[4,128,256]{2,1,0:T(8,128)(2,1)S(1)}, bf16[4,128,256]{2,1,0:T(8,128)(2,1)S(1)}, u32[]{:S(2)}, u32[]{:S(2)}) collective-permute-start(bf16[4,128,256]{2,1,0:T(8,128)(2,1)S(1)} %pad_maximum_fusion.2), channel_id=1, source_target_pairs={{0,64},{1,65},{2,66},{3,67},{4,68},{5,69},{6,70},{7,71},{8,72},{9,... | collective-permute-start | bytes 786440 | tf_op jit(solution)/shard_map/ppermute | solution.py:30
  96.6 31.6 %collective-permute-start.12 = (bf16[2,4096,128]{2,1,0:T(8,128)(2,1)}, bf16[2,4096,128]{2,1,0:T(8,128)(2,1)S(1)}, u32[]{:S(2)}, u32[]{:S(2)}) collective-permute-start(bf16[2,4096,128]{2,1,0:T(8,128)(2,1)} %collective-permute-done.11.refs_2_), channel_id=1, source_target_pairs={{0,1},{1,0},{2,3},{3,2},{4,5},{5,4},{6,7},{7,6},{8,9},{9,8},{10,11... | collective-permute-start | bytes 6291464 | tf_op jit(solution)/shard_map/ppermute | solution.py:21
  101.5 15.4 %collective-permute-start.10 = (bf16[8,128,256]{2,1,0:T(8,128)(2,1)S(1)}, bf16[8,128,256]{2,1,0:T(8,128)(2,1)S(1)}, u32[]{:S(2)}, u32[]{:S(2)}) collective-permute-start(bf16[8,128,256]{2,1,0:T(8,128)(2,1)S(1)} %pad_maximum_fusion.1.second_low), channel_id=1, source_target_pairs={{0,32},{1,33},{2,34},{3,35},{4,36},{5,37},{6,38},{7,39},{8,40},{9,... | collective-permute-start | bytes 1572872 | tf_op jit(solution)/shard_map/ppermute | solution.py:30
  103.4 24.7 %collective-permute-start.6 = (bf16[8,128,256]{2,1,0:T(8,128)(2,1)S(1)}, bf16[8,128,256]{2,1,0:T(8,128)(2,1)S(1)}, u32[]{:S(2)}, u32[]{:S(2)}) collective-permute-start(bf16[8,128,256]{2,1,0:T(8,128)(2,1)S(1)} %pad_maximum_fusion.first_low), channel_id=1, source_target_pairs={{0,32},{1,33},{2,34},{3,35},{4,36},{5,37},{6,38},{7,39},{8,40},{9,... | collective-permute-start | bytes 1572872 | tf_op jit(solution)/shard_map/ppermute | solution.py:30
  135.9 7.0 %collective-permute-start.21 = (bf16[128,512]{1,0:T(8,128)(2,1)S(1)}, bf16[128,512]{1,0:T(8,128)(2,1)S(1)}, u32[]{:S(2)}, u32[]{:S(2)}) collective-permute-start(bf16[128,512]{1,0:T(8,128)(2,1)S(1)} %slice.23), channel_id=1, source_target_pairs={{0,32},{1,481},{2,34},{3,483},{4,36},{5,485},{6,38},{7,487},{8,40}... | collective-permute-start | bytes 393224 | tf_op jit(solution)/shard_map/ppermute | solution.py:30
  142.9 10.2 %collective-permute-start.13 = (bf16[128,512]{1,0:T(8,128)(2,1)S(1)}, bf16[128,512]{1,0:T(8,128)(2,1)S(1)}, u32[]{:S(2)}, u32[]{:S(2)}) collective-permute-start(bf16[128,512]{1,0:T(8,128)(2,1)S(1)} %get-tuple-element.41), channel_id=1, source_target_pairs={{0,32},{1,481},{2,34},{3,483},{4,36},{5,485},{6,38},{7,487},{8,40}... | collective-permute-start | bytes 393224 | tf_op jit(solution)/shard_map/ppermute | solution.py:30
  147.5 34.1 %collective-permute-start.29 = (bf16[2048,256]{1,0:T(8,128)(2,1)S(1)}, bf16[2048,256]{1,0:T(8,128)(2,1)}, u32[]{:S(2)}, u32[]{:S(2)}) collective-permute-start(bf16[2048,256]{1,0:T(8,128)(2,1)S(1)} %bitcast.63), channel_id=1, source_target_pairs={{0,2},{1,3},{2,0},{3,1},{4,6},{5,7},{6,4},{7,5},{8,10},{9,11},{10,... | collective-permute-start | bytes 3145736 | tf_op jit(solution)/shard_map/ppermute | solution.py:25
  151.2 7.5 %collective-permute-start.22 = (bf16[2,128,512]{2,1,0:T(8,128)(2,1)S(1)}, bf16[2,128,512]{2,1,0:T(8,128)(2,1)S(1)}, u32[]{:S(2)}, u32[]{:S(2)}) collective-permute-start(bf16[2,128,512]{2,1,0:T(8,128)(2,1)S(1)} %pad_maximum_fusion.5.refs_8_), channel_id=1, source_target_pairs={{0,480},{1,33},{2,482},{3,35},{4,484},{5,37},{6,486},{7,39},{8,488... | collective-permute-start | bytes 786440 | tf_op jit(solution)/shard_map/ppermute | solution.py:30
  153.2 8.3 %collective-permute-start.14 = (bf16[2,128,512]{2,1,0:T(8,128)(2,1)S(1)}, bf16[2,128,512]{2,1,0:T(8,128)(2,1)S(1)}, u32[]{:S(2)}, u32[]{:S(2)}) collective-permute-start(bf16[2,128,512]{2,1,0:T(8,128)(2,1)S(1)} %pad_maximum_fusion.4.refs_0_), channel_id=1, source_target_pairs={{0,480},{1,33},{2,482},{3,35},{4,484},{5,37},{6,486},{7,39},{8,488... | collective-permute-start | bytes 786440 | tf_op jit(solution)/shard_map/ppermute | solution.py:30
  158.7 8.3 %collective-permute-start.23 = (bf16[2,128,512]{2,1,0:T(8,128)(2,1)S(1)}, bf16[2,128,512]{2,1,0:T(8,128)(2,1)S(1)}, u32[]{:S(2)}, u32[]{:S(2)}) collective-permute-start(bf16[2,128,512]{2,1,0:T(8,128)(2,1)S(1)} %collective-permute-done.22.refs_9_), channel_id=1, source_target_pairs={{0,32},{1,481},{2,34},{3,483},{4,36},{5,485},{6,38},{7,487},{8,40}... | collective-permute-start | bytes 786440 | tf_op jit(solution)/shard_map/ppermute | solution.py:30
  161.5 8.3 %collective-permute-start.15 = (bf16[2,128,512]{2,1,0:T(8,128)(2,1)S(1)}, bf16[2,128,512]{2,1,0:T(8,128)(2,1)S(1)}, u32[]{:S(2)}, u32[]{:S(2)}) collective-permute-start(bf16[2,128,512]{2,1,0:T(8,128)(2,1)S(1)} %collective-permute-done.14.refs_1_), channel_id=1, source_target_pairs={{0,32},{1,481},{2,34},{3,483},{4,36},{5,485},{6,38},{7,487},{8,40}... | collective-permute-start | bytes 786440 | tf_op jit(solution)/shard_map/ppermute | solution.py:30
  167.0 8.0 %collective-permute-start.24 = (bf16[2,128,512]{2,1,0:T(8,128)(2,1)S(1)}, bf16[2,128,512]{2,1,0:T(8,128)(2,1)S(1)}, u32[]{:S(2)}, u32[]{:S(2)}) collective-permute-start(bf16[2,128,512]{2,1,0:T(8,128)(2,1)S(1)} %collective-permute-done.23.refs_10_), channel_id=1, source_target_pairs={{0,480},{1,33},{2,482},{3,35},{4,484},{5,37},{6,486},{7,39},{8,488... | collective-permute-start | bytes 786440 | tf_op jit(solution)/shard_map/ppermute | solution.py:30
  169.8 7.8 %collective-permute-start.16 = (bf16[2,128,512]{2,1,0:T(8,128)(2,1)S(1)}, bf16[2,128,512]{2,1,0:T(8,128)(2,1)S(1)}, u32[]{:S(2)}, u32[]{:S(2)}) collective-permute-start(bf16[2,128,512]{2,1,0:T(8,128)(2,1)S(1)} %collective-permute-done.15.refs_2_), channel_id=1, source_target_pairs={{0,480},{1,33},{2,482},{3,35},{4,484},{5,37},{6,486},{7,39},{8,488... | collective-permute-start | bytes 786440 | tf_op jit(solution)/shard_map/ppermute | solution.py:30
  175.0 12.9 %collective-permute-start.25 = (bf16[2,128,512]{2,1,0:T(8,128)(2,1)S(1)}, bf16[2,128,512]{2,1,0:T(8,128)(2,1)S(1)}, u32[]{:S(2)}, u32[]{:S(2)}) collective-permute-start(bf16[2,128,512]{2,1,0:T(8,128)(2,1)S(1)} %collective-permute-done.24.refs_11_), channel_id=1, source_target_pairs={{0,32},{1,481},{2,34},{3,483},{4,36},{5,485},{6,38},{7,487},{8,40}... | collective-permute-start | bytes 786440 | tf_op jit(solution)/shard_map/ppermute | solution.py:30
  177.6 14.0 %collective-permute-start.17 = (bf16[2,128,512]{2,1,0:T(8,128)(2,1)S(1)}, bf16[2,128,512]{2,1,0:T(8,128)(2,1)S(1)}, u32[]{:S(2)}, u32[]{:S(2)}) collective-permute-start(bf16[2,128,512]{2,1,0:T(8,128)(2,1)S(1)} %collective-permute-done.16.refs_3_), channel_id=1, source_target_pairs={{0,32},{1,481},{2,34},{3,483},{4,36},{5,485},{6,38},{7,487},{8,40}... | collective-permute-start | bytes 786440 | tf_op jit(solution)/shard_map/ppermute | solution.py:30
  181.6 30.4 %collective-permute-start.30 = (bf16[2048,256]{1,0:T(8,128)(2,1)}, bf16[2048,256]{1,0:T(8,128)(2,1)}, u32[]{:S(2)}, u32[]{:S(2)}) collective-permute-start(bf16[2048,256]{1,0:T(8,128)(2,1)} %collective-permute-done.29.refs_18_), channel_id=1, source_target_pairs={{0,1},{1,0},{2,3},{3,2},{4,5},{5,4},{6,7},{7,6},{8,9},{9,8},{10,11... | collective-permute-start | bytes 3145736 | tf_op jit(solution)/shard_map/ppermute | solution.py:21
  187.9 7.7 %collective-permute-start.26 = (bf16[2,128,512]{2,1,0:T(8,128)(2,1)S(1)}, bf16[2,128,512]{2,1,0:T(8,128)(2,1)S(1)}, u32[]{:S(2)}, u32[]{:S(2)}) collective-permute-start(bf16[2,128,512]{2,1,0:T(8,128)(2,1)S(1)} %collective-permute-done.25.refs_12_), channel_id=1, source_target_pairs={{0,480},{1,33},{2,482},{3,35},{4,484},{5,37},{6,486},{7,39},{8,488... | collective-permute-start | bytes 786440 | tf_op jit(solution)/shard_map/ppermute | solution.py:30
  191.6 9.9 %collective-permute-start.18 = (bf16[2,128,512]{2,1,0:T(8,128)(2,1)S(1)}, bf16[2,128,512]{2,1,0:T(8,128)(2,1)S(1)}, u32[]{:S(2)}, u32[]{:S(2)}) collective-permute-start(bf16[2,128,512]{2,1,0:T(8,128)(2,1)S(1)} %collective-permute-done.17.refs_4_), channel_id=1, source_target_pairs={{0,480},{1,33},{2,482},{3,35},{4,484},{5,37},{6,486},{7,39},{8,488... | collective-permute-start | bytes 786440 | tf_op jit(solution)/shard_map/ppermute | solution.py:30
  195.6 10.5 %collective-permute-start.27 = (bf16[2,128,512]{2,1,0:T(8,128)(2,1)S(1)}, bf16[2,128,512]{2,1,0:T(8,128)(2,1)}, u32[]{:S(2)}, u32[]{:S(2)}) collective-permute-start(bf16[2,128,512]{2,1,0:T(8,128)(2,1)S(1)} %collective-permute-done.26.refs_13_), channel_id=1, source_target_pairs={{0,32},{1,481},{2,34},{3,483},{4,36},{5,485},{6,38},{7,487},{8,40}... | collective-permute-start | bytes 786440 | tf_op jit(solution)/shard_map/ppermute | solution.py:30
  201.5 8.4 %collective-permute-start.19 = (bf16[2,128,512]{2,1,0:T(8,128)(2,1)S(1)}, bf16[2,128,512]{2,1,0:T(8,128)(2,1)}, u32[]{:S(2)}, u32[]{:S(2)}) collective-permute-start(bf16[2,128,512]{2,1,0:T(8,128)(2,1)S(1)} %collective-permute-done.18.refs_5_), channel_id=1, source_target_pairs={{0,32},{1,481},{2,34},{3,483},{4,36},{5,485},{6,38},{7,487},{8,40}... | collective-permute-start | bytes 786440 | tf_op jit(solution)/shard_map/ppermute | solution.py:30
  206.1 9.2 %collective-permute-start.28 = (bf16[2,128,512]{2,1,0:T(8,128)(2,1)}, bf16[2,128,512]{2,1,0:T(8,128)(2,1)}, u32[]{:S(2)}, u32[]{:S(2)}) collective-permute-start(bf16[2,128,512]{2,1,0:T(8,128)(2,1)} %collective-permute-done.27.refs_14_), channel_id=1, source_target_pairs={{0,480},{1,33},{2,482},{3,35},{4,484},{5,37},{6,486},{7,39},{8,488... | collective-permute-start | bytes 786440 | tf_op jit(solution)/shard_map/ppermute | solution.py:30
  209.9 7.9 %collective-permute-start.20 = (bf16[2,128,512]{2,1,0:T(8,128)(2,1)}, bf16[2,128,512]{2,1,0:T(8,128)(2,1)}, u32[]{:S(2)}, u32[]{:S(2)}) collective-permute-start(bf16[2,128,512]{2,1,0:T(8,128)(2,1)} %collective-permute-done.19.refs_6_), channel_id=1, source_target_pairs={{0,480},{1,33},{2,482},{3,35},{4,484},{5,37},{6,486},{7,39},{8,488... | collective-permute-start | bytes 786440 | tf_op jit(solution)/shard_map/ppermute | solution.py:30
  223.9 9.2 %collective-permute-start.31 = (bf16[2,128,256]{2,1,0:T(8,128)(2,1)S(1)}, bf16[2,128,256]{2,1,0:T(8,128)(2,1)S(1)}, u32[]{:S(2)}, u32[]{:S(2)}) collective-permute-start(bf16[2,128,256]{2,1,0:T(8,128)(2,1)S(1)} %bitcast.59), channel_id=1, source_target_pairs={{0,1},{1,0},{2,3},{3,2},{4,5},{5,4},{6,7},{7,6},{8,9},{9,8},{10,11... | collective-permute-start | bytes 393224 | tf_op jit(solution)/shard_map/ppermute | solution.py:21
  (8 other events, 163.8 us)

commit v4 on v0

v4 whole, which is shorter than its diff:
```python
import jax
import jax.numpy as jnp
from jax import lax
from jax.experimental import pallas as pl
from jax.experimental.pallas import tpu as pltpu
from jax.sharding import PartitionSpec as P

BLOCK = 128
SPAN = 4
CHIPS = 16
DEPTH = 16
OWNERS = 32
SAME_CORE = [[2 * chip + core for chip in range(CHIPS)] for core in range(2)]
PAIRS = DEPTH // 2


def swap_core(value):
    return lax.ppermute(value, "exp", [(p, p ^ 1) for p in range(OWNERS)])


def swap_pair(value):
    return lax.ppermute(value, "tok", [(z, z ^ 1) for z in range(DEPTH)])


def swap_ring(value, step):
    route = []
    for z in range(DEPTH):
        for p in range(OWNERS):
            place = z // 2
            other = place + 1 if (place + step + p) % 2 == 0 else place - 1
            route.append((z * OWNERS + p, (other % PAIRS * 2 + z % 2) * OWNERS + p))
    return lax.ppermute(value, ("tok", "exp"), route)


def ring_order(place, core):
    turned = lax.rem(place - core + PAIRS, PAIRS)
    couple, odd = turned // 2, lax.rem(turned, 2)
    away = jnp.where(odd == 1, 1, -1)
    couples = [couple]
    for step in range(1, PAIRS // 2):
        reach = (step + 1) // 2
        couples.append(couple + (away * reach if step % 2 else -away * reach))
    places = [2 * c + half + core for c in couples for half in range(2)]
    return odd == 1, lax.rem(jnp.stack(places) + 2 * PAIRS, PAIRS).astype(jnp.int32)


def start_rows(order, sources, held, arrived):
    taken = held.shape[2]
    copies = []
    for number in range(DEPTH):
        for which, (weight, base) in enumerate(sources):
            rows = pl.ds(pl.multiple_of(order[number] * taken + base, taken), taken)
            copy = pltpu.make_async_copy(weight.at[rows, :], held.at[number, which], arrived.at[number, which])
            copy.start()
            copies.append(copy)
    return copies


def hidden_kernel(order, *refs):
    items, weights, (first, second, held, arrived) = refs[:PAIRS], refs[PAIRS:-4], refs[-4:]
    count = 2 * len(weights)
    copies = start_rows(order, [(w.at[kind], 0) for kind in range(2) for w in weights], held, arrived)
    total = None
    for number in range(DEPTH):
        couple, place, half = number // 4, number // 2 % 2, number % 2
        left = jnp.concatenate([items[couple][place, half], items[PAIRS // 2 + couple][place, half]], axis=0)
        for copy in copies[number * count : (number + 1) * count]:
            copy.wait()
        right = jnp.concatenate([held[number, which] for which in range(count)], axis=1)
        term = jnp.dot(left, right, preferred_element_type=jnp.float32)
        total = term if total is None else total + term
    units = total.shape[1] // 2
    gate, up = total[:, :units], total[:, units:]
    hidden = (gate / (1.0 + jnp.exp(-gate)) * up).astype(first.dtype)
    rows = first.shape[0]
    first[...] = hidden[:rows]
    second[...] = hidden[rows:]


def down_kernel(order, scale, *refs):
    items, weights, (kept, given, held, arrived) = refs[:PAIRS], refs[PAIRS:-4], refs[-4:]
    count = 2 * len(weights)
    depth = weights[0].shape[1] // 2
    copies = start_rows(order, [(w.at[2], side * depth) for w in weights for side in range(2)], held, arrived)
    total = None
    for number in range(PAIRS):
        couple, place = number // 2, number % 2
        left = jnp.concatenate([items[couple][place], items[PAIRS // 2 + couple][place]], axis=0)
        for copy in copies[2 * number * count : 2 * (number + 1) * count]:
            copy.wait()
        right = jnp.concatenate(
            [
                jnp.concatenate([held[2 * number + half, 2 * core + which] for which in (0, 1, 4, 5)], axis=1)
                for half in range(2)
                for core in range(2)
            ],
            axis=0,
        )
        term = jnp.dot(left, right, preferred_element_type=jnp.float32)
        total = term if total is None else total + term
    total = (total * scale[...]).astype(kept.dtype)
    columns = kept.shape[1]
    kept[...] = total[:, :columns]
    given[...] = total[:, columns:]


def kernel_call(kernel, name, order, inner, weights, outs, flops, taken):
    count, wide = 2 * len(weights), weights[0].shape[2]
    in_vmem = pl.BlockSpec(memory_space=pltpu.VMEM)
    return pl.pallas_call(
        kernel,
        out_shape=[jax.ShapeDtypeStruct(shape, jnp.bfloat16) for shape in outs],
        in_specs=[pl.BlockSpec(memory_space=pltpu.SMEM)]
        + [in_vmem] * len(inner)
        + [pl.BlockSpec(memory_space=pltpu.HBM)] * len(weights),
        out_specs=[in_vmem] * len(outs),
        scratch_shapes=[
            pltpu.VMEM((DEPTH, count, taken, wide), jnp.bfloat16),
            pltpu.SemaphoreType.DMA((DEPTH, count)),
        ],
        compiler_params=pltpu.CompilerParams(vmem_limit_bytes=24 << 20),
        cost_estimate=pl.CostEstimate(
            flops=flops,
            bytes_accessed=2 * DEPTH * taken * count * wide,
            transcendentals=0,
        ),
        name=name,
    )(order, *inner, *[pltpu.with_memory_space_constraint(w, pltpu.HBM) for w in weights])


def gather_ring(chunk, odd):
    other = swap_ring(chunk, 0)
    items = [jnp.stack([jnp.where(odd, other, chunk), jnp.where(odd, chunk, other)])]
    for step in range(1, PAIRS // 2):
        items.append(swap_ring(items[-1], step))
    return items


def shards(tokens, picked_blocks, gate_scale, w_gate, w_up, w_down):
    position = lax.axis_index("exp")
    z = lax.axis_index("tok")
    core, odd = lax.rem(position, 2), lax.rem(z, 2)
    expert = position // SPAN
    features, units = tokens.shape[1], w_gate.shape[2]
    chosen = lax.dynamic_index_in_dim(picked_blocks, expert, 0, keepdims=False)
    half = chosen.shape[0] // 2
    blocks = half // 2
    rows = blocks * BLOCK
    mine = lax.dynamic_slice_in_dim(chosen, half * core, half)
    theirs = lax.dynamic_slice_in_dim(chosen, half * (1 - core), half)
    here = (lax.rem(mine, 2) == core)[:, None, None]
    second, places = ring_order(z // 2, core)
    order_in = jnp.stack([2 * places, 2 * places + 1], axis=1).reshape(-1)
    order_down = jnp.stack([2 * places + odd, 2 * places + 1 - odd], axis=1).reshape(-1)
    scale = lax.dynamic_index_in_dim(gate_scale, expert, 0, keepdims=False).reshape(2, 2, rows, 1)
    scale = lax.dynamic_index_in_dim(scale, core, 0, keepdims=False)
    scale = lax.dynamic_index_in_dim(scale, odd, 0, keepdims=False)
    names = jnp.concatenate([mine, theirs])
    match = names[None, :] == (2 * jnp.arange(CHIPS, dtype=jnp.int32) + core)[:, None]
    wanted, source = match.any(1)[:, None, None], jnp.argmax(match, 1)

    spread = jnp.broadcast_to(tokens[None], (CHIPS,) + tokens.shape)
    spread, w_gate, w_up, w_down = lax.optimization_barrier((spread, w_gate, w_up, w_down))
    held = lax.all_to_all(spread, "exp", 0, 0, axis_index_groups=SAME_CORE, tiled=True)
    down = jnp.concatenate([w_down[0][:, :units], w_down[0][:, units:]])
    own = jnp.stack([w_gate[0], w_up[0], down])
    far = swap_pair(own)
    near = swap_core(own)
    lent = swap_core(held[theirs // 2])
    selected = jnp.where(here, held[mine // 2], lent)
    selected, near, order_in, order_down, wanted, source, second, scale = lax.optimization_barrier(
        (selected, near, order_in, order_down, wanted, source, second, scale)
    )

    selected = selected.reshape(2, rows, features)
    kept = lax.dynamic_index_in_dim(selected, odd, 0, keepdims=False)
    given = swap_pair(lax.dynamic_index_in_dim(selected, 1 - odd, 0, keepdims=False))
    both = jnp.stack([jnp.where(odd == 1, given, kept), jnp.where(odd == 1, kept, given)])
    chains = [gather_ring(both[:, block * BLOCK : (block + 1) * BLOCK], second) for block in range(blocks)]
    far, _ = lax.optimization_barrier((far, [chain[2] for chain in chains]))
    weights = [own, near, far, swap_core(far)]
    flops = 2 * rows * DEPTH * features * 2 * SPAN * units
    parts = kernel_call(
        hidden_kernel, "hidden", order_in, [item for chain in chains for item in chain], weights,
        [(BLOCK, SPAN * units)] * blocks, flops, features,
    )
    chains = [gather_ring(part, second) for part in parts]
    kept, given = kernel_call(
        down_kernel, "down", order_down, [scale] + [item for chain in chains for item in chain], weights,
        [(rows, features)] * 2, flops // 2, units,
    )
    given = swap_pair(given)
    done = jnp.stack([jnp.where(odd == 1, given, kept), jnp.where(odd == 1, kept, given)])
    done = done.reshape(half, BLOCK, features)

    all_done = jnp.concatenate([done, swap_core(done)])
    outgoing = jnp.where(wanted, all_done[source], 0)
    arrived = lax.all_to_all(outgoing, "exp", 0, 0, axis_index_groups=SAME_CORE, tiled=True)
    return jnp.sum(arrived, axis=0, dtype=jnp.float32).astype(jnp.bfloat16)


def solution(mesh):
    return jax.shard_map(
        shards,
        mesh=mesh,
        in_specs=(
            P("exp", "tok"),
            P(),
            P(),
            P("exp", None, "tok"),
            P("exp", None, "tok"),
            P("exp", None, "tok"),
        ),
        out_specs=P("exp", "tok"),
        check_vma=False,
    )
```

time: 424 us -> 264 us (0.62)
  waiting for transfers between devices: 386 us -> 117 us
  starting transfers between devices: 0.12 us -> 101 us
  blocking collectives: 0 us -> 19.3 us
  between operations: 13.2 us -> 0.56 us
  matrix products: 12.5 us -> 0 us
  Pallas kernels: 0 us -> 10.9 us
    all_gather x3 -> x0, waiting for transfers between devices: 277 us -> none  [the longest x1 120 us: shards(): full_rows = lax.all_gather(selected, 'tok', axis=1, tiled=True)]
    reduce_scatter x1 -> x0, waiting for transfers between devices: 109 us -> none  [shards(): lax.psum_scatter(buffer, 'exp', scatter_dimension=0, tiled=True)]
    ppermute x0 -> x23, waiting for transfers between devices: none -> 101 us  [the longest x16 53.2 us: swap_ring(): return lax.ppermute(value, ('tok', 'exp'), route)]
    ppermute x0 -> x23, starting transfers between devices: none -> 96.9 us  [the longest x16 59 us: swap_ring(): return lax.ppermute(value, ('tok', 'exp'), route)]
    all_to_all x0 -> x1, blocking collectives: none -> 19.3 us  [shards(): lax.all_to_all(outgoing, 'exp', 0, 0, axis_index_groups=SAME_CORE, tiled=...]
    all_to_all x0 -> x1, waiting for transfers between devices: none -> 16.4 us  [shards(): lax.all_to_all(spread, 'exp', 0, 0, axis_index_groups=SAME_CORE, tiled=True)]
    dot_general x3 -> x0, matrix products: 12.5 us -> none  [the longest x1 6.08 us: shards(): jnp.dot(full_rows, gate_local, preferred_element_type=jnp.float32)]
    pallas_call x0 -> x2, Pallas kernels: none -> 10.9 us  [kernel_call(): pl.pallas_call(kernel, out_shape=[jax.ShapeDtypeStruct(shape, jnp.bfloat1...]
  transfers between devices with their start and end apart: 4 -> 24, of which waited for: 4 -> 19; matrix products, arithmetic and copies ran while one was open for 0% -> 2% of each run, Pallas kernels for 0% -> 0%
where the time goes in v4:
time: 264 us; the launch traced here: 262 us
  waiting for transfers between devices  117 us (44%)
  starting transfers between devices  101 us (38%)
  blocking collectives  19.3 us (7%)
  Pallas kernels  10.9 us (4%)
  local copies, waits for them, and re-layouts  8.14 us (3%)
  other arithmetic  5.76 us (2%)
    ppermute x16, starting transfers between devices, swap_ring(): return lax.ppermute(value, ('tok', 'exp'), route)  59 us
    ppermute x16, waiting for transfers between devices, swap_ring(): return lax.ppermute(value, ('tok', 'exp'), route)  53.2 us
    ppermute x3, waiting for transfers between devices, swap_pair(): return lax.ppermute(value, 'tok', [(z, z ^ 1) for z in range(DEPTH)])  46.6 us
    ppermute x4, starting transfers between devices, swap_core(): return lax.ppermute(value, 'exp', [(p, p ^ 1) for p in range(OWNERS)])  28.7 us
    all_to_all x1, blocking collectives, shards(): lax.all_to_all(outgoing, 'exp', 0, 0, axis_index_groups=SAME_CORE, tiled=...  19.3 us
    all_to_all x1, waiting for transfers between devices, shards(): lax.all_to_all(spread, 'exp', 0, 0, axis_index_groups=SAME_CORE, tiled=True)  16.4 us
    pallas_call x2, Pallas kernels, kernel_call(): pl.pallas_call(kernel, out_shape=[jax.ShapeDtypeStruct(shape, jnp.bfloat1...  10.9 us
    ppermute x3, starting transfers between devices, swap_pair(): return lax.ppermute(value, 'tok', [(z, z ^ 1) for z in range(DEPTH)])  9.19 us
  transfers between devices with their start and end apart: 24, of which 19 were waited for; matrix products, arithmetic and copies ran while one was open for 2% of the time, Pallas kernels for 0%

profile of v4, /device:TPU:1, one launch (start us, length us, event | category | flops | bytes accessed | tf_op | source)
XLA Modules:
  0.0 262.5 jit_solution(7157091788181842603)
XLA Ops:
  5.4 8.8 %collective-permute-start.1 = (bf16[3,4096,128]{2,1,0:T(8,128)(2,1)}, bf16[3,4096,128]{2,1,0:T(8,128)(2,1)}, u32[]{:S(2)}, u32[]{:S(2)}) collective-permute-start(bf16[3,4096,128]{2,1,0:T(8,128)(2,1)} %pad_maximum_fusion.refs_8_), channel_id=1, source_target_pairs={{0,1},{1,0},{2,3},{3,2},{4,5},{5,4},{6,7},{7,6},{8,9},{9,8},{10,11... | collective-permute-start | bytes 9437192 | tf_op jit(solution)/shard_map/ppermute | solution.py:18
  16.1 3.7 %all-to-all-start = ((bf16[16,128,256]{2,1,0:T(8,128)(2,1)}), bf16[16,128,256]{2,1,0:T(8,128)(2,1)S(1)}, u32[]{:S(2)}, u32[]{:S(2)}) async-start(bf16[16,128,256]{2,1,0:T(8,128)(2,1)} %broadcast_in_dim.40), calls=%async_computation | async-start | bytes 2097152 | tf_op jit(solution)/shard_map/all_to_all | solution.py:164
  22.6 16.4 %all-to-all-done = bf16[16,128,256]{2,1,0:T(8,128)(2,1)S(1)} async-done(((bf16[16,128,256]{2,1,0:T(8,128)(2,1)}), bf16[16,128,256]{2,1,0:T(8,128)(2,1)S(1)}, u32[]{:S(2)}, u32[]{:S(2)}) %all-to-all-start) | async-done | bytes 1048608 | tf_op jit(solution)/shard_map/all_to_all | solution.py:164
  39.5 2.7 %collective-permute-start = (bf16[4,128,256]{2,1,0:T(8,128)(2,1)S(1)}, bf16[4,128,256]{2,1,0:T(8,128)(2,1)S(1)}, u32[]{:S(2)}, u32[]{:S(2)}) collective-permute-start(bf16[4,128,256]{2,1,0:T(8,128)(2,1)S(1)} %gather_fusion.1), channel_id=1, source_target_pairs={{0,1},{1,0},{2,3},{3,2},{4,5},{5,4},{6,7},{7,6},{8,9},{9,8},{10,11... | collective-permute-start | bytes 786440 | tf_op jit(solution)/shard_map/ppermute | solution.py:18
  46.3 42.6 %collective-permute-done.2 = bf16[256,256]{1,0:T(8,128)(2,1)S(1)} collective-permute-done((bf16[256,256]{1,0:T(8,128)(2,1)S(1)}, bf16[256,256]{1,0:T(8,128)(2,1)S(1)}, u32[]{:S(2)}, u32[]{:S(2)}) %collective-permute-start.2) | collective-permute-done | bytes 131104 | tf_op jit(solution)/shard_map/ppermute | solution.py:22
  88.9 6.2 %collective-permute-start.7 = (bf16[2,128,256]{2,1,0:T(8,128)(2,1)S(1)}, bf16[2,128,256]{2,1,0:T(8,128)(2,1)S(1)}, u32[]{:S(2)}, u32[]{:S(2)}) collective-permute-start(bf16[2,128,256]{2,1,0:T(8,128)(2,1)S(1)} %get-tuple-element.57), channel_id=1, source_target_pairs={{0,64},{1,449},{2,66},{3,451},{4,68},{5,453},{6,70},{7,455},{8,72}... | collective-permute-start | bytes 393224 | tf_op jit(solution)/shard_map/ppermute | solution.py:32
  100.4 3.3 %collective-permute-done.3 = bf16[2,128,256]{2,1,0:T(8,128)(2,1)S(1)} collective-permute-done((bf16[2,128,256]{2,1,0:T(8,128)(2,1)S(1)}, bf16[2,128,256]{2,1,0:T(8,128)(2,1)S(1)}, u32[]{:S(2)}, u32[]{:S(2)}) %collective-permute-start.3) | collective-permute-done | bytes 131104 | tf_op jit(solution)/shard_map/ppermute | solution.py:32
  105.7 2.5 collective-permute-done.8.refs_5_
  108.2 5.8 %collective-permute-start.9 = (bf16[2,2,128,256]{3,2,1,0:T(8,128)(2,1)S(1)}, bf16[2,2,128,256]{3,2,1,0:T(8,128)(2,1)S(1)}, u32[]{:S(2)}, u32[]{:S(2)}) collective-permute-start(bf16[2,2,128,256]{3,2,1,0:T(8,128)(2,1)S(1)} %collective-permute-done.8.refs_5_), channel_id=1, source_target_pairs={{0,64},{1,449},{2,66},{3,451},{4,68},{5,453},{6,70},{7,455},{8,72}... | collective-permute-start | bytes 786440 | tf_op jit(solution)/shard_map/ppermute | solution.py:32
  115.4 4.2 %collective-permute-start.5 = (bf16[2,2,128,256]{3,2,1,0:T(8,128)(2,1)S(1)}, bf16[2,2,128,256]{3,2,1,0:T(8,128)(2,1)S(1)}, u32[]{:S(2)}, u32[]{:S(2)}) collective-permute-start(bf16[2,2,128,256]{3,2,1,0:T(8,128)(2,1)S(1)} %collective-permute-done.4.refs_1_), channel_id=1, source_target_pairs={{0,64},{1,449},{2,66},{3,451},{4,68},{5,453},{6,70},{7,455},{8,72}... | collective-permute-start | bytes 786440 | tf_op jit(solution)/shard_map/ppermute | solution.py:32
  120.7 7.8 %collective-permute-done.5.refs_2_ = bf16[2,2,128,256]{3,2,1,0:T(8,128)(2,1)S(1)} collective-permute-done((bf16[2,2,128,256]{3,2,1,0:T(8,128)(2,1)S(1)}, bf16[2,2,128,256]{3,2,1,0:T(8,128)(2,1)S(1)}, u32[]{:S(2)}, u32[]{:S(2)}) %collective-permute-start.5) | collective-permute-done | bytes 262176 | tf_op jit(solution)/shard_map/ppermute | solution.py:32
  128.5 4.2 %collective-permute-start.12 = (bf16[3,4096,128]{2,1,0:T(8,128)(2,1)}, bf16[3,4096,128]{2,1,0:T(8,128)(2,1)S(1)}, u32[]{:S(2)}, u32[]{:S(2)}) collective-permute-start(bf16[3,4096,128]{2,1,0:T(8,128)(2,1)} %collective-permute-done.11.refs_10_), channel_id=1, source_target_pairs={{0,1},{1,0},{2,3},{3,2},{4,5},{5,4},{6,7},{7,6},{8,9},{9,8},{10,11... | collective-permute-start | bytes 9437192 | tf_op jit(solution)/shard_map/ppermute | solution.py:18
  132.7 3.8 %collective-permute-start.10 = (bf16[2,2,128,256]{3,2,1,0:T(8,128)(2,1)S(1)}, bf16[2,2,128,256]{3,2,1,0:T(8,128)(2,1)S(1)}, u32[]{:S(2)}, u32[]{:S(2)}) collective-permute-start(bf16[2,2,128,256]{3,2,1,0:T(8,128)(2,1)S(1)} %collective-permute-done.9.refs_6_), channel_id=1, source_target_pairs={{0,448},{1,65},{2,450},{3,67},{4,452},{5,69},{6,454},{7,71},{8,456... | collective-permute-start | bytes 786440 | tf_op jit(solution)/shard_map/ppermute | solution.py:32
  136.5 2.4 collective-permute-start.6
  138.9 7.1 %collective-permute-done.10.refs_7_ = bf16[2,2,128,256]{3,2,1,0:T(8,128)(2,1)S(1)} collective-permute-done((bf16[2,2,128,256]{3,2,1,0:T(8,128)(2,1)S(1)}, bf16[2,2,128,256]{3,2,1,0:T(8,128)(2,1)S(1)}, u32[]{:S(2)}, u32[]{:S(2)}) %collective-permute-start.10) | collective-permute-done | bytes 262176 | tf_op jit(solution)/shard_map/ppermute | solution.py:32
  146.0 2.6 collective-permute-done.6.refs_3_
  150.3 6.3 %hidden.1 = (bf16[128,512]{1,0:T(8,128)(2,1)S(1)}, bf16[128,512]{1,0:T(8,128)(2,1)S(1)}) custom-call(s32[16]{0:T(128)S(1)} %reshape.539.order, bf16[2,2,128,256]{3,2,1,0:T(8,128)(2,1)S(1)} %pad_maximum_fusion.2.refs_0_, bf16[2,2,128,256]{3,2,1,0:T(8,128)(2,1)S(1)} %collective-permute-done.4.refs_1_, ...), custom_call_target="tpu_custom_call" | custom-call | flops 2147483648 | bytes 8388608 | tf_op jit(solution)/shard_map/hidden/pallas_call | solution.py:110
  156.5 5.3 %collective-permute-start.17 = (bf16[128,512]{1,0:T(8,128)(2,1)S(1)}, bf16[128,512]{1,0:T(8,128)(2,1)S(1)}, u32[]{:S(2)}, u32[]{:S(2)}) collective-permute-start(bf16[128,512]{1,0:T(8,128)(2,1)S(1)} %get-tuple-element.37), channel_id=1, source_target_pairs={{0,64},{1,449},{2,66},{3,451},{4,68},{5,453},{6,70},{7,455},{8,72}... | collective-permute-start | bytes 393224 | tf_op jit(solution)/shard_map/ppermute | solution.py:32
  164.5 4.5 %collective-permute-start.18 = (bf16[2,128,512]{2,1,0:T(8,128)(2,1)S(1)}, bf16[2,128,512]{2,1,0:T(8,128)(2,1)S(1)}, u32[]{:S(2)}, u32[]{:S(2)}) collective-permute-start(bf16[2,128,512]{2,1,0:T(8,128)(2,1)S(1)} %pad_maximum_fusion.5.refs_4_), channel_id=1, source_target_pairs={{0,448},{1,65},{2,450},{3,67},{4,452},{5,69},{6,454},{7,71},{8,456... | collective-permute-start | bytes 786440 | tf_op jit(solution)/shard_map/ppermute | solution.py:32
  169.0 3.3 %collective-permute-done.13 = bf16[128,512]{1,0:T(8,128)(2,1)S(1)} collective-permute-done((bf16[128,512]{1,0:T(8,128)(2,1)S(1)}, bf16[128,512]{1,0:T(8,128)(2,1)S(1)}, u32[]{:S(2)}, u32[]{:S(2)}) %collective-permute-start.13) | collective-permute-done | bytes 131104 | tf_op jit(solution)/shard_map/ppermute | solution.py:32
  177.1 3.4 %collective-permute-start.19 = (bf16[2,128,512]{2,1,0:T(8,128)(2,1)S(1)}, bf16[2,128,512]{2,1,0:T(8,128)(2,1)S(1)}, u32[]{:S(2)}, u32[]{:S(2)}) collective-permute-start(bf16[2,128,512]{2,1,0:T(8,128)(2,1)S(1)} %collective-permute-done.18.refs_5_), channel_id=1, source_target_pairs={{0,64},{1,449},{2,66},{3,451},{4,68},{5,453},{6,70},{7,455},{8,72}... | collective-permute-start | bytes 786440 | tf_op jit(solution)/shard_map/ppermute | solution.py:32
  180.5 3.4 %collective-permute-done.14.refs_1_ = bf16[2,128,512]{2,1,0:T(8,128)(2,1)S(1)} collective-permute-done((bf16[2,128,512]{2,1,0:T(8,128)(2,1)S(1)}, bf16[2,128,512]{2,1,0:T(8,128)(2,1)S(1)}, u32[]{:S(2)}, u32[]{:S(2)}) %collective-permute-start.14) | collective-permute-done | bytes 262176 | tf_op jit(solution)/shard_map/ppermute | solution.py:32
  186.0 7.5 %collective-permute-done.19.refs_6_ = bf16[2,128,512]{2,1,0:T(8,128)(2,1)S(1)} collective-permute-done((bf16[2,128,512]{2,1,0:T(8,128)(2,1)S(1)}, bf16[2,128,512]{2,1,0:T(8,128)(2,1)S(1)}, u32[]{:S(2)}, u32[]{:S(2)}) %collective-permute-start.19) | collective-permute-done | bytes 262176 | tf_op jit(solution)/shard_map/ppermute | solution.py:32
  193.5 8.2 %collective-permute-start.20 = (bf16[2,128,512]{2,1,0:T(8,128)(2,1)S(1)}, bf16[2,128,512]{2,1,0:T(8,128)(2,1)S(1)}, u32[]{:S(2)}, u32[]{:S(2)}) collective-permute-start(bf16[2,128,512]{2,1,0:T(8,128)(2,1)S(1)} %collective-permute-done.19.refs_6_), channel_id=1, source_target_pairs={{0,448},{1,65},{2,450},{3,67},{4,452},{5,69},{6,454},{7,71},{8,456... | collective-permute-start | bytes 786440 | tf_op jit(solution)/shard_map/ppermute | solution.py:32
  201.8 2.9 %collective-permute-start.16 = (bf16[2,128,512]{2,1,0:T(8,128)(2,1)S(1)}, bf16[2,128,512]{2,1,0:T(8,128)(2,1)S(1)}, u32[]{:S(2)}, u32[]{:S(2)}) collective-permute-start(bf16[2,128,512]{2,1,0:T(8,128)(2,1)S(1)} %collective-permute-done.15.refs_2_), channel_id=1, source_target_pairs={{0,448},{1,65},{2,450},{3,67},{4,452},{5,69},{6,454},{7,71},{8,456... | collective-permute-start | bytes 786440 | tf_op jit(solution)/shard_map/ppermute | solution.py:32
  204.8 3.1 %collective-permute-done.20.refs_7_ = bf16[2,128,512]{2,1,0:T(8,128)(2,1)S(1)} collective-permute-done((bf16[2,128,512]{2,1,0:T(8,128)(2,1)S(1)}, bf16[2,128,512]{2,1,0:T(8,128)(2,1)S(1)}, u32[]{:S(2)}, u32[]{:S(2)}) %collective-permute-start.20) | collective-permute-done | bytes 262176 | tf_op jit(solution)/shard_map/ppermute | solution.py:32
  207.9 5.8 %collective-permute-done.16.refs_3_ = bf16[2,128,512]{2,1,0:T(8,128)(2,1)S(1)} collective-permute-done((bf16[2,128,512]{2,1,0:T(8,128)(2,1)S(1)}, bf16[2,128,512]{2,1,0:T(8,128)(2,1)S(1)}, u32[]{:S(2)}, u32[]{:S(2)}) %collective-permute-start.16) | collective-permute-done | bytes 262176 | tf_op jit(solution)/shard_map/ppermute | solution.py:32
  213.8 4.7 %down.1 = (bf16[256,256]{1,0:T(8,128)(2,1)S(1)}, bf16[256,256]{1,0:T(8,128)(2,1)S(1)}) custom-call(s32[16]{0:T(128)S(1)} %reshape.540.order, f32[256,1]{1,0:T(8,128)S(1)} %copy.13.scale, bf16[2,128,512]{2,1,0:T(8,128)(2,1)S(1)} %pad_maximum_fusion.4.refs_0_, bf16[2,128,512]{2,1,0:T(8,128)(2,1)S(1)} %collective-permute-done.14.refs_1_, ...), custom_call_target="tpu_custom_call" | custom-call | flops 1073741824 | bytes 4194304 | tf_op jit(solution)/shard_map/down/pallas_call | solution.py:110
  218.4 4.9 %collective-permute-start.21 = (bf16[256,256]{1,0:T(8,128)(2,1)S(1)}, bf16[256,256]{1,0:T(8,128)(2,1)S(1)}, u32[]{:S(2)}, u32[]{:S(2)}) collective-permute-start(bf16[256,256]{1,0:T(8,128)(2,1)S(1)} %get-tuple-element.38), channel_id=1, source_target_pairs={{0,32},{32,0},{64,96},{96,64},{128,160},{160,128},{192,224},{224,1... | collective-permute-start | bytes 393224 | tf_op jit(solution)/shard_map/ppermute | solution.py:22
  223.4 4.0 %collective-permute-done.21 = bf16[256,256]{1,0:T(8,128)(2,1)S(1)} collective-permute-done((bf16[256,256]{1,0:T(8,128)(2,1)S(1)}, bf16[256,256]{1,0:T(8,128)(2,1)S(1)}, u32[]{:S(2)}, u32[]{:S(2)}) %collective-permute-start.21) | collective-permute-done | bytes 131104 | tf_op jit(solution)/shard_map/ppermute | solution.py:22
  227.4 13.0 %collective-permute-start.22 = (bf16[4,128,256]{2,1,0:T(8,128)(2,1)S(1)}, bf16[4,128,256]{2,1,0:T(8,128)(2,1)S(1)}, u32[]{:S(2)}, u32[]{:S(2)}) collective-permute-start(bf16[4,128,256]{2,1,0:T(8,128)(2,1)S(1)} %bitcast.80), channel_id=1, source_target_pairs={{0,1},{1,0},{2,3},{3,2},{4,5},{5,4},{6,7},{7,6},{8,9},{9,8},{10,11... | collective-permute-start | bytes 786440 | tf_op jit(solution)/shard_map/ppermute | solution.py:18
  242.4 19.3 %all_to_all.10 = bf16[16,128,256]{2,1,0:T(8,128)(2,1)S(1)} all-to-all(bf16[16,128,256]{2,1,0:T(8,128)(2,1)S(1)} %broadcast_select_fusion), channel_id=1, replica_groups={{0,2,4,6,8,10,12,14,16,18,20,22,24,26,28,30},{1,3,5,7,9,11,13,15,17,19,..., dimensions={0} | all-to-all | bytes 2097152 | tf_op jit(solution)/shard_map/all_to_all | solution.py:198
  (73 shorter events, 38.5 us)
Async XLA Ops:
  0.0 22.5 %copy-start = (f32[8,1024]{1,0:T(8,128)S(1)}, f32[8,1024]{1,0:T(8,128)}, u32[]{:S(2)}) copy-start(f32[8,1024]{1,0:T(8,128)} %param.8) | copy-start | bytes 98308
  0.0 3.4 %copy-start.2 = (bf16[1,4096,128]{2,1,0:T(8,128)(2,1)S(1)}, bf16[1,4096,128]{2,1,0:T(8,128)(2,1)}, u32[]{:S(2)}) copy-start(bf16[1,4096,128]{2,1,0:T(8,128)(2,1)} %param.10) | copy-start | bytes 3145732
  0.0 3.5 %copy-start.3 = (bf16[1,4096,128]{2,1,0:T(8,128)(2,1)S(1)}, bf16[1,4096,128]{2,1,0:T(8,128)(2,1)}, u32[]{:S(2)}) copy-start(bf16[1,4096,128]{2,1,0:T(8,128)(2,1)} %param.9) | copy-start | bytes 3145732
  5.4 38.4 %collective-permute-start.1 = (bf16[3,4096,128]{2,1,0:T(8,128)(2,1)}, bf16[3,4096,128]{2,1,0:T(8,128)(2,1)}, u32[]{:S(2)}, u32[]{:S(2)}) collective-permute-start(bf16[3,4096,128]{2,1,0:T(8,128)(2,1)} %pad_maximum_fusion.refs_8_), channel_id=1, source_target_pairs={{0,1},{1,0},{2,3},{3,2},{4,5},{5,4},{6,7},{7,6},{8,9},{9,8},{10,11... | collective-permute-start | bytes 9437192 | tf_op jit(solution)/shard_map/ppermute | solution.py:18
  14.2 105.4 %collective-permute-start.11 = (bf16[3,4096,128]{2,1,0:T(8,128)(2,1)}, bf16[3,4096,128]{2,1,0:T(8,128)(2,1)}, u32[]{:S(2)}, u32[]{:S(2)}) collective-permute-start(bf16[3,4096,128]{2,1,0:T(8,128)(2,1)} %pad_maximum_fusion.refs_8_), channel_id=1, source_target_pairs={{0,32},{32,0},{64,96},{96,64},{128,160},{160,128},{192,224},{224,1... | collective-permute-start | bytes 9437192 | tf_op jit(solution)/shard_map/ppermute | solution.py:22
  16.1 22.8 %all-to-all-start = ((bf16[16,128,256]{2,1,0:T(8,128)(2,1)}), bf16[16,128,256]{2,1,0:T(8,128)(2,1)S(1)}, u32[]{:S(2)}, u32[]{:S(2)}) async-start(bf16[16,128,256]{2,1,0:T(8,128)(2,1)} %broadcast_in_dim.40), calls=%async_computation | async-start | bytes 2097152 | tf_op jit(solution)/shard_map/all_to_all | solution.py:164
  39.5 4.2 %collective-permute-start = (bf16[4,128,256]{2,1,0:T(8,128)(2,1)S(1)}, bf16[4,128,256]{2,1,0:T(8,128)(2,1)S(1)}, u32[]{:S(2)}, u32[]{:S(2)}) collective-permute-start(bf16[4,128,256]{2,1,0:T(8,128)(2,1)S(1)} %gather_fusion.1), channel_id=1, source_target_pairs={{0,1},{1,0},{2,3},{3,2},{4,5},{5,4},{6,7},{7,6},{8,9},{9,8},{10,11... | collective-permute-start | bytes 786440 | tf_op jit(solution)/shard_map/ppermute | solution.py:18
  43.9 44.9 %collective-permute-start.2 = (bf16[256,256]{1,0:T(8,128)(2,1)S(1)}, bf16[256,256]{1,0:T(8,128)(2,1)S(1)}, u32[]{:S(2)}, u32[]{:S(2)}) collective-permute-start(bf16[256,256]{1,0:T(8,128)(2,1)S(1)} %dynamic-slice_bitcast_fusion), channel_id=1, source_target_pairs={{0,32},{32,0},{64,96},{96,64},{128,160},{160,128},{192,224},{224,1... | collective-permute-start | bytes 393224 | tf_op jit(solution)/shard_map/ppermute | solution.py:22
  88.9 9.5 %collective-permute-start.7 = (bf16[2,128,256]{2,1,0:T(8,128)(2,1)S(1)}, bf16[2,128,256]{2,1,0:T(8,128)(2,1)S(1)}, u32[]{:S(2)}, u32[]{:S(2)}) collective-permute-start(bf16[2,128,256]{2,1,0:T(8,128)(2,1)S(1)} %get-tuple-element.57), channel_id=1, source_target_pairs={{0,64},{1,449},{2,66},{3,451},{4,68},{5,453},{6,70},{7,455},{8,72}... | collective-permute-start | bytes 393224 | tf_op jit(solution)/shard_map/ppermute | solution.py:32
  95.1 8.6 %collective-permute-start.3 = (bf16[2,128,256]{2,1,0:T(8,128)(2,1)S(1)}, bf16[2,128,256]{2,1,0:T(8,128)(2,1)S(1)}, u32[]{:S(2)}, u32[]{:S(2)}) collective-permute-start(bf16[2,128,256]{2,1,0:T(8,128)(2,1)S(1)} %get-tuple-element.58), channel_id=1, source_target_pairs={{0,64},{1,449},{2,66},{3,451},{4,68},{5,453},{6,70},{7,455},{8,72}... | collective-permute-start | bytes 393224 | tf_op jit(solution)/shard_map/ppermute | solution.py:32
  98.5 9.7 %collective-permute-start.8 = (bf16[2,2,128,256]{3,2,1,0:T(8,128)(2,1)S(1)}, bf16[2,2,128,256]{3,2,1,0:T(8,128)(2,1)S(1)}, u32[]{:S(2)}, u32[]{:S(2)}) collective-permute-start(bf16[2,2,128,256]{3,2,1,0:T(8,128)(2,1)S(1)} %pad_maximum_fusion.3.refs_4_), channel_id=1, source_target_pairs={{0,448},{1,65},{2,450},{3,67},{4,452},{5,69},{6,454},{7,71},{8,456... | collective-permute-start | bytes 786440 | tf_op jit(solution)/shard_map/ppermute | solution.py:32
  103.8 11.7 %collective-permute-start.4 = (bf16[2,2,128,256]{3,2,1,0:T(8,128)(2,1)S(1)}, bf16[2,2,128,256]{3,2,1,0:T(8,128)(2,1)S(1)}, u32[]{:S(2)}, u32[]{:S(2)}) collective-permute-start(bf16[2,2,128,256]{3,2,1,0:T(8,128)(2,1)S(1)} %pad_maximum_fusion.2.refs_0_), channel_id=1, source_target_pairs={{0,448},{1,65},{2,450},{3,67},{4,452},{5,69},{6,454},{7,71},{8,456... | collective-permute-start | bytes 786440 | tf_op jit(solution)/shard_map/ppermute | solution.py:32
  108.2 12.5 %collective-permute-start.9 = (bf16[2,2,128,256]{3,2,1,0:T(8,128)(2,1)S(1)}, bf16[2,2,128,256]{3,2,1,0:T(8,128)(2,1)S(1)}, u32[]{:S(2)}, u32[]{:S(2)}) collective-permute-start(bf16[2,2,128,256]{3,2,1,0:T(8,128)(2,1)S(1)} %collective-permute-done.8.refs_5_), channel_id=1, source_target_pairs={{0,64},{1,449},{2,66},{3,451},{4,68},{5,453},{6,70},{7,455},{8,72}... | collective-permute-start | bytes 786440 | tf_op jit(solution)/shard_map/ppermute | solution.py:32
  115.4 13.1 %collective-permute-start.5 = (bf16[2,2,128,256]{3,2,1,0:T(8,128)(2,1)S(1)}, bf16[2,2,128,256]{3,2,1,0:T(8,128)(2,1)S(1)}, u32[]{:S(2)}, u32[]{:S(2)}) collective-permute-start(bf16[2,2,128,256]{3,2,1,0:T(8,128)(2,1)S(1)} %collective-permute-done.4.refs_1_), channel_id=1, source_target_pairs={{0,64},{1,449},{2,66},{3,451},{4,68},{5,453},{6,70},{7,455},{8,72}... | collective-permute-start | bytes 786440 | tf_op jit(solution)/shard_map/ppermute | solution.py:32
  128.5 20.1 %collective-permute-start.12 = (bf16[3,4096,128]{2,1,0:T(8,128)(2,1)}, bf16[3,4096,128]{2,1,0:T(8,128)(2,1)S(1)}, u32[]{:S(2)}, u32[]{:S(2)}) collective-permute-start(bf16[3,4096,128]{2,1,0:T(8,128)(2,1)} %collective-permute-done.11.refs_10_), channel_id=1, source_target_pairs={{0,1},{1,0},{2,3},{3,2},{4,5},{5,4},{6,7},{7,6},{8,9},{9,8},{10,11... | collective-permute-start | bytes 9437192 | tf_op jit(solution)/shard_map/ppermute | solution.py:18
  132.7 13.3 %collective-permute-start.10 = (bf16[2,2,128,256]{3,2,1,0:T(8,128)(2,1)S(1)}, bf16[2,2,128,256]{3,2,1,0:T(8,128)(2,1)S(1)}, u32[]{:S(2)}, u32[]{:S(2)}) collective-permute-start(bf16[2,2,128,256]{3,2,1,0:T(8,128)(2,1)S(1)} %collective-permute-done.9.refs_6_), channel_id=1, source_target_pairs={{0,448},{1,65},{2,450},{3,67},{4,452},{5,69},{6,454},{7,71},{8,456... | collective-permute-start | bytes 786440 | tf_op jit(solution)/shard_map/ppermute | solution.py:32
  136.5 12.1 %collective-permute-start.6 = (bf16[2,2,128,256]{3,2,1,0:T(8,128)(2,1)S(1)}, bf16[2,2,128,256]{3,2,1,0:T(8,128)(2,1)S(1)}, u32[]{:S(2)}, u32[]{:S(2)}) collective-permute-start(bf16[2,2,128,256]{3,2,1,0:T(8,128)(2,1)S(1)} %collective-permute-done.5.refs_2_), channel_id=1, source_target_pairs={{0,448},{1,65},{2,450},{3,67},{4,452},{5,69},{6,454},{7,71},{8,456... | collective-permute-start | bytes 786440 | tf_op jit(solution)/shard_map/ppermute | solution.py:32
  148.6 1.7 copy-start.1
  156.5 7.9 %collective-permute-start.17 = (bf16[128,512]{1,0:T(8,128)(2,1)S(1)}, bf16[128,512]{1,0:T(8,128)(2,1)S(1)}, u32[]{:S(2)}, u32[]{:S(2)}) collective-permute-start(bf16[128,512]{1,0:T(8,128)(2,1)S(1)} %get-tuple-element.37), channel_id=1, source_target_pairs={{0,64},{1,449},{2,66},{3,451},{4,68},{5,453},{6,70},{7,455},{8,72}... | collective-permute-start | bytes 393224 | tf_op jit(solution)/shard_map/ppermute | solution.py:32
  161.8 10.5 %collective-permute-start.13 = (bf16[128,512]{1,0:T(8,128)(2,1)S(1)}, bf16[128,512]{1,0:T(8,128)(2,1)S(1)}, u32[]{:S(2)}, u32[]{:S(2)}) collective-permute-start(bf16[128,512]{1,0:T(8,128)(2,1)S(1)} %get-tuple-element.36), channel_id=1, source_target_pairs={{0,64},{1,449},{2,66},{3,451},{4,68},{5,453},{6,70},{7,455},{8,72}... | collective-permute-start | bytes 393224 | tf_op jit(solution)/shard_map/ppermute | solution.py:32
  164.5 12.6 %collective-permute-start.18 = (bf16[2,128,512]{2,1,0:T(8,128)(2,1)S(1)}, bf16[2,128,512]{2,1,0:T(8,128)(2,1)S(1)}, u32[]{:S(2)}, u32[]{:S(2)}) collective-permute-start(bf16[2,128,512]{2,1,0:T(8,128)(2,1)S(1)} %pad_maximum_fusion.5.refs_4_), channel_id=1, source_target_pairs={{0,448},{1,65},{2,450},{3,67},{4,452},{5,69},{6,454},{7,71},{8,456... | collective-permute-start | bytes 786440 | tf_op jit(solution)/shard_map/ppermute | solution.py:32
  172.4 11.5 %collective-permute-start.14 = (bf16[2,128,512]{2,1,0:T(8,128)(2,1)S(1)}, bf16[2,128,512]{2,1,0:T(8,128)(2,1)S(1)}, u32[]{:S(2)}, u32[]{:S(2)}) collective-permute-start(bf16[2,128,512]{2,1,0:T(8,128)(2,1)S(1)} %pad_maximum_fusion.4.refs_0_), channel_id=1, source_target_pairs={{0,448},{1,65},{2,450},{3,67},{4,452},{5,69},{6,454},{7,71},{8,456... | collective-permute-start | bytes 786440 | tf_op jit(solution)/shard_map/ppermute | solution.py:32
  177.1 16.4 %collective-permute-start.19 = (bf16[2,128,512]{2,1,0:T(8,128)(2,1)S(1)}, bf16[2,128,512]{2,1,0:T(8,128)(2,1)S(1)}, u32[]{:S(2)}, u32[]{:S(2)}) collective-permute-start(bf16[2,128,512]{2,1,0:T(8,128)(2,1)S(1)} %collective-permute-done.18.refs_5_), channel_id=1, source_target_pairs={{0,64},{1,449},{2,66},{3,451},{4,68},{5,453},{6,70},{7,455},{8,72}... | collective-permute-start | bytes 786440 | tf_op jit(solution)/shard_map/ppermute | solution.py:32
  183.9 17.9 %collective-permute-start.15 = (bf16[2,128,512]{2,1,0:T(8,128)(2,1)S(1)}, bf16[2,128,512]{2,1,0:T(8,128)(2,1)S(1)}, u32[]{:S(2)}, u32[]{:S(2)}) collective-permute-start(bf16[2,128,512]{2,1,0:T(8,128)(2,1)S(1)} %collective-permute-done.14.refs_1_), channel_id=1, source_target_pairs={{0,64},{1,449},{2,66},{3,451},{4,68},{5,453},{6,70},{7,455},{8,72}... | collective-permute-start | bytes 786440 | tf_op jit(solution)/shard_map/ppermute | solution.py:32
  193.5 14.4 %collective-permute-start.20 = (bf16[2,128,512]{2,1,0:T(8,128)(2,1)S(1)}, bf16[2,128,512]{2,1,0:T(8,128)(2,1)S(1)}, u32[]{:S(2)}, u32[]{:S(2)}) collective-permute-start(bf16[2,128,512]{2,1,0:T(8,128)(2,1)S(1)} %collective-permute-done.19.refs_6_), channel_id=1, source_target_pairs={{0,448},{1,65},{2,450},{3,67},{4,452},{5,69},{6,454},{7,71},{8,456... | collective-permute-start | bytes 786440 | tf_op jit(solution)/shard_map/ppermute | solution.py:32
  201.8 12.0 %collective-permute-start.16 = (bf16[2,128,512]{2,1,0:T(8,128)(2,1)S(1)}, bf16[2,128,512]{2,1,0:T(8,128)(2,1)S(1)}, u32[]{:S(2)}, u32[]{:S(2)}) collective-permute-start(bf16[2,128,512]{2,1,0:T(8,128)(2,1)S(1)} %collective-permute-done.15.refs_2_), channel_id=1, source_target_pairs={{0,448},{1,65},{2,450},{3,67},{4,452},{5,69},{6,454},{7,71},{8,456... | collective-permute-start | bytes 786440 | tf_op jit(solution)/shard_map/ppermute | solution.py:32
  218.4 8.9 %collective-permute-start.21 = (bf16[256,256]{1,0:T(8,128)(2,1)S(1)}, bf16[256,256]{1,0:T(8,128)(2,1)S(1)}, u32[]{:S(2)}, u32[]{:S(2)}) collective-permute-start(bf16[256,256]{1,0:T(8,128)(2,1)S(1)} %get-tuple-element.38), channel_id=1, source_target_pairs={{0,32},{32,0},{64,96},{96,64},{128,160},{160,128},{192,224},{224,1... | collective-permute-start | bytes 393224 | tf_op jit(solution)/shard_map/ppermute | solution.py:22
  227.4 14.2 %collective-permute-start.22 = (bf16[4,128,256]{2,1,0:T(8,128)(2,1)S(1)}, bf16[4,128,256]{2,1,0:T(8,128)(2,1)S(1)}, u32[]{:S(2)}, u32[]{:S(2)}) collective-permute-start(bf16[4,128,256]{2,1,0:T(8,128)(2,1)S(1)} %bitcast.80), channel_id=1, source_target_pairs={{0,1},{1,0},{2,3},{3,2},{4,5},{5,4},{6,7},{7,6},{8,9},{9,8},{10,11... | collective-permute-start | bytes 786440 | tf_op jit(solution)/shard_map/ppermute | solution.py:18

commit v5 on v1

--- a/solution.py
+++ b/solution.py
@@ -77,7 +77,7 @@
         out_shape=jax.ShapeDtypeStruct((rows, sets * units), jnp.bfloat16),
         in_specs=[pl.BlockSpec(memory_space=pltpu.SMEM)] + [whole] * (len(items) + 2 * sets),
         out_specs=whole,
-        compiler_params=pltpu.CompilerParams(vmem_limit_bytes=32 << 20),
+        compiler_params=pltpu.CompilerParams(vmem_limit_bytes=16 << 20),
         cost_estimate=pl.CostEstimate(
             flops=2 * rows * gates[0].shape[0] * 2 * sets * units,
             bytes_accessed=2 * sets * gates[0].size * 2,
@@ -97,7 +97,7 @@
         right = jnp.concatenate([w[rows, :] for w in weights], axis=0)
         term = jnp.dot(items[number // 2][number % 2], right, preferred_element_type=jnp.float32)
         total = term if total is None else total + term
-    out[...] = (total * scale[...]).astype(out.dtype)
+    out[...] = (total * scale[:, :1]).astype(out.dtype)
 
 
 def down_of(order, items, scale, downs):
@@ -109,7 +109,7 @@
         out_shape=jax.ShapeDtypeStruct((rows, features), jnp.bfloat16),
         in_specs=[pl.BlockSpec(memory_space=pltpu.SMEM)] + [whole] * (len(items) + 1 + len(downs)),
         out_specs=whole,
-        compiler_params=pltpu.CompilerParams(vmem_limit_bytes=32 << 20),
+        compiler_params=pltpu.CompilerParams(vmem_limit_bytes=16 << 20),
         cost_estimate=pl.CostEstimate(
             flops=2 * rows * features * sum(w.shape[0] for w in downs),
             bytes_accessed=2 * sum(w.size for w in downs),
@@ -143,18 +143,23 @@
     odd, order = pair_order(z, core)
     scale = lax.dynamic_index_in_dim(gate_scale, expert, 0, keepdims=False).reshape(2, 2, -1, 1)
     scale = lax.dynamic_index_in_dim(scale, core, 0, keepdims=False)
+    scales = [jnp.broadcast_to(scale[part], (scale.shape[1], 128)) for part in range(2)]
+    names = jnp.concatenate([mine, theirs])
+    match = names[None, :] == (2 * jnp.arange(CHIPS, dtype=jnp.int32) + core)[:, None]
+    wanted, source = match.any(1)[:, None, None], jnp.argmax(match, 1)
+    selected, gates, ups, downs, odd, order, scales, wanted, source = lax.optimization_barrier(
+        (selected, gates, ups, downs, odd, order, scales, wanted, source)
+    )
     parts = []
     for part in range(2):
         rows = selected[part * half // 2 : (part + 1) * half // 2].reshape(-1, features)
         hidden = hidden_of(order, gather_depth(rows, odd), gates, ups)
-        parts.append(down_of(order, gather_depth(hidden, odd), scale[part], downs))
+        parts.append(down_of(order, gather_depth(hidden, odd), scales[part], downs))
     done = jnp.concatenate(parts).reshape(half, BLOCK, features)
 
     others = swap_core(done)
     all_done = jnp.concatenate([done, others])
-    names = jnp.concatenate([mine, theirs])
-    match = names[None, :] == (2 * jnp.arange(CHIPS, dtype=jnp.int32) + core)[:, None]
-    outgoing = jnp.where(match.any(1)[:, None, None], all_done[jnp.argmax(match, 1)], 0)
+    outgoing = jnp.where(wanted, all_done[source], 0)
     arrived = lax.all_to_all(outgoing, "exp", 0, 0, axis_index_groups=SAME_CORE, tiled=True)
     return jnp.sum(arrived, axis=0, dtype=jnp.float32).astype(jnp.bfloat16)
 

time: 240 us -> 244 us (1.017)
  waiting for transfers between devices: 46 us -> 68.6 us
  local copies, waits for them, and re-layouts: 24.4 us -> 8.05 us
  starting transfers between devices: 135 us -> 131 us
    ppermute x32, waiting for transfers between devices: 31.5 us -> 66 us  [swap_depth(): return lax.ppermute(value, ('tok', 'exp'), pairs)]
    unnamed x76 -> x8, local copies, waits for them, and re-layouts: 19.5 us -> 0.02 us
    all_to_all x1, waiting for transfers between devices: 12.9 us -> 1.42 us  [shards(): lax.all_to_all(spread, 'exp', 0, 0, axis_index_groups=SAME_CORE, tiled=True)]
    ppermute x32, starting transfers between devices: 95.1 us -> 91 us  [swap_depth(): return lax.ppermute(value, ('tok', 'exp'), pairs)]
  transfers between devices with their start and end apart: 38 -> 38, of which waited for: 22 -> 27; matrix products, arithmetic and copies ran while one was open for 2% -> 4% of each run, Pallas kernels for 3% -> 3%
where the time goes in v5:
time: 244 us; the launch traced here: 242 us
  starting transfers between devices  131 us (54%)
  waiting for transfers between devices  68.6 us (28%)
  blocking collectives  19.3 us (8%)
  Pallas kernels  9.53 us (4%)
  local copies, waits for them, and re-layouts  8.05 us (3%)
  other arithmetic  4.57 us (2%)
    ppermute x32, starting transfers between devices, swap_depth(): return lax.ppermute(value, ('tok', 'exp'), pairs)  91 us
    ppermute x32, waiting for transfers between devices, swap_depth(): return lax.ppermute(value, ('tok', 'exp'), pairs)  66 us
    ppermute x5, starting transfers between devices, swap_core(): return lax.ppermute(value, 'exp', [(p, p ^ 1) for p in range(OWNERS)])  32.7 us
    all_to_all x1, blocking collectives, shards(): lax.all_to_all(outgoing, 'exp', 0, 0, axis_index_groups=SAME_CORE, tiled=...  19.3 us
    all_to_all x1, starting transfers between devices, shards(): lax.all_to_all(spread, 'exp', 0, 0, axis_index_groups=SAME_CORE, tiled=True)  7.77 us
    pallas_call x2, Pallas kernels, hidden_of(): pl.pallas_call(hidden_kernel, out_shape=jax.ShapeDtypeStruct((rows, sets...  5.64 us
  transfers between devices with their start and end apart: 38, of which 27 were waited for; matrix products, arithmetic and copies ran while one was open for 4% of the time, Pallas kernels for 3%

profile of v5, /device:TPU:1, one launch (start us, length us, event | category | flops | bytes accessed | tf_op | source)
XLA Modules:
  0.0 242.3 jit_solution(4316900347583659992)
XLA Ops:
  2.1 7.8 %all-to-all-start = ((bf16[16,128,256]{2,1,0:T(8,128)(2,1)}), bf16[16,128,256]{2,1,0:T(8,128)(2,1)}, u32[]{:S(2)}, u32[]{:S(2)}) async-start(bf16[16,128,256]{2,1,0:T(8,128)(2,1)} %broadcast_in_dim.54), calls=%async_computation | async-start | bytes 2097152 | tf_op jit(solution)/shard_map/all_to_all | solution.py:136
  9.8 5.5 %collective-permute-start.1 = (bf16[4096,128]{1,0:T(8,128)(2,1)S(1)}, bf16[4096,128]{1,0:T(8,128)(2,1)}, u32[]{:S(2)}, u32[]{:S(2)}) collective-permute-start(bf16[4096,128]{1,0:T(8,128)(2,1)S(1)} %bitcast.74), channel_id=1, source_target_pairs={{0,1},{1,0},{2,3},{3,2},{4,5},{5,4},{6,7},{7,6},{8,9},{9,8},{10,11... | collective-permute-start | bytes 3145736 | tf_op jit(solution)/shard_map/ppermute | solution.py:18
  26.2 6.7 %collective-permute-start = (bf16[4,128,256]{2,1,0:T(8,128)(2,1)}, bf16[4,128,256]{2,1,0:T(8,128)(2,1)}, u32[]{:S(2)}, u32[]{:S(2)}) collective-permute-start(bf16[4,128,256]{2,1,0:T(8,128)(2,1)} %gather_fusion.1), channel_id=1, source_target_pairs={{0,1},{1,0},{2,3},{3,2},{4,5},{5,4},{6,7},{7,6},{8,9},{9,8},{10,11... | collective-permute-start | bytes 786440 | tf_op jit(solution)/shard_map/ppermute | solution.py:18
  36.9 11.1 %collective-permute-start.4 = (bf16[256,256]{1,0:T(8,128)(2,1)S(1)}, bf16[256,256]{1,0:T(8,128)(2,1)S(1)}, u32[]{:S(2)}, u32[]{:S(2)}) collective-permute-start(bf16[256,256]{1,0:T(8,128)(2,1)S(1)} %bitcast.86), channel_id=1, source_target_pairs={{0,32},{1,481},{2,34},{3,483},{4,36},{5,485},{6,38},{7,487},{8,40}... | collective-permute-start | bytes 393224 | tf_op jit(solution)/shard_map/ppermute | solution.py:32
  52.4 2.6 %collective-permute-done.20 = bf16[256,256]{1,0:T(8,128)(2,1)S(1)} collective-permute-done((bf16[256,256]{1,0:T(8,128)(2,1)S(1)}, bf16[256,256]{1,0:T(8,128)(2,1)S(1)}, u32[]{:S(2)}, u32[]{:S(2)}) %collective-permute-start.20) | collective-permute-done | bytes 131104 | tf_op jit(solution)/shard_map/ppermute | solution.py:32
  57.9 4.6 %collective-permute-start.6 = (bf16[2,256,256]{2,1,0:T(8,128)(2,1)S(1)}, bf16[2,256,256]{2,1,0:T(8,128)(2,1)S(1)}, u32[]{:S(2)}, u32[]{:S(2)}) collective-permute-start(bf16[2,256,256]{2,1,0:T(8,128)(2,1)S(1)} %collective-permute-done.5.refs_1_), channel_id=1, source_target_pairs={{0,32},{1,481},{2,34},{3,483},{4,36},{5,485},{6,38},{7,487},{8,40}... | collective-permute-start | bytes 786440 | tf_op jit(solution)/shard_map/ppermute | solution.py:32
  62.4 2.8 %collective-permute-start.22 = (bf16[2,256,256]{2,1,0:T(8,128)(2,1)S(1)}, bf16[2,256,256]{2,1,0:T(8,128)(2,1)S(1)}, u32[]{:S(2)}, u32[]{:S(2)}) collective-permute-start(bf16[2,256,256]{2,1,0:T(8,128)(2,1)S(1)} %collective-permute-done.21.refs_1_), channel_id=1, source_target_pairs={{0,32},{1,481},{2,34},{3,483},{4,36},{5,485},{6,38},{7,487},{8,40}... | collective-permute-start | bytes 786440 | tf_op jit(solution)/shard_map/ppermute | solution.py:32
  72.7 3.5 %collective-permute-done.7.refs_3_ = bf16[2,256,256]{2,1,0:T(8,128)(2,1)S(1)} collective-permute-done((bf16[2,256,256]{2,1,0:T(8,128)(2,1)S(1)}, bf16[2,256,256]{2,1,0:T(8,128)(2,1)S(1)}, u32[]{:S(2)}, u32[]{:S(2)}) %collective-permute-start.7) | collective-permute-done | bytes 262176 | tf_op jit(solution)/shard_map/ppermute | solution.py:32
  78.7 4.0 %collective-permute-start.24 = (bf16[2,256,256]{2,1,0:T(8,128)(2,1)S(1)}, bf16[2,256,256]{2,1,0:T(8,128)(2,1)S(1)}, u32[]{:S(2)}, u32[]{:S(2)}) collective-permute-start(bf16[2,256,256]{2,1,0:T(8,128)(2,1)S(1)} %collective-permute-done.23.refs_3_), channel_id=1, source_target_pairs={{0,32},{1,481},{2,34},{3,483},{4,36},{5,485},{6,38},{7,487},{8,40}... | collective-permute-start | bytes 786440 | tf_op jit(solution)/shard_map/ppermute | solution.py:32
  82.7 4.7 %collective-permute-done.8.refs_4_ = bf16[2,256,256]{2,1,0:T(8,128)(2,1)S(1)} collective-permute-done((bf16[2,256,256]{2,1,0:T(8,128)(2,1)S(1)}, bf16[2,256,256]{2,1,0:T(8,128)(2,1)S(1)}, u32[]{:S(2)}, u32[]{:S(2)}) %collective-permute-start.8) | collective-permute-done | bytes 262176 | tf_op jit(solution)/shard_map/ppermute | solution.py:32
  90.0 2.7 %collective-permute-start.25 = (bf16[2,256,256]{2,1,0:T(8,128)(2,1)S(1)}, bf16[2,256,256]{2,1,0:T(8,128)(2,1)S(1)}, u32[]{:S(2)}, u32[]{:S(2)}) collective-permute-start(bf16[2,256,256]{2,1,0:T(8,128)(2,1)S(1)} %collective-permute-done.24.refs_4_), channel_id=1, source_target_pairs={{0,480},{1,33},{2,482},{3,35},{4,484},{5,37},{6,486},{7,39},{8,488... | collective-permute-start | bytes 786440 | tf_op jit(solution)/shard_map/ppermute | solution.py:32
  92.7 4.1 %collective-permute-done.9.refs_5_ = bf16[2,256,256]{2,1,0:T(8,128)(2,1)S(1)} collective-permute-done((bf16[2,256,256]{2,1,0:T(8,128)(2,1)S(1)}, bf16[2,256,256]{2,1,0:T(8,128)(2,1)S(1)}, u32[]{:S(2)}, u32[]{:S(2)}) %collective-permute-start.9) | collective-permute-done | bytes 262176 | tf_op jit(solution)/shard_map/ppermute | solution.py:32
  100.1 3.2 %collective-permute-start.26 = (bf16[2,256,256]{2,1,0:T(8,128)(2,1)S(1)}, bf16[2,256,256]{2,1,0:T(8,128)(2,1)S(1)}, u32[]{:S(2)}, u32[]{:S(2)}) collective-permute-start(bf16[2,256,256]{2,1,0:T(8,128)(2,1)S(1)} %collective-permute-done.25.refs_5_), channel_id=1, source_target_pairs={{0,32},{1,481},{2,34},{3,483},{4,36},{5,485},{6,38},{7,487},{8,40}... | collective-permute-start | bytes 786440 | tf_op jit(solution)/shard_map/ppermute | solution.py:32
  107.5 3.2 %collective-permute-done.26.refs_6_ = bf16[2,256,256]{2,1,0:T(8,128)(2,1)S(1)} collective-permute-done((bf16[2,256,256]{2,1,0:T(8,128)(2,1)S(1)}, bf16[2,256,256]{2,1,0:T(8,128)(2,1)S(1)}, u32[]{:S(2)}, u32[]{:S(2)}) %collective-permute-start.26) | collective-permute-done | bytes 262176 | tf_op jit(solution)/shard_map/ppermute | solution.py:32
  112.7 2.8 %hidden.2 = bf16[256,256]{1,0:T(8,128)(2,1)S(1)} custom-call(s32[16]{0:T(128)S(1)} %stack.103.order, bf16[2,256,256]{2,1,0:T(8,128)(2,1)S(1)} %pad_maximum_fusion.1.refs_0_, bf16[2,256,256]{2,1,0:T(8,128)(2,1)S(1)} %collective-permute-done.5.refs_1_, bf16[2,256,256]{2,1,0:T(8,128)(2,1)S(1)} %collective-permute-done.6.refs_2_, ...), custom_call_target="tpu_custom_call" | custom-call | flops 1073741824 | bytes 4194304 | tf_op jit(solution)/shard_map/hidden/pallas_call | solution.py:75
  115.5 3.3 %collective-permute-start.12 = (bf16[256,256]{1,0:T(8,128)(2,1)S(1)}, bf16[256,256]{1,0:T(8,128)(2,1)S(1)}, u32[]{:S(2)}, u32[]{:S(2)}) collective-permute-start(bf16[256,256]{1,0:T(8,128)(2,1)S(1)} %hidden.2), channel_id=1, source_target_pairs={{0,32},{1,481},{2,34},{3,483},{4,36},{5,485},{6,38},{7,487},{8,40}... | collective-permute-start | bytes 393224 | tf_op jit(solution)/shard_map/ppermute | solution.py:32
  120.3 2.8 %hidden.3 = bf16[256,256]{1,0:T(8,128)(2,1)S(1)} custom-call(s32[16]{0:T(128)S(1)} %stack.103.order, bf16[2,256,256]{2,1,0:T(8,128)(2,1)S(1)} %pad_maximum_fusion.3.refs_0_, bf16[2,256,256]{2,1,0:T(8,128)(2,1)S(1)} %collective-permute-done.21.refs_1_, bf16[2,256,256]{2,1,0:T(8,128)(2,1)S(1)} %collective-permute-done.22.refs_2_, ...), custom_call_target="tpu_custom_call" | custom-call | flops 1073741824 | bytes 4194304 | tf_op jit(solution)/shard_map/hidden/pallas_call | solution.py:75
  127.6 4.2 %collective-permute-done.28 = bf16[256,256]{1,0:T(8,128)(2,1)S(1)} collective-permute-done((bf16[256,256]{1,0:T(8,128)(2,1)S(1)}, bf16[256,256]{1,0:T(8,128)(2,1)S(1)}, u32[]{:S(2)}, u32[]{:S(2)}) %collective-permute-start.28) | collective-permute-done | bytes 131104 | tf_op jit(solution)/shard_map/ppermute | solution.py:32
  134.2 4.1 %collective-permute-start.14 = (bf16[2,256,256]{2,1,0:T(8,128)(2,1)S(1)}, bf16[2,256,256]{2,1,0:T(8,128)(2,1)S(1)}, u32[]{:S(2)}, u32[]{:S(2)}) collective-permute-start(bf16[2,256,256]{2,1,0:T(8,128)(2,1)S(1)} %collective-permute-done.13.refs_1_), channel_id=1, source_target_pairs={{0,32},{1,481},{2,34},{3,483},{4,36},{5,485},{6,38},{7,487},{8,40}... | collective-permute-start | bytes 786440 | tf_op jit(solution)/shard_map/ppermute | solution.py:32
  138.9 2.6 %collective-permute-start.30 = (bf16[2,256,256]{2,1,0:T(8,128)(2,1)S(1)}, bf16[2,256,256]{2,1,0:T(8,128)(2,1)S(1)}, u32[]{:S(2)}, u32[]{:S(2)}) collective-permute-start(bf16[2,256,256]{2,1,0:T(8,128)(2,1)S(1)} %collective-permute-done.29.refs_1_), channel_id=1, source_target_pairs={{0,32},{1,481},{2,34},{3,483},{4,36},{5,485},{6,38},{7,487},{8,40}... | collective-permute-start | bytes 786440 | tf_op jit(solution)/shard_map/ppermute | solution.py:32
  144.4 5.1 %collective-permute-done.30.refs_2_ = bf16[2,256,256]{2,1,0:T(8,128)(2,1)S(1)} collective-permute-done((bf16[2,256,256]{2,1,0:T(8,128)(2,1)S(1)}, bf16[2,256,256]{2,1,0:T(8,128)(2,1)S(1)}, u32[]{:S(2)}, u32[]{:S(2)}) %collective-permute-start.30) | collective-permute-done | bytes 262176 | tf_op jit(solution)/shard_map/ppermute | solution.py:32
  151.4 3.8 %collective-permute-start.16 = (bf16[2,256,256]{2,1,0:T(8,128)(2,1)S(1)}, bf16[2,256,256]{2,1,0:T(8,128)(2,1)S(1)}, u32[]{:S(2)}, u32[]{:S(2)}) collective-permute-start(bf16[2,256,256]{2,1,0:T(8,128)(2,1)S(1)} %collective-permute-done.15.refs_3_), channel_id=1, source_target_pairs={{0,32},{1,481},{2,34},{3,483},{4,36},{5,485},{6,38},{7,487},{8,40}... | collective-permute-start | bytes 786440 | tf_op jit(solution)/shard_map/ppermute | solution.py:32
  155.2 4.5 %collective-permute-done.31.refs_3_ = bf16[2,256,256]{2,1,0:T(8,128)(2,1)S(1)} collective-permute-done((bf16[2,256,256]{2,1,0:T(8,128)(2,1)S(1)}, bf16[2,256,256]{2,1,0:T(8,128)(2,1)S(1)}, u32[]{:S(2)}, u32[]{:S(2)}) %collective-permute-start.31) | collective-permute-done | bytes 262176 | tf_op jit(solution)/shard_map/ppermute | solution.py:32
  159.7 3.7 %collective-permute-start.32 = (bf16[2,256,256]{2,1,0:T(8,128)(2,1)S(1)}, bf16[2,256,256]{2,1,0:T(8,128)(2,1)S(1)}, u32[]{:S(2)}, u32[]{:S(2)}) collective-permute-start(bf16[2,256,256]{2,1,0:T(8,128)(2,1)S(1)} %collective-permute-done.31.refs_3_), channel_id=1, source_target_pairs={{0,32},{1,481},{2,34},{3,483},{4,36},{5,485},{6,38},{7,487},{8,40}... | collective-permute-start | bytes 786440 | tf_op jit(solution)/shard_map/ppermute | solution.py:32
  165.4 5.2 %collective-permute-done.32.refs_4_ = bf16[2,256,256]{2,1,0:T(8,128)(2,1)S(1)} collective-permute-done((bf16[2,256,256]{2,1,0:T(8,128)(2,1)S(1)}, bf16[2,256,256]{2,1,0:T(8,128)(2,1)S(1)}, u32[]{:S(2)}, u32[]{:S(2)}) %collective-permute-start.32) | collective-permute-done | bytes 262176 | tf_op jit(solution)/shard_map/ppermute | solution.py:32
  172.5 4.3 %collective-permute-start.18 = (bf16[2,256,256]{2,1,0:T(8,128)(2,1)S(1)}, bf16[2,256,256]{2,1,0:T(8,128)(2,1)S(1)}, u32[]{:S(2)}, u32[]{:S(2)}) collective-permute-start(bf16[2,256,256]{2,1,0:T(8,128)(2,1)S(1)} %collective-permute-done.17.refs_5_), channel_id=1, source_target_pairs={{0,32},{1,481},{2,34},{3,483},{4,36},{5,485},{6,38},{7,487},{8,40}... | collective-permute-start | bytes 786440 | tf_op jit(solution)/shard_map/ppermute | solution.py:32
  176.8 4.0 %collective-permute-done.33.refs_5_ = bf16[2,256,256]{2,1,0:T(8,128)(2,1)S(1)} collective-permute-done((bf16[2,256,256]{2,1,0:T(8,128)(2,1)S(1)}, bf16[2,256,256]{2,1,0:T(8,128)(2,1)S(1)}, u32[]{:S(2)}, u32[]{:S(2)}) %collective-permute-start.33) | collective-permute-done | bytes 262176 | tf_op jit(solution)/shard_map/ppermute | solution.py:32
  180.8 4.1 %collective-permute-start.34 = (bf16[2,256,256]{2,1,0:T(8,128)(2,1)S(1)}, bf16[2,256,256]{2,1,0:T(8,128)(2,1)S(1)}, u32[]{:S(2)}, u32[]{:S(2)}) collective-permute-start(bf16[2,256,256]{2,1,0:T(8,128)(2,1)S(1)} %collective-permute-done.33.refs_5_), channel_id=1, source_target_pairs={{0,32},{1,481},{2,34},{3,483},{4,36},{5,485},{6,38},{7,487},{8,40}... | collective-permute-start | bytes 786440 | tf_op jit(solution)/shard_map/ppermute | solution.py:32
  186.9 5.3 %collective-permute-done.34.refs_6_ = bf16[2,256,256]{2,1,0:T(8,128)(2,1)S(1)} collective-permute-done((bf16[2,256,256]{2,1,0:T(8,128)(2,1)S(1)}, bf16[2,256,256]{2,1,0:T(8,128)(2,1)S(1)}, u32[]{:S(2)}, u32[]{:S(2)}) %collective-permute-start.34) | collective-permute-done | bytes 262176 | tf_op jit(solution)/shard_map/ppermute | solution.py:32
  196.0 6.1 %collective-permute-done.35.refs_7_ = bf16[2,256,256]{2,1,0:T(8,128)(2,1)S(1)} collective-permute-done((bf16[2,256,256]{2,1,0:T(8,128)(2,1)S(1)}, bf16[2,256,256]{2,1,0:T(8,128)(2,1)S(1)}, u32[]{:S(2)}, u32[]{:S(2)}) %collective-permute-start.35) | collective-permute-done | bytes 262176 | tf_op jit(solution)/shard_map/ppermute | solution.py:32
  204.1 16.2 %collective-permute-start.36 = (bf16[4,128,256]{2,1,0:T(8,128)(2,1)S(1)}, bf16[4,128,256]{2,1,0:T(8,128)(2,1)S(1)}, u32[]{:S(2)}, u32[]{:S(2)}) collective-permute-start(bf16[4,128,256]{2,1,0:T(8,128)(2,1)S(1)} %bitcast.83), channel_id=1, source_target_pairs={{0,1},{1,0},{2,3},{3,2},{4,5},{5,4},{6,7},{7,6},{8,9},{9,8},{10,11... | collective-permute-start | bytes 786440 | tf_op jit(solution)/shard_map/ppermute | solution.py:18
  222.3 19.3 %all_to_all.10 = bf16[16,128,256]{2,1,0:T(8,128)(2,1)S(1)} all-to-all(bf16[16,128,256]{2,1,0:T(8,128)(2,1)S(1)} %broadcast_select_fusion), channel_id=1, replica_groups={{0,2,4,6,8,10,12,14,16,18,20,22,24,26,28,30},{1,3,5,7,9,11,13,15,17,19,..., dimensions={0} | all-to-all | bytes 2097152 | tf_op jit(solution)/shard_map/all_to_all | solution.py:163
  (92 shorter events, 73.9 us)
Async XLA Ops:
  2.1 21.6 %all-to-all-start = ((bf16[16,128,256]{2,1,0:T(8,128)(2,1)}), bf16[16,128,256]{2,1,0:T(8,128)(2,1)}, u32[]{:S(2)}, u32[]{:S(2)}) async-start(bf16[16,128,256]{2,1,0:T(8,128)(2,1)} %broadcast_in_dim.54), calls=%async_computation | async-start | bytes 2097152 | tf_op jit(solution)/shard_map/all_to_all | solution.py:136
  9.8 26.8 %collective-permute-start.1 = (bf16[4096,128]{1,0:T(8,128)(2,1)S(1)}, bf16[4096,128]{1,0:T(8,128)(2,1)}, u32[]{:S(2)}, u32[]{:S(2)}) collective-permute-start(bf16[4096,128]{1,0:T(8,128)(2,1)S(1)} %bitcast.74), channel_id=1, source_target_pairs={{0,1},{1,0},{2,3},{3,2},{4,5},{5,4},{6,7},{7,6},{8,9},{9,8},{10,11... | collective-permute-start | bytes 3145736 | tf_op jit(solution)/shard_map/ppermute | solution.py:18
  15.3 21.3 %collective-permute-start.2 = (bf16[4096,128]{1,0:T(8,128)(2,1)S(1)}, bf16[4096,128]{1,0:T(8,128)(2,1)}, u32[]{:S(2)}, u32[]{:S(2)}) collective-permute-start(bf16[4096,128]{1,0:T(8,128)(2,1)S(1)} %bitcast.77), channel_id=1, source_target_pairs={{0,1},{1,0},{2,3},{3,2},{4,5},{5,4},{6,7},{7,6},{8,9},{9,8},{10,11... | collective-permute-start | bytes 3145736 | tf_op jit(solution)/shard_map/ppermute | solution.py:18
  17.3 19.4 %collective-permute-start.3 = (bf16[2048,256]{1,0:T(8,128)(2,1)S(1)}, bf16[2048,256]{1,0:T(8,128)(2,1)}, u32[]{:S(2)}, u32[]{:S(2)}) collective-permute-start(bf16[2048,256]{1,0:T(8,128)(2,1)S(1)} %bitcast.80), channel_id=1, source_target_pairs={{0,1},{1,0},{2,3},{3,2},{4,5},{5,4},{6,7},{7,6},{8,9},{9,8},{10,11... | collective-permute-start | bytes 3145736 | tf_op jit(solution)/shard_map/ppermute | solution.py:18
  26.2 9.4 %collective-permute-start = (bf16[4,128,256]{2,1,0:T(8,128)(2,1)}, bf16[4,128,256]{2,1,0:T(8,128)(2,1)}, u32[]{:S(2)}, u32[]{:S(2)}) collective-permute-start(bf16[4,128,256]{2,1,0:T(8,128)(2,1)} %gather_fusion.1), channel_id=1, source_target_pairs={{0,1},{1,0},{2,3},{3,2},{4,5},{5,4},{6,7},{7,6},{8,9},{9,8},{10,11... | collective-permute-start | bytes 786440 | tf_op jit(solution)/shard_map/ppermute | solution.py:18
  36.9 13.5 %collective-permute-start.4 = (bf16[256,256]{1,0:T(8,128)(2,1)S(1)}, bf16[256,256]{1,0:T(8,128)(2,1)S(1)}, u32[]{:S(2)}, u32[]{:S(2)}) collective-permute-start(bf16[256,256]{1,0:T(8,128)(2,1)S(1)} %bitcast.86), channel_id=1, source_target_pairs={{0,32},{1,481},{2,34},{3,483},{4,36},{5,485},{6,38},{7,487},{8,40}... | collective-permute-start | bytes 393224 | tf_op jit(solution)/shard_map/ppermute | solution.py:32
  57.9 9.1 %collective-permute-start.6 = (bf16[2,256,256]{2,1,0:T(8,128)(2,1)S(1)}, bf16[2,256,256]{2,1,0:T(8,128)(2,1)S(1)}, u32[]{:S(2)}, u32[]{:S(2)}) collective-permute-start(bf16[2,256,256]{2,1,0:T(8,128)(2,1)S(1)} %collective-permute-done.5.refs_1_), channel_id=1, source_target_pairs={{0,32},{1,481},{2,34},{3,483},{4,36},{5,485},{6,38},{7,487},{8,40}... | collective-permute-start | bytes 786440 | tf_op jit(solution)/shard_map/ppermute | solution.py:32
  62.4 8.3 %collective-permute-start.22 = (bf16[2,256,256]{2,1,0:T(8,128)(2,1)S(1)}, bf16[2,256,256]{2,1,0:T(8,128)(2,1)S(1)}, u32[]{:S(2)}, u32[]{:S(2)}) collective-permute-start(bf16[2,256,256]{2,1,0:T(8,128)(2,1)S(1)} %collective-permute-done.21.refs_1_), channel_id=1, source_target_pairs={{0,32},{1,481},{2,34},{3,483},{4,36},{5,485},{6,38},{7,487},{8,40}... | collective-permute-start | bytes 786440 | tf_op jit(solution)/shard_map/ppermute | solution.py:32
  66.9 9.2 %collective-permute-start.7 = (bf16[2,256,256]{2,1,0:T(8,128)(2,1)S(1)}, bf16[2,256,256]{2,1,0:T(8,128)(2,1)S(1)}, u32[]{:S(2)}, u32[]{:S(2)}) collective-permute-start(bf16[2,256,256]{2,1,0:T(8,128)(2,1)S(1)} %collective-permute-done.6.refs_2_), channel_id=1, source_target_pairs={{0,480},{1,33},{2,482},{3,35},{4,484},{5,37},{6,486},{7,39},{8,488... | collective-permute-start | bytes 786440 | tf_op jit(solution)/shard_map/ppermute | solution.py:32
  76.2 11.2 %collective-permute-start.8 = (bf16[2,256,256]{2,1,0:T(8,128)(2,1)S(1)}, bf16[2,256,256]{2,1,0:T(8,128)(2,1)S(1)}, u32[]{:S(2)}, u32[]{:S(2)}) collective-permute-start(bf16[2,256,256]{2,1,0:T(8,128)(2,1)S(1)} %collective-permute-done.7.refs_3_), channel_id=1, source_target_pairs={{0,32},{1,481},{2,34},{3,483},{4,36},{5,485},{6,38},{7,487},{8,40}... | collective-permute-start | bytes 786440 | tf_op jit(solution)/shard_map/ppermute | solution.py:32
  78.7 11.3 %collective-permute-start.24 = (bf16[2,256,256]{2,1,0:T(8,128)(2,1)S(1)}, bf16[2,256,256]{2,1,0:T(8,128)(2,1)S(1)}, u32[]{:S(2)}, u32[]{:S(2)}) collective-permute-start(bf16[2,256,256]{2,1,0:T(8,128)(2,1)S(1)} %collective-permute-done.23.refs_3_), channel_id=1, source_target_pairs={{0,32},{1,481},{2,34},{3,483},{4,36},{5,485},{6,38},{7,487},{8,40}... | collective-permute-start | bytes 786440 | tf_op jit(solution)/shard_map/ppermute | solution.py:32
  87.4 9.4 %collective-permute-start.9 = (bf16[2,256,256]{2,1,0:T(8,128)(2,1)S(1)}, bf16[2,256,256]{2,1,0:T(8,128)(2,1)S(1)}, u32[]{:S(2)}, u32[]{:S(2)}) collective-permute-start(bf16[2,256,256]{2,1,0:T(8,128)(2,1)S(1)} %collective-permute-done.8.refs_4_), channel_id=1, source_target_pairs={{0,480},{1,33},{2,482},{3,35},{4,484},{5,37},{6,486},{7,39},{8,488... | collective-permute-start | bytes 786440 | tf_op jit(solution)/shard_map/ppermute | solution.py:32
  90.0 10.1 %collective-permute-start.25 = (bf16[2,256,256]{2,1,0:T(8,128)(2,1)S(1)}, bf16[2,256,256]{2,1,0:T(8,128)(2,1)S(1)}, u32[]{:S(2)}, u32[]{:S(2)}) collective-permute-start(bf16[2,256,256]{2,1,0:T(8,128)(2,1)S(1)} %collective-permute-done.24.refs_4_), channel_id=1, source_target_pairs={{0,480},{1,33},{2,482},{3,35},{4,484},{5,37},{6,486},{7,39},{8,488... | collective-permute-start | bytes 786440 | tf_op jit(solution)/shard_map/ppermute | solution.py:32
  96.8 8.8 %collective-permute-start.10 = (bf16[2,256,256]{2,1,0:T(8,128)(2,1)S(1)}, bf16[2,256,256]{2,1,0:T(8,128)(2,1)S(1)}, u32[]{:S(2)}, u32[]{:S(2)}) collective-permute-start(bf16[2,256,256]{2,1,0:T(8,128)(2,1)S(1)} %collective-permute-done.9.refs_5_), channel_id=1, source_target_pairs={{0,32},{1,481},{2,34},{3,483},{4,36},{5,485},{6,38},{7,487},{8,40}... | collective-permute-start | bytes 786440 | tf_op jit(solution)/shard_map/ppermute | solution.py:32
  100.1 10.6 %collective-permute-start.26 = (bf16[2,256,256]{2,1,0:T(8,128)(2,1)S(1)}, bf16[2,256,256]{2,1,0:T(8,128)(2,1)S(1)}, u32[]{:S(2)}, u32[]{:S(2)}) collective-permute-start(bf16[2,256,256]{2,1,0:T(8,128)(2,1)S(1)} %collective-permute-done.25.refs_5_), channel_id=1, source_target_pairs={{0,32},{1,481},{2,34},{3,483},{4,36},{5,485},{6,38},{7,487},{8,40}... | collective-permute-start | bytes 786440 | tf_op jit(solution)/shard_map/ppermute | solution.py:32
  110.7 9.6 %collective-permute-start.27 = (bf16[2,256,256]{2,1,0:T(8,128)(2,1)S(1)}, bf16[2,256,256]{2,1,0:T(8,128)(2,1)S(1)}, u32[]{:S(2)}, u32[]{:S(2)}) collective-permute-start(bf16[2,256,256]{2,1,0:T(8,128)(2,1)S(1)} %collective-permute-done.26.refs_6_), channel_id=1, source_target_pairs={{0,480},{1,33},{2,482},{3,35},{4,484},{5,37},{6,486},{7,39},{8,488... | collective-permute-start | bytes 786440 | tf_op jit(solution)/shard_map/ppermute | solution.py:32
  115.5 10.0 %collective-permute-start.12 = (bf16[256,256]{1,0:T(8,128)(2,1)S(1)}, bf16[256,256]{1,0:T(8,128)(2,1)S(1)}, u32[]{:S(2)}, u32[]{:S(2)}) collective-permute-start(bf16[256,256]{1,0:T(8,128)(2,1)S(1)} %hidden.2), channel_id=1, source_target_pairs={{0,32},{1,481},{2,34},{3,483},{4,36},{5,485},{6,38},{7,487},{8,40}... | collective-permute-start | bytes 393224 | tf_op jit(solution)/shard_map/ppermute | solution.py:32
  123.2 8.6 %collective-permute-start.28 = (bf16[256,256]{1,0:T(8,128)(2,1)S(1)}, bf16[256,256]{1,0:T(8,128)(2,1)S(1)}, u32[]{:S(2)}, u32[]{:S(2)}) collective-permute-start(bf16[256,256]{1,0:T(8,128)(2,1)S(1)} %hidden.3), channel_id=1, source_target_pairs={{0,32},{1,481},{2,34},{3,483},{4,36},{5,485},{6,38},{7,487},{8,40}... | collective-permute-start | bytes 393224 | tf_op jit(solution)/shard_map/ppermute | solution.py:32
  125.6 8.5 %collective-permute-start.13 = (bf16[2,256,256]{2,1,0:T(8,128)(2,1)S(1)}, bf16[2,256,256]{2,1,0:T(8,128)(2,1)S(1)}, u32[]{:S(2)}, u32[]{:S(2)}) collective-permute-start(bf16[2,256,256]{2,1,0:T(8,128)(2,1)S(1)} %pad_maximum_fusion.2.refs_0_), channel_id=1, source_target_pairs={{0,480},{1,33},{2,482},{3,35},{4,484},{5,37},{6,486},{7,39},{8,488... | collective-permute-start | bytes 786440 | tf_op jit(solution)/shard_map/ppermute | solution.py:32
  134.2 8.3 %collective-permute-start.14 = (bf16[2,256,256]{2,1,0:T(8,128)(2,1)S(1)}, bf16[2,256,256]{2,1,0:T(8,128)(2,1)S(1)}, u32[]{:S(2)}, u32[]{:S(2)}) collective-permute-start(bf16[2,256,256]{2,1,0:T(8,128)(2,1)S(1)} %collective-permute-done.13.refs_1_), channel_id=1, source_target_pairs={{0,32},{1,481},{2,34},{3,483},{4,36},{5,485},{6,38},{7,487},{8,40}... | collective-permute-start | bytes 786440 | tf_op jit(solution)/shard_map/ppermute | solution.py:32
  138.9 10.6 %collective-permute-start.30 = (bf16[2,256,256]{2,1,0:T(8,128)(2,1)S(1)}, bf16[2,256,256]{2,1,0:T(8,128)(2,1)S(1)}, u32[]{:S(2)}, u32[]{:S(2)}) collective-permute-start(bf16[2,256,256]{2,1,0:T(8,128)(2,1)S(1)} %collective-permute-done.29.refs_1_), channel_id=1, source_target_pairs={{0,32},{1,481},{2,34},{3,483},{4,36},{5,485},{6,38},{7,487},{8,40}... | collective-permute-start | bytes 786440 | tf_op jit(solution)/shard_map/ppermute | solution.py:32
  142.5 8.9 %collective-permute-start.15 = (bf16[2,256,256]{2,1,0:T(8,128)(2,1)S(1)}, bf16[2,256,256]{2,1,0:T(8,128)(2,1)S(1)}, u32[]{:S(2)}, u32[]{:S(2)}) collective-permute-start(bf16[2,256,256]{2,1,0:T(8,128)(2,1)S(1)} %collective-permute-done.14.refs_2_), channel_id=1, source_target_pairs={{0,480},{1,33},{2,482},{3,35},{4,484},{5,37},{6,486},{7,39},{8,488... | collective-permute-start | bytes 786440 | tf_op jit(solution)/shard_map/ppermute | solution.py:32
  149.5 10.2 %collective-permute-start.31 = (bf16[2,256,256]{2,1,0:T(8,128)(2,1)S(1)}, bf16[2,256,256]{2,1,0:T(8,128)(2,1)S(1)}, u32[]{:S(2)}, u32[]{:S(2)}) collective-permute-start(bf16[2,256,256]{2,1,0:T(8,128)(2,1)S(1)} %collective-permute-done.30.refs_2_), channel_id=1, source_target_pairs={{0,480},{1,33},{2,482},{3,35},{4,484},{5,37},{6,486},{7,39},{8,488... | collective-permute-start | bytes 786440 | tf_op jit(solution)/shard_map/ppermute | solution.py:32
  151.4 12.1 %collective-permute-start.16 = (bf16[2,256,256]{2,1,0:T(8,128)(2,1)S(1)}, bf16[2,256,256]{2,1,0:T(8,128)(2,1)S(1)}, u32[]{:S(2)}, u32[]{:S(2)}) collective-permute-start(bf16[2,256,256]{2,1,0:T(8,128)(2,1)S(1)} %collective-permute-done.15.refs_3_), channel_id=1, source_target_pairs={{0,32},{1,481},{2,34},{3,483},{4,36},{5,485},{6,38},{7,487},{8,40}... | collective-permute-start | bytes 786440 | tf_op jit(solution)/shard_map/ppermute | solution.py:32
  159.7 10.9 %collective-permute-start.32 = (bf16[2,256,256]{2,1,0:T(8,128)(2,1)S(1)}, bf16[2,256,256]{2,1,0:T(8,128)(2,1)S(1)}, u32[]{:S(2)}, u32[]{:S(2)}) collective-permute-start(bf16[2,256,256]{2,1,0:T(8,128)(2,1)S(1)} %collective-permute-done.31.refs_3_), channel_id=1, source_target_pairs={{0,32},{1,481},{2,34},{3,483},{4,36},{5,485},{6,38},{7,487},{8,40}... | collective-permute-start | bytes 786440 | tf_op jit(solution)/shard_map/ppermute | solution.py:32
  163.5 9.0 %collective-permute-start.17 = (bf16[2,256,256]{2,1,0:T(8,128)(2,1)S(1)}, bf16[2,256,256]{2,1,0:T(8,128)(2,1)S(1)}, u32[]{:S(2)}, u32[]{:S(2)}) collective-permute-start(bf16[2,256,256]{2,1,0:T(8,128)(2,1)S(1)} %collective-permute-done.16.refs_4_), channel_id=1, source_target_pairs={{0,480},{1,33},{2,482},{3,35},{4,484},{5,37},{6,486},{7,39},{8,488... | collective-permute-start | bytes 786440 | tf_op jit(solution)/shard_map/ppermute | solution.py:32
  170.6 10.3 %collective-permute-start.33 = (bf16[2,256,256]{2,1,0:T(8,128)(2,1)S(1)}, bf16[2,256,256]{2,1,0:T(8,128)(2,1)S(1)}, u32[]{:S(2)}, u32[]{:S(2)}) collective-permute-start(bf16[2,256,256]{2,1,0:T(8,128)(2,1)S(1)} %collective-permute-done.32.refs_4_), channel_id=1, source_target_pairs={{0,480},{1,33},{2,482},{3,35},{4,484},{5,37},{6,486},{7,39},{8,488... | collective-permute-start | bytes 786440 | tf_op jit(solution)/shard_map/ppermute | solution.py:32
  172.5 12.5 %collective-permute-start.18 = (bf16[2,256,256]{2,1,0:T(8,128)(2,1)S(1)}, bf16[2,256,256]{2,1,0:T(8,128)(2,1)S(1)}, u32[]{:S(2)}, u32[]{:S(2)}) collective-permute-start(bf16[2,256,256]{2,1,0:T(8,128)(2,1)S(1)} %collective-permute-done.17.refs_5_), channel_id=1, source_target_pairs={{0,32},{1,481},{2,34},{3,483},{4,36},{5,485},{6,38},{7,487},{8,40}... | collective-permute-start | bytes 786440 | tf_op jit(solution)/shard_map/ppermute | solution.py:32
  180.8 11.3 %collective-permute-start.34 = (bf16[2,256,256]{2,1,0:T(8,128)(2,1)S(1)}, bf16[2,256,256]{2,1,0:T(8,128)(2,1)S(1)}, u32[]{:S(2)}, u32[]{:S(2)}) collective-permute-start(bf16[2,256,256]{2,1,0:T(8,128)(2,1)S(1)} %collective-permute-done.33.refs_5_), channel_id=1, source_target_pairs={{0,32},{1,481},{2,34},{3,483},{4,36},{5,485},{6,38},{7,487},{8,40}... | collective-permute-start | bytes 786440 | tf_op jit(solution)/shard_map/ppermute | solution.py:32
  185.0 9.1 %collective-permute-start.19 = (bf16[2,256,256]{2,1,0:T(8,128)(2,1)S(1)}, bf16[2,256,256]{2,1,0:T(8,128)(2,1)S(1)}, u32[]{:S(2)}, u32[]{:S(2)}) collective-permute-start(bf16[2,256,256]{2,1,0:T(8,128)(2,1)S(1)} %collective-permute-done.18.refs_6_), channel_id=1, source_target_pairs={{0,480},{1,33},{2,482},{3,35},{4,484},{5,37},{6,486},{7,39},{8,488... | collective-permute-start | bytes 786440 | tf_op jit(solution)/shard_map/ppermute | solution.py:32
  192.1 10.0 %collective-permute-start.35 = (bf16[2,256,256]{2,1,0:T(8,128)(2,1)S(1)}, bf16[2,256,256]{2,1,0:T(8,128)(2,1)S(1)}, u32[]{:S(2)}, u32[]{:S(2)}) collective-permute-start(bf16[2,256,256]{2,1,0:T(8,128)(2,1)S(1)} %collective-permute-done.34.refs_6_), channel_id=1, source_target_pairs={{0,480},{1,33},{2,482},{3,35},{4,484},{5,37},{6,486},{7,39},{8,488... | collective-permute-start | bytes 786440 | tf_op jit(solution)/shard_map/ppermute | solution.py:32
  204.1 17.4 %collective-permute-start.36 = (bf16[4,128,256]{2,1,0:T(8,128)(2,1)S(1)}, bf16[4,128,256]{2,1,0:T(8,128)(2,1)S(1)}, u32[]{:S(2)}, u32[]{:S(2)}) collective-permute-start(bf16[4,128,256]{2,1,0:T(8,128)(2,1)S(1)} %bitcast.83), channel_id=1, source_target_pairs={{0,1},{1,0},{2,3},{3,2},{4,5},{5,4},{6,7},{7,6},{8,9},{9,8},{10,11... | collective-permute-start | bytes 786440 | tf_op jit(solution)/shard_map/ppermute | solution.py:18
  (10 other events, 104.3 us)

commit v6 on v3

v6 whole, which is shorter than its diff:
```python
import jax
import jax.numpy as jnp
from jax import lax
from jax.experimental import pallas as pl
from jax.experimental.pallas import tpu as pltpu
from jax.sharding import PartitionSpec as P

BLOCK = 128
SPAN = 4
CHIPS = 16
DEPTH = 16
OWNERS = 32
BLOCKS = 2
RELAY = 6
SAME_CORE = [[2 * chip + core for chip in range(CHIPS)] for core in range(2)]


def swap_core(value):
    return lax.ppermute(value, "exp", [(p, p ^ 1) for p in range(OWNERS)])


def swap_across(value):
    return lax.ppermute(value, "exp", [(p, p ^ 2) for p in range(OWNERS)])


def swap_tok(value, partner):
    pairs = [(z * OWNERS + p, partner(z, p % 2) * OWNERS + p) for z in range(DEPTH) for p in range(OWNERS)]
    return lax.ppermute(value, ("tok", "exp"), pairs)


def swap_near(value, step):
    def partner(z, core):
        return (z + 1) % DEPTH if (z + step + core) % 2 == 0 else (z - 1) % DEPTH

    return swap_tok(value, partner)


def near_order(z, core):
    turned = lax.rem(z - core + DEPTH, DEPTH)
    pair, odd = turned // 2, lax.rem(turned, 2)
    away = jnp.where(odd == 1, 1, -1)
    pairs = [pair]
    for step in range(1, DEPTH // 2):
        reach = (step + 1) // 2
        pairs.append(pair + (away * reach if step % 2 else -away * reach))
    chunks = [2 * p + half + core for p in pairs for half in range(2)]
    return odd == 1, lax.rem(jnp.stack(chunks) + 2 * DEPTH, DEPTH).astype(jnp.int32)


def hidden_kernel(order, *refs):
    items, weights, outs = refs[:DEPTH], refs[DEPTH : -BLOCKS], refs[-BLOCKS:]
    depth = items[0].shape[2]
    total = None
    for number in range(DEPTH):
        pair, half = number // 2, number % 2
        left = jnp.concatenate([items[pair][half], items[DEPTH // 2 + pair][half]], axis=0)
        rows = pl.ds(pl.multiple_of(order[number] * depth, depth), depth)
        right = jnp.concatenate([weight[rows, :] for weight in weights], axis=1)
        term = jnp.dot(left, right, preferred_element_type=jnp.float32)
        total = term if total is None else total + term
    units = total.shape[1] // 2
    gate, up = total[:, :units], total[:, units:]
    hidden = (gate / (1.0 + jnp.exp(-gate)) * up).astype(outs[0].dtype)
    for block, out in enumerate(outs):
        out[...] = hidden[block * BLOCK : (block + 1) * BLOCK]


def down_kernel(order, scale, *refs):
    items, weights, out = refs[:DEPTH], refs[DEPTH:-1], refs[-1]
    depth = items[0].shape[2] // len(weights)
    total = None
    for number in range(DEPTH):
        pair, half = number // 2, number % 2
        left = jnp.concatenate([items[pair][half], items[DEPTH // 2 + pair][half]], axis=0)
        rows = pl.ds(pl.multiple_of(order[number] * depth, depth), depth)
        right = jnp.concatenate([weight[rows, :] for weight in weights], axis=0)
        term = jnp.dot(left, right, preferred_element_type=jnp.float32)
        total = term if total is None else total + term
    out[...] = (total * scale[:, :1]).astype(out.dtype)


def kernel_call(kernel, name, order, inner, outs, flops):
    in_vmem = pl.BlockSpec(memory_space=pltpu.VMEM)
    return pl.pallas_call(
        kernel,
        out_shape=[jax.ShapeDtypeStruct(shape, jnp.bfloat16) for shape in outs],
        in_specs=[pl.BlockSpec(memory_space=pltpu.SMEM)] + [in_vmem] * len(inner),
        out_specs=[in_vmem] * len(outs),
        compiler_params=pltpu.CompilerParams(vmem_limit_bytes=20 << 20),
        cost_estimate=pl.CostEstimate(
            flops=flops, bytes_accessed=2 * sum(array.size for array in inner), transcendentals=0
        ),
        name=name,
    )(order, *inner)


def gather_near(chunk, odd):
    other = swap_near(chunk, 0)
    items = [jnp.stack([jnp.where(odd, other, chunk), jnp.where(odd, chunk, other)])]
    for step in range(1, DEPTH // 2):
        items.append(swap_near(items[-1], step))
    return items


def shards(tokens, picked_blocks, gate_scale, w_gate, w_up, w_down):
    position = lax.axis_index("exp")
    z = lax.axis_index("tok")
    core = lax.rem(position, 2)
    share = lax.rem(position, SPAN)
    expert = position // SPAN
    features, units = tokens.shape[1], w_gate.shape[2]
    chosen = lax.dynamic_index_in_dim(picked_blocks, expert, 0, keepdims=False)
    blocks = chosen.shape[0] // SPAN
    rows = blocks * BLOCK
    mine = lax.dynamic_slice_in_dim(chosen, blocks * share, blocks)
    theirs = lax.dynamic_slice_in_dim(chosen, blocks * jnp.bitwise_xor(share, 1), blocks)
    here = (lax.rem(mine, 2) == core)[:, None, None]
    odd, order = near_order(z, core)
    scale = lax.dynamic_index_in_dim(gate_scale, expert, 0, keepdims=False).reshape(SPAN, rows, 1)
    scale = jnp.broadcast_to(lax.dynamic_index_in_dim(scale, share, 0, keepdims=False), (rows, 128))
    names = jnp.concatenate([mine, theirs])
    match = names[None, :] == (2 * jnp.arange(CHIPS, dtype=jnp.int32) + core)[:, None]
    wanted, source = match.any(1)[:, None, None], jnp.argmax(match, 1)

    own = [w_gate[0], w_up[0], w_down[0]]
    spread = jnp.broadcast_to(tokens[None], (CHIPS,) + tokens.shape)
    held = lax.all_to_all(spread, "exp", 0, 0, axis_index_groups=SAME_CORE, tiled=True)
    near = [swap_core(w) for w in own]
    held, sent = lax.optimization_barrier((held, own))
    far = [swap_across(w) for w in sent]
    lent = swap_core(held[theirs // 2])
    selected = jnp.where(here, held[mine // 2], lent)
    selected, near, odd, order, scale, wanted, source = lax.optimization_barrier(
        (selected, near, odd, order, scale, wanted, source)
    )

    chains = [gather_near(selected[block], odd) for block in range(blocks)]
    far_in, _ = lax.optimization_barrier((far[:2], [chain[RELAY] for chain in chains]))
    relayed = [swap_core(w) for w in far_in]
    flops = 2 * rows * DEPTH * features * 2 * SPAN * units
    parts = kernel_call(
        hidden_kernel, "hidden", order,
        [item for chain in chains for item in chain] + [w[kind] for kind in range(2) for w in (own, near, far_in, relayed)],
        [(BLOCK, SPAN * units)] * blocks, flops,
    )

    chains = [gather_near(part, odd) for part in parts]
    far_down, _ = lax.optimization_barrier((far[2], [chain[RELAY // 2] for chain in chains]))
    (done,) = kernel_call(
        down_kernel, "down", order,
        [scale] + [item for chain in chains for item in chain] + [own[2], near[2], far_down, swap_core(far_down)],
        [(rows, features)], flops // 2,
    )
    done = done.reshape(blocks, BLOCK, features)

    all_done = jnp.concatenate([done, swap_core(done)])
    outgoing = jnp.where(wanted, all_done[source], 0)
    arrived = lax.all_to_all(outgoing, "exp", 0, 0, axis_index_groups=SAME_CORE, tiled=True)
    return jnp.sum(arrived, axis=0, dtype=jnp.float32).astype(jnp.bfloat16)


def solution(mesh):
    return jax.shard_map(
        shards,
        mesh=mesh,
        in_specs=(
            P("exp", "tok"),
            P(),
            P(),
            P("exp", None, "tok"),
            P("exp", None, "tok"),
            P("exp", None, "tok"),
        ),
        out_specs=P("exp", "tok"),
        check_vma=False,
    )
```

time: 255 us -> 243 us (0.953)
  waiting for transfers between devices: 88.3 us -> 46.1 us
  starting transfers between devices: 122 us -> 158 us
  Pallas kernels: 12.3 us -> 6.06 us
    ppermute x24 -> x32, waiting for transfers between devices: 72.1 us -> 44.4 us  [swap_tok(): return lax.ppermute(value, ('tok', 'exp'), pairs)]
    ppermute x24 -> x32, starting transfers between devices: 79.9 us -> 96.7 us  [swap_tok(): return lax.ppermute(value, ('tok', 'exp'), pairs)]
    all_to_all x1, waiting for transfers between devices: 14.8 us -> 0.77 us  [shards(): lax.all_to_all(spread, 'exp', 0, 0, axis_index_groups=SAME_CORE, tiled=True)]
    ppermute x6 -> x8, starting transfers between devices: 33 us -> 46.7 us  [swap_core(): return lax.ppermute(value, 'exp', [(p, p ^ 1) for p in range(OWNERS)])]
    pallas_call x2, Pallas kernels: 12.3 us -> 6.06 us  [kernel_call(): pl.pallas_call(kernel, out_shape=[jax.ShapeDtypeStruct(shape, jnp.bfloat1...]
    all_to_all x1, starting transfers between devices: 3.65 us -> 7.77 us  [shards(): lax.all_to_all(spread, 'exp', 0, 0, axis_index_groups=SAME_CORE, tiled=True)]
    unnamed x15 -> x6, local copies, waits for them, and re-layouts: 2.96 us -> 0.01 us
    ppermute x2 -> x3, starting transfers between devices: 5.55 us -> 7.21 us  [swap_across(): return lax.ppermute(value, 'exp', [(p, p ^ 2) for p in range(OWNERS)])]
  transfers between devices with their start and end apart: 33 -> 44, of which waited for: 22 -> 24; matrix products, arithmetic and copies ran while one was open for 3% -> 3% of each run, Pallas kernels for 0% -> 0%
where the time goes in v6:
time: 243 us; the launch traced here: 242 us
  starting transfers between devices  158 us (65%)
  waiting for transfers between devices  46.1 us (19%)
  blocking collectives  19.3 us (8%)
  local copies, waits for them, and re-layouts  7.76 us (3%)
  Pallas kernels  6.06 us (2%)
  other arithmetic  3.52 us (1%)
    ppermute x32, starting transfers between devices, swap_tok(): return lax.ppermute(value, ('tok', 'exp'), pairs)  96.7 us
    ppermute x8, starting transfers between devices, swap_core(): return lax.ppermute(value, 'exp', [(p, p ^ 1) for p in range(OWNERS)])  46.7 us
    ppermute x32, waiting for transfers between devices, swap_tok(): return lax.ppermute(value, ('tok', 'exp'), pairs)  44.4 us
    all_to_all x1, blocking collectives, shards(): lax.all_to_all(outgoing, 'exp', 0, 0, axis_index_groups=SAME_CORE, tiled=...  19.3 us
    all_to_all x1, starting transfers between devices, shards(): lax.all_to_all(spread, 'exp', 0, 0, axis_index_groups=SAME_CORE, tiled=True)  7.77 us
    ppermute x3, starting transfers between devices, swap_across(): return lax.ppermute(value, 'exp', [(p, p ^ 2) for p in range(OWNERS)])  7.21 us
    pallas_call x2, Pallas kernels, kernel_call(): pl.pallas_call(kernel, out_shape=[jax.ShapeDtypeStruct(shape, jnp.bfloat1...  6.06 us
  transfers between devices with their start and end apart: 44, of which 24 were waited for; matrix products, arithmetic and copies ran while one was open for 3% of the time, Pallas kernels for 0%

profile of v6, /device:TPU:1, one launch (start us, length us, event | category | flops | bytes accessed | tf_op | source)
XLA Modules:
  0.0 241.8 jit_solution(519339485488433828)
XLA Ops:
  1.9 7.8 %all-to-all-start = ((bf16[16,128,256]{2,1,0:T(8,128)(2,1)}), bf16[16,128,256]{2,1,0:T(8,128)(2,1)}, u32[]{:S(2)}, u32[]{:S(2)}) async-start(bf16[16,128,256]{2,1,0:T(8,128)(2,1)} %broadcast_in_dim.47), calls=%async_computation | async-start | bytes 2097152 | tf_op jit(solution)/shard_map/all_to_all | solution.py:127
  9.7 5.5 %collective-permute-start.1 = (bf16[4096,128]{1,0:T(8,128)(2,1)S(1)}, bf16[4096,128]{1,0:T(8,128)(2,1)}, u32[]{:S(2)}, u32[]{:S(2)}) collective-permute-start(bf16[4096,128]{1,0:T(8,128)(2,1)S(1)} %bitcast.82), channel_id=1, source_target_pairs={{0,1},{1,0},{2,3},{3,2},{4,5},{5,4},{6,7},{7,6},{8,9},{9,8},{10,11... | collective-permute-start | bytes 3145736 | tf_op jit(solution)/shard_map/ppermute | solution.py:19
  26.0 6.7 %collective-permute-start = (bf16[2,128,256]{2,1,0:T(8,128)(2,1)}, bf16[2,128,256]{2,1,0:T(8,128)(2,1)S(1)}, u32[]{:S(2)}, u32[]{:S(2)}) collective-permute-start(bf16[2,128,256]{2,1,0:T(8,128)(2,1)} %gather_fusion.1), channel_id=1, source_target_pairs={{0,1},{1,0},{2,3},{3,2},{4,5},{5,4},{6,7},{7,6},{8,9},{9,8},{10,11... | collective-permute-start | bytes 393224 | tf_op jit(solution)/shard_map/ppermute | solution.py:19
  34.8 11.1 %collective-permute-start.12 = (bf16[128,256]{1,0:T(8,128)(2,1)S(1)}, bf16[128,256]{1,0:T(8,128)(2,1)S(1)}, u32[]{:S(2)}, u32[]{:S(2)}) collective-permute-start(bf16[128,256]{1,0:T(8,128)(2,1)S(1)} %get-tuple-element.55), channel_id=1, source_target_pairs={{0,32},{1,481},{2,34},{3,483},{4,36},{5,485},{6,38},{7,487},{8,40}... | collective-permute-start | bytes 196616 | tf_op jit(solution)/shard_map/ppermute | solution.py:28
  49.8 3.4 %collective-permute-start.21 = (bf16[4096,128]{1,0:T(8,128)(2,1)}, bf16[4096,128]{1,0:T(8,128)(2,1)S(1)}, u32[]{:S(2)}, u32[]{:S(2)}) collective-permute-start(bf16[4096,128]{1,0:T(8,128)(2,1)} %bitcast.2.refs_20_), channel_id=1, source_target_pairs={{0,2},{1,3},{2,0},{3,1},{4,6},{5,7},{6,4},{7,5},{8,10},{9,11},{10,... | collective-permute-start | bytes 3145736 | tf_op jit(solution)/shard_map/ppermute | solution.py:23
  55.2 3.4 %collective-permute-start.5 = (bf16[2,128,256]{2,1,0:T(8,128)(2,1)S(1)}, bf16[2,128,256]{2,1,0:T(8,128)(2,1)S(1)}, u32[]{:S(2)}, u32[]{:S(2)}) collective-permute-start(bf16[2,128,256]{2,1,0:T(8,128)(2,1)S(1)} %pad_maximum_fusion.3.refs_0_), channel_id=1, source_target_pairs={{0,480},{1,33},{2,482},{3,35},{4,484},{5,37},{6,486},{7,39},{8,488... | collective-permute-start | bytes 393224 | tf_op jit(solution)/shard_map/ppermute | solution.py:28
  59.3 4.6 %collective-permute-start.14 = (bf16[2,128,256]{2,1,0:T(8,128)(2,1)S(1)}, bf16[2,128,256]{2,1,0:T(8,128)(2,1)S(1)}, u32[]{:S(2)}, u32[]{:S(2)}) collective-permute-start(bf16[2,128,256]{2,1,0:T(8,128)(2,1)S(1)} %collective-permute-done.13.refs_9_), channel_id=1, source_target_pairs={{0,32},{1,481},{2,34},{3,483},{4,36},{5,485},{6,38},{7,487},{8,40}... | collective-permute-start | bytes 393224 | tf_op jit(solution)/shard_map/ppermute | solution.py:28
  73.9 2.9 %collective-permute-start.16 = (bf16[2,128,256]{2,1,0:T(8,128)(2,1)S(1)}, bf16[2,128,256]{2,1,0:T(8,128)(2,1)S(1)}, u32[]{:S(2)}, u32[]{:S(2)}) collective-permute-start(bf16[2,128,256]{2,1,0:T(8,128)(2,1)S(1)} %collective-permute-done.15.refs_11_), channel_id=1, source_target_pairs={{0,32},{1,481},{2,34},{3,483},{4,36},{5,485},{6,38},{7,487},{8,40}... | collective-permute-start | bytes 393224 | tf_op jit(solution)/shard_map/ppermute | solution.py:28
  76.8 3.6 %collective-permute-start.8 = (bf16[2,128,256]{2,1,0:T(8,128)(2,1)S(1)}, bf16[2,128,256]{2,1,0:T(8,128)(2,1)S(1)}, u32[]{:S(2)}, u32[]{:S(2)}) collective-permute-start(bf16[2,128,256]{2,1,0:T(8,128)(2,1)S(1)} %collective-permute-done.7.refs_3_), channel_id=1, source_target_pairs={{0,32},{1,481},{2,34},{3,483},{4,36},{5,485},{6,38},{7,487},{8,40}... | collective-permute-start | bytes 393224 | tf_op jit(solution)/shard_map/ppermute | solution.py:28
  83.7 2.8 %collective-permute-start.9 = (bf16[2,128,256]{2,1,0:T(8,128)(2,1)S(1)}, bf16[2,128,256]{2,1,0:T(8,128)(2,1)S(1)}, u32[]{:S(2)}, u32[]{:S(2)}) collective-permute-start(bf16[2,128,256]{2,1,0:T(8,128)(2,1)S(1)} %collective-permute-done.8.refs_4_), channel_id=1, source_target_pairs={{0,480},{1,33},{2,482},{3,35},{4,484},{5,37},{6,486},{7,39},{8,488... | collective-permute-start | bytes 393224 | tf_op jit(solution)/shard_map/ppermute | solution.py:28
  86.9 5.0 %collective-permute-start.18 = (bf16[2,128,256]{2,1,0:T(8,128)(2,1)S(1)}, bf16[2,128,256]{2,1,0:T(8,128)(2,1)S(1)}, u32[]{:S(2)}, u32[]{:S(2)}) collective-permute-start(bf16[2,128,256]{2,1,0:T(8,128)(2,1)S(1)} %collective-permute-done.17.refs_13_), channel_id=1, source_target_pairs={{0,32},{1,481},{2,34},{3,483},{4,36},{5,485},{6,38},{7,487},{8,40}... | collective-permute-start | bytes 393224 | tf_op jit(solution)/shard_map/ppermute | solution.py:28
  94.3 5.3 %collective-permute-done.10.refs_6_ = bf16[2,128,256]{2,1,0:T(8,128)(2,1)S(1)} collective-permute-done((bf16[2,128,256]{2,1,0:T(8,128)(2,1)S(1)}, bf16[2,128,256]{2,1,0:T(8,128)(2,1)S(1)}, u32[]{:S(2)}, u32[]{:S(2)}) %collective-permute-start.10) | collective-permute-done | bytes 131104 | tf_op jit(solution)/shard_map/ppermute | solution.py:28
  99.6 8.8 %collective-permute-start.22 = (bf16[4096,128]{1,0:T(8,128)(2,1)S(1)}, bf16[4096,128]{1,0:T(8,128)(2,1)S(1)}, u32[]{:S(2)}, u32[]{:S(2)}) collective-permute-start(bf16[4096,128]{1,0:T(8,128)(2,1)S(1)} %collective-permute-done.20.refs_18_), channel_id=1, source_target_pairs={{0,1},{1,0},{2,3},{3,2},{4,5},{5,4},{6,7},{7,6},{8,9},{9,8},{10,11... | collective-permute-start | bytes 3145736 | tf_op jit(solution)/shard_map/ppermute | solution.py:19
  112.3 3.4 %collective-permute-start.11 = (bf16[2,128,256]{2,1,0:T(8,128)(2,1)S(1)}, bf16[2,128,256]{2,1,0:T(8,128)(2,1)S(1)}, u32[]{:S(2)}, u32[]{:S(2)}) collective-permute-start(bf16[2,128,256]{2,1,0:T(8,128)(2,1)S(1)} %collective-permute-done.10.refs_6_), channel_id=1, source_target_pairs={{0,480},{1,33},{2,482},{3,35},{4,484},{5,37},{6,486},{7,39},{8,488... | collective-permute-start | bytes 393224 | tf_op jit(solution)/shard_map/ppermute | solution.py:28
  118.3 4.3 %hidden.1 = (bf16[128,512]{1,0:T(8,128)(2,1)S(1)}, bf16[128,512]{1,0:T(8,128)(2,1)S(1)}) custom-call(s32[16]{0:T(128)S(1)} %compare_select_fusion.3.order, bf16[2,128,256]{2,1,0:T(8,128)(2,1)S(1)} %pad_maximum_fusion.3.refs_0_, bf16[2,128,256]{2,1,0:T(8,128)(2,1)S(1)} %collective-permute-done.5.refs_1_, ...), custom_call_target="tpu_custom_call" | custom-call | flops 2147483648 | bytes 10485760 | tf_op jit(solution)/shard_map/hidden/pallas_call | solution.py:84
  122.6 3.5 %collective-permute-start.32 = (bf16[128,512]{1,0:T(8,128)(2,1)S(1)}, bf16[128,512]{1,0:T(8,128)(2,1)S(1)}, u32[]{:S(2)}, u32[]{:S(2)}) collective-permute-start(bf16[128,512]{1,0:T(8,128)(2,1)S(1)} %get-tuple-element.38), channel_id=1, source_target_pairs={{0,32},{1,481},{2,34},{3,483},{4,36},{5,485},{6,38},{7,487},{8,40}... | collective-permute-start | bytes 393224 | tf_op jit(solution)/shard_map/ppermute | solution.py:28
  128.0 3.3 %collective-permute-start.24 = (bf16[128,512]{1,0:T(8,128)(2,1)S(1)}, bf16[128,512]{1,0:T(8,128)(2,1)S(1)}, u32[]{:S(2)}, u32[]{:S(2)}) collective-permute-start(bf16[128,512]{1,0:T(8,128)(2,1)S(1)} %get-tuple-element.37), channel_id=1, source_target_pairs={{0,32},{1,481},{2,34},{3,483},{4,36},{5,485},{6,38},{7,487},{8,40}... | collective-permute-start | bytes 393224 | tf_op jit(solution)/shard_map/ppermute | solution.py:28
  136.9 3.2 %collective-permute-done.33.refs_9_ = bf16[2,128,512]{2,1,0:T(8,128)(2,1)S(1)} collective-permute-done((bf16[2,128,512]{2,1,0:T(8,128)(2,1)S(1)}, bf16[2,128,512]{2,1,0:T(8,128)(2,1)S(1)}, u32[]{:S(2)}, u32[]{:S(2)}) %collective-permute-start.33) | collective-permute-done | bytes 262176 | tf_op jit(solution)/shard_map/ppermute | solution.py:28
  140.1 3.3 %collective-permute-start.34 = (bf16[2,128,512]{2,1,0:T(8,128)(2,1)S(1)}, bf16[2,128,512]{2,1,0:T(8,128)(2,1)S(1)}, u32[]{:S(2)}, u32[]{:S(2)}) collective-permute-start(bf16[2,128,512]{2,1,0:T(8,128)(2,1)S(1)} %collective-permute-done.33.refs_9_), channel_id=1, source_target_pairs={{0,32},{1,481},{2,34},{3,483},{4,36},{5,485},{6,38},{7,487},{8,40}... | collective-permute-start | bytes 786440 | tf_op jit(solution)/shard_map/ppermute | solution.py:28
  143.4 3.2 %collective-permute-start.26 = (bf16[2,128,512]{2,1,0:T(8,128)(2,1)S(1)}, bf16[2,128,512]{2,1,0:T(8,128)(2,1)S(1)}, u32[]{:S(2)}, u32[]{:S(2)}) collective-permute-start(bf16[2,128,512]{2,1,0:T(8,128)(2,1)S(1)} %collective-permute-done.25.refs_1_), channel_id=1, source_target_pairs={{0,32},{1,481},{2,34},{3,483},{4,36},{5,485},{6,38},{7,487},{8,40}... | collective-permute-start | bytes 786440 | tf_op jit(solution)/shard_map/ppermute | solution.py:28
  146.7 4.0 %collective-permute-done.34.refs_10_ = bf16[2,128,512]{2,1,0:T(8,128)(2,1)S(1)} collective-permute-done((bf16[2,128,512]{2,1,0:T(8,128)(2,1)S(1)}, bf16[2,128,512]{2,1,0:T(8,128)(2,1)S(1)}, u32[]{:S(2)}, u32[]{:S(2)}) %collective-permute-start.34) | collective-permute-done | bytes 262176 | tf_op jit(solution)/shard_map/ppermute | solution.py:28
  156.0 4.3 %collective-permute-done.35.refs_11_ = bf16[2,128,512]{2,1,0:T(8,128)(2,1)S(1)} collective-permute-done((bf16[2,128,512]{2,1,0:T(8,128)(2,1)S(1)}, bf16[2,128,512]{2,1,0:T(8,128)(2,1)S(1)}, u32[]{:S(2)}, u32[]{:S(2)}) %collective-permute-start.35) | collective-permute-done | bytes 262176 | tf_op jit(solution)/shard_map/ppermute | solution.py:28
  160.3 3.1 %collective-permute-done.27.refs_3_ = bf16[2,128,512]{2,1,0:T(8,128)(2,1)S(1)} collective-permute-done((bf16[2,128,512]{2,1,0:T(8,128)(2,1)S(1)}, bf16[2,128,512]{2,1,0:T(8,128)(2,1)S(1)}, u32[]{:S(2)}, u32[]{:S(2)}) %collective-permute-start.27) | collective-permute-done | bytes 262176 | tf_op jit(solution)/shard_map/ppermute | solution.py:28
  163.4 3.8 %collective-permute-start.36 = (bf16[2,128,512]{2,1,0:T(8,128)(2,1)S(1)}, bf16[2,128,512]{2,1,0:T(8,128)(2,1)S(1)}, u32[]{:S(2)}, u32[]{:S(2)}) collective-permute-start(bf16[2,128,512]{2,1,0:T(8,128)(2,1)S(1)} %collective-permute-done.35.refs_11_), channel_id=1, source_target_pairs={{0,32},{1,481},{2,34},{3,483},{4,36},{5,485},{6,38},{7,487},{8,40}... | collective-permute-start | bytes 786440 | tf_op jit(solution)/shard_map/ppermute | solution.py:28
  167.2 2.7 %collective-permute-start.28 = (bf16[2,128,512]{2,1,0:T(8,128)(2,1)S(1)}, bf16[2,128,512]{2,1,0:T(8,128)(2,1)S(1)}, u32[]{:S(2)}, u32[]{:S(2)}) collective-permute-start(bf16[2,128,512]{2,1,0:T(8,128)(2,1)S(1)} %collective-permute-done.27.refs_3_), channel_id=1, source_target_pairs={{0,32},{1,481},{2,34},{3,483},{4,36},{5,485},{6,38},{7,487},{8,40}... | collective-permute-start | bytes 786440 | tf_op jit(solution)/shard_map/ppermute | solution.py:28
  169.9 10.9 %collective-permute-start.41 = (bf16[2048,256]{1,0:T(8,128)(2,1)S(1)}, bf16[2048,256]{1,0:T(8,128)(2,1)S(1)}, u32[]{:S(2)}, u32[]{:S(2)}) collective-permute-start(bf16[2048,256]{1,0:T(8,128)(2,1)S(1)} %collective-permute-done.40.refs_18_), channel_id=1, source_target_pairs={{0,1},{1,0},{2,3},{3,2},{4,5},{5,4},{6,7},{7,6},{8,9},{9,8},{10,11... | collective-permute-start | bytes 3145736 | tf_op jit(solution)/shard_map/ppermute | solution.py:19
  180.8 3.2 %collective-permute-start.37 = (bf16[2,128,512]{2,1,0:T(8,128)(2,1)S(1)}, bf16[2,128,512]{2,1,0:T(8,128)(2,1)S(1)}, u32[]{:S(2)}, u32[]{:S(2)}) collective-permute-start(bf16[2,128,512]{2,1,0:T(8,128)(2,1)S(1)} %collective-permute-done.36.refs_12_), channel_id=1, source_target_pairs={{0,480},{1,33},{2,482},{3,35},{4,484},{5,37},{6,486},{7,39},{8,488... | collective-permute-start | bytes 786440 | tf_op jit(solution)/shard_map/ppermute | solution.py:28
  188.2 4.4 %collective-permute-start.38 = (bf16[2,128,512]{2,1,0:T(8,128)(2,1)S(1)}, bf16[2,128,512]{2,1,0:T(8,128)(2,1)S(1)}, u32[]{:S(2)}, u32[]{:S(2)}) collective-permute-start(bf16[2,128,512]{2,1,0:T(8,128)(2,1)S(1)} %collective-permute-done.37.refs_13_), channel_id=1, source_target_pairs={{0,32},{1,481},{2,34},{3,483},{4,36},{5,485},{6,38},{7,487},{8,40}... | collective-permute-start | bytes 786440 | tf_op jit(solution)/shard_map/ppermute | solution.py:28
  192.6 2.8 %collective-permute-start.30 = (bf16[2,128,512]{2,1,0:T(8,128)(2,1)S(1)}, bf16[2,128,512]{2,1,0:T(8,128)(2,1)S(1)}, u32[]{:S(2)}, u32[]{:S(2)}) collective-permute-start(bf16[2,128,512]{2,1,0:T(8,128)(2,1)S(1)} %collective-permute-done.29.refs_5_), channel_id=1, source_target_pairs={{0,32},{1,481},{2,34},{3,483},{4,36},{5,485},{6,38},{7,487},{8,40}... | collective-permute-start | bytes 786440 | tf_op jit(solution)/shard_map/ppermute | solution.py:28
  202.9 4.2 %collective-permute-done.39.refs_15_ = bf16[2,128,512]{2,1,0:T(8,128)(2,1)S(1)} collective-permute-done((bf16[2,128,512]{2,1,0:T(8,128)(2,1)S(1)}, bf16[2,128,512]{2,1,0:T(8,128)(2,1)S(1)}, u32[]{:S(2)}, u32[]{:S(2)}) %collective-permute-start.39) | collective-permute-done | bytes 262176 | tf_op jit(solution)/shard_map/ppermute | solution.py:28
  211.4 8.6 %collective-permute-start.42 = (bf16[2,128,256]{2,1,0:T(8,128)(2,1)S(1)}, bf16[2,128,256]{2,1,0:T(8,128)(2,1)S(1)}, u32[]{:S(2)}, u32[]{:S(2)}) collective-permute-start(bf16[2,128,256]{2,1,0:T(8,128)(2,1)S(1)} %bitcast.85), channel_id=1, source_target_pairs={{0,1},{1,0},{2,3},{3,2},{4,5},{5,4},{6,7},{7,6},{8,9},{9,8},{10,11... | collective-permute-start | bytes 393224 | tf_op jit(solution)/shard_map/ppermute | solution.py:19
  221.8 19.3 %all_to_all.10 = bf16[16,128,256]{2,1,0:T(8,128)(2,1)S(1)} all-to-all(bf16[16,128,256]{2,1,0:T(8,128)(2,1)S(1)} %broadcast_select_fusion), channel_id=1, replica_groups={{0,2,4,6,8,10,12,14,16,18,20,22,24,26,28,30},{1,3,5,7,9,11,13,15,17,19,..., dimensions={0} | all-to-all | bytes 2097152 | tf_op jit(solution)/shard_map/all_to_all | solution.py:158
  (98 shorter events, 74.9 us)
Async XLA Ops:
  1.9 21.6 %all-to-all-start = ((bf16[16,128,256]{2,1,0:T(8,128)(2,1)}), bf16[16,128,256]{2,1,0:T(8,128)(2,1)}, u32[]{:S(2)}, u32[]{:S(2)}) async-start(bf16[16,128,256]{2,1,0:T(8,128)(2,1)} %broadcast_in_dim.47), calls=%async_computation | async-start | bytes 2097152 | tf_op jit(solution)/shard_map/all_to_all | solution.py:127
  9.7 25.0 %collective-permute-start.1 = (bf16[4096,128]{1,0:T(8,128)(2,1)S(1)}, bf16[4096,128]{1,0:T(8,128)(2,1)}, u32[]{:S(2)}, u32[]{:S(2)}) collective-permute-start(bf16[4096,128]{1,0:T(8,128)(2,1)S(1)} %bitcast.82), channel_id=1, source_target_pairs={{0,1},{1,0},{2,3},{3,2},{4,5},{5,4},{6,7},{7,6},{8,9},{9,8},{10,11... | collective-permute-start | bytes 3145736 | tf_op jit(solution)/shard_map/ppermute | solution.py:19
  15.2 19.5 %collective-permute-start.2 = (bf16[4096,128]{1,0:T(8,128)(2,1)}, bf16[4096,128]{1,0:T(8,128)(2,1)}, u32[]{:S(2)}, u32[]{:S(2)}) collective-permute-start(bf16[4096,128]{1,0:T(8,128)(2,1)} %bitcast.2.refs_20_), channel_id=1, source_target_pairs={{0,1},{1,0},{2,3},{3,2},{4,5},{5,4},{6,7},{7,6},{8,9},{9,8},{10,11... | collective-permute-start | bytes 3145736 | tf_op jit(solution)/shard_map/ppermute | solution.py:19
  17.2 17.5 %collective-permute-start.3 = (bf16[2048,256]{1,0:T(8,128)(2,1)S(1)}, bf16[2048,256]{1,0:T(8,128)(2,1)S(1)}, u32[]{:S(2)}, u32[]{:S(2)}) collective-permute-start(bf16[2048,256]{1,0:T(8,128)(2,1)S(1)} %bitcast.79), channel_id=1, source_target_pairs={{0,1},{1,0},{2,3},{3,2},{4,5},{5,4},{6,7},{7,6},{8,9},{9,8},{10,11... | collective-permute-start | bytes 3145736 | tf_op jit(solution)/shard_map/ppermute | solution.py:19
  26.0 8.6 %collective-permute-start = (bf16[2,128,256]{2,1,0:T(8,128)(2,1)}, bf16[2,128,256]{2,1,0:T(8,128)(2,1)S(1)}, u32[]{:S(2)}, u32[]{:S(2)}) collective-permute-start(bf16[2,128,256]{2,1,0:T(8,128)(2,1)} %gather_fusion.1), channel_id=1, source_target_pairs={{0,1},{1,0},{2,3},{3,2},{4,5},{5,4},{6,7},{7,6},{8,9},{9,8},{10,11... | collective-permute-start | bytes 393224 | tf_op jit(solution)/shard_map/ppermute | solution.py:19
  34.8 18.4 %collective-permute-start.12 = (bf16[128,256]{1,0:T(8,128)(2,1)S(1)}, bf16[128,256]{1,0:T(8,128)(2,1)S(1)}, u32[]{:S(2)}, u32[]{:S(2)}) collective-permute-start(bf16[128,256]{1,0:T(8,128)(2,1)S(1)} %get-tuple-element.55), channel_id=1, source_target_pairs={{0,32},{1,481},{2,34},{3,483},{4,36},{5,485},{6,38},{7,487},{8,40}... | collective-permute-start | bytes 196616 | tf_op jit(solution)/shard_map/ppermute | solution.py:28
  47.9 51.7 %collective-permute-start.20 = (bf16[4096,128]{1,0:T(8,128)(2,1)S(1)}, bf16[4096,128]{1,0:T(8,128)(2,1)S(1)}, u32[]{:S(2)}, u32[]{:S(2)}) collective-permute-start(bf16[4096,128]{1,0:T(8,128)(2,1)S(1)} %bitcast.83), channel_id=1, source_target_pairs={{0,2},{1,3},{2,0},{3,1},{4,6},{5,7},{6,4},{7,5},{8,10},{9,11},{10,... | collective-permute-start | bytes 3145736 | tf_op jit(solution)/shard_map/ppermute | solution.py:23
  49.8 49.8 %collective-permute-start.21 = (bf16[4096,128]{1,0:T(8,128)(2,1)}, bf16[4096,128]{1,0:T(8,128)(2,1)S(1)}, u32[]{:S(2)}, u32[]{:S(2)}) collective-permute-start(bf16[4096,128]{1,0:T(8,128)(2,1)} %bitcast.2.refs_20_), channel_id=1, source_target_pairs={{0,2},{1,3},{2,0},{3,1},{4,6},{5,7},{6,4},{7,5},{8,10},{9,11},{10,... | collective-permute-start | bytes 3145736 | tf_op jit(solution)/shard_map/ppermute | solution.py:23
  55.2 8.6 %collective-permute-start.5 = (bf16[2,128,256]{2,1,0:T(8,128)(2,1)S(1)}, bf16[2,128,256]{2,1,0:T(8,128)(2,1)S(1)}, u32[]{:S(2)}, u32[]{:S(2)}) collective-permute-start(bf16[2,128,256]{2,1,0:T(8,128)(2,1)S(1)} %pad_maximum_fusion.3.refs_0_), channel_id=1, source_target_pairs={{0,480},{1,33},{2,482},{3,35},{4,484},{5,37},{6,486},{7,39},{8,488... | collective-permute-start | bytes 393224 | tf_op jit(solution)/shard_map/ppermute | solution.py:28
  59.3 7.6 %collective-permute-start.14 = (bf16[2,128,256]{2,1,0:T(8,128)(2,1)S(1)}, bf16[2,128,256]{2,1,0:T(8,128)(2,1)S(1)}, u32[]{:S(2)}, u32[]{:S(2)}) collective-permute-start(bf16[2,128,256]{2,1,0:T(8,128)(2,1)S(1)} %collective-permute-done.13.refs_9_), channel_id=1, source_target_pairs={{0,32},{1,481},{2,34},{3,483},{4,36},{5,485},{6,38},{7,487},{8,40}... | collective-permute-start | bytes 393224 | tf_op jit(solution)/shard_map/ppermute | solution.py:28
  83.7 8.2 %collective-permute-start.9 = (bf16[2,128,256]{2,1,0:T(8,128)(2,1)S(1)}, bf16[2,128,256]{2,1,0:T(8,128)(2,1)S(1)}, u32[]{:S(2)}, u32[]{:S(2)}) collective-permute-start(bf16[2,128,256]{2,1,0:T(8,128)(2,1)S(1)} %collective-permute-done.8.refs_4_), channel_id=1, source_target_pairs={{0,480},{1,33},{2,482},{3,35},{4,484},{5,37},{6,486},{7,39},{8,488... | collective-permute-start | bytes 393224 | tf_op jit(solution)/shard_map/ppermute | solution.py:28
  91.9 7.6 %collective-permute-start.10 = (bf16[2,128,256]{2,1,0:T(8,128)(2,1)S(1)}, bf16[2,128,256]{2,1,0:T(8,128)(2,1)S(1)}, u32[]{:S(2)}, u32[]{:S(2)}) collective-permute-start(bf16[2,128,256]{2,1,0:T(8,128)(2,1)S(1)} %collective-permute-done.9.refs_5_), channel_id=1, source_target_pairs={{0,32},{1,481},{2,34},{3,483},{4,36},{5,485},{6,38},{7,487},{8,40}... | collective-permute-start | bytes 393224 | tf_op jit(solution)/shard_map/ppermute | solution.py:28
  99.6 18.7 %collective-permute-start.22 = (bf16[4096,128]{1,0:T(8,128)(2,1)S(1)}, bf16[4096,128]{1,0:T(8,128)(2,1)S(1)}, u32[]{:S(2)}, u32[]{:S(2)}) collective-permute-start(bf16[4096,128]{1,0:T(8,128)(2,1)S(1)} %collective-permute-done.20.refs_18_), channel_id=1, source_target_pairs={{0,1},{1,0},{2,3},{3,2},{4,5},{5,4},{6,7},{7,6},{8,9},{9,8},{10,11... | collective-permute-start | bytes 3145736 | tf_op jit(solution)/shard_map/ppermute | solution.py:19
  108.4 9.9 %collective-permute-start.23 = (bf16[4096,128]{1,0:T(8,128)(2,1)S(1)}, bf16[4096,128]{1,0:T(8,128)(2,1)S(1)}, u32[]{:S(2)}, u32[]{:S(2)}) collective-permute-start(bf16[4096,128]{1,0:T(8,128)(2,1)S(1)} %collective-permute-done.21.refs_22_), channel_id=1, source_target_pairs={{0,1},{1,0},{2,3},{3,2},{4,5},{5,4},{6,7},{7,6},{8,9},{9,8},{10,11... | collective-permute-start | bytes 3145736 | tf_op jit(solution)/shard_map/ppermute | solution.py:19
  122.6 8.8 %collective-permute-start.32 = (bf16[128,512]{1,0:T(8,128)(2,1)S(1)}, bf16[128,512]{1,0:T(8,128)(2,1)S(1)}, u32[]{:S(2)}, u32[]{:S(2)}) collective-permute-start(bf16[128,512]{1,0:T(8,128)(2,1)S(1)} %get-tuple-element.38), channel_id=1, source_target_pairs={{0,32},{1,481},{2,34},{3,483},{4,36},{5,485},{6,38},{7,487},{8,40}... | collective-permute-start | bytes 393224 | tf_op jit(solution)/shard_map/ppermute | solution.py:28
  126.1 29.9 %collective-permute-start.40 = (bf16[2048,256]{1,0:T(8,128)(2,1)S(1)}, bf16[2048,256]{1,0:T(8,128)(2,1)S(1)}, u32[]{:S(2)}, u32[]{:S(2)}) collective-permute-start(bf16[2048,256]{1,0:T(8,128)(2,1)S(1)} %bitcast.80), channel_id=1, source_target_pairs={{0,2},{1,3},{2,0},{3,1},{4,6},{5,7},{6,4},{7,5},{8,10},{9,11},{10,... | collective-permute-start | bytes 3145736 | tf_op jit(solution)/shard_map/ppermute | solution.py:23
  131.4 8.7 %collective-permute-start.33 = (bf16[2,128,512]{2,1,0:T(8,128)(2,1)S(1)}, bf16[2,128,512]{2,1,0:T(8,128)(2,1)S(1)}, u32[]{:S(2)}, u32[]{:S(2)}) collective-permute-start(bf16[2,128,512]{2,1,0:T(8,128)(2,1)S(1)} %pad_maximum_fusion.1.refs_8_), channel_id=1, source_target_pairs={{0,480},{1,33},{2,482},{3,35},{4,484},{5,37},{6,486},{7,39},{8,488... | collective-permute-start | bytes 786440 | tf_op jit(solution)/shard_map/ppermute | solution.py:28
  135.0 8.4 %collective-permute-start.25 = (bf16[2,128,512]{2,1,0:T(8,128)(2,1)S(1)}, bf16[2,128,512]{2,1,0:T(8,128)(2,1)S(1)}, u32[]{:S(2)}, u32[]{:S(2)}) collective-permute-start(bf16[2,128,512]{2,1,0:T(8,128)(2,1)S(1)} %pad_maximum_fusion.refs_0_), channel_id=1, source_target_pairs={{0,480},{1,33},{2,482},{3,35},{4,484},{5,37},{6,486},{7,39},{8,488... | collective-permute-start | bytes 786440 | tf_op jit(solution)/shard_map/ppermute | solution.py:28
  140.1 10.5 %collective-permute-start.34 = (bf16[2,128,512]{2,1,0:T(8,128)(2,1)S(1)}, bf16[2,128,512]{2,1,0:T(8,128)(2,1)S(1)}, u32[]{:S(2)}, u32[]{:S(2)}) collective-permute-start(bf16[2,128,512]{2,1,0:T(8,128)(2,1)S(1)} %collective-permute-done.33.refs_9_), channel_id=1, source_target_pairs={{0,32},{1,481},{2,34},{3,483},{4,36},{5,485},{6,38},{7,487},{8,40}... | collective-permute-start | bytes 786440 | tf_op jit(solution)/shard_map/ppermute | solution.py:28
  143.4 10.1 %collective-permute-start.26 = (bf16[2,128,512]{2,1,0:T(8,128)(2,1)S(1)}, bf16[2,128,512]{2,1,0:T(8,128)(2,1)S(1)}, u32[]{:S(2)}, u32[]{:S(2)}) collective-permute-start(bf16[2,128,512]{2,1,0:T(8,128)(2,1)S(1)} %collective-permute-done.25.refs_1_), channel_id=1, source_target_pairs={{0,32},{1,481},{2,34},{3,483},{4,36},{5,485},{6,38},{7,487},{8,40}... | collective-permute-start | bytes 786440 | tf_op jit(solution)/shard_map/ppermute | solution.py:28
  150.7 9.6 %collective-permute-start.35 = (bf16[2,128,512]{2,1,0:T(8,128)(2,1)S(1)}, bf16[2,128,512]{2,1,0:T(8,128)(2,1)S(1)}, u32[]{:S(2)}, u32[]{:S(2)}) collective-permute-start(bf16[2,128,512]{2,1,0:T(8,128)(2,1)S(1)} %collective-permute-done.34.refs_10_), channel_id=1, source_target_pairs={{0,480},{1,33},{2,482},{3,35},{4,484},{5,37},{6,486},{7,39},{8,488... | collective-permute-start | bytes 786440 | tf_op jit(solution)/shard_map/ppermute | solution.py:28
  153.5 9.9 %collective-permute-start.27 = (bf16[2,128,512]{2,1,0:T(8,128)(2,1)S(1)}, bf16[2,128,512]{2,1,0:T(8,128)(2,1)S(1)}, u32[]{:S(2)}, u32[]{:S(2)}) collective-permute-start(bf16[2,128,512]{2,1,0:T(8,128)(2,1)S(1)} %collective-permute-done.26.refs_2_), channel_id=1, source_target_pairs={{0,480},{1,33},{2,482},{3,35},{4,484},{5,37},{6,486},{7,39},{8,488... | collective-permute-start | bytes 786440 | tf_op jit(solution)/shard_map/ppermute | solution.py:28
  163.4 17.4 %collective-permute-start.36 = (bf16[2,128,512]{2,1,0:T(8,128)(2,1)S(1)}, bf16[2,128,512]{2,1,0:T(8,128)(2,1)S(1)}, u32[]{:S(2)}, u32[]{:S(2)}) collective-permute-start(bf16[2,128,512]{2,1,0:T(8,128)(2,1)S(1)} %collective-permute-done.35.refs_11_), channel_id=1, source_target_pairs={{0,32},{1,481},{2,34},{3,483},{4,36},{5,485},{6,38},{7,487},{8,40}... | collective-permute-start | bytes 786440 | tf_op jit(solution)/shard_map/ppermute | solution.py:28
  167.2 16.8 %collective-permute-start.28 = (bf16[2,128,512]{2,1,0:T(8,128)(2,1)S(1)}, bf16[2,128,512]{2,1,0:T(8,128)(2,1)S(1)}, u32[]{:S(2)}, u32[]{:S(2)}) collective-permute-start(bf16[2,128,512]{2,1,0:T(8,128)(2,1)S(1)} %collective-permute-done.27.refs_3_), channel_id=1, source_target_pairs={{0,32},{1,481},{2,34},{3,483},{4,36},{5,485},{6,38},{7,487},{8,40}... | collective-permute-start | bytes 786440 | tf_op jit(solution)/shard_map/ppermute | solution.py:28
  169.9 33.0 %collective-permute-start.41 = (bf16[2048,256]{1,0:T(8,128)(2,1)S(1)}, bf16[2048,256]{1,0:T(8,128)(2,1)S(1)}, u32[]{:S(2)}, u32[]{:S(2)}) collective-permute-start(bf16[2048,256]{1,0:T(8,128)(2,1)S(1)} %collective-permute-done.40.refs_18_), channel_id=1, source_target_pairs={{0,1},{1,0},{2,3},{3,2},{4,5},{5,4},{6,7},{7,6},{8,9},{9,8},{10,11... | collective-permute-start | bytes 3145736 | tf_op jit(solution)/shard_map/ppermute | solution.py:19
  180.8 7.4 %collective-permute-start.37 = (bf16[2,128,512]{2,1,0:T(8,128)(2,1)S(1)}, bf16[2,128,512]{2,1,0:T(8,128)(2,1)S(1)}, u32[]{:S(2)}, u32[]{:S(2)}) collective-permute-start(bf16[2,128,512]{2,1,0:T(8,128)(2,1)S(1)} %collective-permute-done.36.refs_12_), channel_id=1, source_target_pairs={{0,480},{1,33},{2,482},{3,35},{4,484},{5,37},{6,486},{7,39},{8,488... | collective-permute-start | bytes 786440 | tf_op jit(solution)/shard_map/ppermute | solution.py:28
  184.0 8.6 %collective-permute-start.29 = (bf16[2,128,512]{2,1,0:T(8,128)(2,1)S(1)}, bf16[2,128,512]{2,1,0:T(8,128)(2,1)S(1)}, u32[]{:S(2)}, u32[]{:S(2)}) collective-permute-start(bf16[2,128,512]{2,1,0:T(8,128)(2,1)S(1)} %collective-permute-done.28.refs_4_), channel_id=1, source_target_pairs={{0,480},{1,33},{2,482},{3,35},{4,484},{5,37},{6,486},{7,39},{8,488... | collective-permute-start | bytes 786440 | tf_op jit(solution)/shard_map/ppermute | solution.py:28
  188.2 9.4 %collective-permute-start.38 = (bf16[2,128,512]{2,1,0:T(8,128)(2,1)S(1)}, bf16[2,128,512]{2,1,0:T(8,128)(2,1)S(1)}, u32[]{:S(2)}, u32[]{:S(2)}) collective-permute-start(bf16[2,128,512]{2,1,0:T(8,128)(2,1)S(1)} %collective-permute-done.37.refs_13_), channel_id=1, source_target_pairs={{0,32},{1,481},{2,34},{3,483},{4,36},{5,485},{6,38},{7,487},{8,40}... | collective-permute-start | bytes 786440 | tf_op jit(solution)/shard_map/ppermute | solution.py:28
  192.6 8.3 %collective-permute-start.30 = (bf16[2,128,512]{2,1,0:T(8,128)(2,1)S(1)}, bf16[2,128,512]{2,1,0:T(8,128)(2,1)S(1)}, u32[]{:S(2)}, u32[]{:S(2)}) collective-permute-start(bf16[2,128,512]{2,1,0:T(8,128)(2,1)S(1)} %collective-permute-done.29.refs_5_), channel_id=1, source_target_pairs={{0,32},{1,481},{2,34},{3,483},{4,36},{5,485},{6,38},{7,487},{8,40}... | collective-permute-start | bytes 786440 | tf_op jit(solution)/shard_map/ppermute | solution.py:28
  197.6 9.5 %collective-permute-start.39 = (bf16[2,128,512]{2,1,0:T(8,128)(2,1)S(1)}, bf16[2,128,512]{2,1,0:T(8,128)(2,1)S(1)}, u32[]{:S(2)}, u32[]{:S(2)}) collective-permute-start(bf16[2,128,512]{2,1,0:T(8,128)(2,1)S(1)} %collective-permute-done.38.refs_14_), channel_id=1, source_target_pairs={{0,480},{1,33},{2,482},{3,35},{4,484},{5,37},{6,486},{7,39},{8,488... | collective-permute-start | bytes 786440 | tf_op jit(solution)/shard_map/ppermute | solution.py:28
  200.9 8.6 %collective-permute-start.31 = (bf16[2,128,512]{2,1,0:T(8,128)(2,1)S(1)}, bf16[2,128,512]{2,1,0:T(8,128)(2,1)S(1)}, u32[]{:S(2)}, u32[]{:S(2)}) collective-permute-start(bf16[2,128,512]{2,1,0:T(8,128)(2,1)S(1)} %collective-permute-done.30.refs_6_), channel_id=1, source_target_pairs={{0,480},{1,33},{2,482},{3,35},{4,484},{5,37},{6,486},{7,39},{8,488... | collective-permute-start | bytes 786440 | tf_op jit(solution)/shard_map/ppermute | solution.py:28
  211.4 9.6 %collective-permute-start.42 = (bf16[2,128,256]{2,1,0:T(8,128)(2,1)S(1)}, bf16[2,128,256]{2,1,0:T(8,128)(2,1)S(1)}, u32[]{:S(2)}, u32[]{:S(2)}) collective-permute-start(bf16[2,128,256]{2,1,0:T(8,128)(2,1)S(1)} %bitcast.85), channel_id=1, source_target_pairs={{0,1},{1,0},{2,3},{3,2},{4,5},{5,4},{6,7},{7,6},{8,9},{9,8},{10,11... | collective-permute-start | bytes 393224 | tf_op jit(solution)/shard_map/ppermute | solution.py:19
  (15 other events, 124.1 us)

commit v7 on v6

--- a/solution.py
+++ b/solution.py
@@ -11,7 +11,6 @@
 DEPTH = 16
 OWNERS = 32
 BLOCKS = 2
-RELAY = 6
 SAME_CORE = [[2 * chip + core for chip in range(CHIPS)] for core in range(2)]
 
 
@@ -47,16 +46,14 @@
     return odd == 1, lax.rem(jnp.stack(chunks) + 2 * DEPTH, DEPTH).astype(jnp.int32)
 
 
-def hidden_kernel(order, *refs):
-    items, weights, outs = refs[:DEPTH], refs[DEPTH : -BLOCKS], refs[-BLOCKS:]
-    depth = items[0].shape[2]
+def hidden_kernel(gathered, *refs):
+    weights, outs = refs[:-BLOCKS], refs[-BLOCKS:]
+    depth = gathered.shape[2]
     total = None
     for number in range(DEPTH):
-        pair, half = number // 2, number % 2
-        left = jnp.concatenate([items[pair][half], items[DEPTH // 2 + pair][half]], axis=0)
-        rows = pl.ds(pl.multiple_of(order[number] * depth, depth), depth)
+        rows = pl.ds(number * depth, depth)
         right = jnp.concatenate([weight[rows, :] for weight in weights], axis=1)
-        term = jnp.dot(left, right, preferred_element_type=jnp.float32)
+        term = jnp.dot(gathered[number], right, preferred_element_type=jnp.float32)
         total = term if total is None else total + term
     units = total.shape[1] // 2
     gate, up = total[:, :units], total[:, units:]
@@ -79,19 +76,19 @@
     out[...] = (total * scale[:, :1]).astype(out.dtype)
 
 
-def kernel_call(kernel, name, order, inner, outs, flops):
+def kernel_call(kernel, name, orders, inner, outs, flops):
     in_vmem = pl.BlockSpec(memory_space=pltpu.VMEM)
     return pl.pallas_call(
         kernel,
         out_shape=[jax.ShapeDtypeStruct(shape, jnp.bfloat16) for shape in outs],
-        in_specs=[pl.BlockSpec(memory_space=pltpu.SMEM)] + [in_vmem] * len(inner),
+        in_specs=[pl.BlockSpec(memory_space=pltpu.SMEM)] * len(orders) + [in_vmem] * len(inner),
         out_specs=[in_vmem] * len(outs),
         compiler_params=pltpu.CompilerParams(vmem_limit_bytes=20 << 20),
         cost_estimate=pl.CostEstimate(
             flops=flops, bytes_accessed=2 * sum(array.size for array in inner), transcendentals=0
         ),
         name=name,
-    )(order, *inner)
+    )(*orders, *inner)
 
 
 def gather_near(chunk, odd):
@@ -134,21 +131,20 @@
         (selected, near, odd, order, scale, wanted, source)
     )
 
-    chains = [gather_near(selected[block], odd) for block in range(blocks)]
-    far_in, _ = lax.optimization_barrier((far[:2], [chain[RELAY] for chain in chains]))
-    relayed = [swap_core(w) for w in far_in]
+    gathered = lax.all_gather(selected.reshape(rows, features), "tok")
+    relayed = [swap_core(w) for w in far]
+    gathered, relayed = lax.optimization_barrier((gathered, relayed))
     flops = 2 * rows * DEPTH * features * 2 * SPAN * units
     parts = kernel_call(
-        hidden_kernel, "hidden", order,
-        [item for chain in chains for item in chain] + [w[kind] for kind in range(2) for w in (own, near, far_in, relayed)],
+        hidden_kernel, "hidden", [],
+        [gathered] + [w[kind] for kind in range(2) for w in (own, near, far, relayed)],
         [(BLOCK, SPAN * units)] * blocks, flops,
     )
 
     chains = [gather_near(part, odd) for part in parts]
-    far_down, _ = lax.optimization_barrier((far[2], [chain[RELAY // 2] for chain in chains]))
     (done,) = kernel_call(
-        down_kernel, "down", order,
-        [scale] + [item for chain in chains for item in chain] + [own[2], near[2], far_down, swap_core(far_down)],
+        down_kernel, "down", [order],
+        [scale] + [item for chain in chains for item in chain] + [w[2] for w in (own, near, far, relayed)],
         [(rows, features)], flops // 2,
     )
     done = done.reshape(blocks, BLOCK, features)

time: 243 us -> 259 us (1.066)
  starting transfers between devices: 158 us -> 100 us
  waiting for transfers between devices: 46.1 us -> 93.2 us
  between operations: 0.75 us -> 13.9 us
  local copies, waits for them, and re-layouts: 7.76 us -> 20.4 us
    ppermute x3, waiting for transfers between devices: 0.01 us -> 55.8 us  [swap_across(): return lax.ppermute(value, 'exp', [(p, p ^ 2) for p in range(OWNERS)])]
    ppermute x32 -> x16, starting transfers between devices: 96.7 us -> 47.5 us  [swap_tok(): return lax.ppermute(value, ('tok', 'exp'), pairs)]
    unnamed x6 -> x34, local copies, waits for them, and re-layouts: 0.01 us -> 12.5 us
    ppermute x8, starting transfers between devices: 46.7 us -> 37.6 us  [swap_core(): return lax.ppermute(value, 'exp', [(p, p ^ 1) for p in range(OWNERS)])]
    ppermute x32 -> x16, waiting for transfers between devices: 44.4 us -> 35.7 us  [swap_tok(): return lax.ppermute(value, ('tok', 'exp'), pairs)]
  transfers between devices with their start and end apart: 44 -> 29, of which waited for: 24 -> 20; matrix products, arithmetic and copies ran while one was open for 3% -> 3% of each run, Pallas kernels for 0% -> 0%
where the time goes in v7:
time: 259 us; the launch traced here: 258 us
  starting transfers between devices  100 us (39%)
  waiting for transfers between devices  93.2 us (36%)
  local copies, waits for them, and re-layouts  20.4 us (8%)
  blocking collectives  19.3 us (7%)
  between operations  13.9 us (5%)
  Pallas kernels  6.37 us (2%)
  other arithmetic  4.11 us (2%)
    ppermute x3, waiting for transfers between devices, swap_across(): return lax.ppermute(value, 'exp', [(p, p ^ 2) for p in range(OWNERS)])  55.8 us
    ppermute x16, starting transfers between devices, swap_tok(): return lax.ppermute(value, ('tok', 'exp'), pairs)  47.5 us
    ppermute x8, starting transfers between devices, swap_core(): return lax.ppermute(value, 'exp', [(p, p ^ 1) for p in range(OWNERS)])  37.6 us
    ppermute x16, waiting for transfers between devices, swap_tok(): return lax.ppermute(value, ('tok', 'exp'), pairs)  35.7 us
    all_to_all x1, blocking collectives, shards(): lax.all_to_all(outgoing, 'exp', 0, 0, axis_index_groups=SAME_CORE, tiled=...  19.3 us
    unnamed x34, local copies, waits for them, and re-layouts  12.5 us
    all_to_all x1, starting transfers between devices, shards(): lax.all_to_all(spread, 'exp', 0, 0, axis_index_groups=SAME_CORE, tiled=True)  7.64 us
    ppermute x3, starting transfers between devices, swap_across(): return lax.ppermute(value, 'exp', [(p, p ^ 2) for p in range(OWNERS)])  7.58 us
  transfers between devices with their start and end apart: 29, of which 20 were waited for; matrix products, arithmetic and copies ran while one was open for 3% of the time, Pallas kernels for 0%

profile of v7, /device:TPU:1, one launch (start us, length us, event | category | flops | bytes accessed | tf_op | source)
XLA Modules:
  0.0 257.7 jit_solution(6459881868407477158)
XLA Ops:
  6.5 2.1 broadcast_in_dim.47
  8.6 7.6 %all-to-all-start = ((bf16[16,128,256]{2,1,0:T(8,128)(2,1)}), bf16[16,128,256]{2,1,0:T(8,128)(2,1)}, u32[]{:S(2)}, u32[]{:S(2)}) async-start(bf16[16,128,256]{2,1,0:T(8,128)(2,1)} %broadcast_in_dim.47), calls=%async_computation | async-start | bytes 2097152 | tf_op jit(solution)/shard_map/all_to_all | solution.py:124
  16.3 5.5 %collective-permute-start.1 = (bf16[4096,128]{1,0:T(8,128)(2,1)S(1)}, bf16[4096,128]{1,0:T(8,128)(2,1)}, u32[]{:S(2)}, u32[]{:S(2)}) collective-permute-start(bf16[4096,128]{1,0:T(8,128)(2,1)S(1)} %bitcast.60), channel_id=1, source_target_pairs={{0,1},{1,0},{2,3},{3,2},{4,5},{5,4},{6,7},{7,6},{8,9},{9,8},{10,11... | collective-permute-start | bytes 3145736 | tf_op jit(solution)/shard_map/ppermute | solution.py:18
  23.8 2.4 collective-permute-start.3
  30.1 2.4 gather_fusion.1
  32.5 6.7 %collective-permute-start = (bf16[2,128,256]{2,1,0:T(8,128)(2,1)}, bf16[2,128,256]{2,1,0:T(8,128)(2,1)S(1)}, u32[]{:S(2)}, u32[]{:S(2)}) collective-permute-start(bf16[2,128,256]{2,1,0:T(8,128)(2,1)} %gather_fusion.1), channel_id=1, source_target_pairs={{0,1},{1,0},{2,3},{3,2},{4,5},{5,4},{6,7},{7,6},{8,9},{9,8},{10,11... | collective-permute-start | bytes 393224 | tf_op jit(solution)/shard_map/ppermute | solution.py:18
  42.0 2.3 collective-permute-start.4
  44.3 3.0 %collective-permute-start.6 = (bf16[4096,128]{1,0:T(8,128)(2,1)S(1)}, bf16[4096,128]{1,0:T(8,128)(2,1)S(1)}, u32[]{:S(2)}, u32[]{:S(2)}) collective-permute-start(bf16[4096,128]{1,0:T(8,128)(2,1)S(1)} %bitcast.64), channel_id=1, source_target_pairs={{0,2},{1,3},{2,0},{3,1},{4,6},{5,7},{6,4},{7,5},{8,10},{9,11},{10,... | collective-permute-start | bytes 3145736 | tf_op jit(solution)/shard_map/ppermute | solution.py:22
  47.3 2.3 collective-permute-start.8
  49.6 19.1 %collective-permute-done.4.refs_2_ = bf16[4096,128]{1,0:T(8,128)(2,1)S(1)} collective-permute-done((bf16[4096,128]{1,0:T(8,128)(2,1)S(1)}, bf16[4096,128]{1,0:T(8,128)(2,1)S(1)}, u32[]{:S(2)}, u32[]{:S(2)}) %collective-permute-start.4) | collective-permute-done | bytes 1048608 | tf_op jit(solution)/shard_map/ppermute | solution.py:22
  68.7 3.1 %collective-permute-start.5 = (bf16[4096,128]{1,0:T(8,128)(2,1)S(1)}, bf16[4096,128]{1,0:T(8,128)(2,1)S(1)}, u32[]{:S(2)}, u32[]{:S(2)}) collective-permute-start(bf16[4096,128]{1,0:T(8,128)(2,1)S(1)} %collective-permute-done.4.refs_2_), channel_id=1, source_target_pairs={{0,1},{1,0},{2,3},{3,2},{4,5},{5,4},{6,7},{7,6},{8,9},{9,8},{10,11... | collective-permute-start | bytes 3145736 | tf_op jit(solution)/shard_map/ppermute | solution.py:18
  72.8 18.4 %collective-permute-done.6.refs_6_ = bf16[4096,128]{1,0:T(8,128)(2,1)S(1)} collective-permute-done((bf16[4096,128]{1,0:T(8,128)(2,1)S(1)}, bf16[4096,128]{1,0:T(8,128)(2,1)S(1)}, u32[]{:S(2)}, u32[]{:S(2)}) %collective-permute-start.6) | collective-permute-done | bytes 1048608 | tf_op jit(solution)/shard_map/ppermute | solution.py:22
  91.2 3.0 %collective-permute-start.7 = (bf16[4096,128]{1,0:T(8,128)(2,1)S(1)}, bf16[4096,128]{1,0:T(8,128)(2,1)S(1)}, u32[]{:S(2)}, u32[]{:S(2)}) collective-permute-start(bf16[4096,128]{1,0:T(8,128)(2,1)S(1)} %collective-permute-done.6.refs_6_), channel_id=1, source_target_pairs={{0,1},{1,0},{2,3},{3,2},{4,5},{5,4},{6,7},{7,6},{8,9},{9,8},{10,11... | collective-permute-start | bytes 3145736 | tf_op jit(solution)/shard_map/ppermute | solution.py:18
  95.3 18.3 %collective-permute-done.8.refs_18_ = bf16[2048,256]{1,0:T(8,128)(2,1)S(1)} collective-permute-done((bf16[2048,256]{1,0:T(8,128)(2,1)S(1)}, bf16[2048,256]{1,0:T(8,128)(2,1)S(1)}, u32[]{:S(2)}, u32[]{:S(2)}) %collective-permute-start.8) | collective-permute-done | bytes 1048608 | tf_op jit(solution)/shard_map/ppermute | solution.py:22
  113.6 2.7 %collective-permute-start.9 = (bf16[2048,256]{1,0:T(8,128)(2,1)S(1)}, bf16[2048,256]{1,0:T(8,128)(2,1)S(1)}, u32[]{:S(2)}, u32[]{:S(2)}) collective-permute-start(bf16[2048,256]{1,0:T(8,128)(2,1)S(1)} %collective-permute-done.8.refs_18_), channel_id=1, source_target_pairs={{0,1},{1,0},{2,3},{3,2},{4,5},{5,4},{6,7},{7,6},{8,9},{9,8},{10,11... | collective-permute-start | bytes 3145736 | tf_op jit(solution)/shard_map/ppermute | solution.py:18
  126.7 3.9 %hidden.1 = (bf16[128,512]{1,0:T(8,128)(2,1)S(1)}, bf16[128,512]{1,0:T(8,128)(2,1)S(1)}) custom-call(bf16[16,256,256]{2,1,0:T(8,128)(2,1)S(1)} %copy-done.1, bf16[4096,128]{1,0:T(8,128)(2,1)S(1)} %bitcast.62, bf16[4096,128]{1,0:T(8,128)(2,1)} %collective-permute-done.1.refs_1_, bf16[4096,128]{1,0:T(8,128)(2,1)S(1)} %copy-done.10, ...), custom_call_target="tpu_custom_call" | custom-call | flops 2147483648 | bytes 10485760 | tf_op jit(solution)/shard_map/hidden/pallas_call | solution.py:81
  130.6 11.3 %collective-permute-start.18 = (bf16[128,512]{1,0:T(8,128)(2,1)S(1)}, bf16[128,512]{1,0:T(8,128)(2,1)S(1)}, u32[]{:S(2)}, u32[]{:S(2)}) collective-permute-start(bf16[128,512]{1,0:T(8,128)(2,1)S(1)} %get-tuple-element.41), channel_id=1, source_target_pairs={{0,32},{1,481},{2,34},{3,483},{4,36},{5,485},{6,38},{7,487},{8,40}... | collective-permute-start | bytes 393224 | tf_op jit(solution)/shard_map/ppermute | solution.py:27
  146.3 2.6 %collective-permute-done.10 = bf16[128,512]{1,0:T(8,128)(2,1)S(1)} collective-permute-done((bf16[128,512]{1,0:T(8,128)(2,1)S(1)}, bf16[128,512]{1,0:T(8,128)(2,1)S(1)}, u32[]{:S(2)}, u32[]{:S(2)}) %collective-permute-start.10) | collective-permute-done | bytes 131104 | tf_op jit(solution)/shard_map/ppermute | solution.py:27
  151.7 4.6 %collective-permute-start.20 = (bf16[2,128,512]{2,1,0:T(8,128)(2,1)S(1)}, bf16[2,128,512]{2,1,0:T(8,128)(2,1)S(1)}, u32[]{:S(2)}, u32[]{:S(2)}) collective-permute-start(bf16[2,128,512]{2,1,0:T(8,128)(2,1)S(1)} %collective-permute-done.19.refs_9_), channel_id=1, source_target_pairs={{0,32},{1,481},{2,34},{3,483},{4,36},{5,485},{6,38},{7,487},{8,40}... | collective-permute-start | bytes 786440 | tf_op jit(solution)/shard_map/ppermute | solution.py:27
  156.3 2.8 %collective-permute-start.12 = (bf16[2,128,512]{2,1,0:T(8,128)(2,1)S(1)}, bf16[2,128,512]{2,1,0:T(8,128)(2,1)S(1)}, u32[]{:S(2)}, u32[]{:S(2)}) collective-permute-start(bf16[2,128,512]{2,1,0:T(8,128)(2,1)S(1)} %collective-permute-done.11.refs_1_), channel_id=1, source_target_pairs={{0,32},{1,481},{2,34},{3,483},{4,36},{5,485},{6,38},{7,487},{8,40}... | collective-permute-start | bytes 786440 | tf_op jit(solution)/shard_map/ppermute | solution.py:27
  166.6 3.5 %collective-permute-done.21.refs_11_ = bf16[2,128,512]{2,1,0:T(8,128)(2,1)S(1)} collective-permute-done((bf16[2,128,512]{2,1,0:T(8,128)(2,1)S(1)}, bf16[2,128,512]{2,1,0:T(8,128)(2,1)S(1)}, u32[]{:S(2)}, u32[]{:S(2)}) %collective-permute-start.21) | collective-permute-done | bytes 262176 | tf_op jit(solution)/shard_map/ppermute | solution.py:27
  172.6 4.0 %collective-permute-start.14 = (bf16[2,128,512]{2,1,0:T(8,128)(2,1)S(1)}, bf16[2,128,512]{2,1,0:T(8,128)(2,1)S(1)}, u32[]{:S(2)}, u32[]{:S(2)}) collective-permute-start(bf16[2,128,512]{2,1,0:T(8,128)(2,1)S(1)} %collective-permute-done.13.refs_3_), channel_id=1, source_target_pairs={{0,32},{1,481},{2,34},{3,483},{4,36},{5,485},{6,38},{7,487},{8,40}... | collective-permute-start | bytes 786440 | tf_op jit(solution)/shard_map/ppermute | solution.py:27
  176.6 4.7 %collective-permute-done.22.refs_12_ = bf16[2,128,512]{2,1,0:T(8,128)(2,1)S(1)} collective-permute-done((bf16[2,128,512]{2,1,0:T(8,128)(2,1)S(1)}, bf16[2,128,512]{2,1,0:T(8,128)(2,1)S(1)}, u32[]{:S(2)}, u32[]{:S(2)}) %collective-permute-start.22) | collective-permute-done | bytes 262176 | tf_op jit(solution)/shard_map/ppermute | solution.py:27
  183.9 2.7 %collective-permute-start.15 = (bf16[2,128,512]{2,1,0:T(8,128)(2,1)S(1)}, bf16[2,128,512]{2,1,0:T(8,128)(2,1)S(1)}, u32[]{:S(2)}, u32[]{:S(2)}) collective-permute-start(bf16[2,128,512]{2,1,0:T(8,128)(2,1)S(1)} %collective-permute-done.14.refs_4_), channel_id=1, source_target_pairs={{0,480},{1,33},{2,482},{3,35},{4,484},{5,37},{6,486},{7,39},{8,488... | collective-permute-start | bytes 786440 | tf_op jit(solution)/shard_map/ppermute | solution.py:27
  186.5 4.1 %collective-permute-done.23.refs_13_ = bf16[2,128,512]{2,1,0:T(8,128)(2,1)S(1)} collective-permute-done((bf16[2,128,512]{2,1,0:T(8,128)(2,1)S(1)}, bf16[2,128,512]{2,1,0:T(8,128)(2,1)S(1)}, u32[]{:S(2)}, u32[]{:S(2)}) %collective-permute-start.23) | collective-permute-done | bytes 262176 | tf_op jit(solution)/shard_map/ppermute | solution.py:27
  194.0 3.2 %collective-permute-start.16 = (bf16[2,128,512]{2,1,0:T(8,128)(2,1)S(1)}, bf16[2,128,512]{2,1,0:T(8,128)(2,1)S(1)}, u32[]{:S(2)}, u32[]{:S(2)}) collective-permute-start(bf16[2,128,512]{2,1,0:T(8,128)(2,1)S(1)} %collective-permute-done.15.refs_5_), channel_id=1, source_target_pairs={{0,32},{1,481},{2,34},{3,483},{4,36},{5,485},{6,38},{7,487},{8,40}... | collective-permute-start | bytes 786440 | tf_op jit(solution)/shard_map/ppermute | solution.py:27
  197.1 2.3 collective-permute-done.24.refs_14_
  201.4 3.2 %collective-permute-done.16.refs_6_ = bf16[2,128,512]{2,1,0:T(8,128)(2,1)S(1)} collective-permute-done((bf16[2,128,512]{2,1,0:T(8,128)(2,1)S(1)}, bf16[2,128,512]{2,1,0:T(8,128)(2,1)S(1)}, u32[]{:S(2)}, u32[]{:S(2)}) %collective-permute-start.16) | collective-permute-done | bytes 262176 | tf_op jit(solution)/shard_map/ppermute | solution.py:27
  206.6 7.6 %collective-permute-done.17.refs_7_ = bf16[2,128,512]{2,1,0:T(8,128)(2,1)S(1)} collective-permute-done((bf16[2,128,512]{2,1,0:T(8,128)(2,1)S(1)}, bf16[2,128,512]{2,1,0:T(8,128)(2,1)S(1)}, u32[]{:S(2)}, u32[]{:S(2)}) %collective-permute-start.17) | collective-permute-done | bytes 262176 | tf_op jit(solution)/shard_map/ppermute | solution.py:27
  214.2 2.5 down.1
  216.7 12.3 %collective-permute-start.26 = (bf16[2,128,256]{2,1,0:T(8,128)(2,1)S(1)}, bf16[2,128,256]{2,1,0:T(8,128)(2,1)S(1)}, u32[]{:S(2)}, u32[]{:S(2)}) collective-permute-start(bf16[2,128,256]{2,1,0:T(8,128)(2,1)S(1)} %bitcast.69), channel_id=1, source_target_pairs={{0,1},{1,0},{2,3},{3,2},{4,5},{5,4},{6,7},{7,6},{8,9},{9,8},{10,11... | collective-permute-start | bytes 393224 | tf_op jit(solution)/shard_map/ppermute | solution.py:18
  230.8 19.3 %all_to_all.10 = bf16[16,128,256]{2,1,0:T(8,128)(2,1)S(1)} all-to-all(bf16[16,128,256]{2,1,0:T(8,128)(2,1)S(1)} %broadcast_select_fusion), channel_id=1, replica_groups={{0,2,4,6,8,10,12,14,16,18,20,22,24,26,28,30},{1,3,5,7,9,11,13,15,17,19,..., dimensions={0} | all-to-all | bytes 2097152 | tf_op jit(solution)/shard_map/all_to_all | solution.py:154
  (93 shorter events, 50.5 us)
Async XLA Ops:
  6.5 22.1 %copy-start = (f32[8,1024]{1,0:T(8,128)S(1)}, f32[8,1024]{1,0:T(8,128)}, u32[]{:S(2)}) copy-start(f32[8,1024]{1,0:T(8,128)} %param.8) | copy-start | bytes 98308
  8.6 21.5 %all-to-all-start = ((bf16[16,128,256]{2,1,0:T(8,128)(2,1)}), bf16[16,128,256]{2,1,0:T(8,128)(2,1)}, u32[]{:S(2)}, u32[]{:S(2)}) async-start(bf16[16,128,256]{2,1,0:T(8,128)(2,1)} %broadcast_in_dim.47), calls=%async_computation | async-start | bytes 2097152 | tf_op jit(solution)/shard_map/all_to_all | solution.py:124
  16.2 104.0 %all-gather.2.cloned.1.call-start = ((), (), s32[]{:S(2)}) async-start(), calls=%async_computation.2 | async-start | bytes 2228224 | tf_op jit(solution)/shard_map/all_gather | solution.py:134
  16.3 25.6 %collective-permute-start.1 = (bf16[4096,128]{1,0:T(8,128)(2,1)S(1)}, bf16[4096,128]{1,0:T(8,128)(2,1)}, u32[]{:S(2)}, u32[]{:S(2)}) collective-permute-start(bf16[4096,128]{1,0:T(8,128)(2,1)S(1)} %bitcast.60), channel_id=1, source_target_pairs={{0,1},{1,0},{2,3},{3,2},{4,5},{5,4},{6,7},{7,6},{8,9},{9,8},{10,11... | collective-permute-start | bytes 3145736 | tf_op jit(solution)/shard_map/ppermute | solution.py:18
  21.8 20.0 %collective-permute-start.2 = (bf16[4096,128]{1,0:T(8,128)(2,1)S(1)}, bf16[4096,128]{1,0:T(8,128)(2,1)}, u32[]{:S(2)}, u32[]{:S(2)}) collective-permute-start(bf16[4096,128]{1,0:T(8,128)(2,1)S(1)} %bitcast.63), channel_id=1, source_target_pairs={{0,1},{1,0},{2,3},{3,2},{4,5},{5,4},{6,7},{7,6},{8,9},{9,8},{10,11... | collective-permute-start | bytes 3145736 | tf_op jit(solution)/shard_map/ppermute | solution.py:18
  23.8 18.1 %collective-permute-start.3 = (bf16[2048,256]{1,0:T(8,128)(2,1)S(1)}, bf16[2048,256]{1,0:T(8,128)(2,1)}, u32[]{:S(2)}, u32[]{:S(2)}) collective-permute-start(bf16[2048,256]{1,0:T(8,128)(2,1)S(1)} %bitcast.66), channel_id=1, source_target_pairs={{0,1},{1,0},{2,3},{3,2},{4,5},{5,4},{6,7},{7,6},{8,9},{9,8},{10,11... | collective-permute-start | bytes 3145736 | tf_op jit(solution)/shard_map/ppermute | solution.py:18
  32.5 8.6 %collective-permute-start = (bf16[2,128,256]{2,1,0:T(8,128)(2,1)}, bf16[2,128,256]{2,1,0:T(8,128)(2,1)S(1)}, u32[]{:S(2)}, u32[]{:S(2)}) collective-permute-start(bf16[2,128,256]{2,1,0:T(8,128)(2,1)} %gather_fusion.1), channel_id=1, source_target_pairs={{0,1},{1,0},{2,3},{3,2},{4,5},{5,4},{6,7},{7,6},{8,9},{9,8},{10,11... | collective-permute-start | bytes 393224 | tf_op jit(solution)/shard_map/ppermute | solution.py:18
  42.0 26.7 %collective-permute-start.4 = (bf16[4096,128]{1,0:T(8,128)(2,1)S(1)}, bf16[4096,128]{1,0:T(8,128)(2,1)S(1)}, u32[]{:S(2)}, u32[]{:S(2)}) collective-permute-start(bf16[4096,128]{1,0:T(8,128)(2,1)S(1)} %bitcast.61), channel_id=1, source_target_pairs={{0,2},{1,3},{2,0},{3,1},{4,6},{5,7},{6,4},{7,5},{8,10},{9,11},{10,... | collective-permute-start | bytes 3145736 | tf_op jit(solution)/shard_map/ppermute | solution.py:22
  44.3 46.9 %collective-permute-start.6 = (bf16[4096,128]{1,0:T(8,128)(2,1)S(1)}, bf16[4096,128]{1,0:T(8,128)(2,1)S(1)}, u32[]{:S(2)}, u32[]{:S(2)}) collective-permute-start(bf16[4096,128]{1,0:T(8,128)(2,1)S(1)} %bitcast.64), channel_id=1, source_target_pairs={{0,2},{1,3},{2,0},{3,1},{4,6},{5,7},{6,4},{7,5},{8,10},{9,11},{10,... | collective-permute-start | bytes 3145736 | tf_op jit(solution)/shard_map/ppermute | solution.py:22
  47.3 66.3 %collective-permute-start.8 = (bf16[2048,256]{1,0:T(8,128)(2,1)S(1)}, bf16[2048,256]{1,0:T(8,128)(2,1)S(1)}, u32[]{:S(2)}, u32[]{:S(2)}) collective-permute-start(bf16[2048,256]{1,0:T(8,128)(2,1)S(1)} %bitcast.67), channel_id=1, source_target_pairs={{0,2},{1,3},{2,0},{3,1},{4,6},{5,7},{6,4},{7,5},{8,10},{9,11},{10,... | collective-permute-start | bytes 3145736 | tf_op jit(solution)/shard_map/ppermute | solution.py:22
  68.7 48.6 %collective-permute-start.5 = (bf16[4096,128]{1,0:T(8,128)(2,1)S(1)}, bf16[4096,128]{1,0:T(8,128)(2,1)S(1)}, u32[]{:S(2)}, u32[]{:S(2)}) collective-permute-start(bf16[4096,128]{1,0:T(8,128)(2,1)S(1)} %collective-permute-done.4.refs_2_), channel_id=1, source_target_pairs={{0,1},{1,0},{2,3},{3,2},{4,5},{5,4},{6,7},{7,6},{8,9},{9,8},{10,11... | collective-permute-start | bytes 3145736 | tf_op jit(solution)/shard_map/ppermute | solution.py:18
  91.2 27.1 %collective-permute-start.7 = (bf16[4096,128]{1,0:T(8,128)(2,1)S(1)}, bf16[4096,128]{1,0:T(8,128)(2,1)S(1)}, u32[]{:S(2)}, u32[]{:S(2)}) collective-permute-start(bf16[4096,128]{1,0:T(8,128)(2,1)S(1)} %collective-permute-done.6.refs_6_), channel_id=1, source_target_pairs={{0,1},{1,0},{2,3},{3,2},{4,5},{5,4},{6,7},{7,6},{8,9},{9,8},{10,11... | collective-permute-start | bytes 3145736 | tf_op jit(solution)/shard_map/ppermute | solution.py:18
  113.6 5.7 %collective-permute-start.9 = (bf16[2048,256]{1,0:T(8,128)(2,1)S(1)}, bf16[2048,256]{1,0:T(8,128)(2,1)S(1)}, u32[]{:S(2)}, u32[]{:S(2)}) collective-permute-start(bf16[2048,256]{1,0:T(8,128)(2,1)S(1)} %collective-permute-done.8.refs_18_), channel_id=1, source_target_pairs={{0,1},{1,0},{2,3},{3,2},{4,5},{5,4},{6,7},{7,6},{8,9},{9,8},{10,11... | collective-permute-start | bytes 3145736 | tf_op jit(solution)/shard_map/ppermute | solution.py:18
  130.6 83.6 %copy-start.6 = (bf16[2048,256]{1,0:T(8,128)(2,1)S(1)}, bf16[2048,256]{1,0:T(8,128)(2,1)}, u32[]{:S(2)}) copy-start(bf16[2048,256]{1,0:T(8,128)(2,1)} %copy-done.5) | copy-start | bytes 3145732
  130.6 83.6 %copy-start.8 = (bf16[2048,256]{1,0:T(8,128)(2,1)S(1)}, bf16[2048,256]{1,0:T(8,128)(2,1)}, u32[]{:S(2)}) copy-start(bf16[2048,256]{1,0:T(8,128)(2,1)} %copy-done.7) | copy-start | bytes 3145732
  130.6 13.6 %collective-permute-start.18 = (bf16[128,512]{1,0:T(8,128)(2,1)S(1)}, bf16[128,512]{1,0:T(8,128)(2,1)S(1)}, u32[]{:S(2)}, u32[]{:S(2)}) collective-permute-start(bf16[128,512]{1,0:T(8,128)(2,1)S(1)} %get-tuple-element.41), channel_id=1, source_target_pairs={{0,32},{1,481},{2,34},{3,483},{4,36},{5,485},{6,38},{7,487},{8,40}... | collective-permute-start | bytes 393224 | tf_op jit(solution)/shard_map/ppermute | solution.py:27
  141.9 6.9 %collective-permute-start.10 = (bf16[128,512]{1,0:T(8,128)(2,1)S(1)}, bf16[128,512]{1,0:T(8,128)(2,1)S(1)}, u32[]{:S(2)}, u32[]{:S(2)}) collective-permute-start(bf16[128,512]{1,0:T(8,128)(2,1)S(1)} %get-tuple-element.40), channel_id=1, source_target_pairs={{0,32},{1,481},{2,34},{3,483},{4,36},{5,485},{6,38},{7,487},{8,40}... | collective-permute-start | bytes 393224 | tf_op jit(solution)/shard_map/ppermute | solution.py:27
  144.3 7.4 %collective-permute-start.19 = (bf16[2,128,512]{2,1,0:T(8,128)(2,1)S(1)}, bf16[2,128,512]{2,1,0:T(8,128)(2,1)S(1)}, u32[]{:S(2)}, u32[]{:S(2)}) collective-permute-start(bf16[2,128,512]{2,1,0:T(8,128)(2,1)S(1)} %pad_maximum_fusion.1.refs_8_), channel_id=1, source_target_pairs={{0,480},{1,33},{2,482},{3,35},{4,484},{5,37},{6,486},{7,39},{8,488... | collective-permute-start | bytes 786440 | tf_op jit(solution)/shard_map/ppermute | solution.py:27
  148.9 7.4 %collective-permute-start.11 = (bf16[2,128,512]{2,1,0:T(8,128)(2,1)S(1)}, bf16[2,128,512]{2,1,0:T(8,128)(2,1)S(1)}, u32[]{:S(2)}, u32[]{:S(2)}) collective-permute-start(bf16[2,128,512]{2,1,0:T(8,128)(2,1)S(1)} %pad_maximum_fusion.refs_0_), channel_id=1, source_target_pairs={{0,480},{1,33},{2,482},{3,35},{4,484},{5,37},{6,486},{7,39},{8,488... | collective-permute-start | bytes 786440 | tf_op jit(solution)/shard_map/ppermute | solution.py:27
  151.7 9.1 %collective-permute-start.20 = (bf16[2,128,512]{2,1,0:T(8,128)(2,1)S(1)}, bf16[2,128,512]{2,1,0:T(8,128)(2,1)S(1)}, u32[]{:S(2)}, u32[]{:S(2)}) collective-permute-start(bf16[2,128,512]{2,1,0:T(8,128)(2,1)S(1)} %collective-permute-done.19.refs_9_), channel_id=1, source_target_pairs={{0,32},{1,481},{2,34},{3,483},{4,36},{5,485},{6,38},{7,487},{8,40}... | collective-permute-start | bytes 786440 | tf_op jit(solution)/shard_map/ppermute | solution.py:27
  156.3 8.3 %collective-permute-start.12 = (bf16[2,128,512]{2,1,0:T(8,128)(2,1)S(1)}, bf16[2,128,512]{2,1,0:T(8,128)(2,1)S(1)}, u32[]{:S(2)}, u32[]{:S(2)}) collective-permute-start(bf16[2,128,512]{2,1,0:T(8,128)(2,1)S(1)} %collective-permute-done.11.refs_1_), channel_id=1, source_target_pairs={{0,32},{1,481},{2,34},{3,483},{4,36},{5,485},{6,38},{7,487},{8,40}... | collective-permute-start | bytes 786440 | tf_op jit(solution)/shard_map/ppermute | solution.py:27
  160.8 9.2 %collective-permute-start.21 = (bf16[2,128,512]{2,1,0:T(8,128)(2,1)S(1)}, bf16[2,128,512]{2,1,0:T(8,128)(2,1)S(1)}, u32[]{:S(2)}, u32[]{:S(2)}) collective-permute-start(bf16[2,128,512]{2,1,0:T(8,128)(2,1)S(1)} %collective-permute-done.20.refs_10_), channel_id=1, source_target_pairs={{0,480},{1,33},{2,482},{3,35},{4,484},{5,37},{6,486},{7,39},{8,488... | collective-permute-start | bytes 786440 | tf_op jit(solution)/shard_map/ppermute | solution.py:27
  164.6 7.9 %collective-permute-start.13 = (bf16[2,128,512]{2,1,0:T(8,128)(2,1)S(1)}, bf16[2,128,512]{2,1,0:T(8,128)(2,1)S(1)}, u32[]{:S(2)}, u32[]{:S(2)}) collective-permute-start(bf16[2,128,512]{2,1,0:T(8,128)(2,1)S(1)} %collective-permute-done.12.refs_2_), channel_id=1, source_target_pairs={{0,480},{1,33},{2,482},{3,35},{4,484},{5,37},{6,486},{7,39},{8,488... | collective-permute-start | bytes 786440 | tf_op jit(solution)/shard_map/ppermute | solution.py:27
  170.1 11.2 %collective-permute-start.22 = (bf16[2,128,512]{2,1,0:T(8,128)(2,1)S(1)}, bf16[2,128,512]{2,1,0:T(8,128)(2,1)S(1)}, u32[]{:S(2)}, u32[]{:S(2)}) collective-permute-start(bf16[2,128,512]{2,1,0:T(8,128)(2,1)S(1)} %collective-permute-done.21.refs_11_), channel_id=1, source_target_pairs={{0,32},{1,481},{2,34},{3,483},{4,36},{5,485},{6,38},{7,487},{8,40}... | collective-permute-start | bytes 786440 | tf_op jit(solution)/shard_map/ppermute | solution.py:27
  172.6 11.3 %collective-permute-start.14 = (bf16[2,128,512]{2,1,0:T(8,128)(2,1)S(1)}, bf16[2,128,512]{2,1,0:T(8,128)(2,1)S(1)}, u32[]{:S(2)}, u32[]{:S(2)}) collective-permute-start(bf16[2,128,512]{2,1,0:T(8,128)(2,1)S(1)} %collective-permute-done.13.refs_3_), channel_id=1, source_target_pairs={{0,32},{1,481},{2,34},{3,483},{4,36},{5,485},{6,38},{7,487},{8,40}... | collective-permute-start | bytes 786440 | tf_op jit(solution)/shard_map/ppermute | solution.py:27
  181.2 9.4 %collective-permute-start.23 = (bf16[2,128,512]{2,1,0:T(8,128)(2,1)S(1)}, bf16[2,128,512]{2,1,0:T(8,128)(2,1)S(1)}, u32[]{:S(2)}, u32[]{:S(2)}) collective-permute-start(bf16[2,128,512]{2,1,0:T(8,128)(2,1)S(1)} %collective-permute-done.22.refs_12_), channel_id=1, source_target_pairs={{0,480},{1,33},{2,482},{3,35},{4,484},{5,37},{6,486},{7,39},{8,488... | collective-permute-start | bytes 786440 | tf_op jit(solution)/shard_map/ppermute | solution.py:27
  183.9 10.1 %collective-permute-start.15 = (bf16[2,128,512]{2,1,0:T(8,128)(2,1)S(1)}, bf16[2,128,512]{2,1,0:T(8,128)(2,1)S(1)}, u32[]{:S(2)}, u32[]{:S(2)}) collective-permute-start(bf16[2,128,512]{2,1,0:T(8,128)(2,1)S(1)} %collective-permute-done.14.refs_4_), channel_id=1, source_target_pairs={{0,480},{1,33},{2,482},{3,35},{4,484},{5,37},{6,486},{7,39},{8,488... | collective-permute-start | bytes 786440 | tf_op jit(solution)/shard_map/ppermute | solution.py:27
  190.6 8.8 %collective-permute-start.24 = (bf16[2,128,512]{2,1,0:T(8,128)(2,1)S(1)}, bf16[2,128,512]{2,1,0:T(8,128)(2,1)S(1)}, u32[]{:S(2)}, u32[]{:S(2)}) collective-permute-start(bf16[2,128,512]{2,1,0:T(8,128)(2,1)S(1)} %collective-permute-done.23.refs_13_), channel_id=1, source_target_pairs={{0,32},{1,481},{2,34},{3,483},{4,36},{5,485},{6,38},{7,487},{8,40}... | collective-permute-start | bytes 786440 | tf_op jit(solution)/shard_map/ppermute | solution.py:27
  194.0 10.6 %collective-permute-start.16 = (bf16[2,128,512]{2,1,0:T(8,128)(2,1)S(1)}, bf16[2,128,512]{2,1,0:T(8,128)(2,1)S(1)}, u32[]{:S(2)}, u32[]{:S(2)}) collective-permute-start(bf16[2,128,512]{2,1,0:T(8,128)(2,1)S(1)} %collective-permute-done.15.refs_5_), channel_id=1, source_target_pairs={{0,32},{1,481},{2,34},{3,483},{4,36},{5,485},{6,38},{7,487},{8,40}... | collective-permute-start | bytes 786440 | tf_op jit(solution)/shard_map/ppermute | solution.py:27
  199.5 7.1 %collective-permute-start.25 = (bf16[2,128,512]{2,1,0:T(8,128)(2,1)S(1)}, bf16[2,128,512]{2,1,0:T(8,128)(2,1)S(1)}, u32[]{:S(2)}, u32[]{:S(2)}) collective-permute-start(bf16[2,128,512]{2,1,0:T(8,128)(2,1)S(1)} %collective-permute-done.24.refs_14_), channel_id=1, source_target_pairs={{0,480},{1,33},{2,482},{3,35},{4,484},{5,37},{6,486},{7,39},{8,488... | collective-permute-start | bytes 786440 | tf_op jit(solution)/shard_map/ppermute | solution.py:27
  204.6 9.6 %collective-permute-start.17 = (bf16[2,128,512]{2,1,0:T(8,128)(2,1)S(1)}, bf16[2,128,512]{2,1,0:T(8,128)(2,1)S(1)}, u32[]{:S(2)}, u32[]{:S(2)}) collective-permute-start(bf16[2,128,512]{2,1,0:T(8,128)(2,1)S(1)} %collective-permute-done.16.refs_6_), channel_id=1, source_target_pairs={{0,480},{1,33},{2,482},{3,35},{4,484},{5,37},{6,486},{7,39},{8,488... | collective-permute-start | bytes 786440 | tf_op jit(solution)/shard_map/ppermute | solution.py:27
  216.7 13.3 %collective-permute-start.26 = (bf16[2,128,256]{2,1,0:T(8,128)(2,1)S(1)}, bf16[2,128,256]{2,1,0:T(8,128)(2,1)S(1)}, u32[]{:S(2)}, u32[]{:S(2)}) collective-permute-start(bf16[2,128,256]{2,1,0:T(8,128)(2,1)S(1)} %bitcast.69), channel_id=1, source_target_pairs={{0,1},{1,0},{2,3},{3,2},{4,5},{5,4},{6,7},{7,6},{8,9},{9,8},{10,11... | collective-permute-start | bytes 393224 | tf_op jit(solution)/shard_map/ppermute | solution.py:18
  (14 other events, 54.7 us)
Sparse Core Ops, SparseCore 0:
  42.1 64.4 all-gather.1

commit v8 on v0

v8 whole, which is shorter than its diff:
```python
import jax
import jax.numpy as jnp
from jax import lax
from jax.experimental import pallas as pl
from jax.experimental.pallas import tpu as pltpu
from jax.sharding import PartitionSpec as P

BLOCK = 128
SPAN = 4
CHIPS = 16
DEPTH = 16
OWNERS = 32
SAME_CORE = [[2 * chip + core for chip in range(CHIPS)] for core in range(2)]
TAIL = 8
TOP = 14.0


def swap_core(value):
    return lax.ppermute(value, "exp", [(p, p ^ 1) for p in range(OWNERS)])


def encode(value):
    value = value.astype(jnp.float32)
    largest = jnp.maximum(jnp.max(jnp.abs(value)), 1e-30)
    exponent = jnp.ceil(jnp.log2(largest))
    scaled = (value * jnp.exp2(TOP - exponent)).astype(jnp.float16)
    tail = jnp.full((TAIL, value.shape[1]), exponent, jnp.float16)
    return jnp.concatenate([scaled, tail])


def decode(coded):
    exponent = coded[..., -TAIL:, :][..., :1, :1].astype(jnp.float32)
    value = coded[..., :-TAIL, :].astype(jnp.float32) * jnp.exp2(exponent - TOP)
    return value.astype(jnp.bfloat16)


def hidden_kernel(gathered, *refs):
    weights, out = refs[:-1], refs[-1]
    depth = gathered.shape[2]
    total = None
    for number in range(DEPTH):
        rows = pl.ds(number * depth, depth)
        right = jnp.concatenate([weight[rows, :] for weight in weights], axis=1)
        term = jnp.dot(gathered[number], right, preferred_element_type=jnp.float32)
        total = term if total is None else total + term
    units = total.shape[1] // 2
    gate, up = total[:, :units], total[:, units:]
    out[...] = (gate / (1.0 + jnp.exp(-gate)) * up).astype(out.dtype)


def down_kernel(gathered, scale, *refs):
    weights, out = refs[:-1], refs[-1]
    depth = gathered.shape[2] // len(weights)
    total = None
    for number in range(DEPTH):
        rows = pl.ds(number * depth, depth)
        right = jnp.concatenate([weight[rows, :] for weight in weights], axis=0)
        term = jnp.dot(gathered[number], right, preferred_element_type=jnp.float32)
        total = term if total is None else total + term
    out[...] = (total * scale[:, :1]).astype(out.dtype)


def kernel_call(kernel, name, inner, rows, columns, flops):
    in_vmem = pl.BlockSpec(memory_space=pltpu.VMEM)
    return pl.pallas_call(
        kernel,
        out_shape=jax.ShapeDtypeStruct((rows, columns), jnp.bfloat16),
        in_specs=[in_vmem] * len(inner),
        out_specs=in_vmem,
        compiler_params=pltpu.CompilerParams(vmem_limit_bytes=24 << 20),
        cost_estimate=pl.CostEstimate(
            flops=flops, bytes_accessed=2 * sum(array.size for array in inner), transcendentals=0
        ),
        name=name,
    )(*inner)


def shards(tokens, picked_blocks, gate_scale, w_gate, w_up, w_down):
    position = lax.axis_index("exp")
    core = lax.rem(position, 2)
    expert = position // SPAN
    features, units = tokens.shape[1], w_gate.shape[2]
    chosen = lax.dynamic_index_in_dim(picked_blocks, expert, 0, keepdims=False)
    half = chosen.shape[0] // 2
    rows = half * BLOCK
    mine = lax.dynamic_slice_in_dim(chosen, half * core, half)
    theirs = lax.dynamic_slice_in_dim(chosen, half * (1 - core), half)
    scale = lax.dynamic_index_in_dim(gate_scale, expert, 0, keepdims=False).reshape(2, rows, 1)
    scale = jnp.broadcast_to(lax.dynamic_index_in_dim(scale, core, 0, keepdims=False), (rows, 128))
    names = jnp.concatenate([mine, theirs])
    match = names[None, :] == (2 * jnp.arange(CHIPS, dtype=jnp.int32) + core)[:, None]
    wanted, source = match.any(1)[:, None, None], jnp.argmax(match, 1)

    own = [w_gate[0], w_up[0], w_down[0]]
    near = [swap_core(w) for w in own]

    coded = encode(tokens)
    coded, scale, wanted, source, mine = lax.optimization_barrier((coded, scale, wanted, source, mine))
    held = lax.all_gather(coded, "exp")
    picked = jnp.stack([lax.dynamic_index_in_dim(held, mine[pick], 0, keepdims=False) for pick in range(half)])
    gathered = decode(lax.all_gather(picked, "tok")).reshape(DEPTH, rows, features)
    flops = 2 * rows * DEPTH * features * 4 * units
    hidden = kernel_call(
        hidden_kernel, "hidden", [gathered] + [w[kind] for kind in range(2) for w in (own, near)], rows, 2 * units, flops
    )
    gathered = decode(lax.all_gather(encode(hidden)[None], "tok", tiled=True))
    done = kernel_call(
        down_kernel, "down", [gathered, scale] + [w[2] for w in (own, near)], rows, features, flops // 2
    )
    done = done.reshape(half, BLOCK, features)

    all_done = jnp.concatenate([done, swap_core(done)])
    outgoing = jnp.where(wanted, all_done[source], 0)
    arrived = lax.all_to_all(outgoing, "exp", 0, 0, axis_index_groups=SAME_CORE, tiled=True)
    return jnp.sum(arrived, axis=0, dtype=jnp.float32).astype(jnp.bfloat16)


def solution(mesh):
    return jax.shard_map(
        shards,
        mesh=mesh,
        in_specs=(
            P("exp", "tok"),
            P(),
            P(),
            P("exp", None, "tok"),
            P("exp", None, "tok"),
            P("exp", None, "tok"),
        ),
        out_specs=P("exp", "tok"),
        check_vma=False,
    )
```

time: 424 us -> 217 us (0.51)
  waiting for transfers between devices: 386 us -> 1.12 us
  blocking collectives: 0 us -> 158 us
  starting transfers between devices: 0.12 us -> 25.9 us
  matrix products: 12.5 us -> 0 us
  other arithmetic: 2.25 us -> 10.3 us
  Pallas kernels: 0 us -> 6.07 us
    all_gather x3 -> x0, waiting for transfers between devices: 277 us -> none  [the longest x1 120 us: shards(): full_rows = lax.all_gather(selected, 'tok', axis=1, tiled=True)]
    all_gather x0 -> x3, blocking collectives: none -> 137 us  [the longest x1 60.8 us: shards(): lax.all_gather(picked, 'tok')]
    reduce_scatter x1 -> x0, waiting for transfers between devices: 109 us -> none  [shards(): lax.psum_scatter(buffer, 'exp', scatter_dimension=0, tiled=True)]
    ppermute x0 -> x4, starting transfers between devices: none -> 25.9 us  [swap_core(): return lax.ppermute(value, 'exp', [(p, p ^ 1) for p in range(OWNERS)])]
    all_to_all x0 -> x1, blocking collectives: none -> 20.7 us  [shards(): lax.all_to_all(outgoing, 'exp', 0, 0, axis_index_groups=SAME_CORE, tiled=...]
    dot_general x3 -> x0, matrix products: 12.5 us -> none  [the longest x1 6.08 us: shards(): jnp.dot(full_rows, gate_local, preferred_element_type=jnp.float32)]
    pallas_call x0 -> x2, Pallas kernels: none -> 6.07 us  [kernel_call(): pl.pallas_call(kernel, out_shape=jax.ShapeDtypeStruct((rows, columns), jn...]
    convert_element_type x1 -> x4, other arithmetic: 1.54 us -> 6.12 us  [the longest x2 5.2 us: decode(): return value.astype(jnp.bfloat16)]
  transfers between devices with their start and end apart: 4 -> 4, of which waited for: 4 -> 1; matrix products, arithmetic and copies ran while one was open for 0% -> 6% of each run, Pallas kernels for 0% -> 2%
where the time goes in v8:
time: 217 us; the launch traced here: 216 us
  blocking collectives  158 us (73%)
  starting transfers between devices  25.9 us (12%)
  other arithmetic  10.3 us (5%)
  between operations  9.36 us (4%)
  Pallas kernels  6.07 us (3%)
  local copies, waits for them, and re-layouts  5.62 us (3%)
    all_gather x1, blocking collectives, shards(): lax.all_gather(picked, 'tok')  60.8 us
    all_gather x1, blocking collectives, shards(): gathered = decode(lax.all_gather(encode(hidden)[None], 'tok', tiled=True))  52.6 us
    ppermute x4, starting transfers between devices, swap_core(): return lax.ppermute(value, 'exp', [(p, p ^ 1) for p in range(OWNERS)])  25.9 us
    all_gather x1, blocking collectives, shards(): held = lax.all_gather(coded, 'exp')  23.5 us
    all_to_all x1, blocking collectives, shards(): lax.all_to_all(outgoing, 'exp', 0, 0, axis_index_groups=SAME_CORE, tiled=...  20.7 us
    pallas_call x2, Pallas kernels, kernel_call(): pl.pallas_call(kernel, out_shape=jax.ShapeDtypeStruct((rows, columns), jn...  6.07 us
    convert_element_type x2, other arithmetic, decode(): return value.astype(jnp.bfloat16)  5.2 us
  transfers between devices with their start and end apart: 4, of which 1 were waited for; matrix products, arithmetic and copies ran while one was open for 6% of the time, Pallas kernels for 2%

profile of v8, /device:TPU:1, one launch (start us, length us, event | category | flops | bytes accessed | tf_op | source)
XLA Modules:
  0.0 215.8 jit_solution(6801280447854384731)
XLA Ops:
  0.0 8.9 %collective-permute-start = (bf16[4096,128]{1,0:T(8,128)(2,1)}, bf16[4096,128]{1,0:T(8,128)(2,1)S(1)}, u32[]{:S(2)}, u32[]{:S(2)}) collective-permute-start(bf16[4096,128]{1,0:T(8,128)(2,1)} %bitcast.22), channel_id=1, source_target_pairs={{0,1},{1,0},{2,3},{3,2},{4,5},{5,4},{6,7},{7,6},{8,9},{9,8},{10,11... | collective-permute-start | bytes 3145736 | tf_op jit(solution)/shard_map/ppermute | solution.py:19
  8.9 1.9 collective-permute-start.1
  10.9 2.4 %collective-permute-start.2 = (bf16[2048,256]{1,0:T(8,128)(2,1)}, bf16[2048,256]{1,0:T(8,128)(2,1)}, u32[]{:S(2)}, u32[]{:S(2)}) collective-permute-start(bf16[2048,256]{1,0:T(8,128)(2,1)} %bitcast.26), channel_id=1, source_target_pairs={{0,1},{1,0},{2,3},{3,2},{4,5},{5,4},{6,7},{7,6},{8,9},{9,8},{10,11... | collective-permute-start | bytes 3145736 | tf_op jit(solution)/shard_map/ppermute | solution.py:19
  13.3 0.8 dynamic-slice_bitcast_fusion.1
  14.2 0.1 pad_add_fusion
  14.2 0.6 compare_reduce_fusion
  14.8 0.1 compare_reduce_fusion.1
  15.0 1.5 fusion.2
  17.2 0.9 fusion.3
  18.1 0.8 broadcast_in_dim.35.scale
  18.9 0.7 fusion.8
  24.6 23.5 %all-gather.6 = f16[4352,256]{1,0:T(8,128)(2,1)S(1)} all-gather(f16[136,256]{1,0:T(8,128)(2,1)S(1)} %concatenate.12), channel_id=2, replica_groups=mesh['tok'=16,'exp'=32] {'exp'}, dimensions={0}, use_global_device_ids=true | all-gather | bytes 2297856 | tf_op jit(solution)/shard_map/all_gather | solution.py:99
  50.7 0.1 constant_dynamic-slice_fusion.3
  50.7 0.1 pad_maximum_fusion.1
  50.8 60.8 %all-gather.7 = f16[64,136,256]{2,1,0:T(8,128)(2,1)S(1)} all-gather(f16[4,136,256]{2,1,0:T(8,128)(2,1)S(1)} %pad_maximum_fusion.1), channel_id=3, replica_groups=mesh['tok'=16,'exp'=32] {'tok'}, dimensions={0}, use_global_device_ids=true | all-gather | bytes 4734976 | tf_op jit(solution)/shard_map/all_gather | solution.py:101
  111.6 2.2 %copy-done.5 = f16[64,136,256]{2,1,0:T(8,128)(2,1)} copy-done((f16[64,136,256]{2,1,0:T(8,128)(2,1)}, f16[64,136,256]{2,1,0:T(8,128)(2,1)S(1)}, u32[]{:S(2)}) %copy-start.5) | copy-done | bytes 4456472
  113.9 0.1 copy.16
  114.0 0.1 copy.15
  114.1 3.7 %multiply_convert_fusion.1 = bf16[16,4,128,256]{3,2,1,0:T(8,128)(2,1)S(1)} fusion(f16[16,4,136,256]{3,2,1,0:T(8,128)(2,1)} %bitcast.31, f32[16,4]{1,0:T(8,128)S(1)} %copy.15), kind=kLoop, calls=%fused_computation.2 | loop fusion | flops 6291456 | bytes 8388864 | tf_op jit(solution)/shard_map/convert_element_type | solution.py:34
  117.9 3.6 %hidden.1 = bf16[512,256]{1,0:T(8,128)(2,1)S(1)} custom-call(bf16[16,512,256]{2,1,0:T(8,128)(2,1)S(1)} %bitcast.21, bf16[4096,128]{1,0:T(8,128)(2,1)S(1)} %bitcast.23, bf16[4096,128]{1,0:T(8,128)(2,1)S(1)} %collective-permute-done.refs_1_, bf16[4096,128]{1,0:T(8,128)(2,1)S(1)} %bitcast.25, bf16[4096,128]{1,0:T(8,128)(2,1)} %collective-permute-done.1.refs_3_), custom_call_target="tpu_custom_call" | custom-call | flops 2147483648 | bytes 8388608 | tf_op jit(solution)/shard_map/hidden/pallas_call | solution.py:65
  121.5 0.6 fusion
  122.8 0.1 fusion.1
  123.0 52.6 %all-gather.8 = f16[8320,256]{1,0:T(8,128)(2,1)S(1)} all-gather(f16[520,256]{1,0:T(8,128)(2,1)S(1)} %concatenate.14), channel_id=4, replica_groups=mesh['tok'=16,'exp'=32] {'tok'}, dimensions={0}, use_global_device_ids=true | all-gather | bytes 4526080 | tf_op jit(solution)/shard_map/all_gather | solution.py:106
  175.5 0.2 fusion.7
  175.8 1.5 multiply_convert_fusion.gathered
  177.3 2.5 %down.1 = bf16[512,256]{1,0:T(8,128)(2,1)S(1)} custom-call(bf16[16,512,256]{2,1,0:T(8,128)(2,1)S(1)} %multiply_convert_fusion.gathered, f32[512,128]{1,0:T(8,128)S(1)} %copy-done.4, bf16[2048,256]{1,0:T(8,128)(2,1)S(1)} %bitcast.27, bf16[2048,256]{1,0:T(8,128)(2,1)} %collective-permute-done.2.refs_1_), custom_call_target="tpu_custom_call" | custom-call | flops 1073741824 | bytes 6422528 | tf_op jit(solution)/shard_map/down/pallas_call | solution.py:65
  179.8 12.6 %collective-permute-start.3 = (bf16[4,128,256]{2,1,0:T(8,128)(2,1)S(1)}, bf16[4,128,256]{2,1,0:T(8,128)(2,1)S(1)}, u32[]{:S(2)}, u32[]{:S(2)}) collective-permute-start(bf16[4,128,256]{2,1,0:T(8,128)(2,1)S(1)} %bitcast.28), channel_id=1, source_target_pairs={{0,1},{1,0},{2,3},{3,2},{4,5},{5,4},{6,7},{7,6},{8,9},{9,8},{10,11... | collective-permute-start | bytes 786440 | tf_op jit(solution)/shard_map/ppermute | solution.py:19
  192.4 1.1 collective-permute-done.3
  193.6 0.6 gather_fusion
  194.2 0.1 broadcast_select_fusion
  194.4 20.7 %all_to_all.5 = bf16[16,128,256]{2,1,0:T(8,128)(2,1)S(1)} all-to-all(bf16[16,128,256]{2,1,0:T(8,128)(2,1)S(1)} %broadcast_select_fusion), channel_id=1, replica_groups={{0,2,4,6,8,10,12,14,16,18,20,22,24,26,28,30},{1,3,5,7,9,11,13,15,17,19,..., dimensions={0} | all-to-all | bytes 2097152 | tf_op jit(solution)/shard_map/all_to_all | solution.py:114
  215.1 0.8 reduce_sum.12
  (25 shorter events, 0.2 us)
Async XLA Ops:
  0.0 14.9 %copy-start = (f32[8,1024]{1,0:T(8,128)S(1)}, f32[8,1024]{1,0:T(8,128)}, u32[]{:S(2)}) copy-start(f32[8,1024]{1,0:T(8,128)} %param.8) | copy-start | bytes 98308
  0.0 117.8 %collective-permute-start = (bf16[4096,128]{1,0:T(8,128)(2,1)}, bf16[4096,128]{1,0:T(8,128)(2,1)S(1)}, u32[]{:S(2)}, u32[]{:S(2)}) collective-permute-start(bf16[4096,128]{1,0:T(8,128)(2,1)} %bitcast.22), channel_id=1, source_target_pairs={{0,1},{1,0},{2,3},{3,2},{4,5},{5,4},{6,7},{7,6},{8,9},{9,8},{10,11... | collective-permute-start | bytes 3145736 | tf_op jit(solution)/shard_map/ppermute | solution.py:19
  8.9 108.9 %collective-permute-start.1 = (bf16[4096,128]{1,0:T(8,128)(2,1)}, bf16[4096,128]{1,0:T(8,128)(2,1)}, u32[]{:S(2)}, u32[]{:S(2)}) collective-permute-start(bf16[4096,128]{1,0:T(8,128)(2,1)} %bitcast.24), channel_id=1, source_target_pairs={{0,1},{1,0},{2,3},{3,2},{4,5},{5,4},{6,7},{7,6},{8,9},{9,8},{10,11... | collective-permute-start | bytes 3145736 | tf_op jit(solution)/shard_map/ppermute | solution.py:19
  10.9 166.4 %collective-permute-start.2 = (bf16[2048,256]{1,0:T(8,128)(2,1)}, bf16[2048,256]{1,0:T(8,128)(2,1)}, u32[]{:S(2)}, u32[]{:S(2)}) collective-permute-start(bf16[2048,256]{1,0:T(8,128)(2,1)} %bitcast.26), channel_id=1, source_target_pairs={{0,1},{1,0},{2,3},{3,2},{4,5},{5,4},{6,7},{7,6},{8,9},{9,8},{10,11... | collective-permute-start | bytes 3145736 | tf_op jit(solution)/shard_map/ppermute | solution.py:19
  111.6 2.2 %copy-start.5 = (f16[64,136,256]{2,1,0:T(8,128)(2,1)}, f16[64,136,256]{2,1,0:T(8,128)(2,1)S(1)}, u32[]{:S(2)}) copy-start(f16[64,136,256]{2,1,0:T(8,128)(2,1)S(1)} %all-gather.7) | copy-start | bytes 13369348
  111.6 6.2 %copy-start.1 = (bf16[1,4096,128]{2,1,0:T(8,128)(2,1)S(1)}, bf16[1,4096,128]{2,1,0:T(8,128)(2,1)}, u32[]{:S(2)}) copy-start(bf16[1,4096,128]{2,1,0:T(8,128)(2,1)} %param.9) | copy-start | bytes 3145732
  111.6 6.2 %copy-start.2 = (bf16[1,4096,128]{2,1,0:T(8,128)(2,1)S(1)}, bf16[1,4096,128]{2,1,0:T(8,128)(2,1)}, u32[]{:S(2)}) copy-start(bf16[1,4096,128]{2,1,0:T(8,128)(2,1)} %param.10) | copy-start | bytes 3145732
  175.5 1.7 copy-start.3
  175.5 1.7 copy-start.4
  179.8 13.8 %collective-permute-start.3 = (bf16[4,128,256]{2,1,0:T(8,128)(2,1)S(1)}, bf16[4,128,256]{2,1,0:T(8,128)(2,1)S(1)}, u32[]{:S(2)}, u32[]{:S(2)}) collective-permute-start(bf16[4,128,256]{2,1,0:T(8,128)(2,1)S(1)} %bitcast.28), channel_id=1, source_target_pairs={{0,1},{1,0},{2,3},{3,2},{4,5},{5,4},{6,7},{7,6},{8,9},{9,8},{10,11... | collective-permute-start | bytes 786440 | tf_op jit(solution)/shard_map/ppermute | solution.py:19

commit v9 on v8

--- a/solution.py
+++ b/solution.py
@@ -13,6 +13,7 @@
 SAME_CORE = [[2 * chip + core for chip in range(CHIPS)] for core in range(2)]
 TAIL = 8
 TOP = 14.0
+CORE, EXPERT = 8, 9
 
 
 def swap_core(value):
@@ -29,12 +30,12 @@
 
 
 def decode(coded):
-    exponent = coded[..., -TAIL:, :][..., :1, :1].astype(jnp.float32)
+    exponent = jnp.max(coded[..., -TAIL:, :], axis=(-2, -1), keepdims=True).astype(jnp.float32)
     value = coded[..., :-TAIL, :].astype(jnp.float32) * jnp.exp2(exponent - TOP)
     return value.astype(jnp.bfloat16)
 
 
-def hidden_kernel(gathered, *refs):
+def hidden_kernel(facts, gathered, *refs):
     weights, out = refs[:-1], refs[-1]
     depth = gathered.shape[2]
     total = None
@@ -48,7 +49,7 @@
     out[...] = (gate / (1.0 + jnp.exp(-gate)) * up).astype(out.dtype)
 
 
-def down_kernel(gathered, scale, *refs):
+def down_kernel(facts, gathered, scales, *refs):
     weights, out = refs[:-1], refs[-1]
     depth = gathered.shape[2] // len(weights)
     total = None
@@ -57,22 +58,38 @@
         right = jnp.concatenate([weight[rows, :] for weight in weights], axis=0)
         term = jnp.dot(gathered[number], right, preferred_element_type=jnp.float32)
         total = term if total is None else total + term
+    count = total.shape[0]
+    both = scales[pl.ds(facts[EXPERT], 1), :]
+    scale = jnp.where(facts[CORE] == 0, both[:, :count], both[:, count:])
+    scale = jnp.broadcast_to(scale, (128, count)).T
     out[...] = (total * scale[:, :1]).astype(out.dtype)
 
 
-def kernel_call(kernel, name, inner, rows, columns, flops):
+def place_kernel(facts, done, others, out):
+    out[...] = jnp.zeros_like(out)
+    count = done.shape[0]
+    for pick in range(2 * count):
+        block = facts[pick]
+        source = done if pick < count else others
+
+        @pl.when(lax.rem(block, 2) == facts[CORE])
+        def _():
+            out[pl.ds(lax.div(block, 2), 1)] = source[pl.ds(pick % count, 1)]
+
+
+def kernel_call(kernel, name, facts, inner, shape, flops):
     in_vmem = pl.BlockSpec(memory_space=pltpu.VMEM)
     return pl.pallas_call(
         kernel,
-        out_shape=jax.ShapeDtypeStruct((rows, columns), jnp.bfloat16),
-        in_specs=[in_vmem] * len(inner),
+        out_shape=jax.ShapeDtypeStruct(shape, jnp.bfloat16),
+        in_specs=[pl.BlockSpec(memory_space=pltpu.SMEM)] + [in_vmem] * len(inner),
         out_specs=in_vmem,
         compiler_params=pltpu.CompilerParams(vmem_limit_bytes=24 << 20),
         cost_estimate=pl.CostEstimate(
             flops=flops, bytes_accessed=2 * sum(array.size for array in inner), transcendentals=0
         ),
         name=name,
-    )(*inner)
+    )(facts, *inner)
 
 
 def shards(tokens, picked_blocks, gate_scale, w_gate, w_up, w_down):
@@ -85,32 +102,25 @@
     rows = half * BLOCK
     mine = lax.dynamic_slice_in_dim(chosen, half * core, half)
     theirs = lax.dynamic_slice_in_dim(chosen, half * (1 - core), half)
-    scale = lax.dynamic_index_in_dim(gate_scale, expert, 0, keepdims=False).reshape(2, rows, 1)
-    scale = jnp.broadcast_to(lax.dynamic_index_in_dim(scale, core, 0, keepdims=False), (rows, 128))
-    names = jnp.concatenate([mine, theirs])
-    match = names[None, :] == (2 * jnp.arange(CHIPS, dtype=jnp.int32) + core)[:, None]
-    wanted, source = match.any(1)[:, None, None], jnp.argmax(match, 1)
+    facts = jnp.concatenate([mine, theirs, jnp.stack([core, expert]).astype(jnp.int32)])
 
     own = [w_gate[0], w_up[0], w_down[0]]
     near = [swap_core(w) for w in own]
 
-    coded = encode(tokens)
-    coded, scale, wanted, source, mine = lax.optimization_barrier((coded, scale, wanted, source, mine))
+    coded, facts, mine = lax.optimization_barrier((encode(tokens), facts, mine))
     held = lax.all_gather(coded, "exp")
-    picked = jnp.stack([lax.dynamic_index_in_dim(held, mine[pick], 0, keepdims=False) for pick in range(half)])
-    gathered = decode(lax.all_gather(picked, "tok")).reshape(DEPTH, rows, features)
+    gathered = decode(lax.all_gather(held[mine], "tok")).reshape(DEPTH, rows, features)
     flops = 2 * rows * DEPTH * features * 4 * units
     hidden = kernel_call(
-        hidden_kernel, "hidden", [gathered] + [w[kind] for kind in range(2) for w in (own, near)], rows, 2 * units, flops
+        hidden_kernel, "hidden", facts, [gathered] + [w[kind] for kind in range(2) for w in (own, near)],
+        (rows, 2 * units), flops,
     )
     gathered = decode(lax.all_gather(encode(hidden)[None], "tok", tiled=True))
     done = kernel_call(
-        down_kernel, "down", [gathered, scale] + [w[2] for w in (own, near)], rows, features, flops // 2
-    )
-    done = done.reshape(half, BLOCK, features)
+        down_kernel, "down", facts, [gathered, gate_scale] + [w[2] for w in (own, near)], (rows, features), flops // 2
+    ).reshape(half, BLOCK, features)
 
-    all_done = jnp.concatenate([done, swap_core(done)])
-    outgoing = jnp.where(wanted, all_done[source], 0)
+    outgoing = kernel_call(place_kernel, "place", facts, [done, swap_core(done)], (CHIPS, BLOCK, features), 0)
     arrived = lax.all_to_all(outgoing, "exp", 0, 0, axis_index_groups=SAME_CORE, tiled=True)
     return jnp.sum(arrived, axis=0, dtype=jnp.float32).astype(jnp.bfloat16)
 

time: 217 us -> 205 us (0.945)
  between operations: 9.36 us -> 1.62 us
  other arithmetic: 10.3 us -> 7.27 us
  local copies, waits for them, and re-layouts: 5.62 us -> 3.23 us
    unnamed x13 -> x8, local copies, waits for them, and re-layouts: 2.37 us -> 0.02 us
    convert_element_type x2, other arithmetic: 5.2 us -> 2.99 us  [decode(): return value.astype(jnp.bfloat16)]
    pallas_call x2 -> x3, Pallas kernels: 6.07 us -> 5.42 us  [kernel_call(): pl.pallas_call(kernel, out_shape=jax.ShapeDtypeStruct(shape, jnp.bfloat16...]
  transfers between devices with their start and end apart: 4 -> 4, of which waited for: 1 -> 1; matrix products, arithmetic and copies ran while one was open for 6% -> 5% of each run, Pallas kernels for 2% -> 1%
where the time goes in v9:
time: 205 us; the launch traced here: 204 us
  blocking collectives  159 us (78%)
  starting transfers between devices  25.7 us (13%)
  other arithmetic  7.27 us (4%)
  Pallas kernels  5.42 us (3%)
  local copies, waits for them, and re-layouts  3.23 us (2%)
    all_gather x1, blocking collectives, shards(): lax.all_gather(held[mine], 'tok')  60.6 us
    all_gather x1, blocking collectives, shards(): gathered = decode(lax.all_gather(encode(hidden)[None], 'tok', tiled=True))  52.6 us
    ppermute x4, starting transfers between devices, swap_core(): return lax.ppermute(value, 'exp', [(p, p ^ 1) for p in range(OWNERS)])  25.7 us
    all_gather x1, blocking collectives, shards(): held = lax.all_gather(coded, 'exp')  25.4 us
    all_to_all x1, blocking collectives, shards(): lax.all_to_all(outgoing, 'exp', 0, 0, axis_index_groups=SAME_CORE, tiled=...  20.7 us
    pallas_call x3, Pallas kernels, kernel_call(): pl.pallas_call(kernel, out_shape=jax.ShapeDtypeStruct(shape, jnp.bfloat16...  5.42 us
  transfers between devices with their start and end apart: 4, of which 1 were waited for; matrix products, arithmetic and copies ran while one was open for 5% of the time, Pallas kernels for 1%

profile of v9, /device:TPU:1, one launch (start us, length us, event | category | flops | bytes accessed | tf_op | source)
XLA Modules:
  0.0 203.6 jit_solution(15236712619141331660)
XLA Ops:
  0.0 8.8 %collective-permute-start = (bf16[4096,128]{1,0:T(8,128)(2,1)}, bf16[4096,128]{1,0:T(8,128)(2,1)S(1)}, u32[]{:S(2)}, u32[]{:S(2)}) collective-permute-start(bf16[4096,128]{1,0:T(8,128)(2,1)} %bitcast.15), channel_id=1, source_target_pairs={{0,1},{1,0},{2,3},{3,2},{4,5},{5,4},{6,7},{7,6},{8,9},{9,8},{10,11... | collective-permute-start | bytes 3145736 | tf_op jit(solution)/shard_map/ppermute | solution.py:20
  8.8 1.9 collective-permute-start.1
  10.7 2.4 %collective-permute-start.2 = (bf16[2048,256]{1,0:T(8,128)(2,1)}, bf16[2048,256]{1,0:T(8,128)(2,1)S(1)}, u32[]{:S(2)}, u32[]{:S(2)}) collective-permute-start(bf16[2048,256]{1,0:T(8,128)(2,1)} %bitcast.19), channel_id=1, source_target_pairs={{0,1},{1,0},{2,3},{3,2},{4,5},{5,4},{6,7},{7,6},{8,9},{9,8},{10,11... | collective-permute-start | bytes 3145736 | tf_op jit(solution)/shard_map/ppermute | solution.py:20
  13.2 1.4 fusion.2
  15.3 0.9 fusion.3
  16.2 0.8 dynamic-slice_bitcast_fusion.1
  17.0 0.1 pad_add_fusion.facts
  17.1 25.4 %all-gather.6 = f16[4352,256]{1,0:T(8,128)(2,1)} all-gather(f16[136,256]{1,0:T(8,128)(2,1)S(1)} %concatenate.9), channel_id=2, replica_groups=mesh['tok'=16,'exp'=32] {'exp'}, dimensions={0}, use_global_device_ids=true | all-gather | bytes 2297856 | tf_op jit(solution)/shard_map/all_gather | solution.py:111
  42.5 2.3 %gather_fusion = f16[4,136,256]{2,1,0:T(8,128)(2,1)S(1)} fusion(f16[32,136,256]{2,1,0:T(8,128)(2,1)} %bitcast.27, s32[1024]{0:T(1024)S(1)} %pad_clamp_fusion), kind=kCustom, calls=%fused_computation | custom fusion | bytes 557072 | tf_op jit(solution)/shard_map/gather | solution.py:112
  44.8 60.6 %all-gather.7 = f16[64,136,256]{2,1,0:T(8,128)(2,1)S(1)} all-gather(f16[4,136,256]{2,1,0:T(8,128)(2,1)S(1)} %gather_fusion), channel_id=3, replica_groups=mesh['tok'=16,'exp'=32] {'tok'}, dimensions={0}, use_global_device_ids=true | all-gather | bytes 4734976 | tf_op jit(solution)/shard_map/all_gather | solution.py:112
  105.4 0.2 slice_reduce_fusion
  105.6 0.0 copy-start.1
  105.6 1.5 multiply_convert_fusion.1
  107.1 0.0 collective-permute-done.refs_1_
  107.1 0.0 collective-permute-done.1.refs_3_
  107.1 0.0 copy-done
  107.1 0.0 copy-done.1
  107.1 2.9 %hidden.1 = bf16[512,256]{1,0:T(8,128)(2,1)S(1)} custom-call(s32[10]{0:T(128)S(1)} %pad_add_fusion.facts, bf16[16,512,256]{2,1,0:T(8,128)(2,1)S(1)} %bitcast.14, bf16[4096,128]{1,0:T(8,128)(2,1)S(1)} %bitcast.16, bf16[4096,128]{1,0:T(8,128)(2,1)S(1)} %collective-permute-done.refs_1_, bf16[4096,128]{1,0:T(8,128)(2,1)S(1)} %bitcast.18, ...), custom_call_target="tpu_custom_call" | custom-call | flops 2147483648 | bytes 8388608 | tf_op jit(solution)/shard_map/hidden/pallas_call | solution.py:82
  110.1 0.6 fusion
  111.4 0.1 fusion.1
  111.5 0.1 concatenate.11
  111.6 52.6 %all-gather.8 = f16[8320,256]{1,0:T(8,128)(2,1)S(1)} all-gather(f16[520,256]{1,0:T(8,128)(2,1)S(1)} %concatenate.11), channel_id=4, replica_groups=mesh['tok'=16,'exp'=32] {'tok'}, dimensions={0}, use_global_device_ids=true | all-gather | bytes 4526080 | tf_op jit(solution)/shard_map/all_gather | solution.py:118
  164.1 0.2 slice_reduce_fusion.1
  164.4 1.5 multiply_convert_fusion.gathered
  165.8 0.0 collective-permute-done.2.refs_1_
  165.9 0.0 copy-done.2
  165.9 1.8 down.1
  167.7 12.6 %collective-permute-start.3 = (bf16[4,128,256]{2,1,0:T(8,128)(2,1)S(1)}, bf16[4,128,256]{2,1,0:T(8,128)(2,1)S(1)}, u32[]{:S(2)}, u32[]{:S(2)}) collective-permute-start(bf16[4,128,256]{2,1,0:T(8,128)(2,1)S(1)} %bitcast.21), channel_id=1, source_target_pairs={{0,1},{1,0},{2,3},{3,2},{4,5},{5,4},{6,7},{7,6},{8,9},{9,8},{10,11... | collective-permute-start | bytes 786440 | tf_op jit(solution)/shard_map/ppermute | solution.py:20
  180.3 1.1 collective-permute-done.3.others
  181.5 0.7 place.1
  182.2 20.7 %all_to_all.5 = bf16[16,128,256]{2,1,0:T(8,128)(2,1)S(1)} all-to-all(bf16[16,128,256]{2,1,0:T(8,128)(2,1)S(1)} %place.1), channel_id=1, replica_groups={{0,2,4,6,8,10,12,14,16,18,20,22,24,26,28,30},{1,3,5,7,9,11,13,15,17,19,..., dimensions={0} | all-to-all | bytes 2097152 | tf_op jit(solution)/shard_map/all_to_all | solution.py:124
  202.9 0.8 reduce_sum.12
  (9 shorter events, 0.1 us)
Async XLA Ops:
  0.0 107.1 %collective-permute-start = (bf16[4096,128]{1,0:T(8,128)(2,1)}, bf16[4096,128]{1,0:T(8,128)(2,1)S(1)}, u32[]{:S(2)}, u32[]{:S(2)}) collective-permute-start(bf16[4096,128]{1,0:T(8,128)(2,1)} %bitcast.15), channel_id=1, source_target_pairs={{0,1},{1,0},{2,3},{3,2},{4,5},{5,4},{6,7},{7,6},{8,9},{9,8},{10,11... | collective-permute-start | bytes 3145736 | tf_op jit(solution)/shard_map/ppermute | solution.py:20
  8.8 98.3 %collective-permute-start.1 = (bf16[4096,128]{1,0:T(8,128)(2,1)}, bf16[4096,128]{1,0:T(8,128)(2,1)S(1)}, u32[]{:S(2)}, u32[]{:S(2)}) collective-permute-start(bf16[4096,128]{1,0:T(8,128)(2,1)} %bitcast.17), channel_id=1, source_target_pairs={{0,1},{1,0},{2,3},{3,2},{4,5},{5,4},{6,7},{7,6},{8,9},{9,8},{10,11... | collective-permute-start | bytes 3145736 | tf_op jit(solution)/shard_map/ppermute | solution.py:20
  10.7 155.1 %collective-permute-start.2 = (bf16[2048,256]{1,0:T(8,128)(2,1)}, bf16[2048,256]{1,0:T(8,128)(2,1)S(1)}, u32[]{:S(2)}, u32[]{:S(2)}) collective-permute-start(bf16[2048,256]{1,0:T(8,128)(2,1)} %bitcast.19), channel_id=1, source_target_pairs={{0,1},{1,0},{2,3},{3,2},{4,5},{5,4},{6,7},{7,6},{8,9},{9,8},{10,11... | collective-permute-start | bytes 3145736 | tf_op jit(solution)/shard_map/ppermute | solution.py:20
  105.6 1.6 copy-start
  105.6 1.6 copy-start.1
  164.1 1.7 copy-start.2
  164.1 1.7 copy-start.3
  167.7 13.8 %collective-permute-start.3 = (bf16[4,128,256]{2,1,0:T(8,128)(2,1)S(1)}, bf16[4,128,256]{2,1,0:T(8,128)(2,1)S(1)}, u32[]{:S(2)}, u32[]{:S(2)}) collective-permute-start(bf16[4,128,256]{2,1,0:T(8,128)(2,1)S(1)} %bitcast.21), channel_id=1, source_target_pairs={{0,1},{1,0},{2,3},{3,2},{4,5},{5,4},{6,7},{7,6},{8,9},{9,8},{10,11... | collective-permute-start | bytes 786440 | tf_op jit(solution)/shard_map/ppermute | solution.py:20

commit v10 on v9

v10 whole, which is shorter than its diff:
```python
import jax
import jax.numpy as jnp
from jax import lax
from jax.experimental import pallas as pl
from jax.experimental.pallas import tpu as pltpu
from jax.sharding import PartitionSpec as P

BLOCK = 128
SPAN = 4
CHIPS = 16
DEPTH = 16
OWNERS = 32
SAME_CORE = [[2 * chip + core for chip in range(CHIPS)] for core in range(2)]
TAIL = 8
TOP = 14.0
CORE, EXPERT, SHARE = 4, 5, 6


def swap_across(value):
    return lax.ppermute(value, "exp", [(p, p ^ 2) for p in range(OWNERS)])


def swap_core(value):
    return lax.ppermute(value, "exp", [(p, p ^ 1) for p in range(OWNERS)])


def encode(value, largest):
    exponent = jnp.ceil(jnp.log2(jnp.maximum(largest, 1e-30)))
    scaled = (value.astype(jnp.float32) * jnp.exp2(TOP - exponent)).astype(jnp.float16)
    tail = jnp.broadcast_to(exponent.astype(jnp.float16), (TAIL, value.shape[1]))
    return jnp.concatenate([scaled, tail])


def decode(coded):
    exponent = jnp.max(coded[..., -TAIL:, :], axis=-2, keepdims=True).astype(jnp.float32)
    value = coded[..., :-TAIL, :].astype(jnp.float32) * jnp.exp2(exponent - TOP)
    return value.astype(jnp.bfloat16)


def hidden_kernel(facts, gathered, *refs):
    weights, (out, largest) = refs[:-2], refs[-2:]
    depth = gathered.shape[2]
    total = None
    for number in range(DEPTH):
        rows = pl.ds(number * depth, depth)
        right = jnp.concatenate([weight[kind, rows, :] for kind in range(2) for weight in weights], axis=1)
        term = jnp.dot(gathered[number], right, preferred_element_type=jnp.float32)
        total = term if total is None else total + term
    units = total.shape[1] // 2
    gate, up = total[:, :units], total[:, units:]
    hidden = gate / (1.0 + jnp.exp(-gate)) * up
    out[...] = hidden.astype(out.dtype)
    largest[...] = jnp.max(jnp.abs(hidden), axis=0, keepdims=True)


def down_kernel(facts, gathered, scales, *refs):
    weights, out = refs[:-1], refs[-1]
    depth = gathered.shape[2] // len(weights)
    total = None
    for number in range(DEPTH):
        rows = pl.ds(number * depth, depth)
        right = jnp.concatenate([weight[rows, :] for weight in weights], axis=0)
        term = jnp.dot(gathered[number], right, preferred_element_type=jnp.float32)
        total = term if total is None else total + term
    count = total.shape[0]
    columns = pl.ds(pl.multiple_of(facts[SHARE] * count, count), count)
    scale = scales[pl.ds(facts[EXPERT], 1), columns]
    scale = jnp.broadcast_to(scale, (128, count)).T
    out[...] = (total * scale[:, :1]).astype(out.dtype)


def place_kernel(facts, done, others, out):
    out[...] = jnp.zeros_like(out)
    count = done.shape[0]
    for pick in range(2 * count):
        block = facts[pick]
        source = done if pick < count else others

        @pl.when(lax.rem(block, 2) == facts[CORE])
        def _():
            out[pl.ds(lax.div(block, 2), 1)] = source[pl.ds(pick % count, 1)]


def array_of(*shape):
    return jax.ShapeDtypeStruct(shape, jnp.bfloat16)


def kernel_call(kernel, name, facts, inner, outs, flops):
    in_vmem = pl.BlockSpec(memory_space=pltpu.VMEM)
    return pl.pallas_call(
        kernel,
        out_shape=outs,
        in_specs=[pl.BlockSpec(memory_space=pltpu.SMEM)] + [in_vmem] * len(inner),
        out_specs=[in_vmem] * len(outs),
        compiler_params=pltpu.CompilerParams(vmem_limit_bytes=24 << 20),
        cost_estimate=pl.CostEstimate(
            flops=flops, bytes_accessed=2 * sum(array.size for array in inner), transcendentals=0
        ),
        name=name,
    )(facts, *inner)


def shards(tokens, picked_blocks, gate_scale, w_gate, w_up, w_down):
    position = lax.axis_index("exp")
    core = lax.rem(position, 2)
    expert = position // SPAN
    features, units = tokens.shape[1], w_gate.shape[2]
    chosen = lax.dynamic_index_in_dim(picked_blocks, expert, 0, keepdims=False)
    share = lax.rem(position, SPAN)
    blocks = chosen.shape[0] // SPAN
    rows = blocks * BLOCK
    mine = lax.dynamic_slice_in_dim(chosen, blocks * share, blocks)
    theirs = lax.dynamic_slice_in_dim(chosen, blocks * jnp.bitwise_xor(share, 1), blocks)
    facts = jnp.concatenate([mine, theirs, jnp.stack([core, expert, share]).astype(jnp.int32)])

    in_own, down_own = jnp.stack([w_gate[0], w_up[0]]), w_down[0]
    in_near, down_near = swap_core(in_own), swap_core(down_own)
    largest = jnp.max(jnp.abs(tokens.astype(jnp.float32)), axis=0, keepdims=True)
    coded, facts, mine = lax.optimization_barrier((encode(tokens, largest), facts, mine))
    held = lax.all_gather(coded, "exp")
    held, in_sent, down_sent = lax.optimization_barrier((held, in_own, down_own))
    in_far, down_far = swap_across(in_sent), swap_across(down_sent)
    gathered = lax.all_gather(held[mine], "tok")
    gathered, in_far = lax.optimization_barrier((gathered, in_far))
    in_last = swap_core(in_far)
    flops = 2 * rows * DEPTH * features * 2 * SPAN * units
    hidden, largest = kernel_call(
        hidden_kernel, "hidden", facts,
        [decode(gathered).reshape(DEPTH, rows, features), in_own, in_near, in_far, in_last],
        [array_of(rows, SPAN * units), jax.ShapeDtypeStruct((1, SPAN * units), jnp.float32)], flops,
    )
    gathered = lax.all_gather(encode(hidden, largest)[None], "tok", tiled=True)
    gathered, down_far = lax.optimization_barrier((gathered, down_far))
    down_last = swap_core(down_far)
    (done,) = kernel_call(
        down_kernel, "down", facts, [decode(gathered), gate_scale, down_own, down_near, down_far, down_last],
        [array_of(rows, features)], flops // 2,
    )
    done = done.reshape(blocks, BLOCK, features)

    (outgoing,) = kernel_call(
        place_kernel, "place", facts, [done, swap_core(done)], [array_of(CHIPS, BLOCK, features)], 0
    )
    arrived = lax.all_to_all(outgoing, "exp", 0, 0, axis_index_groups=SAME_CORE, tiled=True)
    return jnp.sum(arrived, axis=0, dtype=jnp.float32).astype(jnp.bfloat16)


def solution(mesh):
    return jax.shard_map(
        shards,
        mesh=mesh,
        in_specs=(
            P("exp", "tok"),
            P(),
            P(),
            P("exp", None, "tok"),
            P("exp", None, "tok"),
            P("exp", None, "tok"),
        ),
        out_specs=P("exp", "tok"),
        check_vma=False,
    )
```

time: 205 us -> 199 us (0.971)
  blocking collectives: 159 us -> 152 us
  other arithmetic: 7.27 us -> 4.49 us
    all_gather x2, blocking collectives: 113 us -> 97.7 us  [the longest x1 55.2 us: shards(): gathered = lax.all_gather(encode(hidden, largest)[None], 'tok', tiled=True)]
    all_gather x1, blocking collectives: 25.4 us -> 32.2 us  [shards(): held = lax.all_gather(coded, 'exp')]
    ppermute x0 -> x2, starting transfers between devices: none -> 5.66 us  [swap_across(): return lax.ppermute(value, 'exp', [(p, p ^ 2) for p in range(OWNERS)])]
    ppermute x4 -> x5, starting transfers between devices: 25.7 us -> 21.5 us  [swap_core(): return lax.ppermute(value, 'exp', [(p, p ^ 1) for p in range(OWNERS)])]
  transfers between devices with their start and end apart: 4 -> 7, of which waited for: 1 -> 2; matrix products, arithmetic and copies ran while one was open for 5% -> 2% of each run, Pallas kernels for 1% -> 2%
where the time goes in v10:
time: 199 us; the launch traced here: 198 us
  blocking collectives  152 us (76%)
  starting transfers between devices  27.1 us (14%)
  Pallas kernels  7.09 us (4%)
  local copies, waits for them, and re-layouts  4.74 us (2%)
  other arithmetic  4.49 us (2%)
  waiting for transfers between devices  2.11 us (1%)
    all_gather x1, blocking collectives, shards(): gathered = lax.all_gather(encode(hidden, largest)[None], 'tok', tiled=True)  55.2 us
    all_gather x1, blocking collectives, shards(): gathered = lax.all_gather(held[mine], 'tok')  42.5 us
    all_gather x1, blocking collectives, shards(): held = lax.all_gather(coded, 'exp')  32.2 us
    all_to_all x1, blocking collectives, shards(): lax.all_to_all(outgoing, 'exp', 0, 0, axis_index_groups=SAME_CORE, tiled=...  22.3 us
    ppermute x5, starting transfers between devices, swap_core(): return lax.ppermute(value, 'exp', [(p, p ^ 1) for p in range(OWNERS)])  21.5 us
    pallas_call x3, Pallas kernels, kernel_call(): pl.pallas_call(kernel, out_shape=outs, in_specs=[pl.BlockSpec(memory_spac...  7.09 us
    ppermute x2, starting transfers between devices, swap_across(): return lax.ppermute(value, 'exp', [(p, p ^ 2) for p in range(OWNERS)])  5.66 us
  transfers between devices with their start and end apart: 7, of which 2 were waited for; matrix products, arithmetic and copies ran while one was open for 2% of the time, Pallas kernels for 2%

profile of v10, /device:TPU:1, one launch (start us, length us, event | category | flops | bytes accessed | tf_op | source)
XLA Modules:
  0.0 198.0 jit_solution(11649854898544365643)
XLA Ops:
  0.0 1.0 fusion
  1.0 0.9 fusion.1
  1.9 0.8 dynamic-slice_bitcast_fusion
  2.7 0.1 concatenate.10.facts
  2.8 32.2 %all-gather.6 = f16[4352,256]{1,0:T(8,128)(2,1)} all-gather(f16[136,256]{1,0:T(8,128)(2,1)S(1)} %pad_maximum_fusion.1), channel_id=2, replica_groups=mesh['tok'=16,'exp'=32] {'exp'}, dimensions={0}, use_global_device_ids=true | all-gather | bytes 2297856 | tf_op jit(solution)/shard_map/all_gather | solution.py:120
  35.0 0.1 constant_dynamic-update-slice_fusion.1
  35.1 0.0 copy-start
  35.1 1.4 constant_dynamic-update-slice_fusion.refs_0_
  36.6 3.2 %collective-permute-start = (bf16[2,4096,128]{2,1,0:T(8,128)(2,1)S(1)}, bf16[2,4096,128]{2,1,0:T(8,128)(2,1)}, u32[]{:S(2)}, u32[]{:S(2)}) collective-permute-start(bf16[2,4096,128]{2,1,0:T(8,128)(2,1)S(1)} %constant_dynamic-update-slice_fusion.refs_0_), channel_id=1, source_target_pairs={{0,2},{1,3},{2,0},{3,1},{4,6},{5,7},{6,4},{7,5},{8,10},{9,11},{10,... | collective-permute-start | bytes 6291464 | tf_op jit(solution)/shard_map/ppermute | solution.py:20
  39.8 2.4 %collective-permute-start.1 = (bf16[2,4096,128]{2,1,0:T(8,128)(2,1)S(1)}, bf16[2,4096,128]{2,1,0:T(8,128)(2,1)}, u32[]{:S(2)}, u32[]{:S(2)}) collective-permute-start(bf16[2,4096,128]{2,1,0:T(8,128)(2,1)S(1)} %constant_dynamic-update-slice_fusion.refs_0_), channel_id=1, source_target_pairs={{0,1},{1,0},{2,3},{3,2},{4,5},{5,4},{6,7},{7,6},{8,9},{9,8},{10,11... | collective-permute-start | bytes 6291464 | tf_op jit(solution)/shard_map/ppermute | solution.py:24
  42.2 2.2 %gather_fusion = f16[2,136,256]{2,1,0:T(8,128)(2,1)S(1)} fusion(f16[32,136,256]{2,1,0:T(8,128)(2,1)} %bitcast.24, s32[1024]{0:T(1024)S(1)} %pad_clamp_fusion), kind=kCustom, calls=%fused_computation | custom fusion | bytes 278536 | tf_op jit(solution)/shard_map/gather | solution.py:123
  44.4 42.5 %all-gather.7 = f16[32,136,256]{2,1,0:T(8,128)(2,1)S(1)} all-gather(f16[2,136,256]{2,1,0:T(8,128)(2,1)S(1)} %gather_fusion), channel_id=3, replica_groups=mesh['tok'=16,'exp'=32] {'tok'}, dimensions={0}, use_global_device_ids=true | all-gather | bytes 2367488 | tf_op jit(solution)/shard_map/all_gather | solution.py:123
  86.9 8.2 %collective-permute-start.2 = (bf16[2,4096,128]{2,1,0:T(8,128)(2,1)}, bf16[2,4096,128]{2,1,0:T(8,128)(2,1)S(1)}, u32[]{:S(2)}, u32[]{:S(2)}) collective-permute-start(bf16[2,4096,128]{2,1,0:T(8,128)(2,1)} %collective-permute-done.refs_2_), channel_id=1, source_target_pairs={{0,1},{1,0},{2,3},{3,2},{4,5},{5,4},{6,7},{7,6},{8,9},{9,8},{10,11... | collective-permute-start | bytes 6291464 | tf_op jit(solution)/shard_map/ppermute | solution.py:24
  95.1 1.9 collective-permute-start.4
  97.1 2.4 %collective-permute-start.3 = (bf16[2048,256]{1,0:T(8,128)(2,1)S(1)}, bf16[2048,256]{1,0:T(8,128)(2,1)S(1)}, u32[]{:S(2)}, u32[]{:S(2)}) collective-permute-start(bf16[2048,256]{1,0:T(8,128)(2,1)S(1)} %bitcast.16), channel_id=1, source_target_pairs={{0,2},{1,3},{2,0},{3,1},{4,6},{5,7},{6,4},{7,5},{8,10},{9,11},{10,... | collective-permute-start | bytes 3145736 | tf_op jit(solution)/shard_map/ppermute | solution.py:20
  99.5 0.1 slice_reduce_fusion.1
  99.7 0.5 multiply_convert_fusion.1
  100.2 4.6 %hidden.1 = (bf16[256,512]{1,0:T(8,128)(2,1)S(1)}, f32[1,512]{1,0:T(1,128)S(1)}) custom-call(s32[7]{0:T(128)S(1)} %concatenate.10.facts, bf16[16,256,256]{2,1,0:T(8,128)(2,1)S(1)} %bitcast.14, bf16[2,4096,128]{2,1,0:T(8,128)(2,1)S(1)} %constant_dynamic-update-slice_fusion.refs_0_, bf16[2,4096,128]{2,1,0:T(8,128)(2,1)} %collective-permute-done.1.refs_1_, ...), custom_call_target="tpu_custom_call" | custom-call | flops 2147483648 | bytes 10485760 | tf_op jit(solution)/shard_map/hidden/pallas_call | solution.py:90
  104.9 0.1 multiply_convert_fusion.2
  105.0 0.1 pad_maximum_fusion
  105.0 55.2 %all-gather.8 = f16[4224,512]{1,0:T(8,128)(2,1)S(1)} all-gather(f16[264,512]{1,0:T(8,128)(2,1)S(1)} %pad_maximum_fusion), channel_id=4, replica_groups=mesh['tok'=16,'exp'=32] {'tok'}, dimensions={0}, use_global_device_ids=true | all-gather | bytes 4595712 | tf_op jit(solution)/shard_map/all_gather | solution.py:132
  160.3 6.7 %collective-permute-start.5 = (bf16[2048,256]{1,0:T(8,128)(2,1)S(1)}, bf16[2048,256]{1,0:T(8,128)(2,1)S(1)}, u32[]{:S(2)}, u32[]{:S(2)}) collective-permute-start(bf16[2048,256]{1,0:T(8,128)(2,1)S(1)} %collective-permute-done.3.refs_2_), channel_id=1, source_target_pairs={{0,1},{1,0},{2,3},{3,2},{4,5},{5,4},{6,7},{7,6},{8,9},{9,8},{10,11... | collective-permute-start | bytes 3145736 | tf_op jit(solution)/shard_map/ppermute | solution.py:24
  167.0 0.1 slice_reduce_fusion
  167.1 0.0 copy-start.1
  167.1 1.0 multiply_convert_fusion.gathered
  168.1 1.1 collective-permute-done.5.refs_3_
  169.3 1.8 down.1
  171.0 2.3 %collective-permute-start.6 = (bf16[2,128,256]{2,1,0:T(8,128)(2,1)S(1)}, bf16[2,128,256]{2,1,0:T(8,128)(2,1)S(1)}, u32[]{:S(2)}, u32[]{:S(2)}) collective-permute-start(bf16[2,128,256]{2,1,0:T(8,128)(2,1)S(1)} %bitcast.18), channel_id=1, source_target_pairs={{0,1},{1,0},{2,3},{3,2},{4,5},{5,4},{6,7},{7,6},{8,9},{9,8},{10,11... | collective-permute-start | bytes 393224 | tf_op jit(solution)/shard_map/ppermute | solution.py:24
  173.3 1.0 collective-permute-done.6.others
  174.3 0.7 place.1
  175.0 22.3 %all_to_all.5 = bf16[16,128,256]{2,1,0:T(8,128)(2,1)S(1)} all-to-all(bf16[16,128,256]{2,1,0:T(8,128)(2,1)S(1)} %place.1), channel_id=1, replica_groups={{0,2,4,6,8,10,12,14,16,18,20,22,24,26,28,30},{1,3,5,7,9,11,13,15,17,19,..., dimensions={0} | all-to-all | bytes 2097152 | tf_op jit(solution)/shard_map/all_to_all | solution.py:144
  197.2 0.8 reduce_sum.12
  (20 shorter events, 0.2 us)
Async XLA Ops:
  0.0 35.0 %copy-start.2 = (bf16[1,4096,128]{2,1,0:T(8,128)(2,1)S(1)}, bf16[1,4096,128]{2,1,0:T(8,128)(2,1)}, u32[]{:S(2)}) copy-start(bf16[1,4096,128]{2,1,0:T(8,128)(2,1)} %param.9) | copy-start | bytes 3145732
  35.1 60.0 %copy-start = (bf16[1,2048,256]{2,1,0:T(8,128)(2,1)S(1)}, bf16[1,2048,256]{2,1,0:T(8,128)(2,1)}, u32[]{:S(2)}) copy-start(bf16[1,2048,256]{2,1,0:T(8,128)(2,1)} %param.11) | copy-start | bytes 3145732
  36.6 50.3 %collective-permute-start = (bf16[2,4096,128]{2,1,0:T(8,128)(2,1)S(1)}, bf16[2,4096,128]{2,1,0:T(8,128)(2,1)}, u32[]{:S(2)}, u32[]{:S(2)}) collective-permute-start(bf16[2,4096,128]{2,1,0:T(8,128)(2,1)S(1)} %constant_dynamic-update-slice_fusion.refs_0_), channel_id=1, source_target_pairs={{0,2},{1,3},{2,0},{3,1},{4,6},{5,7},{6,4},{7,5},{8,10},{9,11},{10,... | collective-permute-start | bytes 6291464 | tf_op jit(solution)/shard_map/ppermute | solution.py:20
  39.8 60.4 %collective-permute-start.1 = (bf16[2,4096,128]{2,1,0:T(8,128)(2,1)S(1)}, bf16[2,4096,128]{2,1,0:T(8,128)(2,1)}, u32[]{:S(2)}, u32[]{:S(2)}) collective-permute-start(bf16[2,4096,128]{2,1,0:T(8,128)(2,1)S(1)} %constant_dynamic-update-slice_fusion.refs_0_), channel_id=1, source_target_pairs={{0,1},{1,0},{2,3},{3,2},{4,5},{5,4},{6,7},{7,6},{8,9},{9,8},{10,11... | collective-permute-start | bytes 6291464 | tf_op jit(solution)/shard_map/ppermute | solution.py:24
  86.9 13.3 %collective-permute-start.2 = (bf16[2,4096,128]{2,1,0:T(8,128)(2,1)}, bf16[2,4096,128]{2,1,0:T(8,128)(2,1)S(1)}, u32[]{:S(2)}, u32[]{:S(2)}) collective-permute-start(bf16[2,4096,128]{2,1,0:T(8,128)(2,1)} %collective-permute-done.refs_2_), channel_id=1, source_target_pairs={{0,1},{1,0},{2,3},{3,2},{4,5},{5,4},{6,7},{7,6},{8,9},{9,8},{10,11... | collective-permute-start | bytes 6291464 | tf_op jit(solution)/shard_map/ppermute | solution.py:24
  95.1 73.0 %collective-permute-start.4 = (bf16[2048,256]{1,0:T(8,128)(2,1)S(1)}, bf16[2048,256]{1,0:T(8,128)(2,1)S(1)}, u32[]{:S(2)}, u32[]{:S(2)}) collective-permute-start(bf16[2048,256]{1,0:T(8,128)(2,1)S(1)} %bitcast.15), channel_id=1, source_target_pairs={{0,1},{1,0},{2,3},{3,2},{4,5},{5,4},{6,7},{7,6},{8,9},{9,8},{10,11... | collective-permute-start | bytes 3145736 | tf_op jit(solution)/shard_map/ppermute | solution.py:24
  97.1 63.2 %collective-permute-start.3 = (bf16[2048,256]{1,0:T(8,128)(2,1)S(1)}, bf16[2048,256]{1,0:T(8,128)(2,1)S(1)}, u32[]{:S(2)}, u32[]{:S(2)}) collective-permute-start(bf16[2048,256]{1,0:T(8,128)(2,1)S(1)} %bitcast.16), channel_id=1, source_target_pairs={{0,2},{1,3},{2,0},{3,1},{4,6},{5,7},{6,4},{7,5},{8,10},{9,11},{10,... | collective-permute-start | bytes 3145736 | tf_op jit(solution)/shard_map/ppermute | solution.py:20
  160.3 9.0 %collective-permute-start.5 = (bf16[2048,256]{1,0:T(8,128)(2,1)S(1)}, bf16[2048,256]{1,0:T(8,128)(2,1)S(1)}, u32[]{:S(2)}, u32[]{:S(2)}) collective-permute-start(bf16[2048,256]{1,0:T(8,128)(2,1)S(1)} %collective-permute-done.3.refs_2_), channel_id=1, source_target_pairs={{0,1},{1,0},{2,3},{3,2},{4,5},{5,4},{6,7},{7,6},{8,9},{9,8},{10,11... | collective-permute-start | bytes 3145736 | tf_op jit(solution)/shard_map/ppermute | solution.py:24
  167.1 2.1 %copy-start.1 = (f32[8,1024]{1,0:T(8,128)S(1)}, f32[8,1024]{1,0:T(8,128)}, u32[]{:S(2)}) copy-start(f32[8,1024]{1,0:T(8,128)} %scales.1) | copy-start | bytes 98308
  171.0 3.3 %collective-permute-start.6 = (bf16[2,128,256]{2,1,0:T(8,128)(2,1)S(1)}, bf16[2,128,256]{2,1,0:T(8,128)(2,1)S(1)}, u32[]{:S(2)}, u32[]{:S(2)}) collective-permute-start(bf16[2,128,256]{2,1,0:T(8,128)(2,1)S(1)} %bitcast.18), channel_id=1, source_target_pairs={{0,1},{1,0},{2,3},{3,2},{4,5},{5,4},{6,7},{7,6},{8,9},{9,8},{10,11... | collective-permute-start | bytes 393224 | tf_op jit(solution)/shard_map/ppermute | solution.py:24

commit v11 on v10

--- a/solution.py
+++ b/solution.py
@@ -54,7 +54,7 @@
 
 
 def down_kernel(facts, gathered, scales, *refs):
-    weights, out = refs[:-1], refs[-1]
+    weights, (kept, given) = refs[:-2], refs[-2:]
     depth = gathered.shape[2] // len(weights)
     total = None
     for number in range(DEPTH):
@@ -62,23 +62,27 @@
         right = jnp.concatenate([weight[rows, :] for weight in weights], axis=0)
         term = jnp.dot(gathered[number], right, preferred_element_type=jnp.float32)
         total = term if total is None else total + term
-    count = total.shape[0]
-    columns = pl.ds(pl.multiple_of(facts[SHARE] * count, count), count)
-    scale = scales[pl.ds(facts[EXPERT], 1), columns]
-    scale = jnp.broadcast_to(scale, (128, count)).T
-    out[...] = (total * scale[:, :1]).astype(out.dtype)
+    count = total.shape[0] // 2
+    parts = []
+    for share in (facts[SHARE], facts[SHARE] + 1 - 2 * facts[CORE]):
+        columns = pl.ds(pl.multiple_of(share * count, count), count)
+        parts.append(scales[pl.ds(facts[EXPERT], 1), columns])
+    scale = jnp.broadcast_to(jnp.concatenate(parts, axis=1), (128, 2 * count)).T
+    total = total * scale[:, :1]
+    kept[...] = total
+    given[...] = total.astype(given.dtype)
 
 
-def place_kernel(facts, done, others, out):
+def place_kernel(facts, kept, taken, out):
     out[...] = jnp.zeros_like(out)
-    count = done.shape[0]
-    for pick in range(2 * count):
+    count = kept.shape[0]
+    for pick in range(count):
         block = facts[pick]
-        source = done if pick < count else others
 
         @pl.when(lax.rem(block, 2) == facts[CORE])
         def _():
-            out[pl.ds(lax.div(block, 2), 1)] = source[pl.ds(pick % count, 1)]
+            both = kept[pick] + taken[(pick + count // 2) % count].astype(jnp.float32)
+            out[pl.ds(lax.div(block, 2), 1)] = both.astype(out.dtype)[None]
 
 
 def array_of(*shape):
@@ -114,32 +118,28 @@
     facts = jnp.concatenate([mine, theirs, jnp.stack([core, expert, share]).astype(jnp.int32)])
 
     in_own, down_own = jnp.stack([w_gate[0], w_up[0]]), w_down[0]
-    in_near, down_near = swap_core(in_own), swap_core(down_own)
     largest = jnp.max(jnp.abs(tokens.astype(jnp.float32)), axis=0, keepdims=True)
     coded, facts, mine = lax.optimization_barrier((encode(tokens, largest), facts, mine))
     held = lax.all_gather(coded, "exp")
     held, in_sent, down_sent = lax.optimization_barrier((held, in_own, down_own))
     in_far, down_far = swap_across(in_sent), swap_across(down_sent)
-    gathered = lax.all_gather(held[mine], "tok")
-    gathered, in_far = lax.optimization_barrier((gathered, in_far))
-    in_last = swap_core(in_far)
-    flops = 2 * rows * DEPTH * features * 2 * SPAN * units
+    gathered, in_far = lax.optimization_barrier((lax.all_gather(held[mine], "tok"), in_far))
+    gathered = decode(jnp.concatenate([gathered, swap_core(gathered)], axis=1)).reshape(DEPTH, 2 * rows, features)
+    flops = 4 * rows * DEPTH * features * SPAN * units
     hidden, largest = kernel_call(
-        hidden_kernel, "hidden", facts,
-        [decode(gathered).reshape(DEPTH, rows, features), in_own, in_near, in_far, in_last],
-        [array_of(rows, SPAN * units), jax.ShapeDtypeStruct((1, SPAN * units), jnp.float32)], flops,
+        hidden_kernel, "hidden", facts, [gathered, in_own, in_far],
+        [array_of(2 * rows, 2 * units), jax.ShapeDtypeStruct((1, 2 * units), jnp.float32)], flops,
     )
     gathered = lax.all_gather(encode(hidden, largest)[None], "tok", tiled=True)
-    gathered, down_far = lax.optimization_barrier((gathered, down_far))
-    down_last = swap_core(down_far)
-    (done,) = kernel_call(
-        down_kernel, "down", facts, [decode(gathered), gate_scale, down_own, down_near, down_far, down_last],
-        [array_of(rows, features)], flops // 2,
+    kept, given = kernel_call(
+        down_kernel, "down", facts, [decode(gathered), gate_scale, down_own, down_far],
+        [jax.ShapeDtypeStruct((2 * rows, features), jnp.float32), array_of(2 * rows, features)], flops // 2,
     )
-    done = done.reshape(blocks, BLOCK, features)
 
+    whole = (2 * blocks, BLOCK, features)
     (outgoing,) = kernel_call(
-        place_kernel, "place", facts, [done, swap_core(done)], [array_of(CHIPS, BLOCK, features)], 0
+        place_kernel, "place", facts, [kept.reshape(whole), swap_core(given).reshape(whole)],
+        [array_of(CHIPS, BLOCK, features)], 0,
     )
     arrived = lax.all_to_all(outgoing, "exp", 0, 0, axis_index_groups=SAME_CORE, tiled=True)
     return jnp.sum(arrived, axis=0, dtype=jnp.float32).astype(jnp.bfloat16)

time: 199 us -> 192 us (0.965)
  starting transfers between devices: 27.1 us -> 21 us
  blocking collectives: 152 us -> 149 us
    ppermute x5 -> x2, starting transfers between devices: 21.5 us -> 15.3 us  [swap_core(): return lax.ppermute(value, 'exp', [(p, p ^ 1) for p in range(OWNERS)])]
  transfers between devices with their start and end apart: 7 -> 4, of which waited for: 2 -> 3; matrix products, arithmetic and copies ran while one was open for 2% -> 3% of each run, Pallas kernels for 2% -> 2%
where the time goes in v11:
time: 192 us
  blocking collectives  149 us (78%)
  starting transfers between devices  21 us (11%)
  Pallas kernels  6.43 us (3%)
  local copies, waits for them, and re-layouts  5.81 us (3%)
  other arithmetic  5.23 us (3%)
  waiting for transfers between devices  3.97 us (2%)
    all_gather x1, blocking collectives, shards(): gathered = lax.all_gather(encode(hidden, largest)[None], 'tok', tiled=True)  54.4 us
    all_gather x1, blocking collectives, shards(): lax.all_gather(held[mine], 'tok')  41.7 us
    all_gather x1, blocking collectives, shards(): held = lax.all_gather(coded, 'exp')  32.4 us
    all_to_all x1, blocking collectives, shards(): lax.all_to_all(outgoing, 'exp', 0, 0, axis_index_groups=SAME_CORE, tiled=...  20.7 us
    ppermute x2, starting transfers between devices, swap_core(): return lax.ppermute(value, 'exp', [(p, p ^ 1) for p in range(OWNERS)])  15.3 us
    pallas_call x3, Pallas kernels, kernel_call(): pl.pallas_call(kernel, out_shape=outs, in_specs=[pl.BlockSpec(memory_spac...  6.43 us
    ppermute x2, starting transfers between devices, swap_across(): return lax.ppermute(value, 'exp', [(p, p ^ 2) for p in range(OWNERS)])  5.66 us
  transfers between devices with their start and end apart: 4, of which 3 were waited for; matrix products, arithmetic and copies ran while one was open for 3% of the time, Pallas kernels for 2%

profile of v11, /device:TPU:1, one launch (start us, length us, event | category | flops | bytes accessed | tf_op | source)
XLA Modules:
  0.0 191.8 jit_solution(9471980098501627592)
XLA Ops:
  0.0 0.9 fusion
  0.9 0.9 fusion.1
  1.8 0.8 dynamic-slice_bitcast_fusion
  2.7 0.1 concatenate.13.facts
  2.7 32.4 %all-gather.6 = f16[4352,256]{1,0:T(8,128)(2,1)} all-gather(f16[136,256]{1,0:T(8,128)(2,1)S(1)} %pad_maximum_fusion.1), channel_id=2, replica_groups=mesh['tok'=16,'exp'=32] {'exp'}, dimensions={0}, use_global_device_ids=true | all-gather | bytes 2297856 | tf_op jit(solution)/shard_map/all_gather | solution.py:123
  35.1 1.3 constant_dynamic-update-slice_fusion.1
  36.4 0.0 copy-done.2
  36.4 0.1 constant_dynamic-update-slice_fusion.refs_0_
  36.6 3.2 %collective-permute-start = (bf16[2,4096,128]{2,1,0:T(8,128)(2,1)S(1)}, bf16[2,4096,128]{2,1,0:T(8,128)(2,1)}, u32[]{:S(2)}, u32[]{:S(2)}) collective-permute-start(bf16[2,4096,128]{2,1,0:T(8,128)(2,1)S(1)} %constant_dynamic-update-slice_fusion.refs_0_), channel_id=1, source_target_pairs={{0,2},{1,3},{2,0},{3,1},{4,6},{5,7},{6,4},{7,5},{8,10},{9,11},{10,... | collective-permute-start | bytes 6291464 | tf_op jit(solution)/shard_map/ppermute | solution.py:20
  39.8 2.2 %gather_fusion = f16[2,136,256]{2,1,0:T(8,128)(2,1)S(1)} fusion(f16[32,136,256]{2,1,0:T(8,128)(2,1)} %bitcast.24, s32[1024]{0:T(1024)S(1)} %pad_clamp_fusion), kind=kCustom, calls=%fused_computation | custom fusion | bytes 278536 | tf_op jit(solution)/shard_map/gather | solution.py:126
  42.0 41.7 %all-gather.7 = f16[32,136,256]{2,1,0:T(8,128)(2,1)S(1)} all-gather(f16[2,136,256]{2,1,0:T(8,128)(2,1)S(1)} %gather_fusion), channel_id=3, replica_groups=mesh['tok'=16,'exp'=32] {'tok'}, dimensions={0}, use_global_device_ids=true | all-gather | bytes 2367488 | tf_op jit(solution)/shard_map/all_gather | solution.py:126
  83.7 1.9 %collective-permute-done.refs_1_ = bf16[2,4096,128]{2,1,0:T(8,128)(2,1)} collective-permute-done((bf16[2,4096,128]{2,1,0:T(8,128)(2,1)S(1)}, bf16[2,4096,128]{2,1,0:T(8,128)(2,1)}, u32[]{:S(2)}, u32[]{:S(2)}) %collective-permute-start) | collective-permute-done | bytes 2097184 | tf_op jit(solution)/shard_map/ppermute | solution.py:20
  85.6 7.1 %collective-permute-start.1 = (f16[16,2,136,256]{3,2,1,0:T(8,128)(2,1)S(1)}, f16[16,2,136,256]{3,2,1,0:T(8,128)(2,1)S(1)}, u32[]{:S(2)}, u32[]{:S(2)}) collective-permute-start(f16[16,2,136,256]{3,2,1,0:T(8,128)(2,1)S(1)} %bitcast.22), channel_id=1, source_target_pairs={{0,1},{1,0},{2,3},{3,2},{4,5},{5,4},{6,7},{7,6},{8,9},{9,8},{10,11... | collective-permute-start | bytes 6684680 | tf_op jit(solution)/shard_map/ppermute | solution.py:24
  92.7 2.4 %collective-permute-start.2 = (bf16[2048,256]{1,0:T(8,128)(2,1)S(1)}, bf16[2048,256]{1,0:T(8,128)(2,1)S(1)}, u32[]{:S(2)}, u32[]{:S(2)}) collective-permute-start(bf16[2048,256]{1,0:T(8,128)(2,1)S(1)} %bitcast.16), channel_id=1, source_target_pairs={{0,2},{1,3},{2,0},{3,1},{4,6},{5,7},{6,4},{7,5},{8,10},{9,11},{10,... | collective-permute-start | bytes 3145736 | tf_op jit(solution)/shard_map/ppermute | solution.py:20
  95.2 0.6 constant_dynamic-update-slice_fusion.3
  95.8 0.9 collective-permute-done.1
  96.7 0.6 constant_dynamic-update-slice_fusion.2
  97.3 0.2 slice_reduce_fusion
  97.5 1.3 multiply_convert_fusion.1
  98.8 4.0 %hidden.1 = (bf16[512,256]{1,0:T(8,128)(2,1)S(1)}, f32[1,256]{1,0:T(1,128)S(1)}) custom-call(s32[7]{0:T(128)S(1)} %concatenate.13.facts, bf16[16,512,256]{2,1,0:T(8,128)(2,1)S(1)} %bitcast.15, bf16[2,4096,128]{2,1,0:T(8,128)(2,1)S(1)} %constant_dynamic-update-slice_fusion.refs_0_, bf16[2,4096,128]{2,1,0:T(8,128)(2,1)} %collective-permute-done.refs_1_), custom_call_target="tpu_custom_call" | custom-call | flops 2147483648 | bytes 8388608 | tf_op jit(solution)/shard_map/hidden/pallas_call | solution.py:94
  102.8 0.1 multiply_convert_fusion.2
  102.9 0.1 pad_maximum_fusion
  103.0 54.4 %all-gather.8 = f16[8320,256]{1,0:T(8,128)(2,1)S(1)} all-gather(f16[520,256]{1,0:T(8,128)(2,1)S(1)} %pad_maximum_fusion), channel_id=4, replica_groups=mesh['tok'=16,'exp'=32] {'tok'}, dimensions={0}, use_global_device_ids=true | all-gather | bytes 4526080 | tf_op jit(solution)/shard_map/all_gather | solution.py:133
  157.5 0.0 copy-start.1
  157.5 1.0 multiply_convert_fusion.gathered
  158.5 0.0 collective-permute-done.2.refs_1_
  158.5 1.8 down.1
  160.3 8.2 %collective-permute-start.3 = (bf16[512,256]{1,0:T(8,128)(2,1)S(1)}, bf16[512,256]{1,0:T(8,128)(2,1)S(1)}, u32[]{:S(2)}, u32[]{:S(2)}) collective-permute-start(bf16[512,256]{1,0:T(8,128)(2,1)S(1)} %get-tuple-element.28), channel_id=1, source_target_pairs={{0,1},{1,0},{2,3},{3,2},{4,5},{5,4},{6,7},{7,6},{8,9},{9,8},{10,11... | collective-permute-start | bytes 786440 | tf_op jit(solution)/shard_map/ppermute | solution.py:24
  168.5 1.1 collective-permute-done.3
  169.7 0.7 place.1
  170.3 20.7 %all_to_all.5 = bf16[16,128,256]{2,1,0:T(8,128)(2,1)S(1)} all-to-all(bf16[16,128,256]{2,1,0:T(8,128)(2,1)S(1)} %place.1), channel_id=1, replica_groups={{0,2,4,6,8,10,12,14,16,18,20,22,24,26,28,30},{1,3,5,7,9,11,13,15,17,19,..., dimensions={0} | all-to-all | bytes 2097152 | tf_op jit(solution)/shard_map/all_to_all | solution.py:144
  191.0 0.8 reduce_sum.12
  (15 shorter events, 0.2 us)
Async XLA Ops:
  2.7 33.7 %copy-start.2 = (bf16[1,4096,128]{2,1,0:T(8,128)(2,1)S(1)}, bf16[1,4096,128]{2,1,0:T(8,128)(2,1)}, u32[]{:S(2)}) copy-start(bf16[1,4096,128]{2,1,0:T(8,128)(2,1)} %param.10) | copy-start | bytes 3145732
  2.7 90.0 %copy-start = (bf16[1,2048,256]{2,1,0:T(8,128)(2,1)S(1)}, bf16[1,2048,256]{2,1,0:T(8,128)(2,1)}, u32[]{:S(2)}) copy-start(bf16[1,2048,256]{2,1,0:T(8,128)(2,1)} %param.11) | copy-start | bytes 3145732
  36.6 49.1 %collective-permute-start = (bf16[2,4096,128]{2,1,0:T(8,128)(2,1)S(1)}, bf16[2,4096,128]{2,1,0:T(8,128)(2,1)}, u32[]{:S(2)}, u32[]{:S(2)}) collective-permute-start(bf16[2,4096,128]{2,1,0:T(8,128)(2,1)S(1)} %constant_dynamic-update-slice_fusion.refs_0_), channel_id=1, source_target_pairs={{0,2},{1,3},{2,0},{3,1},{4,6},{5,7},{6,4},{7,5},{8,10},{9,11},{10,... | collective-permute-start | bytes 6291464 | tf_op jit(solution)/shard_map/ppermute | solution.py:20
  85.6 11.1 %collective-permute-start.1 = (f16[16,2,136,256]{3,2,1,0:T(8,128)(2,1)S(1)}, f16[16,2,136,256]{3,2,1,0:T(8,128)(2,1)S(1)}, u32[]{:S(2)}, u32[]{:S(2)}) collective-permute-start(f16[16,2,136,256]{3,2,1,0:T(8,128)(2,1)S(1)} %bitcast.22), channel_id=1, source_target_pairs={{0,1},{1,0},{2,3},{3,2},{4,5},{5,4},{6,7},{7,6},{8,9},{9,8},{10,11... | collective-permute-start | bytes 6684680 | tf_op jit(solution)/shard_map/ppermute | solution.py:24
  92.7 65.7 %collective-permute-start.2 = (bf16[2048,256]{1,0:T(8,128)(2,1)S(1)}, bf16[2048,256]{1,0:T(8,128)(2,1)S(1)}, u32[]{:S(2)}, u32[]{:S(2)}) collective-permute-start(bf16[2048,256]{1,0:T(8,128)(2,1)S(1)} %bitcast.16), channel_id=1, source_target_pairs={{0,2},{1,3},{2,0},{3,1},{4,6},{5,7},{6,4},{7,5},{8,10},{9,11},{10,... | collective-permute-start | bytes 3145736 | tf_op jit(solution)/shard_map/ppermute | solution.py:20
  157.5 1.0 copy-start.1
  160.3 9.4 %collective-permute-start.3 = (bf16[512,256]{1,0:T(8,128)(2,1)S(1)}, bf16[512,256]{1,0:T(8,128)(2,1)S(1)}, u32[]{:S(2)}, u32[]{:S(2)}) collective-permute-start(bf16[512,256]{1,0:T(8,128)(2,1)S(1)} %get-tuple-element.28), channel_id=1, source_target_pairs={{0,1},{1,0},{2,3},{3,2},{4,5},{5,4},{6,7},{7,6},{8,9},{9,8},{10,11... | collective-permute-start | bytes 786440 | tf_op jit(solution)/shard_map/ppermute | solution.py:24

commit v12 on v11

--- a/solution.py
+++ b/solution.py
@@ -10,10 +10,11 @@
 CHIPS = 16
 DEPTH = 16
 OWNERS = 32
+LINES = [[z * OWNERS + 2 * chip + core for z in range(DEPTH) for core in range(2)] for chip in range(CHIPS)]
 SAME_CORE = [[2 * chip + core for chip in range(CHIPS)] for core in range(2)]
 TAIL = 8
 TOP = 14.0
-CORE, EXPERT, SHARE = 4, 5, 6
+CORE, EXPERT, HALF = 4, 5, 6
 
 
 def swap_across(value):
@@ -62,12 +63,9 @@
         right = jnp.concatenate([weight[rows, :] for weight in weights], axis=0)
         term = jnp.dot(gathered[number], right, preferred_element_type=jnp.float32)
         total = term if total is None else total + term
-    count = total.shape[0] // 2
-    parts = []
-    for share in (facts[SHARE], facts[SHARE] + 1 - 2 * facts[CORE]):
-        columns = pl.ds(pl.multiple_of(share * count, count), count)
-        parts.append(scales[pl.ds(facts[EXPERT], 1), columns])
-    scale = jnp.broadcast_to(jnp.concatenate(parts, axis=1), (128, 2 * count)).T
+    count = total.shape[0]
+    columns = pl.ds(pl.multiple_of(facts[HALF] * count, count), count)
+    scale = jnp.broadcast_to(scales[pl.ds(facts[EXPERT], 1), columns], (128, count)).T
     total = total * scale[:, :1]
     kept[...] = total
     given[...] = total.astype(given.dtype)
@@ -81,7 +79,7 @@
 
         @pl.when(lax.rem(block, 2) == facts[CORE])
         def _():
-            both = kept[pick] + taken[(pick + count // 2) % count].astype(jnp.float32)
+            both = kept[pick] + taken[pick].astype(jnp.float32)
             out[pl.ds(lax.div(block, 2), 1)] = both.astype(out.dtype)[None]
 
 
@@ -110,12 +108,12 @@
     expert = position // SPAN
     features, units = tokens.shape[1], w_gate.shape[2]
     chosen = lax.dynamic_index_in_dim(picked_blocks, expert, 0, keepdims=False)
-    share = lax.rem(position, SPAN)
-    blocks = chosen.shape[0] // SPAN
-    rows = blocks * BLOCK
-    mine = lax.dynamic_slice_in_dim(chosen, blocks * share, blocks)
-    theirs = lax.dynamic_slice_in_dim(chosen, blocks * jnp.bitwise_xor(share, 1), blocks)
-    facts = jnp.concatenate([mine, theirs, jnp.stack([core, expert, share]).astype(jnp.int32)])
+    side = lax.rem(position, SPAN) // 2
+    half = chosen.shape[0] // 2
+    rows = half * BLOCK
+    picks = lax.dynamic_slice_in_dim(chosen, half * side, half)
+    mine = lax.dynamic_slice_in_dim(picks, half // 2 * core, half // 2)
+    facts = jnp.concatenate([picks, jnp.stack([core, expert, side]).astype(jnp.int32)])
 
     in_own, down_own = jnp.stack([w_gate[0], w_up[0]]), w_down[0]
     largest = jnp.max(jnp.abs(tokens.astype(jnp.float32)), axis=0, keepdims=True)
@@ -123,20 +121,21 @@
     held = lax.all_gather(coded, "exp")
     held, in_sent, down_sent = lax.optimization_barrier((held, in_own, down_own))
     in_far, down_far = swap_across(in_sent), swap_across(down_sent)
-    gathered, in_far = lax.optimization_barrier((lax.all_gather(held[mine], "tok"), in_far))
-    gathered = decode(jnp.concatenate([gathered, swap_core(gathered)], axis=1)).reshape(DEPTH, 2 * rows, features)
-    flops = 4 * rows * DEPTH * features * SPAN * units
+    gathered = lax.all_gather(held[mine], ("tok", "exp"), axis_index_groups=LINES)
+    gathered, in_far = lax.optimization_barrier((gathered, in_far))
+    gathered = decode(gathered).reshape(DEPTH, rows, features)
+    flops = 2 * rows * DEPTH * features * SPAN * units
     hidden, largest = kernel_call(
         hidden_kernel, "hidden", facts, [gathered, in_own, in_far],
-        [array_of(2 * rows, 2 * units), jax.ShapeDtypeStruct((1, 2 * units), jnp.float32)], flops,
+        [array_of(rows, 2 * units), jax.ShapeDtypeStruct((1, 2 * units), jnp.float32)], flops,
     )
     gathered = lax.all_gather(encode(hidden, largest)[None], "tok", tiled=True)
     kept, given = kernel_call(
         down_kernel, "down", facts, [decode(gathered), gate_scale, down_own, down_far],
-        [jax.ShapeDtypeStruct((2 * rows, features), jnp.float32), array_of(2 * rows, features)], flops // 2,
+        [jax.ShapeDtypeStruct((rows, features), jnp.float32), array_of(rows, features)], flops // 2,
     )
 
-    whole = (2 * blocks, BLOCK, features)
+    whole = (half, BLOCK, features)
     (outgoing,) = kernel_call(
         place_kernel, "place", facts, [kept.reshape(whole), swap_core(given).reshape(whole)],
         [array_of(CHIPS, BLOCK, features)], 0,

time: 192 us -> 188 us (0.979)
  blocking collectives: 149 us -> 156 us
  starting transfers between devices: 21 us -> 14.6 us
  waiting for transfers between devices: 3.97 us -> 1.15 us
    all_gather x1, blocking collectives: 41.7 us -> 49.4 us  [shards(): lax.all_gather(held[mine], ('tok', 'exp'), axis_index_groups=LINES)]
    ppermute x2 -> x1, starting transfers between devices: 15.3 us -> 9.35 us  [swap_core(): return lax.ppermute(value, 'exp', [(p, p ^ 1) for p in range(OWNERS)])]
    ppermute x2, waiting for transfers between devices: 1.93 us -> 0.01 us  [swap_across(): return lax.ppermute(value, 'exp', [(p, p ^ 2) for p in range(OWNERS)])]
  transfers between devices with their start and end apart: 4 -> 3, of which waited for: 3 -> 1; matrix products, arithmetic and copies ran while one was open for 3% -> 3% of each run, Pallas kernels for 2% -> 2%
where the time goes in v12:
time: 188 us
  blocking collectives  156 us (83%)
  starting transfers between devices  14.6 us (8%)
  Pallas kernels  7.15 us (4%)
  other arithmetic  5.35 us (3%)
  local copies, waits for them, and re-layouts  3.91 us (2%)
    all_gather x1, blocking collectives, shards(): gathered = lax.all_gather(encode(hidden, largest)[None], 'tok', tiled=True)  53.2 us
    all_gather x1, blocking collectives, shards(): lax.all_gather(held[mine], ('tok', 'exp'), axis_index_groups=LINES)  49.4 us
    all_gather x1, blocking collectives, shards(): held = lax.all_gather(coded, 'exp')  32.4 us
    all_to_all x1, blocking collectives, shards(): lax.all_to_all(outgoing, 'exp', 0, 0, axis_index_groups=SAME_CORE, tiled=...  20.7 us
    ppermute x1, starting transfers between devices, swap_core(): return lax.ppermute(value, 'exp', [(p, p ^ 1) for p in range(OWNERS)])  9.35 us
    pallas_call x3, Pallas kernels, kernel_call(): pl.pallas_call(kernel, out_shape=outs, in_specs=[pl.BlockSpec(memory_spac...  7.15 us
    ppermute x2, starting transfers between devices, swap_across(): return lax.ppermute(value, 'exp', [(p, p ^ 2) for p in range(OWNERS)])  5.28 us
  transfers between devices with their start and end apart: 3, of which 1 were waited for; matrix products, arithmetic and copies ran while one was open for 3% of the time, Pallas kernels for 2%

profile of v12, /device:TPU:1, one launch (start us, length us, event | category | flops | bytes accessed | tf_op | source)
XLA Modules:
  0.0 188.0 jit_solution(12944568401934908532)
XLA Ops:
  0.0 0.0 copy-start
  0.0 1.0 fusion
  1.0 0.9 fusion.1
  1.9 0.0 copy-done
  1.9 0.0 copy-start.3
  1.9 0.1 dynamic-slice_bitcast_fusion.1
  2.0 0.1 dynamic-slice_bitcast_fusion
  2.1 0.1 pad_add_fusion.facts
  2.2 32.4 %all-gather.6 = f16[4352,256]{1,0:T(8,128)(2,1)} all-gather(f16[136,256]{1,0:T(8,128)(2,1)S(1)} %pad_maximum_fusion.1), channel_id=2, replica_groups=mesh['tok'=16,'exp'=32] {'exp'}, dimensions={0}, use_global_device_ids=true | all-gather | bytes 2297856 | tf_op jit(solution)/shard_map/all_gather | solution.py:121
  34.5 1.3 constant_dynamic-update-slice_fusion.1
  35.8 0.1 constant_dynamic-update-slice_fusion.refs_0_
  36.0 3.2 %collective-permute-start = (bf16[2,4096,128]{2,1,0:T(8,128)(2,1)S(1)}, bf16[2,4096,128]{2,1,0:T(8,128)(2,1)}, u32[]{:S(2)}, u32[]{:S(2)}) collective-permute-start(bf16[2,4096,128]{2,1,0:T(8,128)(2,1)S(1)} %constant_dynamic-update-slice_fusion.refs_0_), channel_id=1, source_target_pairs={{0,2},{1,3},{2,0},{3,1},{4,6},{5,7},{6,4},{7,5},{8,10},{9,11},{10,... | collective-permute-start | bytes 6291464 | tf_op jit(solution)/shard_map/ppermute | solution.py:21
  39.2 2.1 %collective-permute-start.1 = (bf16[2048,256]{1,0:T(8,128)(2,1)S(1)}, bf16[2048,256]{1,0:T(8,128)(2,1)}, u32[]{:S(2)}, u32[]{:S(2)}) collective-permute-start(bf16[2048,256]{1,0:T(8,128)(2,1)S(1)} %bitcast.16), channel_id=1, source_target_pairs={{0,2},{1,3},{2,0},{3,1},{4,6},{5,7},{6,4},{7,5},{8,10},{9,11},{10,... | collective-permute-start | bytes 3145736 | tf_op jit(solution)/shard_map/ppermute | solution.py:21
  41.3 2.2 %gather_fusion = f16[2,136,256]{2,1,0:T(8,128)(2,1)S(1)} fusion(f16[32,136,256]{2,1,0:T(8,128)(2,1)} %bitcast.24, s32[1024]{0:T(1024)S(1)} %pad_clamp_fusion), kind=kCustom, calls=%fused_computation | custom fusion | bytes 278536 | tf_op jit(solution)/shard_map/gather | solution.py:124
  43.5 49.4 %all-gather.7 = f16[64,136,256]{2,1,0:T(8,128)(2,1)S(1)} all-gather(f16[2,136,256]{2,1,0:T(8,128)(2,1)S(1)} %gather_fusion), channel_id=3, replica_groups={{0,1,32,33,64,65,96,97,128,129,160,161,192,193,224,225,256,257,288,289,..., dimensions={0}, use_global_device_ids=true | all-gather | bytes 4595712 | tf_op jit(solution)/shard_map/all_gather | solution.py:124
  92.9 0.0 collective-permute-done.refs_1_
  92.9 0.2 slice_reduce_fusion
  93.2 0.1 copy.9
  93.2 1.2 multiply_convert_fusion.1
  94.4 4.0 %hidden.1 = (bf16[512,256]{1,0:T(8,128)(2,1)S(1)}, f32[1,256]{1,0:T(1,128)S(1)}) custom-call(s32[7]{0:T(128)S(1)} %pad_add_fusion.facts, bf16[16,512,256]{2,1,0:T(8,128)(2,1)S(1)} %bitcast.15, bf16[2,4096,128]{2,1,0:T(8,128)(2,1)S(1)} %constant_dynamic-update-slice_fusion.refs_0_, bf16[2,4096,128]{2,1,0:T(8,128)(2,1)} %collective-permute-done.refs_1_), custom_call_target="tpu_custom_call" | custom-call | flops 2147483648 | bytes 8388608 | tf_op jit(solution)/shard_map/hidden/pallas_call | solution.py:92
  98.5 0.1 multiply_convert_fusion.2
  98.6 0.1 pad_maximum_fusion
  98.7 53.2 %all-gather.8 = f16[8320,256]{1,0:T(8,128)(2,1)S(1)} all-gather(f16[520,256]{1,0:T(8,128)(2,1)S(1)} %pad_maximum_fusion), channel_id=4, replica_groups=mesh['tok'=16,'exp'=32] {'tok'}, dimensions={0}, use_global_device_ids=true | all-gather | bytes 4526080 | tf_op jit(solution)/shard_map/all_gather | solution.py:132
  151.9 0.0 copy-start.2
  151.9 1.0 multiply_convert_fusion.gathered
  152.9 0.0 collective-permute-done.1.refs_1_
  152.9 2.5 %down.1 = (f32[512,256]{1,0:T(8,128)S(1)}, bf16[512,256]{1,0:T(8,128)(2,1)S(1)}) custom-call(s32[7]{0:T(128)S(1)} %pad_add_fusion.facts, bf16[16,512,256]{2,1,0:T(8,128)(2,1)S(1)} %multiply_convert_fusion.gathered, f32[8,1024]{1,0:T(8,128)S(1)} %copy-done.2, bf16[2048,256]{1,0:T(8,128)(2,1)S(1)} %bitcast.17, bf16[2048,256]{1,0:T(8,128)(2,1)} %collective-permute-done.1.refs_1_), custom_call_target="tpu_custom_call" | custom-call | flops 1073741824 | bytes 6307840 | tf_op jit(solution)/shard_map/down/pallas_call | solution.py:92
  155.4 9.4 %collective-permute-start.2 = (bf16[512,256]{1,0:T(8,128)(2,1)S(1)}, bf16[512,256]{1,0:T(8,128)(2,1)S(1)}, u32[]{:S(2)}, u32[]{:S(2)}) collective-permute-start(bf16[512,256]{1,0:T(8,128)(2,1)S(1)} %get-tuple-element.28), channel_id=1, source_target_pairs={{0,1},{1,0},{2,3},{3,2},{4,5},{5,4},{6,7},{7,6},{8,9},{9,8},{10,11... | collective-permute-start | bytes 786440 | tf_op jit(solution)/shard_map/ppermute | solution.py:25
  164.8 1.1 collective-permute-done.2
  165.9 0.7 place.1
  166.6 20.7 %all_to_all.5 = bf16[16,128,256]{2,1,0:T(8,128)(2,1)S(1)} all-to-all(bf16[16,128,256]{2,1,0:T(8,128)(2,1)S(1)} %place.1), channel_id=1, replica_groups={{0,2,4,6,8,10,12,14,16,18,20,22,24,26,28,30},{1,3,5,7,9,11,13,15,17,19,..., dimensions={0} | all-to-all | bytes 2097152 | tf_op jit(solution)/shard_map/all_to_all | solution.py:143
  187.3 0.8 reduce_sum.12
  (15 shorter events, 0.2 us)
Async XLA Ops:
  0.0 1.9 copy-start
  0.0 39.2 %copy-start.1 = (bf16[1,2048,256]{2,1,0:T(8,128)(2,1)S(1)}, bf16[1,2048,256]{2,1,0:T(8,128)(2,1)}, u32[]{:S(2)}) copy-start(bf16[1,2048,256]{2,1,0:T(8,128)(2,1)} %param.11) | copy-start | bytes 3145732
  1.9 33.9 %copy-start.3 = (bf16[1,4096,128]{2,1,0:T(8,128)(2,1)S(1)}, bf16[1,4096,128]{2,1,0:T(8,128)(2,1)}, u32[]{:S(2)}) copy-start(bf16[1,4096,128]{2,1,0:T(8,128)(2,1)} %param.10) | copy-start | bytes 3145732
  36.0 57.0 %collective-permute-start = (bf16[2,4096,128]{2,1,0:T(8,128)(2,1)S(1)}, bf16[2,4096,128]{2,1,0:T(8,128)(2,1)}, u32[]{:S(2)}, u32[]{:S(2)}) collective-permute-start(bf16[2,4096,128]{2,1,0:T(8,128)(2,1)S(1)} %constant_dynamic-update-slice_fusion.refs_0_), channel_id=1, source_target_pairs={{0,2},{1,3},{2,0},{3,1},{4,6},{5,7},{6,4},{7,5},{8,10},{9,11},{10,... | collective-permute-start | bytes 6291464 | tf_op jit(solution)/shard_map/ppermute | solution.py:21
  39.2 113.7 %collective-permute-start.1 = (bf16[2048,256]{1,0:T(8,128)(2,1)S(1)}, bf16[2048,256]{1,0:T(8,128)(2,1)}, u32[]{:S(2)}, u32[]{:S(2)}) collective-permute-start(bf16[2048,256]{1,0:T(8,128)(2,1)S(1)} %bitcast.16), channel_id=1, source_target_pairs={{0,2},{1,3},{2,0},{3,1},{4,6},{5,7},{6,4},{7,5},{8,10},{9,11},{10,... | collective-permute-start | bytes 3145736 | tf_op jit(solution)/shard_map/ppermute | solution.py:21
  151.9 1.0 copy-start.2
  155.4 10.5 %collective-permute-start.2 = (bf16[512,256]{1,0:T(8,128)(2,1)S(1)}, bf16[512,256]{1,0:T(8,128)(2,1)S(1)}, u32[]{:S(2)}, u32[]{:S(2)}) collective-permute-start(bf16[512,256]{1,0:T(8,128)(2,1)S(1)} %get-tuple-element.28), channel_id=1, source_target_pairs={{0,1},{1,0},{2,3},{3,2},{4,5},{5,4},{6,7},{7,6},{8,9},{9,8},{10,11... | collective-permute-start | bytes 786440 | tf_op jit(solution)/shard_map/ppermute | solution.py:25

commit v13 on v12

--- a/solution.py
+++ b/solution.py
@@ -38,15 +38,33 @@
     return value.astype(jnp.bfloat16)
 
 
-def hidden_kernel(facts, gathered, *refs):
-    weights, (out, largest) = refs[:-2], refs[-2:]
-    depth = gathered.shape[2]
+def start_rows(sources, held, arrived):
+    taken = held.shape[2]
+    copies = []
+    for number in range(DEPTH):
+        for which, weight in enumerate(sources):
+            rows = weight.at[pl.ds(number * taken, taken), :]
+            copies.append(pltpu.make_async_copy(rows, held.at[number, which], arrived.at[number, which]))
+            copies[-1].start()
+    return copies
+
+
+def product(gathered, copies, held, join):
+    count = held.shape[1]
     total = None
     for number in range(DEPTH):
-        rows = pl.ds(number * depth, depth)
-        right = jnp.concatenate([weight[kind, rows, :] for kind in range(2) for weight in weights], axis=1)
+        for copy in copies[number * count : (number + 1) * count]:
+            copy.wait()
+        right = jnp.concatenate([held[number, which] for which in range(count)], axis=join)
         term = jnp.dot(gathered[number], right, preferred_element_type=jnp.float32)
         total = term if total is None else total + term
+    return total
+
+
+def hidden_kernel(facts, gathered, *refs):
+    weights, (out, largest, held, arrived) = refs[:-4], refs[-4:]
+    copies = start_rows([weight.at[kind] for kind in range(2) for weight in weights], held, arrived)
+    total = product(gathered, copies, held, 1)
     units = total.shape[1] // 2
     gate, up = total[:, :units], total[:, units:]
     hidden = gate / (1.0 + jnp.exp(-gate)) * up
@@ -55,14 +73,9 @@
 
 
 def down_kernel(facts, gathered, scales, *refs):
-    weights, (kept, given) = refs[:-2], refs[-2:]
-    depth = gathered.shape[2] // len(weights)
-    total = None
-    for number in range(DEPTH):
-        rows = pl.ds(number * depth, depth)
-        right = jnp.concatenate([weight[rows, :] for weight in weights], axis=0)
-        term = jnp.dot(gathered[number], right, preferred_element_type=jnp.float32)
-        total = term if total is None else total + term
+    weights, (kept, given, held, arrived) = refs[:-4], refs[-4:]
+    copies = start_rows(weights, held, arrived)
+    total = product(gathered, copies, held, 0)
     count = total.shape[0]
     columns = pl.ds(pl.multiple_of(facts[HALF] * count, count), count)
     scale = jnp.broadcast_to(scales[pl.ds(facts[EXPERT], 1), columns], (128, count)).T
@@ -87,19 +100,29 @@
     return jax.ShapeDtypeStruct(shape, jnp.bfloat16)
 
 
-def kernel_call(kernel, name, facts, inner, outs, flops):
+def kernel_call(kernel, name, facts, inner, outs, flops, weights=(), rows=None):
     in_vmem = pl.BlockSpec(memory_space=pltpu.VMEM)
+    scratch = []
+    if weights:
+        count = sum(weight.size for weight in weights) // (DEPTH * rows * weights[0].shape[-1])
+        scratch = [
+            pltpu.VMEM((DEPTH, count, rows, weights[0].shape[-1]), jnp.bfloat16),
+            pltpu.SemaphoreType.DMA((DEPTH, count)),
+        ]
     return pl.pallas_call(
         kernel,
         out_shape=outs,
-        in_specs=[pl.BlockSpec(memory_space=pltpu.SMEM)] + [in_vmem] * len(inner),
+        in_specs=[pl.BlockSpec(memory_space=pltpu.SMEM)]
+        + [in_vmem] * len(inner)
+        + [pl.BlockSpec(memory_space=pltpu.HBM)] * len(weights),
         out_specs=[in_vmem] * len(outs),
+        scratch_shapes=scratch,
         compiler_params=pltpu.CompilerParams(vmem_limit_bytes=24 << 20),
         cost_estimate=pl.CostEstimate(
-            flops=flops, bytes_accessed=2 * sum(array.size for array in inner), transcendentals=0
+            flops=flops, bytes_accessed=2 * sum(array.size for array in [*inner, *weights]), transcendentals=0
         ),
         name=name,
-    )(facts, *inner)
+    )(facts, *inner, *[pltpu.with_memory_space_constraint(weight, pltpu.HBM) for weight in weights])
 
 
 def shards(tokens, picked_blocks, gate_scale, w_gate, w_up, w_down):
@@ -126,13 +149,14 @@
     gathered = decode(gathered).reshape(DEPTH, rows, features)
     flops = 2 * rows * DEPTH * features * SPAN * units
     hidden, largest = kernel_call(
-        hidden_kernel, "hidden", facts, [gathered, in_own, in_far],
-        [array_of(rows, 2 * units), jax.ShapeDtypeStruct((1, 2 * units), jnp.float32)], flops,
+        hidden_kernel, "hidden", facts, [gathered],
+        [array_of(rows, 2 * units), jax.ShapeDtypeStruct((1, 2 * units), jnp.float32)], flops, [in_own, in_far], features,
     )
     gathered = lax.all_gather(encode(hidden, largest)[None], "tok", tiled=True)
     kept, given = kernel_call(
-        down_kernel, "down", facts, [decode(gathered), gate_scale, down_own, down_far],
+        down_kernel, "down", facts, [decode(gathered), gate_scale],
         [jax.ShapeDtypeStruct((rows, features), jnp.float32), array_of(rows, features)], flops // 2,
+        [down_own, down_far], units,
     )
 
     whole = (half, BLOCK, features)

time: 188 us -> 192 us (1.021)
  Pallas kernels: 7.15 us -> 10.6 us
    pallas_call x3, Pallas kernels: 7.15 us -> 10.6 us  [kernel_call(): pl.pallas_call(kernel, out_shape=outs, in_specs=[pl.BlockSpec(memory_spac...]
  transfers between devices with their start and end apart: 3 -> 3, of which waited for: 1 -> 1; matrix products, arithmetic and copies ran while one was open for 3% -> 3% of each run, Pallas kernels for 2% -> 3%
where the time goes in v13:
time: 192 us; the launch traced here: 191 us
  blocking collectives  156 us (81%)
  starting transfers between devices  14.6 us (8%)
  Pallas kernels  10.6 us (6%)
  other arithmetic  5.35 us (3%)
  local copies, waits for them, and re-layouts  3.91 us (2%)
    all_gather x1, blocking collectives, shards(): gathered = lax.all_gather(encode(hidden, largest)[None], 'tok', tiled=True)  53.2 us
    all_gather x1, blocking collectives, shards(): lax.all_gather(held[mine], ('tok', 'exp'), axis_index_groups=LINES)  49.4 us
    all_gather x1, blocking collectives, shards(): held = lax.all_gather(coded, 'exp')  32.4 us
    all_to_all x1, blocking collectives, shards(): lax.all_to_all(outgoing, 'exp', 0, 0, axis_index_groups=SAME_CORE, tiled=...  20.7 us
    pallas_call x3, Pallas kernels, kernel_call(): pl.pallas_call(kernel, out_shape=outs, in_specs=[pl.BlockSpec(memory_spac...  10.6 us
    ppermute x1, starting transfers between devices, swap_core(): return lax.ppermute(value, 'exp', [(p, p ^ 1) for p in range(OWNERS)])  9.34 us
    ppermute x2, starting transfers between devices, swap_across(): return lax.ppermute(value, 'exp', [(p, p ^ 2) for p in range(OWNERS)])  5.28 us
  transfers between devices with their start and end apart: 3, of which 1 were waited for; matrix products, arithmetic and copies ran while one was open for 3% of the time, Pallas kernels for 3%

profile of v13, /device:TPU:1, one launch (start us, length us, event | category | flops | bytes accessed | tf_op | source)
XLA Modules:
  0.0 191.5 jit_solution(14527809742996629062)
XLA Ops:
  0.0 1.0 fusion
  1.0 0.9 fusion.1
  1.9 0.0 copy-done
  1.9 0.0 copy-start.4
  1.9 0.1 dynamic-slice_bitcast_fusion.1
  2.0 0.1 dynamic-slice_bitcast_fusion
  2.1 0.1 pad_add_fusion.facts
  2.2 32.4 %all-gather.6 = f16[4352,256]{1,0:T(8,128)(2,1)} all-gather(f16[136,256]{1,0:T(8,128)(2,1)S(1)} %pad_maximum_fusion.1), channel_id=2, replica_groups=mesh['tok'=16,'exp'=32] {'exp'}, dimensions={0}, use_global_device_ids=true | all-gather | bytes 2297856 | tf_op jit(solution)/shard_map/all_gather | solution.py:144
  34.5 1.3 constant_dynamic-update-slice_fusion.1
  35.8 0.1 constant_dynamic-update-slice_fusion.refs_0_
  36.0 3.2 %collective-permute-start = (bf16[2,4096,128]{2,1,0:T(8,128)(2,1)S(1)}, bf16[2,4096,128]{2,1,0:T(8,128)(2,1)}, u32[]{:S(2)}, u32[]{:S(2)}) collective-permute-start(bf16[2,4096,128]{2,1,0:T(8,128)(2,1)S(1)} %constant_dynamic-update-slice_fusion.refs_0_), channel_id=1, source_target_pairs={{0,2},{1,3},{2,0},{3,1},{4,6},{5,7},{6,4},{7,5},{8,10},{9,11},{10,... | collective-permute-start | bytes 6291464 | tf_op jit(solution)/shard_map/ppermute | solution.py:21
  39.2 2.1 %collective-permute-start.1 = (bf16[2048,256]{1,0:T(8,128)(2,1)S(1)}, bf16[2048,256]{1,0:T(8,128)(2,1)}, u32[]{:S(2)}, u32[]{:S(2)}) collective-permute-start(bf16[2048,256]{1,0:T(8,128)(2,1)S(1)} %bitcast.24), channel_id=1, source_target_pairs={{0,2},{1,3},{2,0},{3,1},{4,6},{5,7},{6,4},{7,5},{8,10},{9,11},{10,... | collective-permute-start | bytes 3145736 | tf_op jit(solution)/shard_map/ppermute | solution.py:21
  41.3 2.2 %gather_fusion = f16[2,136,256]{2,1,0:T(8,128)(2,1)S(1)} fusion(f16[32,136,256]{2,1,0:T(8,128)(2,1)} %bitcast.22, s32[1024]{0:T(1024)S(1)} %pad_clamp_fusion), kind=kCustom, calls=%fused_computation | custom fusion | bytes 278536 | tf_op jit(solution)/shard_map/gather | solution.py:147
  43.5 49.4 %all-gather.7 = f16[64,136,256]{2,1,0:T(8,128)(2,1)S(1)} all-gather(f16[2,136,256]{2,1,0:T(8,128)(2,1)S(1)} %gather_fusion), channel_id=3, replica_groups={{0,1,32,33,64,65,96,97,128,129,160,161,192,193,224,225,256,257,288,289,..., dimensions={0}, use_global_device_ids=true | all-gather | bytes 4595712 | tf_op jit(solution)/shard_map/all_gather | solution.py:147
  92.9 0.0 collective-permute-done.refs_1_
  92.9 0.2 slice_reduce_fusion
  93.2 0.1 copy.9
  93.2 1.2 multiply_convert_fusion.1
  94.5 5.2 %hidden.1 = (bf16[512,256]{1,0:T(8,128)(2,1)S(1)}, f32[1,256]{1,0:T(1,128)S(1)}) custom-call(s32[7]{0:T(128)S(1)} %pad_add_fusion.facts, bf16[16,512,256]{2,1,0:T(8,128)(2,1)S(1)} %bitcast.15, bf16[2,4096,128]{2,1,0:T(8,128)(2,1)} %copy-done.2, bf16[2,4096,128]{2,1,0:T(8,128)(2,1)} %collective-permute-done.refs_1_), custom_call_target="tpu_custom_call" | custom-call | flops 2147483648 | bytes 8388608 | tf_op jit(solution)/shard_map/hidden/pallas_call | solution.py:112
  99.8 0.1 multiply_convert_fusion.2
  99.8 0.1 pad_maximum_fusion
  99.9 53.2 %all-gather.8 = f16[8320,256]{1,0:T(8,128)(2,1)S(1)} all-gather(f16[520,256]{1,0:T(8,128)(2,1)S(1)} %pad_maximum_fusion), channel_id=4, replica_groups=mesh['tok'=16,'exp'=32] {'tok'}, dimensions={0}, use_global_device_ids=true | all-gather | bytes 4526080 | tf_op jit(solution)/shard_map/all_gather | solution.py:155
  153.2 0.0 copy-start.1
  153.2 1.0 multiply_convert_fusion.gathered
  154.1 0.0 collective-permute-done.1.refs_1_
  154.2 0.0 copy-done.1
  154.2 4.7 %down.1 = (f32[512,256]{1,0:T(8,128)S(1)}, bf16[512,256]{1,0:T(8,128)(2,1)S(1)}) custom-call(s32[7]{0:T(128)S(1)} %pad_add_fusion.facts, bf16[16,512,256]{2,1,0:T(8,128)(2,1)S(1)} %multiply_convert_fusion.gathered, f32[8,1024]{1,0:T(8,128)S(1)} %copy-done.1, bf16[2048,256]{1,0:T(8,128)(2,1)} %bitcast.23, bf16[2048,256]{1,0:T(8,128)(2,1)} %collective-permute-done.1.refs_1_), custom_call_target="tpu_custom_call" | custom-call | flops 1073741824 | bytes 6307840 | tf_op jit(solution)/shard_map/down/pallas_call | solution.py:112
  158.8 9.3 %collective-permute-start.2 = (bf16[512,256]{1,0:T(8,128)(2,1)S(1)}, bf16[512,256]{1,0:T(8,128)(2,1)S(1)}, u32[]{:S(2)}, u32[]{:S(2)}) collective-permute-start(bf16[512,256]{1,0:T(8,128)(2,1)S(1)} %get-tuple-element.28), channel_id=1, source_target_pairs={{0,1},{1,0},{2,3},{3,2},{4,5},{5,4},{6,7},{7,6},{8,9},{9,8},{10,11... | collective-permute-start | bytes 786440 | tf_op jit(solution)/shard_map/ppermute | solution.py:25
  168.2 1.1 collective-permute-done.2
  169.3 0.7 place.1
  170.0 20.7 %all_to_all.5 = bf16[16,128,256]{2,1,0:T(8,128)(2,1)S(1)} all-to-all(bf16[16,128,256]{2,1,0:T(8,128)(2,1)S(1)} %place.1), channel_id=1, replica_groups={{0,2,4,6,8,10,12,14,16,18,20,22,24,26,28,30},{1,3,5,7,9,11,13,15,17,19,..., dimensions={0} | all-to-all | bytes 2097152 | tf_op jit(solution)/shard_map/all_to_all | solution.py:167
  190.7 0.8 reduce_sum.12
  (17 shorter events, 0.2 us)
Async XLA Ops:
  0.0 1.9 copy-start
  0.0 39.2 %copy-start.3 = (bf16[1,2048,256]{2,1,0:T(8,128)(2,1)S(1)}, bf16[1,2048,256]{2,1,0:T(8,128)(2,1)}, u32[]{:S(2)}) copy-start(bf16[1,2048,256]{2,1,0:T(8,128)(2,1)} %param.11) | copy-start | bytes 3145732
  1.9 33.9 %copy-start.4 = (bf16[1,4096,128]{2,1,0:T(8,128)(2,1)S(1)}, bf16[1,4096,128]{2,1,0:T(8,128)(2,1)}, u32[]{:S(2)}) copy-start(bf16[1,4096,128]{2,1,0:T(8,128)(2,1)} %param.10) | copy-start | bytes 3145732
  36.0 58.5 %copy-start.2 = (bf16[2,4096,128]{2,1,0:T(8,128)(2,1)}, bf16[2,4096,128]{2,1,0:T(8,128)(2,1)S(1)}, u32[]{:S(2)}) copy-start(bf16[2,4096,128]{2,1,0:T(8,128)(2,1)S(1)} %constant_dynamic-update-slice_fusion.refs_0_) | copy-start | bytes 6291460
  36.0 57.0 %collective-permute-start = (bf16[2,4096,128]{2,1,0:T(8,128)(2,1)S(1)}, bf16[2,4096,128]{2,1,0:T(8,128)(2,1)}, u32[]{:S(2)}, u32[]{:S(2)}) collective-permute-start(bf16[2,4096,128]{2,1,0:T(8,128)(2,1)S(1)} %constant_dynamic-update-slice_fusion.refs_0_), channel_id=1, source_target_pairs={{0,2},{1,3},{2,0},{3,1},{4,6},{5,7},{6,4},{7,5},{8,10},{9,11},{10,... | collective-permute-start | bytes 6291464 | tf_op jit(solution)/shard_map/ppermute | solution.py:21
  39.2 114.9 %collective-permute-start.1 = (bf16[2048,256]{1,0:T(8,128)(2,1)S(1)}, bf16[2048,256]{1,0:T(8,128)(2,1)}, u32[]{:S(2)}, u32[]{:S(2)}) collective-permute-start(bf16[2048,256]{1,0:T(8,128)(2,1)S(1)} %bitcast.24), channel_id=1, source_target_pairs={{0,2},{1,3},{2,0},{3,1},{4,6},{5,7},{6,4},{7,5},{8,10},{9,11},{10,... | collective-permute-start | bytes 3145736 | tf_op jit(solution)/shard_map/ppermute | solution.py:21
  153.2 1.0 copy-start.1
  158.8 10.5 %collective-permute-start.2 = (bf16[512,256]{1,0:T(8,128)(2,1)S(1)}, bf16[512,256]{1,0:T(8,128)(2,1)S(1)}, u32[]{:S(2)}, u32[]{:S(2)}) collective-permute-start(bf16[512,256]{1,0:T(8,128)(2,1)S(1)} %get-tuple-element.28), channel_id=1, source_target_pairs={{0,1},{1,0},{2,3},{3,2},{4,5},{5,4},{6,7},{7,6},{8,9},{9,8},{10,11... | collective-permute-start | bytes 786440 | tf_op jit(solution)/shard_map/ppermute | solution.py:25

commit v14 on v12

--- a/solution.py
+++ b/solution.py
@@ -118,10 +118,10 @@
     in_own, down_own = jnp.stack([w_gate[0], w_up[0]]), w_down[0]
     largest = jnp.max(jnp.abs(tokens.astype(jnp.float32)), axis=0, keepdims=True)
     coded, facts, mine = lax.optimization_barrier((encode(tokens, largest), facts, mine))
-    held = lax.all_gather(coded, "exp")
-    held, in_sent, down_sent = lax.optimization_barrier((held, in_own, down_own))
+    picked = lax.all_gather(coded, "exp")[mine]
+    picked, in_sent, down_sent = lax.optimization_barrier((picked, in_own, down_own))
     in_far, down_far = swap_across(in_sent), swap_across(down_sent)
-    gathered = lax.all_gather(held[mine], ("tok", "exp"), axis_index_groups=LINES)
+    gathered = lax.all_gather(picked, ("tok", "exp"), axis_index_groups=LINES)
     gathered, in_far = lax.optimization_barrier((gathered, in_far))
     gathered = decode(gathered).reshape(DEPTH, rows, features)
     flops = 2 * rows * DEPTH * features * SPAN * units

time: 188 us -> 190 us (1.011)
  blocking collectives: 156 us -> 158 us
    all_gather x1, blocking collectives: 53.2 us -> 55.4 us  [shards(): gathered = lax.all_gather(encode(hidden, largest)[None], 'tok', tiled=True)]
  transfers between devices with their start and end apart: 3 -> 3, of which waited for: 1 -> 1; matrix products, arithmetic and copies ran while one was open for 3% -> 1% of each run, Pallas kernels for 2% -> 2%
where the time goes in v14:
time: 190 us; the launch traced here: 189 us
  blocking collectives  158 us (83%)
  starting transfers between devices  14.3 us (8%)
  other arithmetic  5.41 us (3%)
  Pallas kernels  5.34 us (3%)
  local copies, waits for them, and re-layouts  5.13 us (3%)
    all_gather x1, blocking collectives, shards(): gathered = lax.all_gather(encode(hidden, largest)[None], 'tok', tiled=True)  55.4 us
    all_gather x1, blocking collectives, shards(): gathered = lax.all_gather(picked, ('tok', 'exp'), axis_index_groups=LINES)  49.4 us
    all_gather x1, blocking collectives, shards(): picked = lax.all_gather(coded, 'exp')[mine]  32.2 us
    all_to_all x1, blocking collectives, shards(): lax.all_to_all(outgoing, 'exp', 0, 0, axis_index_groups=SAME_CORE, tiled=...  20.7 us
    ppermute x1, starting transfers between devices, swap_core(): return lax.ppermute(value, 'exp', [(p, p ^ 1) for p in range(OWNERS)])  9.01 us
    pallas_call x3, Pallas kernels, kernel_call(): pl.pallas_call(kernel, out_shape=outs, in_specs=[pl.BlockSpec(memory_spac...  5.34 us
    ppermute x2, starting transfers between devices, swap_across(): return lax.ppermute(value, 'exp', [(p, p ^ 2) for p in range(OWNERS)])  5.28 us
  transfers between devices with their start and end apart: 3, of which 1 were waited for; matrix products, arithmetic and copies ran while one was open for 1% of the time, Pallas kernels for 2%

profile of v14, /device:TPU:1, one launch (start us, length us, event | category | flops | bytes accessed | tf_op | source)
XLA Modules:
  0.0 189.2 jit_solution(12690648131344291983)
XLA Ops:
  0.0 0.0 copy-start
  0.0 1.0 fusion
  1.0 0.9 fusion.1
  1.9 0.0 copy-done
  1.9 0.1 dynamic-slice_bitcast_fusion.1
  2.0 0.1 dynamic-slice_bitcast_fusion
  2.1 0.1 pad_add_fusion.facts
  2.1 32.2 %all-gather.6 = f16[4352,256]{1,0:T(8,128)(2,1)} all-gather(f16[136,256]{1,0:T(8,128)(2,1)S(1)} %pad_maximum_fusion.1), channel_id=2, replica_groups=mesh['tok'=16,'exp'=32] {'exp'}, dimensions={0}, use_global_device_ids=true | all-gather | bytes 2297856 | tf_op jit(solution)/shard_map/all_gather | solution.py:121
  34.4 1.3 constant_dynamic-update-slice_fusion.1
  35.7 2.2 %gather_fusion = f16[2,136,256]{2,1,0:T(8,128)(2,1)S(1)} fusion(f16[32,136,256]{2,1,0:T(8,128)(2,1)} %bitcast.24, s32[1024]{0:T(1024)S(1)} %pad_clamp_fusion), kind=kCustom, calls=%fused_computation | custom fusion | bytes 278536 | tf_op jit(solution)/shard_map/gather | solution.py:121
  37.9 1.4 constant_dynamic-update-slice_fusion.refs_0_
  39.3 3.2 %collective-permute-start = (bf16[2,4096,128]{2,1,0:T(8,128)(2,1)S(1)}, bf16[2,4096,128]{2,1,0:T(8,128)(2,1)S(1)}, u32[]{:S(2)}, u32[]{:S(2)}) collective-permute-start(bf16[2,4096,128]{2,1,0:T(8,128)(2,1)S(1)} %constant_dynamic-update-slice_fusion.refs_0_), channel_id=1, source_target_pairs={{0,2},{1,3},{2,0},{3,1},{4,6},{5,7},{6,4},{7,5},{8,10},{9,11},{10,... | collective-permute-start | bytes 6291464 | tf_op jit(solution)/shard_map/ppermute | solution.py:21
  42.5 0.0 copy-done.1
  42.5 2.1 %collective-permute-start.1 = (bf16[2048,256]{1,0:T(8,128)(2,1)S(1)}, bf16[2048,256]{1,0:T(8,128)(2,1)S(1)}, u32[]{:S(2)}, u32[]{:S(2)}) collective-permute-start(bf16[2048,256]{1,0:T(8,128)(2,1)S(1)} %bitcast.16), channel_id=1, source_target_pairs={{0,2},{1,3},{2,0},{3,1},{4,6},{5,7},{6,4},{7,5},{8,10},{9,11},{10,... | collective-permute-start | bytes 3145736 | tf_op jit(solution)/shard_map/ppermute | solution.py:21
  44.6 49.4 %all-gather.7 = f16[64,136,256]{2,1,0:T(8,128)(2,1)S(1)} all-gather(f16[2,136,256]{2,1,0:T(8,128)(2,1)S(1)} %gather_fusion), channel_id=3, replica_groups={{0,1,32,33,64,65,96,97,128,129,160,161,192,193,224,225,256,257,288,289,..., dimensions={0}, use_global_device_ids=true | all-gather | bytes 4595712 | tf_op jit(solution)/shard_map/all_gather | solution.py:124
  94.0 0.0 collective-permute-done.refs_1_
  94.0 0.2 slice_reduce_fusion
  94.2 0.1 copy.9
  94.3 1.2 multiply_convert_fusion.1
  95.5 2.9 %hidden.1 = (bf16[512,256]{1,0:T(8,128)(2,1)S(1)}, f32[1,256]{1,0:T(1,128)S(1)}) custom-call(s32[7]{0:T(128)S(1)} %pad_add_fusion.facts, bf16[16,512,256]{2,1,0:T(8,128)(2,1)S(1)} %bitcast.15, bf16[2,4096,128]{2,1,0:T(8,128)(2,1)S(1)} %constant_dynamic-update-slice_fusion.refs_0_, bf16[2,4096,128]{2,1,0:T(8,128)(2,1)S(1)} %collective-permute-done.refs_1_), custom_call_target="tpu_custom_call" | custom-call | flops 2147483648 | bytes 8388608 | tf_op jit(solution)/shard_map/hidden/pallas_call | solution.py:92
  98.4 0.1 multiply_convert_fusion.2
  98.5 0.1 pad_maximum_fusion
  98.6 55.4 %all-gather.8 = f16[8320,256]{1,0:T(8,128)(2,1)S(1)} all-gather(f16[520,256]{1,0:T(8,128)(2,1)S(1)} %pad_maximum_fusion), channel_id=4, replica_groups=mesh['tok'=16,'exp'=32] {'tok'}, dimensions={0}, use_global_device_ids=true | all-gather | bytes 4526080 | tf_op jit(solution)/shard_map/all_gather | solution.py:132
  154.0 0.0 copy-start.2
  154.0 1.0 multiply_convert_fusion.gathered
  155.1 0.0 collective-permute-done.1.refs_1_
  155.1 1.8 down.1
  156.9 9.0 %collective-permute-start.2 = (bf16[512,256]{1,0:T(8,128)(2,1)S(1)}, bf16[512,256]{1,0:T(8,128)(2,1)S(1)}, u32[]{:S(2)}, u32[]{:S(2)}) collective-permute-start(bf16[512,256]{1,0:T(8,128)(2,1)S(1)} %get-tuple-element.28), channel_id=1, source_target_pairs={{0,1},{1,0},{2,3},{3,2},{4,5},{5,4},{6,7},{7,6},{8,9},{9,8},{10,11... | collective-permute-start | bytes 786440 | tf_op jit(solution)/shard_map/ppermute | solution.py:25
  165.9 1.1 collective-permute-done.2
  167.1 0.7 place.1
  167.7 20.7 %all_to_all.5 = bf16[16,128,256]{2,1,0:T(8,128)(2,1)S(1)} all-to-all(bf16[16,128,256]{2,1,0:T(8,128)(2,1)S(1)} %place.1), channel_id=1, replica_groups={{0,2,4,6,8,10,12,14,16,18,20,22,24,26,28,30},{1,3,5,7,9,11,13,15,17,19,..., dimensions={0} | all-to-all | bytes 2097152 | tf_op jit(solution)/shard_map/all_to_all | solution.py:143
  188.4 0.8 reduce_sum.12
  (13 shorter events, 0.2 us)
Async XLA Ops:
  0.0 1.9 copy-start
  0.0 42.5 %copy-start.1 = (bf16[1,2048,256]{2,1,0:T(8,128)(2,1)S(1)}, bf16[1,2048,256]{2,1,0:T(8,128)(2,1)}, u32[]{:S(2)}) copy-start(bf16[1,2048,256]{2,1,0:T(8,128)(2,1)} %param.11) | copy-start | bytes 3145732
  39.3 54.7 %collective-permute-start = (bf16[2,4096,128]{2,1,0:T(8,128)(2,1)S(1)}, bf16[2,4096,128]{2,1,0:T(8,128)(2,1)S(1)}, u32[]{:S(2)}, u32[]{:S(2)}) collective-permute-start(bf16[2,4096,128]{2,1,0:T(8,128)(2,1)S(1)} %constant_dynamic-update-slice_fusion.refs_0_), channel_id=1, source_target_pairs={{0,2},{1,3},{2,0},{3,1},{4,6},{5,7},{6,4},{7,5},{8,10},{9,11},{10,... | collective-permute-start | bytes 6291464 | tf_op jit(solution)/shard_map/ppermute | solution.py:21
  42.5 112.6 %collective-permute-start.1 = (bf16[2048,256]{1,0:T(8,128)(2,1)S(1)}, bf16[2048,256]{1,0:T(8,128)(2,1)S(1)}, u32[]{:S(2)}, u32[]{:S(2)}) collective-permute-start(bf16[2048,256]{1,0:T(8,128)(2,1)S(1)} %bitcast.16), channel_id=1, source_target_pairs={{0,2},{1,3},{2,0},{3,1},{4,6},{5,7},{6,4},{7,5},{8,10},{9,11},{10,... | collective-permute-start | bytes 3145736 | tf_op jit(solution)/shard_map/ppermute | solution.py:21
  154.0 1.0 copy-start.2
  156.9 10.2 %collective-permute-start.2 = (bf16[512,256]{1,0:T(8,128)(2,1)S(1)}, bf16[512,256]{1,0:T(8,128)(2,1)S(1)}, u32[]{:S(2)}, u32[]{:S(2)}) collective-permute-start(bf16[512,256]{1,0:T(8,128)(2,1)S(1)} %get-tuple-element.28), channel_id=1, source_target_pairs={{0,1},{1,0},{2,3},{3,2},{4,5},{5,4},{6,7},{7,6},{8,9},{9,8},{10,11... | collective-permute-start | bytes 786440 | tf_op jit(solution)/shard_map/ppermute | solution.py:25

commit v15 on v14

--- a/solution.py
+++ b/solution.py
@@ -44,7 +44,7 @@
     total = None
     for number in range(DEPTH):
         rows = pl.ds(number * depth, depth)
-        right = jnp.concatenate([weight[kind, rows, :] for kind in range(2) for weight in weights], axis=1)
+        right = jnp.concatenate([weight[rows, :] for weight in weights], axis=1)
         term = jnp.dot(gathered[number], right, preferred_element_type=jnp.float32)
         total = term if total is None else total + term
     units = total.shape[1] // 2
@@ -115,23 +115,23 @@
     mine = lax.dynamic_slice_in_dim(picks, half // 2 * core, half // 2)
     facts = jnp.concatenate([picks, jnp.stack([core, expert, side]).astype(jnp.int32)])
 
-    in_own, down_own = jnp.stack([w_gate[0], w_up[0]]), w_down[0]
+    own = [w_gate[0], w_up[0], w_down[0]]
     largest = jnp.max(jnp.abs(tokens.astype(jnp.float32)), axis=0, keepdims=True)
     coded, facts, mine = lax.optimization_barrier((encode(tokens, largest), facts, mine))
     picked = lax.all_gather(coded, "exp")[mine]
-    picked, in_sent, down_sent = lax.optimization_barrier((picked, in_own, down_own))
-    in_far, down_far = swap_across(in_sent), swap_across(down_sent)
+    picked, sent = lax.optimization_barrier((picked, own))
+    far = [swap_across(weight) for weight in sent]
     gathered = lax.all_gather(picked, ("tok", "exp"), axis_index_groups=LINES)
-    gathered, in_far = lax.optimization_barrier((gathered, in_far))
+    gathered, far[:2] = lax.optimization_barrier((gathered, far[:2]))
     gathered = decode(gathered).reshape(DEPTH, rows, features)
     flops = 2 * rows * DEPTH * features * SPAN * units
     hidden, largest = kernel_call(
-        hidden_kernel, "hidden", facts, [gathered, in_own, in_far],
+        hidden_kernel, "hidden", facts, [gathered, own[0], far[0], own[1], far[1]],
         [array_of(rows, 2 * units), jax.ShapeDtypeStruct((1, 2 * units), jnp.float32)], flops,
     )
     gathered = lax.all_gather(encode(hidden, largest)[None], "tok", tiled=True)
     kept, given = kernel_call(
-        down_kernel, "down", facts, [decode(gathered), gate_scale, down_own, down_far],
+        down_kernel, "down", facts, [decode(gathered), gate_scale, own[2], far[2]],
         [jax.ShapeDtypeStruct((rows, features), jnp.float32), array_of(rows, features)], flops // 2,
     )
 

time: 190 us -> 184 us (0.968)
  local copies, waits for them, and re-layouts: 5.13 us -> 1.36 us
  blocking collectives: 158 us -> 155 us
    ppermute x2 -> x3, starting transfers between devices: 5.28 us -> 8.73 us  [swap_across(): return lax.ppermute(value, 'exp', [(p, p ^ 2) for p in range(OWNERS)])]
    ppermute x1, starting transfers between devices: 9.01 us -> 5.96 us  [swap_core(): return lax.ppermute(value, 'exp', [(p, p ^ 1) for p in range(OWNERS)])]
    all_gather x1, blocking collectives: 32.2 us -> 30 us  [shards(): picked = lax.all_gather(coded, 'exp')[mine]]
  transfers between devices with their start and end apart: 3 -> 4, of which waited for: 1 -> 1; matrix products, arithmetic and copies ran while one was open for 1% -> 1% of each run, Pallas kernels for 2% -> 2%
where the time goes in v15:
time: 184 us; the launch traced here: 183 us
  blocking collectives  155 us (84%)
  starting transfers between devices  14.7 us (8%)
  Pallas kernels  5.33 us (3%)
  other arithmetic  5.25 us (3%)
    all_gather x1, blocking collectives, shards(): gathered = lax.all_gather(encode(hidden, largest)[None], 'tok', tiled=True)  54.5 us
    all_gather x1, blocking collectives, shards(): gathered = lax.all_gather(picked, ('tok', 'exp'), axis_index_groups=LINES)  49 us
    all_gather x1, blocking collectives, shards(): picked = lax.all_gather(coded, 'exp')[mine]  30 us
    all_to_all x1, blocking collectives, shards(): lax.all_to_all(outgoing, 'exp', 0, 0, axis_index_groups=SAME_CORE, tiled=...  21.2 us
    ppermute x3, starting transfers between devices, swap_across(): return lax.ppermute(value, 'exp', [(p, p ^ 2) for p in range(OWNERS)])  8.73 us
    ppermute x1, starting transfers between devices, swap_core(): return lax.ppermute(value, 'exp', [(p, p ^ 1) for p in range(OWNERS)])  5.96 us
    pallas_call x3, Pallas kernels, kernel_call(): pl.pallas_call(kernel, out_shape=outs, in_specs=[pl.BlockSpec(memory_spac...  5.33 us
  transfers between devices with their start and end apart: 4, of which 1 were waited for; matrix products, arithmetic and copies ran while one was open for 1% of the time, Pallas kernels for 2%

profile of v15, /device:TPU:1, one launch (start us, length us, event | category | flops | bytes accessed | tf_op | source)
XLA Modules:
  0.0 182.8 jit_solution(11208604238999663484)
XLA Ops:
  0.0 0.9 fusion
  0.9 0.9 fusion.1
  1.8 0.1 dynamic-slice_bitcast_fusion.1
  1.9 0.1 dynamic-slice_bitcast_fusion
  2.0 0.1 pad_add_fusion.facts
  2.1 30.0 %all-gather.6 = f16[4352,256]{1,0:T(8,128)(2,1)S(1)} all-gather(f16[136,256]{1,0:T(8,128)(2,1)S(1)} %pad_maximum_fusion.1), channel_id=2, replica_groups=mesh['tok'=16,'exp'=32] {'exp'}, dimensions={0}, use_global_device_ids=true | all-gather | bytes 2297856 | tf_op jit(solution)/shard_map/all_gather | solution.py:121
  32.1 0.6 gather_fusion
  32.7 3.4 %collective-permute-start = (bf16[4096,128]{1,0:T(8,128)(2,1)}, bf16[4096,128]{1,0:T(8,128)(2,1)S(1)}, u32[]{:S(2)}, u32[]{:S(2)}) collective-permute-start(bf16[4096,128]{1,0:T(8,128)(2,1)} %bitcast.18), channel_id=1, source_target_pairs={{0,2},{1,3},{2,0},{3,1},{4,6},{5,7},{6,4},{7,5},{8,10},{9,11},{10,... | collective-permute-start | bytes 3145736 | tf_op jit(solution)/shard_map/ppermute | solution.py:21
  36.2 1.9 %collective-permute-start.1 = (bf16[4096,128]{1,0:T(8,128)(2,1)}, bf16[4096,128]{1,0:T(8,128)(2,1)S(1)}, u32[]{:S(2)}, u32[]{:S(2)}) collective-permute-start(bf16[4096,128]{1,0:T(8,128)(2,1)} %bitcast.20), channel_id=1, source_target_pairs={{0,2},{1,3},{2,0},{3,1},{4,6},{5,7},{6,4},{7,5},{8,10},{9,11},{10,... | collective-permute-start | bytes 3145736 | tf_op jit(solution)/shard_map/ppermute | solution.py:21
  38.1 3.4 %collective-permute-start.2 = (bf16[2048,256]{1,0:T(8,128)(2,1)}, bf16[2048,256]{1,0:T(8,128)(2,1)S(1)}, u32[]{:S(2)}, u32[]{:S(2)}) collective-permute-start(bf16[2048,256]{1,0:T(8,128)(2,1)} %bitcast.22), channel_id=1, source_target_pairs={{0,2},{1,3},{2,0},{3,1},{4,6},{5,7},{6,4},{7,5},{8,10},{9,11},{10,... | collective-permute-start | bytes 3145736 | tf_op jit(solution)/shard_map/ppermute | solution.py:21
  41.5 49.0 %all-gather.7 = f16[64,136,256]{2,1,0:T(8,128)(2,1)S(1)} all-gather(f16[2,136,256]{2,1,0:T(8,128)(2,1)S(1)} %gather_fusion), channel_id=3, replica_groups={{0,1,32,33,64,65,96,97,128,129,160,161,192,193,224,225,256,257,288,289,..., dimensions={0}, use_global_device_ids=true | all-gather | bytes 4595712 | tf_op jit(solution)/shard_map/all_gather | solution.py:124
  90.5 0.0 collective-permute-done.refs_1_
  90.5 0.0 collective-permute-done.1.refs_3_
  90.5 0.2 slice_reduce_fusion
  90.7 0.1 copy.9
  90.8 0.0 copy-start.1
  90.8 0.0 copy-start.2
  90.8 1.2 multiply_convert_fusion.1
  92.0 0.0 copy-done.1
  92.0 0.3 copy-done.2
  92.3 2.9 %hidden.1 = (bf16[512,256]{1,0:T(8,128)(2,1)S(1)}, f32[1,256]{1,0:T(1,128)S(1)}) custom-call(s32[7]{0:T(128)S(1)} %pad_add_fusion.facts, bf16[16,512,256]{2,1,0:T(8,128)(2,1)S(1)} %bitcast.17, bf16[4096,128]{1,0:T(8,128)(2,1)S(1)} %bitcast.19, bf16[4096,128]{1,0:T(8,128)(2,1)S(1)} %collective-permute-done.refs_1_, bf16[4096,128]{1,0:T(8,128)(2,1)S(1)} %bitcast.21, ...), custom_call_target="tpu_custom_call" | custom-call | flops 2147483648 | bytes 8388608 | tf_op jit(solution)/shard_map/hidden/pallas_call | solution.py:92
  95.3 0.1 multiply_convert_fusion.2
  95.4 0.1 pad_maximum_fusion
  95.4 54.5 %all-gather.8 = f16[8320,256]{1,0:T(8,128)(2,1)S(1)} all-gather(f16[520,256]{1,0:T(8,128)(2,1)S(1)} %pad_maximum_fusion), channel_id=4, replica_groups=mesh['tok'=16,'exp'=32] {'tok'}, dimensions={0}, use_global_device_ids=true | all-gather | bytes 4526080 | tf_op jit(solution)/shard_map/all_gather | solution.py:132
  150.0 1.0 multiply_convert_fusion.gathered
  151.0 0.2 copy-done.3
  151.2 1.8 down.1
  153.0 6.0 %collective-permute-start.3 = (bf16[512,256]{1,0:T(8,128)(2,1)S(1)}, bf16[512,256]{1,0:T(8,128)(2,1)S(1)}, u32[]{:S(2)}, u32[]{:S(2)}) collective-permute-start(bf16[512,256]{1,0:T(8,128)(2,1)S(1)} %get-tuple-element.32), channel_id=1, source_target_pairs={{0,1},{1,0},{2,3},{3,2},{4,5},{5,4},{6,7},{7,6},{8,9},{9,8},{10,11... | collective-permute-start | bytes 786440 | tf_op jit(solution)/shard_map/ppermute | solution.py:25
  159.0 1.1 collective-permute-done.3
  160.1 0.6 place.1
  160.8 21.2 %all_to_all.5 = bf16[16,128,256]{2,1,0:T(8,128)(2,1)S(1)} all-to-all(bf16[16,128,256]{2,1,0:T(8,128)(2,1)S(1)} %place.1), channel_id=1, replica_groups={{0,2,4,6,8,10,12,14,16,18,20,22,24,26,28,30},{1,3,5,7,9,11,13,15,17,19,..., dimensions={0} | all-to-all | bytes 2097152 | tf_op jit(solution)/shard_map/all_to_all | solution.py:143
  182.0 0.8 reduce_sum.12
  (17 shorter events, 0.2 us)
Async XLA Ops:
  0.0 1.8 copy-start
  32.7 57.7 %collective-permute-start = (bf16[4096,128]{1,0:T(8,128)(2,1)}, bf16[4096,128]{1,0:T(8,128)(2,1)S(1)}, u32[]{:S(2)}, u32[]{:S(2)}) collective-permute-start(bf16[4096,128]{1,0:T(8,128)(2,1)} %bitcast.18), channel_id=1, source_target_pairs={{0,2},{1,3},{2,0},{3,1},{4,6},{5,7},{6,4},{7,5},{8,10},{9,11},{10,... | collective-permute-start | bytes 3145736 | tf_op jit(solution)/shard_map/ppermute | solution.py:21
  36.2 54.3 %collective-permute-start.1 = (bf16[4096,128]{1,0:T(8,128)(2,1)}, bf16[4096,128]{1,0:T(8,128)(2,1)S(1)}, u32[]{:S(2)}, u32[]{:S(2)}) collective-permute-start(bf16[4096,128]{1,0:T(8,128)(2,1)} %bitcast.20), channel_id=1, source_target_pairs={{0,2},{1,3},{2,0},{3,1},{4,6},{5,7},{6,4},{7,5},{8,10},{9,11},{10,... | collective-permute-start | bytes 3145736 | tf_op jit(solution)/shard_map/ppermute | solution.py:21
  38.1 112.9 %collective-permute-start.2 = (bf16[2048,256]{1,0:T(8,128)(2,1)}, bf16[2048,256]{1,0:T(8,128)(2,1)S(1)}, u32[]{:S(2)}, u32[]{:S(2)}) collective-permute-start(bf16[2048,256]{1,0:T(8,128)(2,1)} %bitcast.22), channel_id=1, source_target_pairs={{0,2},{1,3},{2,0},{3,1},{4,6},{5,7},{6,4},{7,5},{8,10},{9,11},{10,... | collective-permute-start | bytes 3145736 | tf_op jit(solution)/shard_map/ppermute | solution.py:21
  90.8 1.2 copy-start.1
  90.8 1.5 copy-start.2
  150.0 1.2 copy-start.3
  150.0 1.2 copy-start.4
  153.0 7.1 %collective-permute-start.3 = (bf16[512,256]{1,0:T(8,128)(2,1)S(1)}, bf16[512,256]{1,0:T(8,128)(2,1)S(1)}, u32[]{:S(2)}, u32[]{:S(2)}) collective-permute-start(bf16[512,256]{1,0:T(8,128)(2,1)S(1)} %get-tuple-element.32), channel_id=1, source_target_pairs={{0,1},{1,0},{2,3},{3,2},{4,5},{5,4},{6,7},{7,6},{8,9},{9,8},{10,11... | collective-permute-start | bytes 786440 | tf_op jit(solution)/shard_map/ppermute | solution.py:25

commit v16 on v15

--- a/solution.py
+++ b/solution.py
@@ -119,10 +119,11 @@
     largest = jnp.max(jnp.abs(tokens.astype(jnp.float32)), axis=0, keepdims=True)
     coded, facts, mine = lax.optimization_barrier((encode(tokens, largest), facts, mine))
     picked = lax.all_gather(coded, "exp")[mine]
-    picked, sent = lax.optimization_barrier((picked, own))
+    picked, *sent = lax.optimization_barrier((picked, *own[:2]))
     far = [swap_across(weight) for weight in sent]
     gathered = lax.all_gather(picked, ("tok", "exp"), axis_index_groups=LINES)
-    gathered, far[:2] = lax.optimization_barrier((gathered, far[:2]))
+    gathered, far, down_sent = lax.optimization_barrier((gathered, far, own[2]))
+    far.append(swap_across(down_sent))
     gathered = decode(gathered).reshape(DEPTH, rows, features)
     flops = 2 * rows * DEPTH * features * SPAN * units
     hidden, largest = kernel_call(

time: 184 us -> 186 us (1.011)
    ppermute x1, starting transfers between devices: 5.96 us -> 7.88 us  [swap_core(): return lax.ppermute(value, 'exp', [(p, p ^ 1) for p in range(OWNERS)])]
  transfers between devices with their start and end apart: 4 -> 4, of which waited for: 1 -> 1; matrix products, arithmetic and copies ran while one was open for 1% -> 1% of each run, Pallas kernels for 2% -> 0%
where the time goes in v16:
time: 186 us
  blocking collectives  156 us (84%)
  starting transfers between devices  16 us (9%)
  Pallas kernels  5.36 us (3%)
  other arithmetic  5.23 us (3%)
    all_gather x1, blocking collectives, shards(): gathered = lax.all_gather(encode(hidden, largest)[None], 'tok', tiled=True)  55.4 us
    all_gather x1, blocking collectives, shards(): gathered = lax.all_gather(picked, ('tok', 'exp'), axis_index_groups=LINES)  49.6 us
    all_gather x1, blocking collectives, shards(): picked = lax.all_gather(coded, 'exp')[mine]  30.1 us
    all_to_all x1, blocking collectives, shards(): lax.all_to_all(outgoing, 'exp', 0, 0, axis_index_groups=SAME_CORE, tiled=...  20.9 us
    ppermute x3, starting transfers between devices, swap_across(): return lax.ppermute(value, 'exp', [(p, p ^ 2) for p in range(OWNERS)])  8.11 us
    ppermute x1, starting transfers between devices, swap_core(): return lax.ppermute(value, 'exp', [(p, p ^ 1) for p in range(OWNERS)])  7.88 us
    pallas_call x3, Pallas kernels, kernel_call(): pl.pallas_call(kernel, out_shape=outs, in_specs=[pl.BlockSpec(memory_spac...  5.36 us
  transfers between devices with their start and end apart: 4, of which 1 were waited for; matrix products, arithmetic and copies ran while one was open for 1% of the time, Pallas kernels for 0%

profile of v16, /device:TPU:1, one launch (start us, length us, event | category | flops | bytes accessed | tf_op | source)
XLA Modules:
  0.0 185.8 jit_solution(10356548130250888759)
XLA Ops:
  0.0 0.7 copy-done
  0.7 0.1 dynamic-slice_bitcast_fusion.1
  0.8 0.1 dynamic-slice_bitcast_fusion
  0.8 0.9 fusion
  1.7 0.9 fusion.1
  2.6 0.1 pad_add_fusion.facts
  2.7 30.1 %all-gather.6 = f16[4352,256]{1,0:T(8,128)(2,1)S(1)} all-gather(f16[136,256]{1,0:T(8,128)(2,1)S(1)} %pad_maximum_fusion.1), channel_id=2, replica_groups=mesh['tok'=16,'exp'=32] {'exp'}, dimensions={0}, use_global_device_ids=true | all-gather | bytes 2297856 | tf_op jit(solution)/shard_map/all_gather | solution.py:121
  32.8 0.6 gather_fusion
  33.4 3.4 %collective-permute-start = (bf16[4096,128]{1,0:T(8,128)(2,1)}, bf16[4096,128]{1,0:T(8,128)(2,1)S(1)}, u32[]{:S(2)}, u32[]{:S(2)}) collective-permute-start(bf16[4096,128]{1,0:T(8,128)(2,1)} %bitcast.18), channel_id=1, source_target_pairs={{0,2},{1,3},{2,0},{3,1},{4,6},{5,7},{6,4},{7,5},{8,10},{9,11},{10,... | collective-permute-start | bytes 3145736 | tf_op jit(solution)/shard_map/ppermute | solution.py:21
  36.8 1.9 %collective-permute-start.1 = (bf16[4096,128]{1,0:T(8,128)(2,1)}, bf16[4096,128]{1,0:T(8,128)(2,1)S(1)}, u32[]{:S(2)}, u32[]{:S(2)}) collective-permute-start(bf16[4096,128]{1,0:T(8,128)(2,1)} %bitcast.20), channel_id=1, source_target_pairs={{0,2},{1,3},{2,0},{3,1},{4,6},{5,7},{6,4},{7,5},{8,10},{9,11},{10,... | collective-permute-start | bytes 3145736 | tf_op jit(solution)/shard_map/ppermute | solution.py:21
  38.8 49.6 %all-gather.7 = f16[64,136,256]{2,1,0:T(8,128)(2,1)S(1)} all-gather(f16[2,136,256]{2,1,0:T(8,128)(2,1)S(1)} %gather_fusion), channel_id=3, replica_groups={{0,1,32,33,64,65,96,97,128,129,160,161,192,193,224,225,256,257,288,289,..., dimensions={0}, use_global_device_ids=true | all-gather | bytes 4595712 | tf_op jit(solution)/shard_map/all_gather | solution.py:124
  88.4 0.0 collective-permute-done.refs_1_
  88.4 0.2 slice_reduce_fusion
  88.7 0.1 copy.9
  88.7 0.0 copy-start.1
  88.7 0.0 copy-start.2
  88.8 1.2 multiply_convert_fusion.1
  89.9 0.0 copy-start.3
  89.9 0.0 copy-done.1
  90.0 0.3 copy-done.2
  90.3 2.9 %hidden.1 = (bf16[512,256]{1,0:T(8,128)(2,1)S(1)}, f32[1,256]{1,0:T(1,128)S(1)}) custom-call(s32[7]{0:T(128)S(1)} %pad_add_fusion.facts, bf16[16,512,256]{2,1,0:T(8,128)(2,1)S(1)} %bitcast.17, bf16[4096,128]{1,0:T(8,128)(2,1)S(1)} %bitcast.19, bf16[4096,128]{1,0:T(8,128)(2,1)S(1)} %collective-permute-done.refs_1_, bf16[4096,128]{1,0:T(8,128)(2,1)S(1)} %bitcast.21, ...), custom_call_target="tpu_custom_call" | custom-call | flops 2147483648 | bytes 8388608 | tf_op jit(solution)/shard_map/hidden/pallas_call | solution.py:92
  93.2 2.7 %collective-permute-start.2 = (bf16[2048,256]{1,0:T(8,128)(2,1)S(1)}, bf16[2048,256]{1,0:T(8,128)(2,1)S(1)}, u32[]{:S(2)}, u32[]{:S(2)}) collective-permute-start(bf16[2048,256]{1,0:T(8,128)(2,1)S(1)} %bitcast.22), channel_id=1, source_target_pairs={{0,2},{1,3},{2,0},{3,1},{4,6},{5,7},{6,4},{7,5},{8,10},{9,11},{10,... | collective-permute-start | bytes 3145736 | tf_op jit(solution)/shard_map/ppermute | solution.py:21
  96.0 0.1 multiply_convert_fusion.2
  96.1 0.1 pad_maximum_fusion
  96.1 55.4 %all-gather.8 = f16[8320,256]{1,0:T(8,128)(2,1)S(1)} all-gather(f16[520,256]{1,0:T(8,128)(2,1)S(1)} %pad_maximum_fusion), channel_id=4, replica_groups=mesh['tok'=16,'exp'=32] {'tok'}, dimensions={0}, use_global_device_ids=true | all-gather | bytes 4526080 | tf_op jit(solution)/shard_map/all_gather | solution.py:133
  151.6 1.0 multiply_convert_fusion.gathered
  152.6 1.8 down.1
  154.4 7.9 %collective-permute-start.3 = (bf16[512,256]{1,0:T(8,128)(2,1)S(1)}, bf16[512,256]{1,0:T(8,128)(2,1)S(1)}, u32[]{:S(2)}, u32[]{:S(2)}) collective-permute-start(bf16[512,256]{1,0:T(8,128)(2,1)S(1)} %get-tuple-element.32), channel_id=1, source_target_pairs={{0,1},{1,0},{2,3},{3,2},{4,5},{5,4},{6,7},{7,6},{8,9},{9,8},{10,11... | collective-permute-start | bytes 786440 | tf_op jit(solution)/shard_map/ppermute | solution.py:25
  162.3 1.1 collective-permute-done.3
  163.4 0.7 place.1
  164.1 20.9 %all_to_all.5 = bf16[16,128,256]{2,1,0:T(8,128)(2,1)S(1)} all-to-all(bf16[16,128,256]{2,1,0:T(8,128)(2,1)S(1)} %place.1), channel_id=1, replica_groups={{0,2,4,6,8,10,12,14,16,18,20,22,24,26,28,30},{1,3,5,7,9,11,13,15,17,19,..., dimensions={0} | all-to-all | bytes 2097152 | tf_op jit(solution)/shard_map/all_to_all | solution.py:144
  185.0 0.8 reduce_sum.12
  (17 shorter events, 0.2 us)
Async XLA Ops:
  0.0 0.7 copy-start
  33.4 55.0 %collective-permute-start = (bf16[4096,128]{1,0:T(8,128)(2,1)}, bf16[4096,128]{1,0:T(8,128)(2,1)S(1)}, u32[]{:S(2)}, u32[]{:S(2)}) collective-permute-start(bf16[4096,128]{1,0:T(8,128)(2,1)} %bitcast.18), channel_id=1, source_target_pairs={{0,2},{1,3},{2,0},{3,1},{4,6},{5,7},{6,4},{7,5},{8,10},{9,11},{10,... | collective-permute-start | bytes 3145736 | tf_op jit(solution)/shard_map/ppermute | solution.py:21
  36.8 51.6 %collective-permute-start.1 = (bf16[4096,128]{1,0:T(8,128)(2,1)}, bf16[4096,128]{1,0:T(8,128)(2,1)S(1)}, u32[]{:S(2)}, u32[]{:S(2)}) collective-permute-start(bf16[4096,128]{1,0:T(8,128)(2,1)} %bitcast.20), channel_id=1, source_target_pairs={{0,2},{1,3},{2,0},{3,1},{4,6},{5,7},{6,4},{7,5},{8,10},{9,11},{10,... | collective-permute-start | bytes 3145736 | tf_op jit(solution)/shard_map/ppermute | solution.py:21
  88.7 1.2 copy-start.1
  88.7 1.5 copy-start.2
  89.9 3.3 %copy-start.3 = (bf16[1,2048,256]{2,1,0:T(8,128)(2,1)S(1)}, bf16[1,2048,256]{2,1,0:T(8,128)(2,1)}, u32[]{:S(2)}) copy-start(bf16[1,2048,256]{2,1,0:T(8,128)(2,1)} %param.11) | copy-start | bytes 3145732
  93.2 59.3 %collective-permute-start.2 = (bf16[2048,256]{1,0:T(8,128)(2,1)S(1)}, bf16[2048,256]{1,0:T(8,128)(2,1)S(1)}, u32[]{:S(2)}, u32[]{:S(2)}) collective-permute-start(bf16[2048,256]{1,0:T(8,128)(2,1)S(1)} %bitcast.22), channel_id=1, source_target_pairs={{0,2},{1,3},{2,0},{3,1},{4,6},{5,7},{6,4},{7,5},{8,10},{9,11},{10,... | collective-permute-start | bytes 3145736 | tf_op jit(solution)/shard_map/ppermute | solution.py:21
  151.5 1.0 copy-start.4
  154.4 9.0 %collective-permute-start.3 = (bf16[512,256]{1,0:T(8,128)(2,1)S(1)}, bf16[512,256]{1,0:T(8,128)(2,1)S(1)}, u32[]{:S(2)}, u32[]{:S(2)}) collective-permute-start(bf16[512,256]{1,0:T(8,128)(2,1)S(1)} %get-tuple-element.32), channel_id=1, source_target_pairs={{0,1},{1,0},{2,3},{3,2},{4,5},{5,4},{6,7},{7,6},{8,9},{9,8},{10,11... | collective-permute-start | bytes 786440 | tf_op jit(solution)/shard_map/ppermute | solution.py:25

commit v17 on v14

--- a/solution.py
+++ b/solution.py
@@ -115,12 +115,12 @@
     mine = lax.dynamic_slice_in_dim(picks, half // 2 * core, half // 2)
     facts = jnp.concatenate([picks, jnp.stack([core, expert, side]).astype(jnp.int32)])
 
-    in_own, down_own = jnp.stack([w_gate[0], w_up[0]]), w_down[0]
     largest = jnp.max(jnp.abs(tokens.astype(jnp.float32)), axis=0, keepdims=True)
     coded, facts, mine = lax.optimization_barrier((encode(tokens, largest), facts, mine))
     picked = lax.all_gather(coded, "exp")[mine]
-    picked, in_sent, down_sent = lax.optimization_barrier((picked, in_own, down_own))
-    in_far, down_far = swap_across(in_sent), swap_across(down_sent)
+    picked, w_gate, w_up, w_down = lax.optimization_barrier((picked, w_gate, w_up, w_down))
+    in_own, down_own = jnp.stack([w_gate[0], w_up[0]]), w_down[0]
+    in_far, down_far = swap_across(in_own), swap_across(down_own)
     gathered = lax.all_gather(picked, ("tok", "exp"), axis_index_groups=LINES)
     gathered, in_far = lax.optimization_barrier((gathered, in_far))
     gathered = decode(gathered).reshape(DEPTH, rows, features)

time: 190 us -> 186 us (0.979)
  blocking collectives: 158 us -> 156 us
    all_gather x1, blocking collectives: 32.2 us -> 30 us  [shards(): picked = lax.all_gather(coded, 'exp')[mine]]
where the time goes in v17:
time: 186 us
  blocking collectives  156 us (84%)
  starting transfers between devices  14.4 us (8%)
  other arithmetic  5.41 us (3%)
  Pallas kernels  5.35 us (3%)
  local copies, waits for them, and re-layouts  3.5 us (2%)
    all_gather x1, blocking collectives, shards(): gathered = lax.all_gather(encode(hidden, largest)[None], 'tok', tiled=True)  55.4 us
    all_gather x1, blocking collectives, shards(): gathered = lax.all_gather(picked, ('tok', 'exp'), axis_index_groups=LINES)  49.6 us
    all_gather x1, blocking collectives, shards(): picked = lax.all_gather(coded, 'exp')[mine]  30 us
    all_to_all x1, blocking collectives, shards(): lax.all_to_all(outgoing, 'exp', 0, 0, axis_index_groups=SAME_CORE, tiled=...  20.7 us
    ppermute x1, starting transfers between devices, swap_core(): return lax.ppermute(value, 'exp', [(p, p ^ 1) for p in range(OWNERS)])  9.02 us
    ppermute x2, starting transfers between devices, swap_across(): return lax.ppermute(value, 'exp', [(p, p ^ 2) for p in range(OWNERS)])  5.36 us
    pallas_call x3, Pallas kernels, kernel_call(): pl.pallas_call(kernel, out_shape=outs, in_specs=[pl.BlockSpec(memory_spac...  5.35 us
  transfers between devices with their start and end apart: 3, of which 1 were waited for; matrix products, arithmetic and copies ran while one was open for 1% of the time, Pallas kernels for 2%

profile of v17, /device:TPU:1, one launch (start us, length us, event | category | flops | bytes accessed | tf_op | source)
XLA Modules:
  0.0 185.7 jit_solution(16967699589271558758)
XLA Ops:
  0.0 0.0 copy-start
  0.0 1.0 fusion
  1.0 0.9 fusion.1
  1.9 0.0 copy-done
  1.9 0.1 dynamic-slice_bitcast_fusion.1
  2.0 0.1 dynamic-slice_bitcast_fusion
  2.1 0.1 pad_add_fusion.facts
  2.1 30.0 %all-gather.6 = f16[4352,256]{1,0:T(8,128)(2,1)S(1)} all-gather(f16[136,256]{1,0:T(8,128)(2,1)S(1)} %pad_maximum_fusion.1), channel_id=2, replica_groups=mesh['tok'=16,'exp'=32] {'exp'}, dimensions={0}, use_global_device_ids=true | all-gather | bytes 2297856 | tf_op jit(solution)/shard_map/all_gather | solution.py:120
  32.2 0.6 gather_fusion
  32.8 1.3 constant_dynamic-update-slice_fusion.1
  34.1 1.4 constant_dynamic-update-slice_fusion.refs_0_
  35.5 3.4 %collective-permute-start = (bf16[2,4096,128]{2,1,0:T(8,128)(2,1)S(1)}, bf16[2,4096,128]{2,1,0:T(8,128)(2,1)S(1)}, u32[]{:S(2)}, u32[]{:S(2)}) collective-permute-start(bf16[2,4096,128]{2,1,0:T(8,128)(2,1)S(1)} %constant_dynamic-update-slice_fusion.refs_0_), channel_id=1, source_target_pairs={{0,2},{1,3},{2,0},{3,1},{4,6},{5,7},{6,4},{7,5},{8,10},{9,11},{10,... | collective-permute-start | bytes 6291464 | tf_op jit(solution)/shard_map/ppermute | solution.py:21
  38.9 0.0 copy-done.1
  38.9 1.9 %collective-permute-start.1 = (bf16[2048,256]{1,0:T(8,128)(2,1)S(1)}, bf16[2048,256]{1,0:T(8,128)(2,1)S(1)}, u32[]{:S(2)}, u32[]{:S(2)}) collective-permute-start(bf16[2048,256]{1,0:T(8,128)(2,1)S(1)} %bitcast.16), channel_id=1, source_target_pairs={{0,2},{1,3},{2,0},{3,1},{4,6},{5,7},{6,4},{7,5},{8,10},{9,11},{10,... | collective-permute-start | bytes 3145736 | tf_op jit(solution)/shard_map/ppermute | solution.py:21
  40.9 49.6 %all-gather.7 = f16[64,136,256]{2,1,0:T(8,128)(2,1)S(1)} all-gather(f16[2,136,256]{2,1,0:T(8,128)(2,1)S(1)} %gather_fusion), channel_id=3, replica_groups={{0,1,32,33,64,65,96,97,128,129,160,161,192,193,224,225,256,257,288,289,..., dimensions={0}, use_global_device_ids=true | all-gather | bytes 4595712 | tf_op jit(solution)/shard_map/all_gather | solution.py:124
  90.5 0.0 collective-permute-done.refs_1_
  90.5 0.2 slice_reduce_fusion
  90.7 0.1 copy.9
  90.8 1.2 multiply_convert_fusion.1
  92.0 2.9 %hidden.1 = (bf16[512,256]{1,0:T(8,128)(2,1)S(1)}, f32[1,256]{1,0:T(1,128)S(1)}) custom-call(s32[7]{0:T(128)S(1)} %pad_add_fusion.facts, bf16[16,512,256]{2,1,0:T(8,128)(2,1)S(1)} %bitcast.15, bf16[2,4096,128]{2,1,0:T(8,128)(2,1)S(1)} %constant_dynamic-update-slice_fusion.refs_0_, bf16[2,4096,128]{2,1,0:T(8,128)(2,1)S(1)} %collective-permute-done.refs_1_), custom_call_target="tpu_custom_call" | custom-call | flops 2147483648 | bytes 8388608 | tf_op jit(solution)/shard_map/hidden/pallas_call | solution.py:92
  95.0 0.1 multiply_convert_fusion.2
  95.0 0.1 pad_maximum_fusion
  95.1 55.4 %all-gather.8 = f16[8320,256]{1,0:T(8,128)(2,1)S(1)} all-gather(f16[520,256]{1,0:T(8,128)(2,1)S(1)} %pad_maximum_fusion), channel_id=4, replica_groups=mesh['tok'=16,'exp'=32] {'tok'}, dimensions={0}, use_global_device_ids=true | all-gather | bytes 4526080 | tf_op jit(solution)/shard_map/all_gather | solution.py:132
  150.5 0.0 copy-start.2
  150.6 1.0 multiply_convert_fusion.gathered
  151.6 0.0 collective-permute-done.1.refs_1_
  151.6 1.8 down.1
  153.4 9.0 %collective-permute-start.2 = (bf16[512,256]{1,0:T(8,128)(2,1)S(1)}, bf16[512,256]{1,0:T(8,128)(2,1)S(1)}, u32[]{:S(2)}, u32[]{:S(2)}) collective-permute-start(bf16[512,256]{1,0:T(8,128)(2,1)S(1)} %get-tuple-element.30), channel_id=1, source_target_pairs={{0,1},{1,0},{2,3},{3,2},{4,5},{5,4},{6,7},{7,6},{8,9},{9,8},{10,11... | collective-permute-start | bytes 786440 | tf_op jit(solution)/shard_map/ppermute | solution.py:25
  162.4 1.1 collective-permute-done.2
  163.6 0.7 place.1
  164.2 20.7 %all_to_all.5 = bf16[16,128,256]{2,1,0:T(8,128)(2,1)S(1)} all-to-all(bf16[16,128,256]{2,1,0:T(8,128)(2,1)S(1)} %place.1), channel_id=1, replica_groups={{0,2,4,6,8,10,12,14,16,18,20,22,24,26,28,30},{1,3,5,7,9,11,13,15,17,19,..., dimensions={0} | all-to-all | bytes 2097152 | tf_op jit(solution)/shard_map/all_to_all | solution.py:143
  185.0 0.8 reduce_sum.12
  (13 shorter events, 0.2 us)
Async XLA Ops:
  0.0 1.9 %copy-start = (s32[8,8]{1,0:T(8,128)S(1)}, s32[8,8]{1,0:T(8,128)}, u32[]{:S(2)}) copy-start(s32[8,8]{1,0:T(8,128)} %param.7) | copy-start | bytes 772
  0.0 38.9 %copy-start.1 = (bf16[1,2048,256]{2,1,0:T(8,128)(2,1)S(1)}, bf16[1,2048,256]{2,1,0:T(8,128)(2,1)}, u32[]{:S(2)}) copy-start(bf16[1,2048,256]{2,1,0:T(8,128)(2,1)} %param.11) | copy-start | bytes 3145732
  35.5 55.0 %collective-permute-start = (bf16[2,4096,128]{2,1,0:T(8,128)(2,1)S(1)}, bf16[2,4096,128]{2,1,0:T(8,128)(2,1)S(1)}, u32[]{:S(2)}, u32[]{:S(2)}) collective-permute-start(bf16[2,4096,128]{2,1,0:T(8,128)(2,1)S(1)} %constant_dynamic-update-slice_fusion.refs_0_), channel_id=1, source_target_pairs={{0,2},{1,3},{2,0},{3,1},{4,6},{5,7},{6,4},{7,5},{8,10},{9,11},{10,... | collective-permute-start | bytes 6291464 | tf_op jit(solution)/shard_map/ppermute | solution.py:21
  38.9 112.7 %collective-permute-start.1 = (bf16[2048,256]{1,0:T(8,128)(2,1)S(1)}, bf16[2048,256]{1,0:T(8,128)(2,1)S(1)}, u32[]{:S(2)}, u32[]{:S(2)}) collective-permute-start(bf16[2048,256]{1,0:T(8,128)(2,1)S(1)} %bitcast.16), channel_id=1, source_target_pairs={{0,2},{1,3},{2,0},{3,1},{4,6},{5,7},{6,4},{7,5},{8,10},{9,11},{10,... | collective-permute-start | bytes 3145736 | tf_op jit(solution)/shard_map/ppermute | solution.py:21
  150.5 1.0 copy-start.2
  153.4 10.2 %collective-permute-start.2 = (bf16[512,256]{1,0:T(8,128)(2,1)S(1)}, bf16[512,256]{1,0:T(8,128)(2,1)S(1)}, u32[]{:S(2)}, u32[]{:S(2)}) collective-permute-start(bf16[512,256]{1,0:T(8,128)(2,1)S(1)} %get-tuple-element.30), channel_id=1, source_target_pairs={{0,1},{1,0},{2,3},{3,2},{4,5},{5,4},{6,7},{7,6},{8,9},{9,8},{10,11... | collective-permute-start | bytes 786440 | tf_op jit(solution)/shard_map/ppermute | solution.py:25

commit v18 on v15

--- a/solution.py
+++ b/solution.py
@@ -83,6 +83,20 @@
             out[pl.ds(lax.div(block, 2), 1)] = both.astype(out.dtype)[None]
 
 
+def arrive_kernel(picks, owner, arrived, out):
+    found, first, second = jnp.int32(0), jnp.int32(0), jnp.int32(0)
+    experts, count = picks.shape
+    for expert in range(experts):
+        for pick in range(count):
+            chip = 2 * expert + pick // (count // 2)
+            hit = picks[expert, pick] == owner[0]
+            first = jnp.where(hit & (found == 0), chip, first)
+            second = jnp.where(hit & (found == 1), chip, second)
+            found = jnp.where(hit, found + 1, found)
+    both = arrived[pl.ds(first, 1)].astype(jnp.float32) + arrived[pl.ds(second, 1)].astype(jnp.float32)
+    out[...] = both[0].astype(out.dtype)
+
+
 def array_of(*shape):
     return jax.ShapeDtypeStruct(shape, jnp.bfloat16)
 
@@ -117,7 +131,8 @@
 
     own = [w_gate[0], w_up[0], w_down[0]]
     largest = jnp.max(jnp.abs(tokens.astype(jnp.float32)), axis=0, keepdims=True)
-    coded, facts, mine = lax.optimization_barrier((encode(tokens, largest), facts, mine))
+    owner = position.astype(jnp.int32).reshape(1)
+    coded, facts, mine, owner = lax.optimization_barrier((encode(tokens, largest), facts, mine, owner))
     picked = lax.all_gather(coded, "exp")[mine]
     picked, sent = lax.optimization_barrier((picked, own))
     far = [swap_across(weight) for weight in sent]
@@ -141,7 +156,14 @@
         [array_of(CHIPS, BLOCK, features)], 0,
     )
     arrived = lax.all_to_all(outgoing, "exp", 0, 0, axis_index_groups=SAME_CORE, tiled=True)
-    return jnp.sum(arrived, axis=0, dtype=jnp.float32).astype(jnp.bfloat16)
+    in_smem, in_vmem = pl.BlockSpec(memory_space=pltpu.SMEM), pl.BlockSpec(memory_space=pltpu.VMEM)
+    return pl.pallas_call(
+        arrive_kernel,
+        out_shape=array_of(BLOCK, features),
+        in_specs=[in_smem, in_smem, in_vmem],
+        out_specs=in_vmem,
+        name="arrive",
+    )(picked_blocks, owner, pltpu.with_memory_space_constraint(arrived, pltpu.VMEM))
 
 
 def solution(mesh):

time: 184 us -> 186 us (1.011)
  no operation moved by 1% of the time
where the time goes in v18:
time: 186 us; the launch traced here: 185 us
  blocking collectives  155 us (83%)
  starting transfers between devices  14.7 us (8%)
  Pallas kernels  6.87 us (4%)
  other arithmetic  4.46 us (2%)
  local copies, waits for them, and re-layouts  2.74 us (1%)
    all_gather x1, blocking collectives, shards(): gathered = lax.all_gather(encode(hidden, largest)[None], 'tok', tiled=True)  54.5 us
    all_gather x1, blocking collectives, shards(): gathered = lax.all_gather(picked, ('tok', 'exp'), axis_index_groups=LINES)  49 us
    all_gather x1, blocking collectives, shards(): picked = lax.all_gather(coded, 'exp')[mine]  30 us
    all_to_all x1, blocking collectives, shards(): lax.all_to_all(outgoing, 'exp', 0, 0, axis_index_groups=SAME_CORE, tiled=...  21.2 us
    ppermute x3, starting transfers between devices, swap_across(): return lax.ppermute(value, 'exp', [(p, p ^ 2) for p in range(OWNERS)])  8.73 us
    ppermute x1, starting transfers between devices, swap_core(): return lax.ppermute(value, 'exp', [(p, p ^ 1) for p in range(OWNERS)])  5.96 us
    pallas_call x3, Pallas kernels, kernel_call(): pl.pallas_call(kernel, out_shape=outs, in_specs=[pl.BlockSpec(memory_spac...  5.34 us
  transfers between devices with their start and end apart: 4, of which 1 were waited for; matrix products, arithmetic and copies ran while one was open for 1% of the time, Pallas kernels for 2%

profile of v18, /device:TPU:1, one launch (start us, length us, event | category | flops | bytes accessed | tf_op | source)
XLA Modules:
  0.0 184.9 jit_solution(15269916804540713746)
XLA Ops:
  0.0 0.9 fusion
  0.9 0.9 fusion.1
  1.8 0.8 dynamic-slice_bitcast_fusion.1
  2.5 0.8 dynamic-slice_bitcast_fusion
  3.3 0.1 pad_add_fusion.facts
  3.4 30.0 %all-gather.6 = f16[4352,256]{1,0:T(8,128)(2,1)S(1)} all-gather(f16[136,256]{1,0:T(8,128)(2,1)S(1)} %pad_maximum_fusion.1), channel_id=2, replica_groups=mesh['tok'=16,'exp'=32] {'exp'}, dimensions={0}, use_global_device_ids=true | all-gather | bytes 2297856 | tf_op jit(solution)/shard_map/all_gather | solution.py:136
  33.5 0.6 gather_fusion
  34.1 3.4 %collective-permute-start = (bf16[4096,128]{1,0:T(8,128)(2,1)}, bf16[4096,128]{1,0:T(8,128)(2,1)S(1)}, u32[]{:S(2)}, u32[]{:S(2)}) collective-permute-start(bf16[4096,128]{1,0:T(8,128)(2,1)} %bitcast.19), channel_id=1, source_target_pairs={{0,2},{1,3},{2,0},{3,1},{4,6},{5,7},{6,4},{7,5},{8,10},{9,11},{10,... | collective-permute-start | bytes 3145736 | tf_op jit(solution)/shard_map/ppermute | solution.py:21
  37.5 1.9 %collective-permute-start.1 = (bf16[4096,128]{1,0:T(8,128)(2,1)}, bf16[4096,128]{1,0:T(8,128)(2,1)S(1)}, u32[]{:S(2)}, u32[]{:S(2)}) collective-permute-start(bf16[4096,128]{1,0:T(8,128)(2,1)} %bitcast.21), channel_id=1, source_target_pairs={{0,2},{1,3},{2,0},{3,1},{4,6},{5,7},{6,4},{7,5},{8,10},{9,11},{10,... | collective-permute-start | bytes 3145736 | tf_op jit(solution)/shard_map/ppermute | solution.py:21
  39.5 3.4 %collective-permute-start.2 = (bf16[2048,256]{1,0:T(8,128)(2,1)}, bf16[2048,256]{1,0:T(8,128)(2,1)S(1)}, u32[]{:S(2)}, u32[]{:S(2)}) collective-permute-start(bf16[2048,256]{1,0:T(8,128)(2,1)} %bitcast.23), channel_id=1, source_target_pairs={{0,2},{1,3},{2,0},{3,1},{4,6},{5,7},{6,4},{7,5},{8,10},{9,11},{10,... | collective-permute-start | bytes 3145736 | tf_op jit(solution)/shard_map/ppermute | solution.py:21
  42.8 49.0 %all-gather.7 = f16[64,136,256]{2,1,0:T(8,128)(2,1)S(1)} all-gather(f16[2,136,256]{2,1,0:T(8,128)(2,1)S(1)} %gather_fusion), channel_id=3, replica_groups={{0,1,32,33,64,65,96,97,128,129,160,161,192,193,224,225,256,257,288,289,..., dimensions={0}, use_global_device_ids=true | all-gather | bytes 4595712 | tf_op jit(solution)/shard_map/all_gather | solution.py:139
  91.8 0.0 collective-permute-done.refs_1_
  91.8 0.0 collective-permute-done.1.refs_3_
  91.8 0.2 slice_reduce_fusion
  92.1 0.1 copy.9
  92.1 0.0 copy-start
  92.1 0.0 copy-start.1
  92.2 1.2 multiply_convert_fusion.1
  93.3 0.0 copy-done
  93.4 0.3 copy-done.1
  93.7 2.9 %hidden.1 = (bf16[512,256]{1,0:T(8,128)(2,1)S(1)}, f32[1,256]{1,0:T(1,128)S(1)}) custom-call(s32[7]{0:T(128)S(1)} %pad_add_fusion.facts, bf16[16,512,256]{2,1,0:T(8,128)(2,1)S(1)} %bitcast.18, bf16[4096,128]{1,0:T(8,128)(2,1)S(1)} %bitcast.20, bf16[4096,128]{1,0:T(8,128)(2,1)S(1)} %collective-permute-done.refs_1_, bf16[4096,128]{1,0:T(8,128)(2,1)S(1)} %bitcast.22, ...), custom_call_target="tpu_custom_call" | custom-call | flops 2147483648 | bytes 8388608 | tf_op jit(solution)/shard_map/hidden/pallas_call | solution.py:106
  96.6 0.1 multiply_convert_fusion.2
  96.7 0.1 pad_maximum_fusion
  96.8 54.5 %all-gather.8 = f16[8320,256]{1,0:T(8,128)(2,1)S(1)} all-gather(f16[520,256]{1,0:T(8,128)(2,1)S(1)} %pad_maximum_fusion), channel_id=4, replica_groups=mesh['tok'=16,'exp'=32] {'tok'}, dimensions={0}, use_global_device_ids=true | all-gather | bytes 4526080 | tf_op jit(solution)/shard_map/all_gather | solution.py:147
  151.4 1.0 multiply_convert_fusion.gathered
  152.4 0.2 copy-done.2
  152.6 1.8 down.1
  154.4 6.0 %collective-permute-start.3 = (bf16[512,256]{1,0:T(8,128)(2,1)S(1)}, bf16[512,256]{1,0:T(8,128)(2,1)S(1)}, u32[]{:S(2)}, u32[]{:S(2)}) collective-permute-start(bf16[512,256]{1,0:T(8,128)(2,1)S(1)} %get-tuple-element.34), channel_id=1, source_target_pairs={{0,1},{1,0},{2,3},{3,2},{4,5},{5,4},{6,7},{7,6},{8,9},{9,8},{10,11... | collective-permute-start | bytes 786440 | tf_op jit(solution)/shard_map/ppermute | solution.py:25
  160.3 1.1 collective-permute-done.3
  161.5 0.7 place.1
  162.1 21.2 %all_to_all.5.arrived = bf16[16,128,256]{2,1,0:T(8,128)(2,1)S(1)} all-to-all(bf16[16,128,256]{2,1,0:T(8,128)(2,1)S(1)} %place.1), channel_id=1, replica_groups={{0,2,4,6,8,10,12,14,16,18,20,22,24,26,28,30},{1,3,5,7,9,11,13,15,17,19,..., dimensions={0} | all-to-all | bytes 2097152 | tf_op jit(solution)/shard_map/all_to_all | solution.py:158
  183.4 1.5 arrive.1
  (15 shorter events, 0.2 us)
Async XLA Ops:
  34.1 57.7 %collective-permute-start = (bf16[4096,128]{1,0:T(8,128)(2,1)}, bf16[4096,128]{1,0:T(8,128)(2,1)S(1)}, u32[]{:S(2)}, u32[]{:S(2)}) collective-permute-start(bf16[4096,128]{1,0:T(8,128)(2,1)} %bitcast.19), channel_id=1, source_target_pairs={{0,2},{1,3},{2,0},{3,1},{4,6},{5,7},{6,4},{7,5},{8,10},{9,11},{10,... | collective-permute-start | bytes 3145736 | tf_op jit(solution)/shard_map/ppermute | solution.py:21
  37.5 54.3 %collective-permute-start.1 = (bf16[4096,128]{1,0:T(8,128)(2,1)}, bf16[4096,128]{1,0:T(8,128)(2,1)S(1)}, u32[]{:S(2)}, u32[]{:S(2)}) collective-permute-start(bf16[4096,128]{1,0:T(8,128)(2,1)} %bitcast.21), channel_id=1, source_target_pairs={{0,2},{1,3},{2,0},{3,1},{4,6},{5,7},{6,4},{7,5},{8,10},{9,11},{10,... | collective-permute-start | bytes 3145736 | tf_op jit(solution)/shard_map/ppermute | solution.py:21
  39.5 112.9 %collective-permute-start.2 = (bf16[2048,256]{1,0:T(8,128)(2,1)}, bf16[2048,256]{1,0:T(8,128)(2,1)S(1)}, u32[]{:S(2)}, u32[]{:S(2)}) collective-permute-start(bf16[2048,256]{1,0:T(8,128)(2,1)} %bitcast.23), channel_id=1, source_target_pairs={{0,2},{1,3},{2,0},{3,1},{4,6},{5,7},{6,4},{7,5},{8,10},{9,11},{10,... | collective-permute-start | bytes 3145736 | tf_op jit(solution)/shard_map/ppermute | solution.py:21
  92.1 1.2 copy-start
  92.1 1.5 copy-start.1
  151.3 1.2 copy-start.2
  151.3 1.2 copy-start.3
  154.4 7.1 %collective-permute-start.3 = (bf16[512,256]{1,0:T(8,128)(2,1)S(1)}, bf16[512,256]{1,0:T(8,128)(2,1)S(1)}, u32[]{:S(2)}, u32[]{:S(2)}) collective-permute-start(bf16[512,256]{1,0:T(8,128)(2,1)S(1)} %get-tuple-element.34), channel_id=1, source_target_pairs={{0,1},{1,0},{2,3},{3,2},{4,5},{5,4},{6,7},{7,6},{8,9},{9,8},{10,11... | collective-permute-start | bytes 786440 | tf_op jit(solution)/shard_map/ppermute | solution.py:25

commit v19 on v15

--- a/solution.py
+++ b/solution.py
@@ -129,9 +129,10 @@
         hidden_kernel, "hidden", facts, [gathered, own[0], far[0], own[1], far[1]],
         [array_of(rows, 2 * units), jax.ShapeDtypeStruct((1, 2 * units), jnp.float32)], flops,
     )
-    gathered = lax.all_gather(encode(hidden, largest)[None], "tok", tiled=True)
+    coded = jnp.stack([encode(part, largest) for part in jnp.split(hidden, 2)])
+    gathered = lax.all_gather(coded, "tok")
     kept, given = kernel_call(
-        down_kernel, "down", facts, [decode(gathered), gate_scale, own[2], far[2]],
+        down_kernel, "down", facts, [decode(gathered).reshape(DEPTH, rows, 2 * units), gate_scale, own[2], far[2]],
         [jax.ShapeDtypeStruct((rows, features), jnp.float32), array_of(rows, features)], flops // 2,
     )
 

time: 184 us -> 184 us (level)
  transfers between devices with their start and end apart: 4 -> 4, of which waited for: 1 -> 1; matrix products, arithmetic and copies ran while one was open for 1% -> 2% of each run, Pallas kernels for 2% -> 2%
where the time goes in v19:
time: 184 us; the launch traced here: 183 us
  blocking collectives  155 us (84%)
  starting transfers between devices  14.6 us (8%)
  other arithmetic  5.45 us (3%)
  Pallas kernels  5.33 us (3%)
    all_gather x1, blocking collectives, shards(): gathered = lax.all_gather(coded, 'tok')  55 us
    all_gather x1, blocking collectives, shards(): gathered = lax.all_gather(picked, ('tok', 'exp'), axis_index_groups=LINES)  49 us
    all_gather x1, blocking collectives, shards(): picked = lax.all_gather(coded, 'exp')[mine]  30 us
    all_to_all x1, blocking collectives, shards(): lax.all_to_all(outgoing, 'exp', 0, 0, axis_index_groups=SAME_CORE, tiled=...  21.5 us
    ppermute x3, starting transfers between devices, swap_across(): return lax.ppermute(value, 'exp', [(p, p ^ 2) for p in range(OWNERS)])  8.73 us
    ppermute x1, starting transfers between devices, swap_core(): return lax.ppermute(value, 'exp', [(p, p ^ 1) for p in range(OWNERS)])  5.91 us
    pallas_call x3, Pallas kernels, kernel_call(): pl.pallas_call(kernel, out_shape=outs, in_specs=[pl.BlockSpec(memory_spac...  5.33 us
  transfers between devices with their start and end apart: 4, of which 1 were waited for; matrix products, arithmetic and copies ran while one was open for 2% of the time, Pallas kernels for 2%

profile of v19, /device:TPU:1, one launch (start us, length us, event | category | flops | bytes accessed | tf_op | source)
XLA Modules:
  0.0 183.4 jit_solution(12610399293348403955)
XLA Ops:
  0.0 0.9 fusion.2
  0.9 0.9 fusion.3
  1.8 0.1 dynamic-slice_bitcast_fusion.1
  1.9 0.1 dynamic-slice_bitcast_fusion
  2.0 0.1 pad_add_fusion.facts
  2.1 30.0 %all-gather.6 = f16[4352,256]{1,0:T(8,128)(2,1)S(1)} all-gather(f16[136,256]{1,0:T(8,128)(2,1)S(1)} %pad_maximum_fusion.3), channel_id=2, replica_groups=mesh['tok'=16,'exp'=32] {'exp'}, dimensions={0}, use_global_device_ids=true | all-gather | bytes 2297856 | tf_op jit(solution)/shard_map/all_gather | solution.py:121
  32.1 0.6 gather_fusion
  32.7 3.4 %collective-permute-start = (bf16[4096,128]{1,0:T(8,128)(2,1)}, bf16[4096,128]{1,0:T(8,128)(2,1)S(1)}, u32[]{:S(2)}, u32[]{:S(2)}) collective-permute-start(bf16[4096,128]{1,0:T(8,128)(2,1)} %bitcast.24), channel_id=1, source_target_pairs={{0,2},{1,3},{2,0},{3,1},{4,6},{5,7},{6,4},{7,5},{8,10},{9,11},{10,... | collective-permute-start | bytes 3145736 | tf_op jit(solution)/shard_map/ppermute | solution.py:21
  36.2 1.9 %collective-permute-start.1 = (bf16[4096,128]{1,0:T(8,128)(2,1)}, bf16[4096,128]{1,0:T(8,128)(2,1)S(1)}, u32[]{:S(2)}, u32[]{:S(2)}) collective-permute-start(bf16[4096,128]{1,0:T(8,128)(2,1)} %bitcast.26), channel_id=1, source_target_pairs={{0,2},{1,3},{2,0},{3,1},{4,6},{5,7},{6,4},{7,5},{8,10},{9,11},{10,... | collective-permute-start | bytes 3145736 | tf_op jit(solution)/shard_map/ppermute | solution.py:21
  38.1 3.4 %collective-permute-start.2 = (bf16[2048,256]{1,0:T(8,128)(2,1)}, bf16[2048,256]{1,0:T(8,128)(2,1)S(1)}, u32[]{:S(2)}, u32[]{:S(2)}) collective-permute-start(bf16[2048,256]{1,0:T(8,128)(2,1)} %bitcast.28), channel_id=1, source_target_pairs={{0,2},{1,3},{2,0},{3,1},{4,6},{5,7},{6,4},{7,5},{8,10},{9,11},{10,... | collective-permute-start | bytes 3145736 | tf_op jit(solution)/shard_map/ppermute | solution.py:21
  41.5 49.0 %all-gather.7 = f16[64,136,256]{2,1,0:T(8,128)(2,1)S(1)} all-gather(f16[2,136,256]{2,1,0:T(8,128)(2,1)S(1)} %gather_fusion), channel_id=3, replica_groups={{0,1,32,33,64,65,96,97,128,129,160,161,192,193,224,225,256,257,288,289,..., dimensions={0}, use_global_device_ids=true | all-gather | bytes 4595712 | tf_op jit(solution)/shard_map/all_gather | solution.py:124
  90.5 0.0 collective-permute-done.refs_1_
  90.5 0.2 slice_reduce_fusion
  90.7 0.0 copy-start.1
  90.7 0.0 copy-start.2
  90.7 0.1 copy.10
  90.8 1.2 multiply_convert_fusion.1
  92.0 0.2 copy-done.2
  92.2 2.9 %hidden.1 = (bf16[512,256]{1,0:T(8,128)(2,1)S(1)}, f32[1,256]{1,0:T(1,128)S(1)}) custom-call(s32[7]{0:T(128)S(1)} %pad_add_fusion.facts, bf16[16,512,256]{2,1,0:T(8,128)(2,1)S(1)} %bitcast.23, bf16[4096,128]{1,0:T(8,128)(2,1)S(1)} %bitcast.25, bf16[4096,128]{1,0:T(8,128)(2,1)S(1)} %collective-permute-done.refs_1_, bf16[4096,128]{1,0:T(8,128)(2,1)S(1)} %bitcast.27, ...), custom_call_target="tpu_custom_call" | custom-call | flops 2147483648 | bytes 8388608 | tf_op jit(solution)/shard_map/hidden/pallas_call | solution.py:92
  95.2 0.1 multiply_convert_fusion.3
  95.3 0.1 fusion
  95.3 0.1 pad_maximum_fusion
  95.4 55.0 %all-gather.8 = f16[32,264,256]{2,1,0:T(8,128)(2,1)S(1)} all-gather(f16[2,264,256]{2,1,0:T(8,128)(2,1)S(1)} %pad_maximum_fusion), channel_id=4, replica_groups=mesh['tok'=16,'exp'=32] {'tok'}, dimensions={0}, use_global_device_ids=true | all-gather | bytes 4595712 | tf_op jit(solution)/shard_map/all_gather | solution.py:133
  150.4 0.1 slice_reduce_fusion.1
  150.5 1.0 multiply_convert_fusion
  151.6 0.0 copy-done.3
  151.6 1.8 down.1
  153.4 5.9 %collective-permute-start.3 = (bf16[512,256]{1,0:T(8,128)(2,1)S(1)}, bf16[512,256]{1,0:T(8,128)(2,1)S(1)}, u32[]{:S(2)}, u32[]{:S(2)}) collective-permute-start(bf16[512,256]{1,0:T(8,128)(2,1)S(1)} %get-tuple-element.32), channel_id=1, source_target_pairs={{0,1},{1,0},{2,3},{3,2},{4,5},{5,4},{6,7},{7,6},{8,9},{9,8},{10,11... | collective-permute-start | bytes 786440 | tf_op jit(solution)/shard_map/ppermute | solution.py:25
  159.3 1.1 collective-permute-done.3
  160.5 0.7 place.1
  161.1 21.5 %all_to_all.5 = bf16[16,128,256]{2,1,0:T(8,128)(2,1)S(1)} all-to-all(bf16[16,128,256]{2,1,0:T(8,128)(2,1)S(1)} %place.1), channel_id=1, replica_groups={{0,2,4,6,8,10,12,14,16,18,20,22,24,26,28,30},{1,3,5,7,9,11,13,15,17,19,..., dimensions={0} | all-to-all | bytes 2097152 | tf_op jit(solution)/shard_map/all_to_all | solution.py:144
  182.6 0.8 reduce_sum.12
  (19 shorter events, 0.2 us)
Async XLA Ops:
  0.0 1.8 copy-start
  32.7 57.7 %collective-permute-start = (bf16[4096,128]{1,0:T(8,128)(2,1)}, bf16[4096,128]{1,0:T(8,128)(2,1)S(1)}, u32[]{:S(2)}, u32[]{:S(2)}) collective-permute-start(bf16[4096,128]{1,0:T(8,128)(2,1)} %bitcast.24), channel_id=1, source_target_pairs={{0,2},{1,3},{2,0},{3,1},{4,6},{5,7},{6,4},{7,5},{8,10},{9,11},{10,... | collective-permute-start | bytes 3145736 | tf_op jit(solution)/shard_map/ppermute | solution.py:21
  36.2 54.3 %collective-permute-start.1 = (bf16[4096,128]{1,0:T(8,128)(2,1)}, bf16[4096,128]{1,0:T(8,128)(2,1)S(1)}, u32[]{:S(2)}, u32[]{:S(2)}) collective-permute-start(bf16[4096,128]{1,0:T(8,128)(2,1)} %bitcast.26), channel_id=1, source_target_pairs={{0,2},{1,3},{2,0},{3,1},{4,6},{5,7},{6,4},{7,5},{8,10},{9,11},{10,... | collective-permute-start | bytes 3145736 | tf_op jit(solution)/shard_map/ppermute | solution.py:21
  38.1 113.5 %collective-permute-start.2 = (bf16[2048,256]{1,0:T(8,128)(2,1)}, bf16[2048,256]{1,0:T(8,128)(2,1)S(1)}, u32[]{:S(2)}, u32[]{:S(2)}) collective-permute-start(bf16[2048,256]{1,0:T(8,128)(2,1)} %bitcast.28), channel_id=1, source_target_pairs={{0,2},{1,3},{2,0},{3,1},{4,6},{5,7},{6,4},{7,5},{8,10},{9,11},{10,... | collective-permute-start | bytes 3145736 | tf_op jit(solution)/shard_map/ppermute | solution.py:21
  90.7 1.3 copy-start.1
  90.7 1.5 copy-start.2
  150.4 1.2 copy-start.3
  150.4 1.2 copy-start.4
  153.4 7.1 %collective-permute-start.3 = (bf16[512,256]{1,0:T(8,128)(2,1)S(1)}, bf16[512,256]{1,0:T(8,128)(2,1)S(1)}, u32[]{:S(2)}, u32[]{:S(2)}) collective-permute-start(bf16[512,256]{1,0:T(8,128)(2,1)S(1)} %get-tuple-element.32), channel_id=1, source_target_pairs={{0,1},{1,0},{2,3},{3,2},{4,5},{5,4},{6,7},{7,6},{8,9},{9,8},{10,11... | collective-permute-start | bytes 786440 | tf_op jit(solution)/shard_map/ppermute | solution.py:25
